TPU v7x, 128 devices: a whole 4x4x4 slice. The times are simulated.
128 devices in a mesh: fsdp: 16 (over y_lo, z, core), tp: 8 (over x, y_hi).
Axes of the slice: x: 4, y: 4 (y_hi: 2, y_lo: 2; y = y_hi * 2 + y_lo), z: 4, core: 2. Of those that a mesh axis runs over, the one named last changes fastest.
Arguments:
- hidden: bfloat16 [2, 1280, 8192], P(None, 'fsdp'), may hold values from -6 to 6
- qkv_rows: float32 [8192, 10240], P(('fsdp', 'tp')), may hold values from -0.0625 to 0.0625
- o_rows: float32 [8192, 8192], P(('fsdp', 'tp')), may hold values from -0.0625 to 0.0625
- block_owner: int32 [2, 128], replicated, may hold values from 0 to 127, each once within a row
- cache: bfloat16 [2, 1280, 256, 1024], P(None, 'fsdp', None, 'tp'), may hold values from -240 to 240
- lengths: int32 [1280], P('fsdp'), may hold values from 32 to 256, as said below
Outputs:
- attended: bfloat16 [2, 1280, 8192], P(None, 'fsdp', 'tp')
Inputs may be any that keep to these rules, and one draw needn't show every extreme that they name: Each row of block_owner is a permutation. `lengths`: the first row of each aligned block of 80 rows holds exactly 256 positions.
All inputs are finite; a program needn't handle non-finite values.
Results may differ from a plain program's by a relative error of at most 0.017.
Values may be sent and summed in bfloat16 or wider, within the bound.
No kernel may reach another device: no remote copies, remote signals or barrier semaphores. Data moves between devices by JAX's collectives and lax.ppermute only.
A program may use at most 192 MiB of HBM per device.

v0:
```python
import math

import jax
import jax.numpy as jnp
from jax import lax
from jax.sharding import PartitionSpec as P

HQ = 64
HK = 8
HD = 128


def by_group(array, sections, groups):
    pieces = []
    begin = 0
    for width in sections:
        pieces.append(
            array[:, begin : begin + width].reshape(array.shape[0], groups, width // groups)
        )
        begin = begin + width
    return jnp.concatenate(pieces, axis=2)


def flatten(received):
    return received.reshape(received.shape[0], received.shape[2])


def rotary(values, position):
    half = HD // 2
    freq = 1000000.0 ** (-jnp.arange(half, dtype=jnp.float32) * 2.0 / HD)
    angle = position.astype(jnp.float32)[..., None, None] * freq
    cosine = jnp.cos(angle)
    sine = jnp.sin(angle)
    first = values[..., :half]
    second = values[..., half:]
    return jnp.concatenate(
        [first * cosine - second * sine, second * cosine + first * sine], axis=-1
    )


def attention(proj, cache, lengths, groups):
    rows = lengths.shape[0]
    heads = HQ // groups
    kv_heads = HK // groups
    query_cols = heads * HD
    kv_cols = kv_heads * HD
    proj = proj.reshape(2, rows, -1)
    position = lengths[None, :] + jnp.arange(2, dtype=jnp.int32)[:, None]
    query = rotary(proj[..., :query_cols].reshape(2, rows, heads, HD), position).astype(
        jnp.bfloat16
    )
    new_keys = rotary(
        proj[..., query_cols : query_cols + kv_cols].reshape(2, rows, kv_heads, HD), position
    ).astype(jnp.bfloat16)
    new_vals = proj[..., query_cols + kv_cols :].reshape(2, rows, kv_heads, HD).astype(jnp.bfloat16)
    query = query.reshape(2, rows, kv_heads, HQ // HK, HD)
    keys = cache[0].reshape(rows, -1, kv_heads, HD)
    vals = cache[1].reshape(rows, -1, kv_heads, HD)
    factor = 1.0 / math.sqrt(HD)
    old = jnp.einsum("srgjd,rpgd->srgjp", query, keys, preferred_element_type=jnp.float32) * factor
    fresh = (
        jnp.einsum("srgjd,trgd->srgjt", query, new_keys, preferred_element_type=jnp.float32)
        * factor
    )
    live = jnp.arange(keys.shape[1])[None, :] < lengths[:, None]
    old = jnp.where(live[None, :, None, None, :], old, -jnp.inf)
    seen = jnp.arange(2)[None, :] <= jnp.arange(2)[:, None]
    fresh = jnp.where(seen[:, None, None, None, :], fresh, -jnp.inf)
    top = jnp.maximum(jnp.max(old, -1), jnp.max(fresh, -1))[..., None]
    old_w = jnp.exp(old - top)
    fresh_w = jnp.exp(fresh - top)
    total = jnp.sum(old_w, -1, keepdims=True) + jnp.sum(fresh_w, -1, keepdims=True)
    old_p = (old_w / total).astype(jnp.bfloat16)
    fresh_p = (fresh_w / total).astype(jnp.bfloat16)
    mixed = jnp.einsum("srgjp,rpgd->srgjd", old_p, vals, preferred_element_type=jnp.float32)
    mixed = mixed + jnp.einsum(
        "srgjt,trgd->srgjd", fresh_p, new_vals, preferred_element_type=jnp.float32
    )
    return mixed.astype(jnp.bfloat16).reshape(2 * rows, query_cols)


def project_back(mixed, weight):
    return lax.dot_general(
        mixed, weight, (((1,), (1,)), ((), ())), preferred_element_type=jnp.float32
    )


def body(hidden, qkv_rows, o_rows, block_owner, cache, lengths):
    groups = lax.axis_size("tp")
    steps, rows, width = hidden.shape
    owned = qkv_rows.shape[0]
    blocks = width // owned
    query_cols = HQ * HD
    kv_cols = HK * HD
    qkv_copy = by_group(qkv_rows.astype(jnp.bfloat16), (query_cols, kv_cols, kv_cols), groups)
    out_copy = o_rows.astype(jnp.bfloat16).reshape(owned, groups, query_cols // groups)
    flat = hidden.reshape(steps * rows, width)
    shuffled = flat.reshape(steps * rows, blocks, owned)[:, block_owner[0], :].reshape(
        steps * rows, width
    )
    got = (
        lax.all_to_all(qkv_copy, "tp", split_axis=1, concat_axis=0, tiled=True),
        lax.all_to_all(out_copy, "tp", split_axis=1, concat_axis=0, tiled=True),
    )
    whole = (
        lax.all_gather(flatten(got[0]), "fsdp", axis=0, tiled=True),
        lax.all_gather(flatten(got[1]), "fsdp", axis=0, tiled=True),
    )
    proj = jnp.dot(shuffled, whole[0], preferred_element_type=jnp.float32)
    mixed = attention(proj, cache, lengths, groups)
    outcome = project_back(mixed, whole[1])
    pieces = outcome.reshape(steps * rows, blocks, owned)
    ordered = (
        jnp.zeros_like(pieces).at[:, block_owner[1], :].set(pieces).reshape(steps, rows, width)
    )
    summed = lax.psum_scatter(ordered.astype(jnp.bfloat16), "tp", scatter_dimension=2, tiled=True)
    return summed


def solution(mesh):
    in_specs = (
        P(None, "fsdp", None),
        P(("fsdp", "tp"), None),
        P(("fsdp", "tp"), None),
        P(),
        P(None, "fsdp", None, "tp"),
        P("fsdp"),
    )
    out_specs = P(None, "fsdp", "tp")
    return jax.shard_map(body, mesh=mesh, in_specs=in_specs, out_specs=out_specs, check_vma=False)
```

profile of v0, /device:TPU:0, one launch (start us, length us, event | category | flops | bytes accessed | tf_op | source)
XLA Modules:
  0.0 421.7 jit_solution(11004878006180517672)
XLA Ops:
  6.5 1.9 convert_element_type.45
  8.7 0.1 pad_maximum_fusion
  8.8 26.6 %all_to_all.30 = bf16[64,8,1280]{2,0,1:T(8,128)(2,1)} all-to-all(bf16[64,8,1280]{2,0,1:T(8,128)(2,1)S(1)} %pad_maximum_fusion), channel_id=1, replica_groups=mesh['fsdp'=16,'tp'=8] {'tp'}, dimensions={1} | all-to-all | bytes 2621440 | tf_op jit(solution)/shard_map/all_to_all | solution.py:102
  35.5 1.8 convert_element_type.52
  37.4 20.1 %all_to_all.31 = bf16[64,8,1024]{2,0,1:T(8,128)(2,1)} all-to-all(bf16[64,8,1024]{2,0,1:T(8,128)(2,1)S(1)} %bitcast.127), channel_id=1, replica_groups=mesh['fsdp'=16,'tp'=8] {'tp'}, dimensions={1} | all-to-all | bytes 2097152 | tf_op jit(solution)/shard_map/all_to_all | solution.py:103
  57.6 6.7 %reshape_reshape.3 = bf16[160,128,64]{2,1,0:T(8,128)(2,1)} reshape(bf16[2,80,8192]{2,1,0:T(8,128)(2,1)S(1)} %copy-done) | data formatting | bytes 5242880 | tf_op jit(solution)/shard_map/reshape;reshape | solution.py:98
  64.3 8.8 %copy.61 = bf16[160,128,64]{0,2,1:T(8,128)(2,1)} copy(bf16[160,128,64]{2,1,0:T(8,128)(2,1)} %reshape_reshape.3) | data formatting | bytes 5242880 | tf_op jit(solution)/shard_map/reshape;reshape | solution.py:98
  73.1 5.2 %gather_fusion = bf16[128,160,64]{1,2,0:T(8,128)(2,1)} fusion(bf16[160,128,64]{0,2,1:T(8,128)(2,1)} %copy.61, s32[1024]{0:T(1024)S(1)} %pad_clamp_fusion), kind=kCustom, calls=%fused_computation | custom fusion | bytes 5243392 | tf_op jit(solution)/shard_map/gather | solution.py:98
  78.3 7.5 %reshape.291 = bf16[2,80,8192]{1,0,2:T(2,128)(2,1)} reshape(bf16[160,128,64]{0,2,1:T(8,128)(2,1)} %bitcast.120) | data formatting | bytes 5242880 | tf_op jit(solution)/shard_map/dot_general | solution.py:109
  86.1 1.3 multiply_cosine_fusion.1
  87.4 65.1 %all-gather.3.cloned.1.call-done = bf16[8192,1280]{1,0:T(8,128)(2,1)} async-done(((bf16[512,1280]{1,0:T(8,128)(2,1)}), bf16[8192,1280]{1,0:T(8,128)(2,1)}) %all-gather.3.cloned.1.call-update) | async-done | bytes 20971536 | tf_op jit(solution)/shard_map/all_gather | solution.py:106
  152.5 10.6 %fusion = f32[2,80,1280]{2,1,0:T(8,128)S(1)} fusion(bf16[8192,1280]{1,0:T(8,128)(2,1)} %all-gather.3.cloned.1.call-done, bf16[2,80,8192]{1,0,2:T(2,128)(2,1)} %reshape.291), kind=kOutput, calls=%fused_computation.2 | convolution fusion | flops 3355443200 | bytes 24412160 | tf_op jit(solution)/shard_map/dot_general | solution.py:109
  163.2 0.1 copy.92
  163.3 0.4 fusion.49
  163.8 0.2 fusion.54
  164.0 0.2 subtract_convert_fusion
  164.2 1.7 fusion.55
  165.9 4.3 %bitcast_reduce_fusion = (f32[2,80,8]{2,0,1:T(2,128)S(1)}, f32[80,1,256,2,8]{2,4,3,0,1:T(8,128)S(1)}) fusion(bf16[2,80,256,128]{3,2,1,0:T(8,128)(2,1)} %param.10, bf16[2,80,8,64]{3,2,0,1:T(8,128)(2,1)S(1)} %get-tuple-element.6, bf16[2,80,8,64]{3,2,0,1:T(8,128)(2,1)S(1)} %get-tuple-element.5, pred[80,256]{1,0:T(8,128)(4,1)S(1)} %iota_compare_fusion), kind=kOutput, calls=%fused_computation.18 | convolution fusion | flops 85523200 | bytes 6906880 | tf_op jit(solution)/shard_map/srgjd,rpgd->srgjp/dot_general | solution.py:60
  170.3 0.3 fusion.38
  170.6 0.5 fusion.29
  171.2 1.1 fusion.24
  172.3 0.4 fusion.28
  172.7 0.1 reshape.290
  172.9 75.5 %all-gather.5.cloned.1.call-done = bf16[8192,1024]{1,0:T(8,128)(2,1)} async-done(((bf16[512,1024]{1,0:T(8,128)(2,1)}), bf16[8192,1024]{1,0:T(8,128)(2,1)}) %all-gather.5.cloned.1.call-update) | async-done | bytes 16777232 | tf_op jit(solution)/shard_map/all_gather | solution.py:107
  248.4 29.9 %fusion.11 = f32[128,160,64]{0,1,2:T(8,128)} fusion(bf16[160,1024,1]{1,0,2:T(8,128)(2,1)S(1)} %reshape.290, bf16[128,64,1024]{2,1,0:T(8,128)(2,1)} %bitcast.131), kind=kOutput, calls=%fused_computation.13 | convolution fusion | flops 2684354560 | bytes 22347776 | tf_op jit(solution)/shard_map/dot_general | solution.py:83
  278.4 8.9 %copy.74 = f32[128,160,64]{1,2,0:T(8,128)} copy(f32[128,160,64]{0,1,2:T(8,128)} %fusion.11) | data formatting | bytes 10485760 | tf_op jit(solution)/shard_map/dot_general | solution.py:83
  287.3 4.3 %broadcast_in_dim.22 = f32[160,128,64]{0,2,1:T(8,128)} broadcast(f32[]{:T(128)} %constant.7.clone.1), dimensions={} | broadcast | bytes 5242884 | tf_op jit(solution)/shard_map/broadcast_in_dim | solution.py:114
  291.6 23.5 %scatter_fusion = f32[160,128,64]{0,2,1:T(8,128)} fusion(f32[160,128,64]{0,2,1:T(8,128)} %broadcast_in_dim.22, s32[128]{0:T(128)S(1)} %get-tuple-element.16, f32[128,160,64]{1,2,0:T(8,128)} %copy.74), kind=kCustom, calls=%fused_computation.1 | custom fusion | bytes 15729152 | tf_op jit(solution)/shard_map/scatter | solution.py:114
  315.1 8.8 %copy.75 = bf16[160,128,64]{1,2,0:T(8,128)(2,1)S(1)} copy(f32[160,128,64]{0,2,1:T(8,128)} %scatter_fusion) | data formatting | bytes 7864320 | tf_op jit(solution)/shard_map/scatter | solution.py:114
  323.9 4.1 copy.76
  328.0 8.1 %convert_element_type.54 = bf16[2,80,8192]{2,1,0:T(8,128)(2,1)} reshape(bf16[160,128,64]{2,1,0:T(8,128)(2,1)} %copy.76) | data formatting | bytes 5242880 | tf_op jit(solution)/shard_map/convert_element_type | solution.py:116
  336.1 79.0 %reduce-scatter.2.cloned.1.call-done = bf16[2,80,1024]{2,1,0:T(8,128)(2,1)} async-done(((bf16[2,80,8192]{2,1,0:T(8,128)(2,1)}), bf16[2,80,1024]{2,1,0:T(8,128)(2,1)}) %reduce-scatter.2.cloned.1.call-update) | async-done | bytes 327696 | tf_op jit(solution)/shard_map/reduce_scatter | solution.py:116
  (38 shorter events, 1.0 us)
Async XLA Ops:
  6.5 145.9 %all-gather.3.cloned.1.call-start = ((), (), s32[]{:S(2)}) async-start(), calls=%async_computation.3 | async-start | bytes 22282240 | tf_op jit(solution)/shard_map/all_gather | solution.py:106
  35.4 22.2 %copy-start = (bf16[2,80,8192]{2,1,0:T(8,128)(2,1)S(1)}, bf16[2,80,8192]{2,1,0:T(8,128)(2,1)}, u32[]{:S(2)}) copy-start(bf16[2,80,8192]{2,1,0:T(8,128)(2,1)} %param.6) | copy-start | bytes 7864324
  35.4 213.0 %all-gather.5.cloned.1.call-start = ((), (), s32[]{:S(2)}) async-start(), calls=%async_computation.4 | async-start | bytes 17825792 | tf_op jit(solution)/shard_map/all_gather | solution.py:107
  57.6 357.6 %reduce-scatter.2.cloned.1.call-start = ((), (), s32[]{:S(2)}) async-start(), calls=%async_computation.5 | async-start | bytes 2949120 | tf_op jit(solution)/shard_map/reduce_scatter | solution.py:116
  64.3 8.8 %copy-start.1 = (s32[2,128]{1,0:T(2,128)S(1)}, s32[2,128]{1,0:T(2,128)}, u32[]{:S(2)}) copy-start(s32[2,128]{1,0:T(2,128)} %param.9) | copy-start | bytes 3076
  78.3 7.5 %copy-start.2 = (s32[80]{0:T(128)S(1)}, s32[80]{0:T(128)}, u32[]{:S(2)}) copy-start(s32[80]{0:T(128)} %param.11) | copy-start | bytes 964
  152.5 18.7 %slice-start = ((s8[10485760]{0:T(1024)(128)(4,1)}), s8[4194304]{0:T(1024)(128)(4,1)S(1)}, s32[]{:S(2)}) async-start(s8[10485760]{0:T(1024)(128)(4,1)} %bitcast.128), calls=%async_computation.6 | async-start | bytes 8388608
  152.5 18.7 %slice-start.1 = ((s8[10485760]{0:T(1024)(128)(4,1)}), s8[4194304]{0:T(1024)(128)(4,1)S(1)}, s32[]{:S(2)}) async-start(s8[10485760]{0:T(1024)(128)(4,1)} %bitcast.128), calls=%async_computation.7 | async-start | bytes 8388608
  163.8 7.4 %slice-start.2 = ((s8[10485760]{0:T(1024)(128)(4,1)}), s8[2097152]{0:T(1024)(128)(4,1)S(1)}, s32[]{:S(2)}) async-start(s8[10485760]{0:T(1024)(128)(4,1)} %bitcast.128), calls=%async_computation.8 | async-start | bytes 4194304
Sparse Core Ops, SparseCore 0:
  35.5 116.8 all-gather.2
  154.2 94.2 all-gather.4
  336.2 78.8 reduce-scatter.1
where the time goes:
time: 423 us; the launch traced here: 422 us
  waiting for transfers between devices  220 us (52%)
  local copies, waits for them, and re-layouts  86.9 us (21%)
  matrix products  48 us (11%)
  blocking collectives  46.7 us (11%)
  between operations  13.4 us (3%)
  other arithmetic  6.86 us (2%)
    reduce_scatter x1, waiting for transfers between devices, body(): lax.psum_scatter(ordered.astype(jnp.bfloat16), 'tp', scatter_dimension=2,...  79 us
    all_gather x1, waiting for transfers between devices, body(): lax.all_gather(flatten(got[1]), 'fsdp', axis=0, tiled=True)  75.5 us
    all_gather x1, waiting for transfers between devices, body(): lax.all_gather(flatten(got[0]), 'fsdp', axis=0, tiled=True)  65.1 us
    scatter x2, local copies, waits for them, and re-layouts, body(): jnp.zeros_like(pieces).at[:, block_owner[1], :].set(pieces)  32.3 us
    dot_general x1, matrix products, project_back(): lax.dot_general(mixed, weight, (((1,), (1,)), ((), ())), preferred_elemen...  29.9 us
    all_to_all x1, blocking collectives, body(): lax.all_to_all(qkv_copy, 'tp', split_axis=1, concat_axis=0, tiled=True)  26.6 us
    all_to_all x1, blocking collectives, body(): lax.all_to_all(out_copy, 'tp', split_axis=1, concat_axis=0, tiled=True)  20.1 us
    another operation x2, local copies, waits for them, and re-layouts, body(): flat.reshape(steps * rows, blocks, owned)[:, block_owner[0], :]  15.4 us
  transfers between devices with their start and end apart: 3, of which 3 were waited for; matrix products, arithmetic and copies ran while one was open for 12% of the time, Pallas kernels for 0%

commit v1 on v0

--- a/solution.py
+++ b/solution.py
@@ -1,13 +1,27 @@
+import functools
 import math
 
 import jax
 import jax.numpy as jnp
 from jax import lax
+from jax.experimental import pallas as pl
+from jax.experimental.pallas import tpu as pltpu
 from jax.sharding import PartitionSpec as P
 
 HQ = 64
 HK = 8
 HD = 128
+NZ = 4
+MIB = 1024 * 1024
+
+
+def z_shift(value, k):
+    pairs = [(f, (f // 8) * 8 + ((f // 2 + k) % NZ) * 2 + f % 2) for f in range(16)]
+    return lax.ppermute(value, "fsdp", pairs)
+
+
+def flip(value, bit):
+    return lax.ppermute(value, "fsdp", [(f, f ^ bit) for f in range(16)])
 
 
 def by_group(array, sections, groups):
@@ -23,6 +37,168 @@
 
 def flatten(received):
     return received.reshape(received.shape[0], received.shape[2])
+
+
+def shuffle_kernel(owner_ref, hidden_ref, *out_refs):
+    f = lax.axis_index("fsdp")
+    y_lo, z, core = f // 8, lax.rem(f // 2, 4), lax.rem(f, 2)
+    rows = hidden_ref.shape[0]
+    low = lax.broadcasted_iota(jnp.int32, (rows, 128), 1) < 64
+
+    for k, out_ref in enumerate(out_refs):
+        zz = lax.rem(z + k, 4)
+
+        def step(n, carry, zz=zz, out_ref=out_ref):
+            q, p = n // 4, lax.rem(n, 4)
+            yy = lax.rem(y_lo + lax.rem(q, 2), 2)
+            cc = lax.rem(core + q // 2, 2)
+            i = yy * 64 + zz * 16 + cc * 8 + 2 * p
+            s0, s1 = owner_ref[0, i], owner_ref[0, i + 1]
+            a = hidden_ref[:, pl.ds(pl.multiple_of((s0 // 2) * 128, 128), 128)].astype(jnp.float32)
+            b = hidden_ref[:, pl.ds(pl.multiple_of((s1 // 2) * 128, 128), 128)].astype(jnp.float32)
+            a = pltpu.roll(a, 64 * lax.rem(s0, 2), 1)
+            b = pltpu.roll(b, 64 * (1 - lax.rem(s1, 2)), 1)
+            out_ref[:, pl.ds(pl.multiple_of(n * 128, 128), 128)] = jnp.where(low, a, b).astype(
+                jnp.bfloat16
+            )
+            return carry
+
+        lax.fori_loop(0, 16, step, 0)
+
+
+def shuffle(hidden, block_owner):
+    rows, width = hidden.shape
+    part = jax.ShapeDtypeStruct((rows, width // NZ), jnp.bfloat16)
+    return pl.pallas_call(
+        shuffle_kernel,
+        out_shape=[part] * NZ,
+        in_specs=[
+            pl.BlockSpec(memory_space=pltpu.SMEM),
+            pl.BlockSpec(memory_space=pltpu.VMEM),
+        ],
+        out_specs=[pl.BlockSpec(memory_space=pltpu.VMEM)] * NZ,
+        compiler_params=pltpu.CompilerParams(vmem_limit_bytes=24 * MIB),
+        cost_estimate=pl.CostEstimate(
+            flops=rows * width * 8, bytes_accessed=4 * rows * width, transcendentals=0
+        ),
+        name="shuffle",
+    )(block_owner, hidden)
+
+
+def partial_kernel(h0, h1, h2, h3, w0, w1, w2, w3, p0, p1, p2, p3, stacked):
+    rows = h0.shape[0]
+
+    @pl.when(pl.program_id(0) == 0)
+    def _():
+        for k, h in enumerate((h0, h1, h2, h3)):
+            stacked[pl.ds(k * rows, rows), :] = h[...]
+
+    depth = w0.shape[0]
+    total = jnp.zeros((NZ * rows, w0.shape[1]), jnp.float32)
+    for q, w in enumerate((w0, w1, w2, w3)):
+        total = total + jnp.dot(
+            stacked[:, q * depth : (q + 1) * depth], w[...], preferred_element_type=jnp.float32
+        )
+    for k, out in enumerate((p0, p1, p2, p3)):
+        out[...] = total[k * rows : (k + 1) * rows].astype(out.dtype)
+
+
+def partials(parts, weights):
+    rows, width = parts[0].shape
+    depth, cols = weights[0].shape
+    tile = 256
+    return pl.pallas_call(
+        partial_kernel,
+        grid=(cols // tile,),
+        out_shape=[jax.ShapeDtypeStruct((rows, cols), jnp.float32)]
+        + [jax.ShapeDtypeStruct((rows, cols), jnp.bfloat16)] * 3,
+        in_specs=[pl.BlockSpec((rows, width), lambda j: (0, 0))] * NZ
+        + [pl.BlockSpec((depth, tile), lambda j: (0, j))] * NZ,
+        out_specs=[pl.BlockSpec((rows, tile), lambda j: (0, j))] * NZ,
+        scratch_shapes=[pltpu.VMEM((NZ * rows, width), jnp.bfloat16)],
+        compiler_params=pltpu.CompilerParams(vmem_limit_bytes=32 * MIB),
+        cost_estimate=pl.CostEstimate(
+            flops=2 * NZ * rows * width * cols,
+            bytes_accessed=2 * (NZ * rows * width + width * cols + NZ * rows * cols),
+            transcendentals=0,
+        ),
+        name="partials",
+    )(*parts, *weights)
+
+
+def back_kernel(blocks, owned, owner_ref, mixed_ref, weight_ref, out_ref, place, held, sems):
+    t = pl.program_id(0)
+    steps = pl.num_programs(0)
+
+    @pl.when(t == 0)
+    def _():
+        def note(i, carry):
+            place[owner_ref[1, i]] = i
+            return carry
+
+        lax.fori_loop(0, owner_ref.shape[1], note, 0)
+
+    def fetch(step, slot):
+        def one(j, carry):
+            source = place[step * blocks + j]
+            pltpu.make_async_copy(
+                weight_ref.at[pl.ds(pl.multiple_of(source * owned, owned), owned)],
+                held.at[slot, pl.ds(pl.multiple_of(j * owned, owned), owned)],
+                sems.at[slot],
+            ).start()
+            return carry
+
+        lax.fori_loop(0, blocks, one, 0)
+
+    slot = lax.rem(t, 2)
+
+    @pl.when(t == 0)
+    def _():
+        fetch(t, slot)
+
+    @pl.when(t + 1 < steps)
+    def _():
+        fetch(t + 1, 1 - slot)
+
+    pltpu.make_async_copy(
+        weight_ref.at[pl.ds(0, blocks * owned)], held.at[slot], sems.at[slot]
+    ).wait()
+    out_ref[0] = lax.dot_general(
+        mixed_ref[...],
+        held[slot],
+        (((1,), (1,)), ((), ())),
+        preferred_element_type=jnp.float32,
+    ).astype(out_ref.dtype)
+
+
+def project_back(mixed, weight, block_owner, groups):
+    rows, depth = mixed.shape
+    width = weight.shape[0]
+    total = block_owner.shape[1]
+    blocks, owned = total // groups, width // total
+    return pl.pallas_call(
+        functools.partial(back_kernel, blocks, owned),
+        grid=(groups,),
+        out_shape=jax.ShapeDtypeStruct((groups, rows, width // groups), jnp.bfloat16),
+        in_specs=[
+            pl.BlockSpec(memory_space=pltpu.SMEM),
+            pl.BlockSpec((rows, depth), lambda t: (0, 0)),
+            pl.BlockSpec(memory_space=pltpu.HBM),
+        ],
+        out_specs=pl.BlockSpec((1, rows, width // groups), lambda t: (t, 0, 0)),
+        scratch_shapes=[
+            pltpu.SMEM((total,), jnp.int32),
+            pltpu.VMEM((2, width // groups, depth), jnp.bfloat16),
+            pltpu.SemaphoreType.DMA((2,)),
+        ],
+        compiler_params=pltpu.CompilerParams(vmem_limit_bytes=54 * MIB),
+        cost_estimate=pl.CostEstimate(
+            flops=2 * rows * depth * width,
+            bytes_accessed=2 * (rows * depth + depth * width + rows * width),
+            transcendentals=0,
+        ),
+        name="project_back",
+    )(block_owner, mixed, weight)
 
 
 def rotary(values, position):
@@ -79,42 +255,35 @@
     return mixed.astype(jnp.bfloat16).reshape(2 * rows, query_cols)
 
 
-def project_back(mixed, weight):
-    return lax.dot_general(
-        mixed, weight, (((1,), (1,)), ((), ())), preferred_element_type=jnp.float32
-    )
-
-
 def body(hidden, qkv_rows, o_rows, block_owner, cache, lengths):
     groups = lax.axis_size("tp")
     steps, rows, width = hidden.shape
     owned = qkv_rows.shape[0]
-    blocks = width // owned
     query_cols = HQ * HD
     kv_cols = HK * HD
     qkv_copy = by_group(qkv_rows.astype(jnp.bfloat16), (query_cols, kv_cols, kv_cols), groups)
     out_copy = o_rows.astype(jnp.bfloat16).reshape(owned, groups, query_cols // groups)
-    flat = hidden.reshape(steps * rows, width)
-    shuffled = flat.reshape(steps * rows, blocks, owned)[:, block_owner[0], :].reshape(
-        steps * rows, width
-    )
-    got = (
-        lax.all_to_all(qkv_copy, "tp", split_axis=1, concat_axis=0, tiled=True),
-        lax.all_to_all(out_copy, "tp", split_axis=1, concat_axis=0, tiled=True),
-    )
-    whole = (
-        lax.all_gather(flatten(got[0]), "fsdp", axis=0, tiled=True),
-        lax.all_gather(flatten(got[1]), "fsdp", axis=0, tiled=True),
-    )
-    proj = jnp.dot(shuffled, whole[0], preferred_element_type=jnp.float32)
+
+    parts = shuffle(hidden.reshape(steps * rows, width), block_owner)
+    qkv_copy, out_copy, *parts = lax.optimization_barrier((qkv_copy, out_copy, *parts))
+    parts = [parts[0]] + [z_shift(parts[k], k) for k in range(1, NZ)]
+
+    w = flatten(lax.all_to_all(qkv_copy, "tp", split_axis=1, concat_axis=0, tiled=True))
+    w_y = flip(w, 8)
+    w_c = flip(w, 1)
+    w_yc = flip(w_y, 1)
+    sums = partials(parts, (w, w_y, w_c, w_yc))
+    got_o = lax.all_to_all(out_copy, "tp", split_axis=1, concat_axis=0, tiled=True)
+    whole_o = lax.all_gather(flatten(got_o), "fsdp", axis=0, tiled=True)
+
+    proj = sums[0]
+    for k in range(1, NZ):
+        proj = proj + z_shift(sums[k], -k).astype(jnp.float32)
     mixed = attention(proj, cache, lengths, groups)
-    outcome = project_back(mixed, whole[1])
-    pieces = outcome.reshape(steps * rows, blocks, owned)
-    ordered = (
-        jnp.zeros_like(pieces).at[:, block_owner[1], :].set(pieces).reshape(steps, rows, width)
-    )
-    summed = lax.psum_scatter(ordered.astype(jnp.bfloat16), "tp", scatter_dimension=2, tiled=True)
-    return summed
+    terms = project_back(mixed, whole_o, block_owner, groups)
+    terms = lax.all_to_all(terms, "tp", split_axis=0, concat_axis=0, tiled=True)
+    summed = jnp.sum(terms.astype(jnp.float32), axis=0).astype(jnp.bfloat16)
+    return summed.reshape(steps, rows, width // groups)
 
 
 def solution(mesh):

time: 423 us -> 291 us (0.69)
  waiting for transfers between devices: 220 us -> 128 us
  local copies, waits for them, and re-layouts: 86.9 us -> 5.53 us
  matrix products: 48 us -> 7.53 us
  blocking collectives: 46.7 us -> 85.5 us
  Pallas kernels: 0 us -> 30.3 us
  starting transfers between devices: 0.09 us -> 11.4 us
    all_gather x2 -> x1, waiting for transfers between devices: 141 us -> 0.01 us  [body(): whole_o = lax.all_gather(flatten(got_o), 'fsdp', axis=0, tiled=True)]
    ppermute x0 -> x9, waiting for transfers between devices: none -> 128 us  [the longest x6 71.1 us: z_shift(): return lax.ppermute(value, 'fsdp', pairs)]
    reduce_scatter x1 -> x0, waiting for transfers between devices: 79 us -> none  [body(): lax.psum_scatter(ordered.astype(jnp.bfloat16), 'tp', scatter_dimension=2,...]
    dot_general x2 -> x0, matrix products: 40.5 us -> none  [the longest x1 29.9 us: project_back(): lax.dot_general(mixed, weight, (((1,), (1,)), ((), ())), preferred_elemen...]
    all_to_all x0 -> x1, blocking collectives: none -> 39.8 us  [body(): terms = lax.all_to_all(terms, 'tp', split_axis=0, concat_axis=0, tiled=True)]
    scatter x2 -> x0, local copies, waits for them, and re-layouts: 32.3 us -> none  [body(): jnp.zeros_like(pieces).at[:, block_owner[1], :].set(pieces)]
    pallas_call x0 -> x3, Pallas kernels: none -> 30.3 us  [the longest x1 14.4 us: project_back(): pl.pallas_call(functools.partial(back_kernel, blocks, owned), grid=(group...]
    dot_general x2 -> x0, local copies, waits for them, and re-layouts: 16.5 us -> none  [the longest x1 8.94 us: project_back(): lax.dot_general(mixed, weight, (((1,), (1,)), ((), ())), preferred_elemen...]
  transfers between devices with their start and end apart: 3 -> 10, of which waited for: 3 -> 6; matrix products, arithmetic and copies ran while one was open for 12% -> 4% of each run, Pallas kernels for 0% -> 2%
where the time goes in v1:
time: 291 us; the launch traced here: 290 us
  waiting for transfers between devices  128 us (44%)
  blocking collectives  85.5 us (29%)
  Pallas kernels  30.3 us (10%)
  between operations  13.7 us (5%)
  starting transfers between devices  11.4 us (4%)
  other arithmetic  7.86 us (3%)
  matrix products  7.53 us (3%)
  local copies, waits for them, and re-layouts  5.53 us (2%)
    ppermute x6, waiting for transfers between devices, z_shift(): return lax.ppermute(value, 'fsdp', pairs)  71.1 us
    ppermute x3, waiting for transfers between devices, flip(): return lax.ppermute(value, 'fsdp', [(f, f ^ bit) for f in range(16)])  57.4 us
    all_to_all x1, blocking collectives, body(): terms = lax.all_to_all(terms, 'tp', split_axis=0, concat_axis=0, tiled=True)  39.8 us
    all_to_all x1, blocking collectives, body(): lax.all_to_all(out_copy, 'tp', split_axis=1, concat_axis=0, tiled=True)  23.8 us
    all_to_all x1, blocking collectives, body(): lax.all_to_all(qkv_copy, 'tp', split_axis=1, concat_axis=0, tiled=True)  21.9 us
    pallas_call x1, Pallas kernels, project_back(): pl.pallas_call(functools.partial(back_kernel, blocks, owned), grid=(group...  14.4 us
    ppermute x6, starting transfers between devices, z_shift(): return lax.ppermute(value, 'fsdp', pairs)  10.6 us
    pallas_call x1, Pallas kernels, shuffle(): pl.pallas_call(shuffle_kernel, out_shape=[part] * NZ, in_specs=[pl.BlockS...  9.19 us
  transfers between devices with their start and end apart: 10, of which 6 were waited for; matrix products, arithmetic and copies ran while one was open for 4% of the time, Pallas kernels for 2%

profile of v1, /device:TPU:0, one launch (start us, length us, event | category | flops | bytes accessed | tf_op | source)
XLA Modules:
  0.0 290.2 jit_solution(12458736401859067944)
XLA Ops:
  6.5 1.9 convert_element_type.50
  8.6 1.5 copy-done.3
  10.2 0.6 copy.43
  10.9 1.0 copy-done
  12.0 9.2 %shuffle.1 = (bf16[160,2048]{1,0:T(8,128)(2,1)S(1)}, bf16[160,2048]{1,0:T(8,128)(2,1)S(1)}, bf16[160,2048]{1,0:T(8,128)(2,1)}, bf16[160,2048]{1,0:T(8,128)(2,1)}) custom-call(s32[2,128]{1,0:T(2,128)S(1)} %copy-done.1, bf16[160,8192]{1,0:T(8,128)(2,1)S(1)} %bitcast.146), custom_call_target="tpu_custom_call" | custom-call | flops 10485760 | bytes 5242880 | tf_op jit(solution)/shard_map/shuffle/pallas_call | solution.py:72
  21.2 1.3 pad_maximum_fusion
  22.4 0.6 copy.28
  23.0 23.8 %all_to_all.35 = bf16[64,8,1024]{2,0,1:T(8,128)(2,1)} all-to-all(bf16[64,8,1024]{2,0,1:T(8,128)(2,1)S(1)} %copy.28), channel_id=1, replica_groups=mesh['fsdp'=16,'tp'=8] {'tp'}, dimensions={1} | all-to-all | bytes 2097152 | tf_op jit(solution)/shard_map/all_to_all | solution.py:276
  46.8 21.9 %all_to_all.36 = bf16[64,8,1280]{2,0,1:T(8,128)(2,1)S(1)} all-to-all(bf16[64,8,1280]{2,0,1:T(8,128)(2,1)} %pad_maximum_fusion), channel_id=1, replica_groups=mesh['fsdp'=16,'tp'=8] {'tp'}, dimensions={1} | all-to-all | bytes 2621440 | tf_op jit(solution)/shard_map/all_to_all | solution.py:271
  68.7 0.8 collective-permute-start.3
  69.5 57.4 %collective-permute-done.3.w1 = bf16[512,1280]{1,0:T(8,128)(2,1)S(1)} collective-permute-done((bf16[512,1280]{1,0:T(8,128)(2,1)S(1)}, bf16[512,1280]{1,0:T(8,128)(2,1)S(1)}, u32[]{:S(2)}, u32[]{:S(2)}) %collective-permute-start.3) | collective-permute-done | bytes 1310752 | tf_op jit(solution)/shard_map/ppermute | solution.py:24
  126.8 6.4 %collective-permute-start.1 = (bf16[160,2048]{1,0:T(8,128)(2,1)}, bf16[160,2048]{1,0:T(8,128)(2,1)}, u32[]{:S(2)}, u32[]{:S(2)}) collective-permute-start(bf16[160,2048]{1,0:T(8,128)(2,1)} %get-tuple-element.25), channel_id=1, source_target_pairs={{0,32},{8,40},{16,48},{24,56},{32,0},{40,8},{48,16},{56,24},{64,96... | collective-permute-start | bytes 1966088 | tf_op jit(solution)/shard_map/ppermute | solution.py:20
  133.4 22.5 %collective-permute-done.h1 = bf16[160,2048]{1,0:T(8,128)(2,1)} collective-permute-done((bf16[160,2048]{1,0:T(8,128)(2,1)}, bf16[160,2048]{1,0:T(8,128)(2,1)}, u32[]{:S(2)}, u32[]{:S(2)}) %collective-permute-start) | collective-permute-done | bytes 655392 | tf_op jit(solution)/shard_map/ppermute | solution.py:20
  155.9 32.1 %collective-permute-done.1.h2 = bf16[160,2048]{1,0:T(8,128)(2,1)} collective-permute-done((bf16[160,2048]{1,0:T(8,128)(2,1)}, bf16[160,2048]{1,0:T(8,128)(2,1)}, u32[]{:S(2)}, u32[]{:S(2)}) %collective-permute-start.1) | collective-permute-done | bytes 655392 | tf_op jit(solution)/shard_map/ppermute | solution.py:20
  188.0 6.7 %partials.1 = (f32[160,1280]{1,0:T(8,128)S(1)}, bf16[160,1280]{1,0:T(8,128)(2,1)S(1)}, bf16[160,1280]{1,0:T(8,128)(2,1)S(1)}, bf16[160,1280]{1,0:T(8,128)(2,1)S(1)}) custom-call(bf16[160,2048]{1,0:T(8,128)(2,1)S(1)} %get-tuple-element.23.h0, bf16[160,2048]{1,0:T(8,128)(2,1)} %collective-permute-done.h1, bf16[160,2048]{1,0:T(8,128)(2,1)} %collective-permute-done.1.h2, ...), custom_call_target="tpu_custom_call" | custom-call | flops 3355443200 | bytes 9502720 | tf_op jit(solution)/shard_map/partials/pallas_call | solution.py:110
  194.8 0.8 collective-permute-start.6
  195.6 2.0 collective-permute-start.7
  197.6 1.3 collective-permute-start.8
  199.0 1.3 multiply_cosine_fusion
  200.4 6.9 %collective-permute-done.6 = bf16[160,1280]{1,0:T(8,128)(2,1)S(1)} collective-permute-done((bf16[160,1280]{1,0:T(8,128)(2,1)S(1)}, bf16[160,1280]{1,0:T(8,128)(2,1)S(1)}, u32[]{:S(2)}, u32[]{:S(2)}) %collective-permute-start.6) | collective-permute-done | bytes 409632 | tf_op jit(solution)/shard_map/ppermute | solution.py:20
  207.2 2.3 collective-permute-done.7
  209.6 7.3 %collective-permute-done.8 = bf16[160,1280]{1,0:T(8,128)(2,1)S(1)} collective-permute-done((bf16[160,1280]{1,0:T(8,128)(2,1)S(1)}, bf16[160,1280]{1,0:T(8,128)(2,1)S(1)}, u32[]{:S(2)}, u32[]{:S(2)}) %collective-permute-start.8) | collective-permute-done | bytes 409632 | tf_op jit(solution)/shard_map/ppermute | solution.py:20
  217.2 0.3 fusion.40
  218.5 1.8 fusion.45
  220.3 4.3 %bitcast_reduce_fusion = (f32[2,80,8]{2,0,1:T(2,128)S(1)}, f32[80,1,256,2,8]{2,4,3,0,1:T(8,128)S(1)}) fusion(bf16[2,80,256,128]{3,2,1,0:T(8,128)(2,1)} %param.10, bf16[2,80,8,64]{3,2,0,1:T(8,128)(2,1)S(1)} %get-tuple-element.34, bf16[2,80,8,64]{3,2,0,1:T(8,128)(2,1)S(1)} %get-tuple-element.33, pred[80,256]{1,0:T(8,128)(4,1)S(1)} %iota_compare_fusion), kind=kOutput, calls=%fused_computation.10 | convolution fusion | flops 85523200 | bytes 6906880 | tf_op jit(solution)/shard_map/srgjd,rpgd->srgjp/dot_general | solution.py:236
  225.0 0.5 fusion.21
  225.6 1.1 fusion.16
  226.7 0.4 fusion.20
  227.1 0.8 copy.58
  227.9 14.4 %project_back.1 = bf16[8,160,1024]{2,1,0:T(8,128)(2,1)} custom-call(s32[2,128]{1,0:T(2,128)} %owner_ref.3, bf16[160,1024]{1,0:T(8,128)(2,1)} %bitcast.163, bf16[8192,1024]{1,0:T(8,128)(2,1)} %all-gather.2.cloned.1.call-done.weight_ref), custom_call_target="tpu_custom_call" | custom-call | flops 2684354560 | bytes 19726336 | tf_op jit(solution)/shard_map/project_back/pallas_call | solution.py:179
  242.3 39.8 %all_to_all.37 = bf16[8,160,1024]{2,1,0:T(8,128)(2,1)S(1)} all-to-all(bf16[8,160,1024]{2,1,0:T(8,128)(2,1)} %project_back.1), channel_id=1, replica_groups=mesh['fsdp'=16,'tp'=8] {'tp'}, dimensions={0} | all-to-all | bytes 5242880 | tf_op jit(solution)/shard_map/all_to_all | solution.py:284
  282.1 1.3 reduce_sum.32
  (50 shorter events, 2.4 us)
Async XLA Ops:
  6.5 221.4 %all-gather.2.cloned.1.call-start = ((), (), s32[]{:S(2)}) async-start(), calls=%async_computation.3 | async-start | bytes 17825792 | tf_op jit(solution)/shard_map/all_gather | solution.py:277
  8.5 1.6 copy-start.3
  10.2 1.7 copy-start
  10.2 1.7 copy-start.1
  21.2 25.7 %copy-start.2 = (bf16[160,2048]{1,0:T(8,128)(2,1)}, bf16[160,2048]{1,0:T(8,128)(2,1)S(1)}, u32[]{:S(2)}) copy-start(bf16[160,2048]{1,0:T(8,128)(2,1)S(1)} %get-tuple-element.24) | copy-start | bytes 1966084
  46.8 86.4 %copy-start.4 = (s32[80]{0:T(128)S(1)}, s32[80]{0:T(128)}, u32[]{:S(2)}) copy-start(s32[80]{0:T(128)} %param.11) | copy-start | bytes 964
  68.7 58.1 %collective-permute-start.3 = (bf16[512,1280]{1,0:T(8,128)(2,1)S(1)}, bf16[512,1280]{1,0:T(8,128)(2,1)S(1)}, u32[]{:S(2)}, u32[]{:S(2)}) collective-permute-start(bf16[512,1280]{1,0:T(8,128)(2,1)S(1)} %bitcast.147), channel_id=1, source_target_pairs={{0,64},{8,72},{16,80},{24,88},{32,96},{40,104},{48,112},{56,120},{... | collective-permute-start | bytes 3932168 | tf_op jit(solution)/shard_map/ppermute | solution.py:24
  69.5 118.6 %collective-permute-start.4 = (bf16[512,1280]{1,0:T(8,128)(2,1)S(1)}, bf16[512,1280]{1,0:T(8,128)(2,1)}, u32[]{:S(2)}, u32[]{:S(2)}) collective-permute-start(bf16[512,1280]{1,0:T(8,128)(2,1)S(1)} %bitcast.148), channel_id=1, source_target_pairs={{0,8},{8,0},{16,24},{24,16},{32,40},{40,32},{48,56},{56,48},{64,72... | collective-permute-start | bytes 3932168 | tf_op jit(solution)/shard_map/ppermute | solution.py:24
  126.8 61.2 %collective-permute-start.5 = (bf16[512,1280]{1,0:T(8,128)(2,1)S(1)}, bf16[512,1280]{1,0:T(8,128)(2,1)}, u32[]{:S(2)}, u32[]{:S(2)}) collective-permute-start(bf16[512,1280]{1,0:T(8,128)(2,1)S(1)} %collective-permute-done.3.w1), channel_id=1, source_target_pairs={{0,8},{8,0},{16,24},{24,16},{32,40},{40,32},{48,56},{56,48},{64,72... | collective-permute-start | bytes 3932168 | tf_op jit(solution)/shard_map/ppermute | solution.py:24
  126.8 29.1 %collective-permute-start = (bf16[160,2048]{1,0:T(8,128)(2,1)}, bf16[160,2048]{1,0:T(8,128)(2,1)}, u32[]{:S(2)}, u32[]{:S(2)}) collective-permute-start(bf16[160,2048]{1,0:T(8,128)(2,1)} %copy-done.2), channel_id=1, source_target_pairs={{0,16},{8,24},{16,32},{24,40},{32,48},{40,56},{48,0},{56,8},{64,80... | collective-permute-start | bytes 1966088 | tf_op jit(solution)/shard_map/ppermute | solution.py:20
  126.8 61.2 %collective-permute-start.1 = (bf16[160,2048]{1,0:T(8,128)(2,1)}, bf16[160,2048]{1,0:T(8,128)(2,1)}, u32[]{:S(2)}, u32[]{:S(2)}) collective-permute-start(bf16[160,2048]{1,0:T(8,128)(2,1)} %get-tuple-element.25), channel_id=1, source_target_pairs={{0,32},{8,40},{16,48},{24,56},{32,0},{40,8},{48,16},{56,24},{64,96... | collective-permute-start | bytes 1966088 | tf_op jit(solution)/shard_map/ppermute | solution.py:20
  133.3 54.8 %collective-permute-start.2 = (bf16[160,2048]{1,0:T(8,128)(2,1)}, bf16[160,2048]{1,0:T(8,128)(2,1)}, u32[]{:S(2)}, u32[]{:S(2)}) collective-permute-start(bf16[160,2048]{1,0:T(8,128)(2,1)} %get-tuple-element.26), channel_id=1, source_target_pairs={{0,48},{8,56},{16,0},{24,8},{32,16},{40,24},{48,32},{56,40},{64,11... | collective-permute-start | bytes 1966088 | tf_op jit(solution)/shard_map/ppermute | solution.py:20
  194.8 12.5 %collective-permute-start.6 = (bf16[160,1280]{1,0:T(8,128)(2,1)S(1)}, bf16[160,1280]{1,0:T(8,128)(2,1)S(1)}, u32[]{:S(2)}, u32[]{:S(2)}) collective-permute-start(bf16[160,1280]{1,0:T(8,128)(2,1)S(1)} %get-tuple-element.29), channel_id=1, source_target_pairs={{0,48},{8,56},{16,0},{24,8},{32,16},{40,24},{48,32},{56,40},{64,11... | collective-permute-start | bytes 1228808 | tf_op jit(solution)/shard_map/ppermute | solution.py:20
  195.6 13.9 %collective-permute-start.7 = (bf16[160,1280]{1,0:T(8,128)(2,1)S(1)}, bf16[160,1280]{1,0:T(8,128)(2,1)S(1)}, u32[]{:S(2)}, u32[]{:S(2)}) collective-permute-start(bf16[160,1280]{1,0:T(8,128)(2,1)S(1)} %get-tuple-element.30), channel_id=1, source_target_pairs={{0,32},{8,40},{16,48},{24,56},{32,0},{40,8},{48,16},{56,24},{64,96... | collective-permute-start | bytes 1228808 | tf_op jit(solution)/shard_map/ppermute | solution.py:20
  197.6 19.2 %collective-permute-start.8 = (bf16[160,1280]{1,0:T(8,128)(2,1)S(1)}, bf16[160,1280]{1,0:T(8,128)(2,1)S(1)}, u32[]{:S(2)}, u32[]{:S(2)}) collective-permute-start(bf16[160,1280]{1,0:T(8,128)(2,1)S(1)} %get-tuple-element.31), channel_id=1, source_target_pairs={{0,16},{8,24},{16,32},{24,40},{32,48},{40,56},{48,0},{56,8},{64,80... | collective-permute-start | bytes 1228808 | tf_op jit(solution)/shard_map/ppermute | solution.py:20
  216.8 8.7 %slice-start = ((s8[10485760]{0:T(1024)(128)(4,1)}), s8[2097152]{0:T(1024)(128)(4,1)S(1)}, s32[]{:S(2)}) async-start(s8[10485760]{0:T(1024)(128)(4,1)} %bitcast.159), calls=%async_computation.4 | async-start | bytes 4194304
  218.1 7.5 %slice-start.1 = ((s8[10485760]{0:T(1024)(128)(4,1)}), s8[4194304]{0:T(1024)(128)(4,1)S(1)}, s32[]{:S(2)}) async-start(s8[10485760]{0:T(1024)(128)(4,1)} %bitcast.159), calls=%async_computation.5 | async-start | bytes 8388608
  220.3 5.3 %slice-start.2 = ((s8[10485760]{0:T(1024)(128)(4,1)}), s8[4194304]{0:T(1024)(128)(4,1)S(1)}, s32[]{:S(2)}) async-start(s8[10485760]{0:T(1024)(128)(4,1)} %bitcast.159), calls=%async_computation.6 | async-start | bytes 8388608
Sparse Core Ops, SparseCore 0:
  46.9 144.5 all-gather.1

commit v2 on v1

--- a/solution.py
+++ b/solution.py
@@ -63,7 +63,7 @@
             )
             return carry
 
-        lax.fori_loop(0, 16, step, 0)
+        lax.fori_loop(0, 16, step, 0, unroll=4)
 
 
 def shuffle(hidden, block_owner):
@@ -126,79 +126,94 @@
     )(*parts, *weights)
 
 
-def back_kernel(blocks, owned, owner_ref, mixed_ref, weight_ref, out_ref, place, held, sems):
-    t = pl.program_id(0)
-    steps = pl.num_programs(0)
-
-    @pl.when(t == 0)
-    def _():
-        def note(i, carry):
-            place[owner_ref[1, i]] = i
-            return carry
-
-        lax.fori_loop(0, owner_ref.shape[1], note, 0)
-
-    def fetch(step, slot):
-        def one(j, carry):
-            source = place[step * blocks + j]
-            pltpu.make_async_copy(
-                weight_ref.at[pl.ds(pl.multiple_of(source * owned, owned), owned)],
-                held.at[slot, pl.ds(pl.multiple_of(j * owned, owned), owned)],
-                sems.at[slot],
-            ).start()
-            return carry
-
-        lax.fori_loop(0, blocks, one, 0)
-
-    slot = lax.rem(t, 2)
-
-    @pl.when(t == 0)
-    def _():
-        fetch(t, slot)
-
-    @pl.when(t + 1 < steps)
-    def _():
-        fetch(t + 1, 1 - slot)
-
-    pltpu.make_async_copy(
-        weight_ref.at[pl.ds(0, blocks * owned)], held.at[slot], sems.at[slot]
-    ).wait()
-    out_ref[0] = lax.dot_general(
-        mixed_ref[...],
-        held[slot],
-        (((1,), (1,)), ((), ())),
-        preferred_element_type=jnp.float32,
-    ).astype(out_ref.dtype)
-
-
-def project_back(mixed, weight, block_owner, groups):
+def back_kernel(spots, groups, owner_ref, mixed_ref, *refs):
+    count = len(spots)
+    sources, out_ref, held, placed, sems = refs[:count], *refs[count:]
+    f = lax.axis_index("fsdp")
+    y_lo, z, core = f // 8, lax.rem(f // 2, NZ), lax.rem(f, 2)
+    rows, depth = mixed_ref.shape
+    width = held.shape[0]
+    owned = width // owner_ref.shape[1]
+
+    copies = []
+    begin = 0
+    for n, source in enumerate(sources):
+        size = source.shape[0]
+        copies.append(
+            pltpu.make_async_copy(source, held.at[pl.ds(begin, size)], sems.at[n])
+        )
+        copies[-1].start()
+        begin += size
+    turned = mixed_ref[...].astype(jnp.float32).T.astype(jnp.bfloat16)
+
+    begin = 0
+    for n, (dy, dz, dc, t0) in enumerate(spots):
+        size = sources[n].shape[0]
+        first = (
+            lax.rem(y_lo + dy, 2) * 64 + lax.rem(z + dz, NZ) * 16 + lax.rem(core + dc, 2) * 8 + t0
+        )
+        copies[n].wait()
+        terms = jnp.dot(held[begin : begin + size], turned, preferred_element_type=jnp.float32)
+        terms = terms.astype(jnp.bfloat16)
+        for b in range(size // owned):
+            spot = pl.multiple_of(owner_ref[1, first + b] * owned, owned)
+            placed[pl.ds(spot, owned), :] = terms[b * owned : (b + 1) * owned]
+        begin += size
+
+    slab = width // groups
+    for t in range(groups):
+        out_ref[t] = placed[t * slab : (t + 1) * slab].T
+
+
+def project_back(mixed, sources, spots, block_owner, groups):
     rows, depth = mixed.shape
-    width = weight.shape[0]
-    total = block_owner.shape[1]
-    blocks, owned = total // groups, width // total
+    width = sum(source.shape[0] for source in sources)
     return pl.pallas_call(
-        functools.partial(back_kernel, blocks, owned),
-        grid=(groups,),
+        functools.partial(back_kernel, spots, groups),
         out_shape=jax.ShapeDtypeStruct((groups, rows, width // groups), jnp.bfloat16),
         in_specs=[
             pl.BlockSpec(memory_space=pltpu.SMEM),
-            pl.BlockSpec((rows, depth), lambda t: (0, 0)),
-            pl.BlockSpec(memory_space=pltpu.HBM),
+            pl.BlockSpec(memory_space=pltpu.VMEM),
+        ]
+        + [pl.BlockSpec(memory_space=pl.ANY)] * len(sources),
+        out_specs=pl.BlockSpec(memory_space=pltpu.VMEM),
+        scratch_shapes=[
+            pltpu.VMEM((width, depth), jnp.bfloat16),
+            pltpu.VMEM((width, rows), jnp.bfloat16),
+            pltpu.SemaphoreType.DMA((len(sources),)),
         ],
-        out_specs=pl.BlockSpec((1, rows, width // groups), lambda t: (t, 0, 0)),
-        scratch_shapes=[
-            pltpu.SMEM((total,), jnp.int32),
-            pltpu.VMEM((2, width // groups, depth), jnp.bfloat16),
-            pltpu.SemaphoreType.DMA((2,)),
-        ],
-        compiler_params=pltpu.CompilerParams(vmem_limit_bytes=54 * MIB),
+        compiler_params=pltpu.CompilerParams(vmem_limit_bytes=48 * MIB),
         cost_estimate=pl.CostEstimate(
             flops=2 * rows * depth * width,
             bytes_accessed=2 * (rows * depth + depth * width + rows * width),
             transcendentals=0,
         ),
         name="project_back",
-    )(block_owner, mixed, weight)
+    )(block_owner, mixed, *sources)
+
+
+def gather_rows(own):
+    half = own.shape[0] // 2
+    across = flip(own, 8)
+    below, above = z_shift(own, 1), z_shift(own, -1)
+    far_a, far_b = z_shift(above[:half], -1), z_shift(below[half:], 1)
+    across_below, across_above = z_shift(across, 1), z_shift(across, -1)
+    across_far_a, across_far_b = flip(far_a, 8), flip(far_b, 8)
+    held = [
+        (own, (0, 0), 0),
+        (across, (1, 0), 0),
+        (below, (0, 3), 0),
+        (above, (0, 1), 0),
+        (far_a, (0, 2), 0),
+        (far_b, (0, 2), 4),
+        (across_below, (1, 3), 0),
+        (across_above, (1, 1), 0),
+        (across_far_a, (1, 2), 0),
+        (across_far_b, (1, 2), 4),
+    ]
+    sources = [value for value, _, _ in held] + [flip(value, 1) for value, _, _ in held]
+    spots = [(*at, core, t0) for core in (0, 1) for _, at, t0 in held]
+    return sources, tuple(spots)
 
 
 def rotary(values, position):
@@ -269,18 +284,19 @@
     parts = [parts[0]] + [z_shift(parts[k], k) for k in range(1, NZ)]
 
     w = flatten(lax.all_to_all(qkv_copy, "tp", split_axis=1, concat_axis=0, tiled=True))
+    w, out_copy = lax.optimization_barrier((w, out_copy))
     w_y = flip(w, 8)
     w_c = flip(w, 1)
     w_yc = flip(w_y, 1)
+    got_o = flatten(lax.all_to_all(out_copy, "tp", split_axis=1, concat_axis=0, tiled=True))
     sums = partials(parts, (w, w_y, w_c, w_yc))
-    got_o = lax.all_to_all(out_copy, "tp", split_axis=1, concat_axis=0, tiled=True)
-    whole_o = lax.all_gather(flatten(got_o), "fsdp", axis=0, tiled=True)
+    sources, spots = gather_rows(got_o)
 
     proj = sums[0]
     for k in range(1, NZ):
         proj = proj + z_shift(sums[k], -k).astype(jnp.float32)
     mixed = attention(proj, cache, lengths, groups)
-    terms = project_back(mixed, whole_o, block_owner, groups)
+    terms = project_back(mixed, sources, spots, block_owner, groups)
     terms = lax.all_to_all(terms, "tp", split_axis=0, concat_axis=0, tiled=True)
     summed = jnp.sum(terms.astype(jnp.float32), axis=0).astype(jnp.bfloat16)
     return summed.reshape(steps, rows, width // groups)

time: 291 us -> 259 us (0.89)
  waiting for transfers between devices: 128 us -> 92.9 us
  starting transfers between devices: 11.4 us -> 29.2 us
  blocking collectives: 85.5 us -> 69.1 us
  local copies, waits for them, and re-layouts: 5.53 us -> 19.1 us
  between operations: 13.7 us -> 0.5 us
  Pallas kernels: 30.3 us -> 27.3 us
    ppermute x3 -> x16, waiting for transfers between devices: 57.4 us -> 19.8 us  [flip(): return lax.ppermute(value, 'fsdp', [(f, f ^ bit) for f in range(16)])]
    all_to_all x1 -> x0, blocking collectives: 23.8 us -> none  [body(): lax.all_to_all(out_copy, 'tp', split_axis=1, concat_axis=0, tiled=True)]
    all_to_all x0 -> x1, waiting for transfers between devices: none -> 15.4 us  [body(): lax.all_to_all(out_copy, 'tp', split_axis=1, concat_axis=0, tiled=True)]
    ppermute x6 -> x12, waiting for transfers between devices: 71.1 us -> 57.8 us  [z_shift(): return lax.ppermute(value, 'fsdp', pairs)]
    ppermute x6 -> x12, starting transfers between devices: 10.6 us -> 19.1 us  [z_shift(): return lax.ppermute(value, 'fsdp', pairs)]
    unnamed x21 -> x47, local copies, waits for them, and re-layouts: 4.2 us -> 11.9 us
    ppermute x3 -> x16, starting transfers between devices: 0.76 us -> 6.4 us  [flip(): return lax.ppermute(value, 'fsdp', [(f, f ^ bit) for f in range(16)])]
    all_to_all x1, blocking collectives: 21.9 us -> 26.5 us  [body(): lax.all_to_all(qkv_copy, 'tp', split_axis=1, concat_axis=0, tiled=True)]
  transfers between devices with their start and end apart: 10 -> 29, of which waited for: 6 -> 10; matrix products, arithmetic and copies ran while one was open for 4% -> 8% of each run, Pallas kernels for 2% -> 3%
where the time goes in v2:
time: 259 us; the launch traced here: 258 us
  waiting for transfers between devices  92.9 us (36%)
  blocking collectives  69.1 us (27%)
  starting transfers between devices  29.2 us (11%)
  Pallas kernels  27.3 us (11%)
  local copies, waits for them, and re-layouts  19.1 us (7%)
  other arithmetic  10.3 us (4%)
  matrix products  9.39 us (4%)
    ppermute x12, waiting for transfers between devices, z_shift(): return lax.ppermute(value, 'fsdp', pairs)  57.8 us
    all_to_all x1, blocking collectives, body(): terms = lax.all_to_all(terms, 'tp', split_axis=0, concat_axis=0, tiled=True)  42.6 us
    all_to_all x1, blocking collectives, body(): lax.all_to_all(qkv_copy, 'tp', split_axis=1, concat_axis=0, tiled=True)  26.5 us
    ppermute x16, waiting for transfers between devices, flip(): return lax.ppermute(value, 'fsdp', [(f, f ^ bit) for f in range(16)])  19.8 us
    ppermute x12, starting transfers between devices, z_shift(): return lax.ppermute(value, 'fsdp', pairs)  19.1 us
    pallas_call x1, Pallas kernels, project_back(): pl.pallas_call(functools.partial(back_kernel, spots, groups), out_shape=j...  15.7 us
    all_to_all x1, waiting for transfers between devices, body(): lax.all_to_all(out_copy, 'tp', split_axis=1, concat_axis=0, tiled=True)  15.4 us
    unnamed x47, local copies, waits for them, and re-layouts  11.9 us
  transfers between devices with their start and end apart: 29, of which 10 were waited for; matrix products, arithmetic and copies ran while one was open for 8% of the time, Pallas kernels for 3%

profile of v2, /device:TPU:0, one launch (start us, length us, event | category | flops | bytes accessed | tf_op | source)
XLA Modules:
  0.0 257.8 jit_solution(317296114446373578)
XLA Ops:
  0.0 1.9 convert_element_type.50
  2.1 1.5 copy-done.12
  5.4 4.9 %shuffle.1 = (bf16[160,2048]{1,0:T(8,128)(2,1)S(1)}, bf16[160,2048]{1,0:T(8,128)(2,1)S(1)}, bf16[160,2048]{1,0:T(8,128)(2,1)S(1)}, bf16[160,2048]{1,0:T(8,128)(2,1)}) custom-call(s32[2,128]{1,0:T(2,128)S(1)} %copy-done.1, bf16[160,8192]{1,0:T(8,128)(2,1)S(1)} %bitcast.151), custom_call_target="tpu_custom_call" | custom-call | flops 10485760 | bytes 5242880 | tf_op jit(solution)/shard_map/shuffle/pallas_call | solution.py:72
  11.4 26.5 %all_to_all.35 = bf16[64,8,1280]{2,0,1:T(8,128)(2,1)S(1)} all-to-all(bf16[64,8,1280]{2,0,1:T(8,128)(2,1)S(1)} %pad_maximum_fusion), channel_id=1, replica_groups=mesh['fsdp'=16,'tp'=8] {'tp'}, dimensions={1} | all-to-all | bytes 2621440 | tf_op jit(solution)/shard_map/all_to_all | solution.py:286
  37.9 1.6 copy.28
  39.4 3.7 %all-to-all-start.1 = ((bf16[64,8,1024]{2,0,1:T(8,128)(2,1)}), bf16[64,8,1024]{2,0,1:T(8,128)(2,1)S(1)}, u32[]{:S(2)}, u32[]{:S(2)}) async-start(bf16[64,8,1024]{2,0,1:T(8,128)(2,1)} %copy.28), calls=%async_computation.1 | async-start | bytes 2097152 | tf_op jit(solution)/shard_map/all_to_all | solution.py:291
  43.9 15.4 %all-to-all-done.1 = bf16[64,8,1024]{2,0,1:T(8,128)(2,1)S(1)} async-done(((bf16[64,8,1024]{2,0,1:T(8,128)(2,1)}), bf16[64,8,1024]{2,0,1:T(8,128)(2,1)S(1)}, u32[]{:S(2)}, u32[]{:S(2)}) %all-to-all-start.1) | async-done | bytes 1048608 | tf_op jit(solution)/shard_map/all_to_all | solution.py:291
  59.3 4.0 %collective-permute-start.11 = (bf16[512,1024]{1,0:T(8,128)(2,1)S(1)}, bf16[512,1024]{1,0:T(8,128)(2,1)S(1)}, u32[]{:S(2)}, u32[]{:S(2)}) collective-permute-start(bf16[512,1024]{1,0:T(8,128)(2,1)S(1)} %bitcast.146), channel_id=1, source_target_pairs={{0,48},{8,56},{16,0},{24,8},{32,16},{40,24},{48,32},{56,40},{64,11... | collective-permute-start | bytes 3145736 | tf_op jit(solution)/shard_map/ppermute | solution.py:20
  63.3 19.0 %collective-permute-done.3.w1 = bf16[512,1280]{1,0:T(8,128)(2,1)} collective-permute-done((bf16[512,1280]{1,0:T(8,128)(2,1)S(1)}, bf16[512,1280]{1,0:T(8,128)(2,1)}, u32[]{:S(2)}, u32[]{:S(2)}) %collective-permute-start.3) | collective-permute-done | bytes 1310752 | tf_op jit(solution)/shard_map/ppermute | solution.py:24
  82.3 17.2 %collective-permute-done.h1 = bf16[160,2048]{1,0:T(8,128)(2,1)S(1)} collective-permute-done((bf16[160,2048]{1,0:T(8,128)(2,1)}, bf16[160,2048]{1,0:T(8,128)(2,1)S(1)}, u32[]{:S(2)}, u32[]{:S(2)}) %collective-permute-start) | collective-permute-done | bytes 655392 | tf_op jit(solution)/shard_map/ppermute | solution.py:20
  106.6 7.3 %collective-permute-done.1.h2 = bf16[160,2048]{1,0:T(8,128)(2,1)} collective-permute-done((bf16[160,2048]{1,0:T(8,128)(2,1)S(1)}, bf16[160,2048]{1,0:T(8,128)(2,1)}, u32[]{:S(2)}, u32[]{:S(2)}) %collective-permute-start.1) | collective-permute-done | bytes 655392 | tf_op jit(solution)/shard_map/ppermute | solution.py:20
  113.9 6.0 %collective-permute-start.12 = (bf16[256,1024]{1,0:T(8,128)(2,1)S(1)}, bf16[256,1024]{1,0:T(8,128)(2,1)S(1)}, u32[]{:S(2)}, u32[]{:S(2)}) collective-permute-start(bf16[256,1024]{1,0:T(8,128)(2,1)S(1)} %slice.67), channel_id=1, source_target_pairs={{0,48},{8,56},{16,0},{24,8},{32,16},{40,24},{48,32},{56,40},{64,11... | collective-permute-start | bytes 1572872 | tf_op jit(solution)/shard_map/ppermute | solution.py:20
  120.0 10.6 %collective-permute-done.2.h3 = bf16[160,2048]{1,0:T(8,128)(2,1)} collective-permute-done((bf16[160,2048]{1,0:T(8,128)(2,1)}, bf16[160,2048]{1,0:T(8,128)(2,1)}, u32[]{:S(2)}, u32[]{:S(2)}) %collective-permute-start.2) | collective-permute-done | bytes 655392 | tf_op jit(solution)/shard_map/ppermute | solution.py:20
  131.7 6.7 %partials.1 = (f32[160,1280]{1,0:T(8,128)S(1)}, bf16[160,1280]{1,0:T(8,128)(2,1)S(1)}, bf16[160,1280]{1,0:T(8,128)(2,1)S(1)}, bf16[160,1280]{1,0:T(8,128)(2,1)S(1)}) custom-call(bf16[160,2048]{1,0:T(8,128)(2,1)S(1)} %copy-done.3, bf16[160,2048]{1,0:T(8,128)(2,1)S(1)} %copy-done.5, bf16[160,2048]{1,0:T(8,128)(2,1)} %collective-permute-done.1.h2, ...), custom_call_target="tpu_custom_call" | custom-call | flops 3355443200 | bytes 9502720 | tf_op jit(solution)/shard_map/partials/pallas_call | solution.py:110
  138.4 3.3 %collective-permute-start.6 = (bf16[160,1280]{1,0:T(8,128)(2,1)S(1)}, bf16[160,1280]{1,0:T(8,128)(2,1)S(1)}, u32[]{:S(2)}, u32[]{:S(2)}) collective-permute-start(bf16[160,1280]{1,0:T(8,128)(2,1)S(1)} %get-tuple-element.33), channel_id=1, source_target_pairs={{0,48},{8,56},{16,0},{24,8},{32,16},{40,24},{48,32},{56,40},{64,11... | collective-permute-start | bytes 1228808 | tf_op jit(solution)/shard_map/ppermute | solution.py:20
  141.7 1.8 collective-permute-start.7
  143.6 1.3 multiply_cosine_fusion
  145.0 1.4 collective-permute-done.13.refs_5_
  146.8 7.7 %collective-permute-done.6 = bf16[160,1280]{1,0:T(8,128)(2,1)S(1)} collective-permute-done((bf16[160,1280]{1,0:T(8,128)(2,1)S(1)}, bf16[160,1280]{1,0:T(8,128)(2,1)S(1)}, u32[]{:S(2)}, u32[]{:S(2)}) %collective-permute-start.6) | collective-permute-done | bytes 409632 | tf_op jit(solution)/shard_map/ppermute | solution.py:20
  154.5 1.3 collective-permute-start.16
  155.8 6.4 %collective-permute-done.8 = bf16[160,1280]{1,0:T(8,128)(2,1)S(1)} collective-permute-done((bf16[160,1280]{1,0:T(8,128)(2,1)S(1)}, bf16[160,1280]{1,0:T(8,128)(2,1)S(1)}, u32[]{:S(2)}, u32[]{:S(2)}) %collective-permute-start.8) | collective-permute-done | bytes 409632 | tf_op jit(solution)/shard_map/ppermute | solution.py:20
  162.2 1.3 collective-permute-start.17
  167.1 1.3 fusion.44
  169.8 2.8 %collective-permute-start.15 = (bf16[512,1024]{1,0:T(8,128)(2,1)}, bf16[512,1024]{1,0:T(8,128)(2,1)S(1)}, u32[]{:S(2)}, u32[]{:S(2)}) collective-permute-start(bf16[512,1024]{1,0:T(8,128)(2,1)} %collective-permute-done.9.refs_1_), channel_id=1, source_target_pairs={{0,48},{8,56},{16,0},{24,8},{32,16},{40,24},{48,32},{56,40},{64,11... | collective-permute-start | bytes 3145736 | tf_op jit(solution)/shard_map/ppermute | solution.py:20
  172.7 1.5 subtract_convert_fusion
  175.0 1.8 fusion.45
  177.4 4.1 %bitcast_reduce_fusion = (f32[2,80,8]{2,0,1:T(2,128)S(1)}, f32[80,1,256,2,8]{2,4,3,0,1:T(8,128)S(1)}) fusion(bf16[2,80,256,128]{3,2,1,0:T(8,128)(2,1)} %param.10, bf16[2,80,8,64]{3,2,0,1:T(8,128)(2,1)S(1)} %get-tuple-element.38, bf16[2,80,8,64]{3,2,0,1:T(8,128)(2,1)S(1)} %get-tuple-element.37, pred[80,256]{1,0:T(8,128)(4,1)S(1)} %iota_compare_fusion), kind=kOutput, calls=%fused_computation.10 | convolution fusion | flops 85523200 | bytes 6906880 | tf_op jit(solution)/shard_map/srgjd,rpgd->srgjp/dot_general | solution.py:251
  182.5 7.1 %collective-permute-done.15.refs_7_ = bf16[512,1024]{1,0:T(8,128)(2,1)S(1)} collective-permute-done((bf16[512,1024]{1,0:T(8,128)(2,1)}, bf16[512,1024]{1,0:T(8,128)(2,1)S(1)}, u32[]{:S(2)}, u32[]{:S(2)}) %collective-permute-start.15) | collective-permute-done | bytes 1048608 | tf_op jit(solution)/shard_map/ppermute | solution.py:20
  191.1 3.1 %fusion.16 = f32[80,128,2,8]{1,3,2,0:T(8,128)S(1)} fusion(bf16[2,80,256,128]{3,2,1,0:T(8,128)(2,1)} %param.10, f32[80,1,256,2,8]{2,4,3,0,1:T(8,128)S(1)} %get-tuple-element.46, f32[2,80,8]{2,0,1:T(2,128)S(1)} %add.53, f32[2,80,8]{2,0,1:T(2,128)S(1)} %max.9), kind=kOutput, calls=%fused_computation.14 | convolution fusion | flops 84869120 | bytes 7219200 | tf_op jit(solution)/shard_map/srgjp,rpgd->srgjd/dot_general | solution.py:266
  196.5 15.7 %project_back.1 = bf16[8,160,1024]{2,1,0:T(8,128)(2,1)} custom-call(s32[2,128]{1,0:T(2,128)S(1)} %copy-done.1, bf16[160,1024]{1,0:T(8,128)(2,1)S(1)} %bitcast.155, bf16[512,1024]{1,0:T(8,128)(2,1)S(1)} %bitcast.150, bf16[512,1024]{1,0:T(8,128)(2,1)} %collective-permute-done.9.refs_1_, bf16[512,1024]{1,0:T(8,128)(2,1)} %copy-done.10, ...), custom_call_target="tpu_custom_call" | custom-call | flops 2684354560 | bytes 19726336 | tf_op jit(solution)/shard_map/project_back/pallas_call | solution.py:171
  212.1 42.6 %all_to_all.36 = bf16[8,160,1024]{2,1,0:T(8,128)(2,1)} all-to-all(bf16[8,160,1024]{2,1,0:T(8,128)(2,1)} %project_back.1), channel_id=1, replica_groups=mesh['fsdp'=16,'tp'=8] {'tp'}, dimensions={0} | all-to-all | bytes 5242880 | tf_op jit(solution)/shard_map/all_to_all | solution.py:300
  254.8 3.0 %reduce_sum.32 = bf16[160,1024]{1,0:T(8,128)(2,1)} reduce(bf16[8,160,1024]{2,1,0:T(8,128)(2,1)} %all_to_all.36, bf16[]{:T(256)} %constant.15.clone.1), dimensions={0}, to_apply=%region_4.5 | reduce | flops 1146880 | bytes 2949122 | tf_op jit(solution)/shard_map/reduce_sum | solution.py:301
  (113 shorter events, 23.3 us)
Async XLA Ops:
  39.4 64.3 %copy-start.19 = (s32[80]{0:T(128)S(1)}, s32[80]{0:T(128)}, u32[]{:S(2)}) copy-start(s32[80]{0:T(128)} %param.11) | copy-start | bytes 964
  39.4 19.9 %all-to-all-start.1 = ((bf16[64,8,1024]{2,0,1:T(8,128)(2,1)}), bf16[64,8,1024]{2,0,1:T(8,128)(2,1)S(1)}, u32[]{:S(2)}, u32[]{:S(2)}) async-start(bf16[64,8,1024]{2,0,1:T(8,128)(2,1)} %copy.28), calls=%async_computation.1 | async-start | bytes 2097152 | tf_op jit(solution)/shard_map/all_to_all | solution.py:291
  43.1 39.2 %collective-permute-start.3 = (bf16[512,1280]{1,0:T(8,128)(2,1)S(1)}, bf16[512,1280]{1,0:T(8,128)(2,1)}, u32[]{:S(2)}, u32[]{:S(2)}) collective-permute-start(bf16[512,1280]{1,0:T(8,128)(2,1)S(1)} %bitcast.152), channel_id=1, source_target_pairs={{0,64},{8,72},{16,80},{24,88},{32,96},{40,104},{48,112},{56,120},{... | collective-permute-start | bytes 3932168 | tf_op jit(solution)/shard_map/ppermute | solution.py:24
  59.3 41.7 %collective-permute-start.11 = (bf16[512,1024]{1,0:T(8,128)(2,1)S(1)}, bf16[512,1024]{1,0:T(8,128)(2,1)S(1)}, u32[]{:S(2)}, u32[]{:S(2)}) collective-permute-start(bf16[512,1024]{1,0:T(8,128)(2,1)S(1)} %bitcast.146), channel_id=1, source_target_pairs={{0,48},{8,56},{16,0},{24,8},{32,16},{40,24},{48,32},{56,40},{64,11... | collective-permute-start | bytes 3145736 | tf_op jit(solution)/shard_map/ppermute | solution.py:20
  63.3 37.7 %collective-permute-start.10 = (bf16[512,1024]{1,0:T(8,128)(2,1)S(1)}, bf16[512,1024]{1,0:T(8,128)(2,1)S(1)}, u32[]{:S(2)}, u32[]{:S(2)}) collective-permute-start(bf16[512,1024]{1,0:T(8,128)(2,1)S(1)} %bitcast.147), channel_id=1, source_target_pairs={{0,16},{8,24},{16,32},{24,40},{32,48},{40,56},{48,0},{56,8},{64,80... | collective-permute-start | bytes 3145736 | tf_op jit(solution)/shard_map/ppermute | solution.py:20
  63.3 36.2 %collective-permute-start = (bf16[160,2048]{1,0:T(8,128)(2,1)}, bf16[160,2048]{1,0:T(8,128)(2,1)S(1)}, u32[]{:S(2)}, u32[]{:S(2)}) collective-permute-start(bf16[160,2048]{1,0:T(8,128)(2,1)} %copy-done.6), channel_id=1, source_target_pairs={{0,16},{8,24},{16,32},{24,40},{32,48},{40,56},{48,0},{56,8},{64,80... | collective-permute-start | bytes 1966088 | tf_op jit(solution)/shard_map/ppermute | solution.py:20
  63.3 67.3 %collective-permute-start.4 = (bf16[512,1280]{1,0:T(8,128)(2,1)S(1)}, bf16[512,1280]{1,0:T(8,128)(2,1)}, u32[]{:S(2)}, u32[]{:S(2)}) collective-permute-start(bf16[512,1280]{1,0:T(8,128)(2,1)S(1)} %bitcast.153), channel_id=1, source_target_pairs={{0,8},{8,0},{16,24},{24,16},{32,40},{40,32},{48,56},{56,48},{64,72... | collective-permute-start | bytes 3932168 | tf_op jit(solution)/shard_map/ppermute | solution.py:24
  82.3 48.3 %collective-permute-start.5 = (bf16[512,1280]{1,0:T(8,128)(2,1)}, bf16[512,1280]{1,0:T(8,128)(2,1)}, u32[]{:S(2)}, u32[]{:S(2)}) collective-permute-start(bf16[512,1280]{1,0:T(8,128)(2,1)} %collective-permute-done.3.w1), channel_id=1, source_target_pairs={{0,8},{8,0},{16,24},{24,16},{32,40},{40,32},{48,56},{56,48},{64,72... | collective-permute-start | bytes 3932168 | tf_op jit(solution)/shard_map/ppermute | solution.py:24
  100.3 43.1 %collective-permute-start.9 = (bf16[512,1024]{1,0:T(8,128)(2,1)S(1)}, bf16[512,1024]{1,0:T(8,128)(2,1)}, u32[]{:S(2)}, u32[]{:S(2)}) collective-permute-start(bf16[512,1024]{1,0:T(8,128)(2,1)S(1)} %bitcast.148), channel_id=1, source_target_pairs={{0,64},{8,72},{16,80},{24,88},{32,96},{40,104},{48,112},{56,120},{... | collective-permute-start | bytes 3145736 | tf_op jit(solution)/shard_map/ppermute | solution.py:24
  101.0 12.9 %collective-permute-start.1 = (bf16[160,2048]{1,0:T(8,128)(2,1)S(1)}, bf16[160,2048]{1,0:T(8,128)(2,1)}, u32[]{:S(2)}, u32[]{:S(2)}) collective-permute-start(bf16[160,2048]{1,0:T(8,128)(2,1)S(1)} %get-tuple-element.27), channel_id=1, source_target_pairs={{0,32},{8,40},{16,48},{24,56},{32,0},{40,8},{48,16},{56,24},{64,96... | collective-permute-start | bytes 1966088 | tf_op jit(solution)/shard_map/ppermute | solution.py:20
  103.0 27.6 %collective-permute-start.2 = (bf16[160,2048]{1,0:T(8,128)(2,1)}, bf16[160,2048]{1,0:T(8,128)(2,1)}, u32[]{:S(2)}, u32[]{:S(2)}) collective-permute-start(bf16[160,2048]{1,0:T(8,128)(2,1)} %get-tuple-element.28), channel_id=1, source_target_pairs={{0,48},{8,56},{16,0},{24,8},{32,16},{40,24},{48,32},{56,40},{64,11... | collective-permute-start | bytes 1966088 | tf_op jit(solution)/shard_map/ppermute | solution.py:20
  103.9 26.7 %copy-start.5 = (bf16[160,2048]{1,0:T(8,128)(2,1)S(1)}, bf16[160,2048]{1,0:T(8,128)(2,1)}, u32[]{:S(2)}) copy-start(bf16[160,2048]{1,0:T(8,128)(2,1)} %copy-done.4) | copy-start | bytes 1966084
  113.9 31.0 %collective-permute-start.12 = (bf16[256,1024]{1,0:T(8,128)(2,1)S(1)}, bf16[256,1024]{1,0:T(8,128)(2,1)S(1)}, u32[]{:S(2)}, u32[]{:S(2)}) collective-permute-start(bf16[256,1024]{1,0:T(8,128)(2,1)S(1)} %slice.67), channel_id=1, source_target_pairs={{0,48},{8,56},{16,0},{24,8},{32,16},{40,24},{48,32},{56,40},{64,11... | collective-permute-start | bytes 1572872 | tf_op jit(solution)/shard_map/ppermute | solution.py:20
  130.6 15.9 %collective-permute-start.13 = (bf16[256,1024]{1,0:T(8,128)(2,1)S(1)}, bf16[256,1024]{1,0:T(8,128)(2,1)S(1)}, u32[]{:S(2)}, u32[]{:S(2)}) collective-permute-start(bf16[256,1024]{1,0:T(8,128)(2,1)S(1)} %slice.68), channel_id=1, source_target_pairs={{0,16},{8,24},{16,32},{24,40},{32,48},{40,56},{48,0},{56,8},{64,80... | collective-permute-start | bytes 1572872 | tf_op jit(solution)/shard_map/ppermute | solution.py:20
  138.4 16.1 %collective-permute-start.6 = (bf16[160,1280]{1,0:T(8,128)(2,1)S(1)}, bf16[160,1280]{1,0:T(8,128)(2,1)S(1)}, u32[]{:S(2)}, u32[]{:S(2)}) collective-permute-start(bf16[160,1280]{1,0:T(8,128)(2,1)S(1)} %get-tuple-element.33), channel_id=1, source_target_pairs={{0,48},{8,56},{16,0},{24,8},{32,16},{40,24},{48,32},{56,40},{64,11... | collective-permute-start | bytes 1228808 | tf_op jit(solution)/shard_map/ppermute | solution.py:20
  141.7 14.1 %collective-permute-start.7 = (bf16[160,1280]{1,0:T(8,128)(2,1)S(1)}, bf16[160,1280]{1,0:T(8,128)(2,1)S(1)}, u32[]{:S(2)}, u32[]{:S(2)}) collective-permute-start(bf16[160,1280]{1,0:T(8,128)(2,1)S(1)} %get-tuple-element.34), channel_id=1, source_target_pairs={{0,32},{8,40},{16,48},{24,56},{32,0},{40,8},{48,16},{56,24},{64,96... | collective-permute-start | bytes 1228808 | tf_op jit(solution)/shard_map/ppermute | solution.py:20
  143.5 18.7 %collective-permute-start.8 = (bf16[160,1280]{1,0:T(8,128)(2,1)S(1)}, bf16[160,1280]{1,0:T(8,128)(2,1)S(1)}, u32[]{:S(2)}, u32[]{:S(2)}) collective-permute-start(bf16[160,1280]{1,0:T(8,128)(2,1)S(1)} %get-tuple-element.35), channel_id=1, source_target_pairs={{0,16},{8,24},{16,32},{24,40},{32,48},{40,56},{48,0},{56,8},{64,80... | collective-permute-start | bytes 1228808 | tf_op jit(solution)/shard_map/ppermute | solution.py:20
  144.9 24.9 %collective-permute-start.18 = (bf16[512,1024]{1,0:T(8,128)(2,1)S(1)}, bf16[512,1024]{1,0:T(8,128)(2,1)}, u32[]{:S(2)}, u32[]{:S(2)}) collective-permute-start(bf16[512,1024]{1,0:T(8,128)(2,1)S(1)} %bitcast.149), channel_id=1, source_target_pairs={{0,8},{8,0},{16,24},{24,16},{32,40},{40,32},{48,56},{56,48},{64,72... | collective-permute-start | bytes 3145736 | tf_op jit(solution)/shard_map/ppermute | solution.py:24
  146.4 35.6 %collective-permute-start.14 = (bf16[512,1024]{1,0:T(8,128)(2,1)}, bf16[512,1024]{1,0:T(8,128)(2,1)}, u32[]{:S(2)}, u32[]{:S(2)}) collective-permute-start(bf16[512,1024]{1,0:T(8,128)(2,1)} %collective-permute-done.9.refs_1_), channel_id=1, source_target_pairs={{0,16},{8,24},{16,32},{24,40},{32,48},{40,56},{48,0},{56,8},{64,80... | collective-permute-start | bytes 3145736 | tf_op jit(solution)/shard_map/ppermute | solution.py:20
  154.5 19.7 %collective-permute-start.16 = (bf16[256,1024]{1,0:T(8,128)(2,1)S(1)}, bf16[256,1024]{1,0:T(8,128)(2,1)S(1)}, u32[]{:S(2)}, u32[]{:S(2)}) collective-permute-start(bf16[256,1024]{1,0:T(8,128)(2,1)S(1)} %collective-permute-done.12.refs_4_), channel_id=1, source_target_pairs={{0,64},{8,72},{16,80},{24,88},{32,96},{40,104},{48,112},{56,120},{... | collective-permute-start | bytes 1572872 | tf_op jit(solution)/shard_map/ppermute | solution.py:24
  155.8 20.9 %collective-permute-start.22 = (bf16[256,1024]{1,0:T(8,128)(2,1)S(1)}, bf16[256,1024]{1,0:T(8,128)(2,1)S(1)}, u32[]{:S(2)}, u32[]{:S(2)}) collective-permute-start(bf16[256,1024]{1,0:T(8,128)(2,1)S(1)} %collective-permute-done.12.refs_4_), channel_id=1, source_target_pairs={{0,8},{8,0},{16,24},{24,16},{32,40},{40,32},{48,56},{56,48},{64,72... | collective-permute-start | bytes 1572872 | tf_op jit(solution)/shard_map/ppermute | solution.py:24
  162.2 12.8 %collective-permute-start.17 = (bf16[256,1024]{1,0:T(8,128)(2,1)S(1)}, bf16[256,1024]{1,0:T(8,128)(2,1)}, u32[]{:S(2)}, u32[]{:S(2)}) collective-permute-start(bf16[256,1024]{1,0:T(8,128)(2,1)S(1)} %collective-permute-done.13.refs_5_), channel_id=1, source_target_pairs={{0,64},{8,72},{16,80},{24,88},{32,96},{40,104},{48,112},{56,120},{... | collective-permute-start | bytes 1572872 | tf_op jit(solution)/shard_map/ppermute | solution.py:24
  168.4 6.6 %copy-start.20 = (pred[2,2]{1,0:T(4,128)(4,1)S(1)}, pred[2,2]{1,0:T(4,128)(4,1)}, u32[]{:S(2)}) copy-start(pred[2,2]{1,0:T(4,128)(4,1)} %iota_compare_fusion.1) | copy-start | bytes 16
  169.8 19.8 %collective-permute-start.15 = (bf16[512,1024]{1,0:T(8,128)(2,1)}, bf16[512,1024]{1,0:T(8,128)(2,1)S(1)}, u32[]{:S(2)}, u32[]{:S(2)}) collective-permute-start(bf16[512,1024]{1,0:T(8,128)(2,1)} %collective-permute-done.9.refs_1_), channel_id=1, source_target_pairs={{0,48},{8,56},{16,0},{24,8},{32,16},{40,24},{48,32},{56,40},{64,11... | collective-permute-start | bytes 3145736 | tf_op jit(solution)/shard_map/ppermute | solution.py:20
  174.1 16.1 %collective-permute-start.19 = (bf16[512,1024]{1,0:T(8,128)(2,1)}, bf16[512,1024]{1,0:T(8,128)(2,1)S(1)}, u32[]{:S(2)}, u32[]{:S(2)}) collective-permute-start(bf16[512,1024]{1,0:T(8,128)(2,1)} %collective-permute-done.9.refs_1_), channel_id=1, source_target_pairs={{0,8},{8,0},{16,24},{24,16},{32,40},{40,32},{48,56},{56,48},{64,72... | collective-permute-start | bytes 3145736 | tf_op jit(solution)/shard_map/ppermute | solution.py:24
  175.0 15.8 %collective-permute-start.20 = (bf16[512,1024]{1,0:T(8,128)(2,1)S(1)}, bf16[512,1024]{1,0:T(8,128)(2,1)S(1)}, u32[]{:S(2)}, u32[]{:S(2)}) collective-permute-start(bf16[512,1024]{1,0:T(8,128)(2,1)S(1)} %copy-done.11), channel_id=1, source_target_pairs={{0,8},{8,0},{16,24},{24,16},{32,40},{40,32},{48,56},{56,48},{64,72... | collective-permute-start | bytes 3145736 | tf_op jit(solution)/shard_map/ppermute | solution.py:24
  176.8 5.1 %collective-permute-start.23 = (bf16[256,1024]{1,0:T(8,128)(2,1)S(1)}, bf16[256,1024]{1,0:T(8,128)(2,1)S(1)}, u32[]{:S(2)}, u32[]{:S(2)}) collective-permute-start(bf16[256,1024]{1,0:T(8,128)(2,1)S(1)} %collective-permute-done.13.refs_5_), channel_id=1, source_target_pairs={{0,8},{8,0},{16,24},{24,16},{32,40},{40,32},{48,56},{56,48},{64,72... | collective-permute-start | bytes 1572872 | tf_op jit(solution)/shard_map/ppermute | solution.py:24
  181.9 12.9 %collective-permute-start.21 = (bf16[512,1024]{1,0:T(8,128)(2,1)S(1)}, bf16[512,1024]{1,0:T(8,128)(2,1)S(1)}, u32[]{:S(2)}, u32[]{:S(2)}) collective-permute-start(bf16[512,1024]{1,0:T(8,128)(2,1)S(1)} %copy-done.9), channel_id=1, source_target_pairs={{0,8},{8,0},{16,24},{24,16},{32,40},{40,32},{48,56},{56,48},{64,72... | collective-permute-start | bytes 3145736 | tf_op jit(solution)/shard_map/ppermute | solution.py:24
  182.1 12.8 %collective-permute-start.24 = (bf16[512,1024]{1,0:T(8,128)(2,1)}, bf16[512,1024]{1,0:T(8,128)(2,1)S(1)}, u32[]{:S(2)}, u32[]{:S(2)}) collective-permute-start(bf16[512,1024]{1,0:T(8,128)(2,1)} %collective-permute-done.14.refs_6_), channel_id=1, source_target_pairs={{0,8},{8,0},{16,24},{24,16},{32,40},{40,32},{48,56},{56,48},{64,72... | collective-permute-start | bytes 3145736 | tf_op jit(solution)/shard_map/ppermute | solution.py:24
  189.6 5.2 %collective-permute-start.25 = (bf16[512,1024]{1,0:T(8,128)(2,1)S(1)}, bf16[512,1024]{1,0:T(8,128)(2,1)S(1)}, u32[]{:S(2)}, u32[]{:S(2)}) collective-permute-start(bf16[512,1024]{1,0:T(8,128)(2,1)S(1)} %collective-permute-done.15.refs_7_), channel_id=1, source_target_pairs={{0,8},{8,0},{16,24},{24,16},{32,40},{40,32},{48,56},{56,48},{64,72... | collective-permute-start | bytes 3145736 | tf_op jit(solution)/shard_map/ppermute | solution.py:24
  190.2 4.6 %collective-permute-start.26 = (bf16[256,1024]{1,0:T(8,128)(2,1)S(1)}, bf16[256,1024]{1,0:T(8,128)(2,1)S(1)}, u32[]{:S(2)}, u32[]{:S(2)}) collective-permute-start(bf16[256,1024]{1,0:T(8,128)(2,1)S(1)} %collective-permute-done.16.refs_8_), channel_id=1, source_target_pairs={{0,8},{8,0},{16,24},{24,16},{32,40},{40,32},{48,56},{56,48},{64,72... | collective-permute-start | bytes 1572872 | tf_op jit(solution)/shard_map/ppermute | solution.py:24
  190.8 4.0 %collective-permute-start.27 = (bf16[256,1024]{1,0:T(8,128)(2,1)}, bf16[256,1024]{1,0:T(8,128)(2,1)S(1)}, u32[]{:S(2)}, u32[]{:S(2)}) collective-permute-start(bf16[256,1024]{1,0:T(8,128)(2,1)} %collective-permute-done.17.refs_9_), channel_id=1, source_target_pairs={{0,8},{8,0},{16,24},{24,16},{32,40},{40,32},{48,56},{56,48},{64,72... | collective-permute-start | bytes 1572872 | tf_op jit(solution)/shard_map/ppermute | solution.py:24
  (18 other events, 38.3 us)

commit v3 on v2

--- a/solution.py
+++ b/solution.py
@@ -284,7 +284,7 @@
     parts = [parts[0]] + [z_shift(parts[k], k) for k in range(1, NZ)]
 
     w = flatten(lax.all_to_all(qkv_copy, "tp", split_axis=1, concat_axis=0, tiled=True))
-    w, out_copy = lax.optimization_barrier((w, out_copy))
+    w, out_copy, *parts = lax.optimization_barrier((w, out_copy, *parts))
     w_y = flip(w, 8)
     w_c = flip(w, 1)
     w_yc = flip(w_y, 1)

time: 259 us -> 255 us (0.985)
  blocking collectives: 69.1 us -> 39.5 us
  waiting for transfers between devices: 92.9 us -> 110 us
  starting transfers between devices: 29.2 us -> 37.9 us
    all_to_all x1 -> x0, blocking collectives: 26.5 us -> none  [body(): lax.all_to_all(qkv_copy, 'tp', split_axis=1, concat_axis=0, tiled=True)]
    ppermute x12, waiting for transfers between devices: 57.8 us -> 73.9 us  [z_shift(): return lax.ppermute(value, 'fsdp', pairs)]
    ppermute x16, waiting for transfers between devices: 19.8 us -> 32.7 us  [flip(): return lax.ppermute(value, 'fsdp', [(f, f ^ bit) for f in range(16)])]
    all_to_all x1, waiting for transfers between devices: 15.4 us -> 3.51 us  [body(): lax.all_to_all(out_copy, 'tp', split_axis=1, concat_axis=0, tiled=True)]
    all_to_all x0 -> x1, starting transfers between devices: none -> 7.01 us  [body(): lax.all_to_all(qkv_copy, 'tp', split_axis=1, concat_axis=0, tiled=True)]
    all_to_all x1, starting transfers between devices: 3.69 us -> 7.66 us  [body(): lax.all_to_all(out_copy, 'tp', split_axis=1, concat_axis=0, tiled=True)]
    all_to_all x1, blocking collectives: 42.6 us -> 39.5 us  [body(): terms = lax.all_to_all(terms, 'tp', split_axis=0, concat_axis=0, tiled=True)]
    ppermute x16, starting transfers between devices: 6.4 us -> 3.37 us  [flip(): return lax.ppermute(value, 'fsdp', [(f, f ^ bit) for f in range(16)])]
  transfers between devices with their start and end apart: 29 -> 30, of which waited for: 10 -> 10; matrix products, arithmetic and copies ran while one was open for 8% -> 9% of each run, Pallas kernels for 3% -> 2%
where the time goes in v3:
time: 255 us; the launch traced here: 254 us
  waiting for transfers between devices  110 us (43%)
  blocking collectives  39.5 us (15%)
  starting transfers between devices  37.9 us (15%)
  Pallas kernels  26 us (10%)
  local copies, waits for them, and re-layouts  19 us (7%)
  other arithmetic  11.5 us (5%)
  matrix products  9.39 us (4%)
    ppermute x12, waiting for transfers between devices, z_shift(): return lax.ppermute(value, 'fsdp', pairs)  73.9 us
    all_to_all x1, blocking collectives, body(): terms = lax.all_to_all(terms, 'tp', split_axis=0, concat_axis=0, tiled=True)  39.5 us
    ppermute x16, waiting for transfers between devices, flip(): return lax.ppermute(value, 'fsdp', [(f, f ^ bit) for f in range(16)])  32.7 us
    ppermute x12, starting transfers between devices, z_shift(): return lax.ppermute(value, 'fsdp', pairs)  19.9 us
    pallas_call x1, Pallas kernels, project_back(): pl.pallas_call(functools.partial(back_kernel, spots, groups), out_shape=j...  15.7 us
    unnamed x53, local copies, waits for them, and re-layouts  11.5 us
    all_to_all x1, starting transfers between devices, body(): lax.all_to_all(out_copy, 'tp', split_axis=1, concat_axis=0, tiled=True)  7.66 us
    all_to_all x1, starting transfers between devices, body(): lax.all_to_all(qkv_copy, 'tp', split_axis=1, concat_axis=0, tiled=True)  7.01 us
  transfers between devices with their start and end apart: 30, of which 10 were waited for; matrix products, arithmetic and copies ran while one was open for 9% of the time, Pallas kernels for 2%

profile of v3, /device:TPU:0, one launch (start us, length us, event | category | flops | bytes accessed | tf_op | source)
XLA Modules:
  0.0 253.9 jit_solution(1477129988355603671)
XLA Ops:
  0.0 1.9 convert_element_type.50
  2.1 1.5 copy-done.15
  3.7 1.6 copy.43
  5.8 4.1 %shuffle.1 = (bf16[160,2048]{1,0:T(8,128)(2,1)S(1)}, bf16[160,2048]{1,0:T(8,128)(2,1)S(1)}, bf16[160,2048]{1,0:T(8,128)(2,1)S(1)}, bf16[160,2048]{1,0:T(8,128)(2,1)S(1)}) custom-call(s32[2,128]{1,0:T(2,128)S(1)} %copy-done.1, bf16[160,8192]{1,0:T(8,128)(2,1)S(1)} %bitcast.151), custom_call_target="tpu_custom_call" | custom-call | flops 10485760 | bytes 5242880 | tf_op jit(solution)/shard_map/shuffle/pallas_call | solution.py:72
  9.9 1.4 pad_maximum_fusion
  11.6 7.0 %all-to-all-start = ((bf16[64,8,1280]{2,0,1:T(8,128)(2,1)}), bf16[64,8,1280]{2,0,1:T(8,128)(2,1)S(1)}, u32[]{:S(2)}, u32[]{:S(2)}) async-start(bf16[64,8,1280]{2,0,1:T(8,128)(2,1)} %pad_maximum_fusion), calls=%async_computation | async-start | bytes 2621440 | tf_op jit(solution)/shard_map/all_to_all | solution.py:286
  18.6 1.9 collective-permute-start
  20.5 3.6 %collective-permute-start.1 = (bf16[160,2048]{1,0:T(8,128)(2,1)}, bf16[160,2048]{1,0:T(8,128)(2,1)S(1)}, u32[]{:S(2)}, u32[]{:S(2)}) collective-permute-start(bf16[160,2048]{1,0:T(8,128)(2,1)} %copy-done.10), channel_id=1, source_target_pairs={{0,32},{8,40},{16,48},{24,56},{32,0},{40,8},{48,16},{56,24},{64,96... | collective-permute-start | bytes 1966088 | tf_op jit(solution)/shard_map/ppermute | solution.py:20
  25.1 12.5 %collective-permute-done.h1 = bf16[160,2048]{1,0:T(8,128)(2,1)S(1)} collective-permute-done((bf16[160,2048]{1,0:T(8,128)(2,1)}, bf16[160,2048]{1,0:T(8,128)(2,1)S(1)}, u32[]{:S(2)}, u32[]{:S(2)}) %collective-permute-start) | collective-permute-done | bytes 655392 | tf_op jit(solution)/shard_map/ppermute | solution.py:20
  37.6 14.9 %collective-permute-done.1.h2 = bf16[160,2048]{1,0:T(8,128)(2,1)S(1)} collective-permute-done((bf16[160,2048]{1,0:T(8,128)(2,1)}, bf16[160,2048]{1,0:T(8,128)(2,1)S(1)}, u32[]{:S(2)}, u32[]{:S(2)}) %collective-permute-start.1) | collective-permute-done | bytes 655392 | tf_op jit(solution)/shard_map/ppermute | solution.py:20
  54.9 2.8 %copy.28 = bf16[64,8,1024]{2,0,1:T(8,128)(2,1)} copy(bf16[64,8,1024]{2,1,0:T(8,128)(2,1)} %bitcast.158) | data formatting | bytes 2097152 | tf_op jit(solution)/shard_map/optimization_barrier | solution.py:287
  57.7 7.7 %all-to-all-start.1 = ((bf16[64,8,1024]{2,0,1:T(8,128)(2,1)}), bf16[64,8,1024]{2,0,1:T(8,128)(2,1)S(1)}, u32[]{:S(2)}, u32[]{:S(2)}) async-start(bf16[64,8,1024]{2,0,1:T(8,128)(2,1)} %copy.28), calls=%async_computation.1 | async-start | bytes 2097152 | tf_op jit(solution)/shard_map/all_to_all | solution.py:291
  65.4 28.1 %collective-permute-done.3.w1 = bf16[512,1280]{1,0:T(8,128)(2,1)} collective-permute-done((bf16[512,1280]{1,0:T(8,128)(2,1)S(1)}, bf16[512,1280]{1,0:T(8,128)(2,1)}, u32[]{:S(2)}, u32[]{:S(2)}) %collective-permute-start.3) | collective-permute-done | bytes 1310752 | tf_op jit(solution)/shard_map/ppermute | solution.py:24
  93.5 3.5 %all-to-all-done.1 = bf16[64,8,1024]{2,0,1:T(8,128)(2,1)S(1)} async-done(((bf16[64,8,1024]{2,0,1:T(8,128)(2,1)}), bf16[64,8,1024]{2,0,1:T(8,128)(2,1)S(1)}, u32[]{:S(2)}, u32[]{:S(2)}) %all-to-all-start.1) | async-done | bytes 1048608 | tf_op jit(solution)/shard_map/all_to_all | solution.py:291
  97.0 2.9 %collective-permute-start.11 = (bf16[512,1024]{1,0:T(8,128)(2,1)S(1)}, bf16[512,1024]{1,0:T(8,128)(2,1)S(1)}, u32[]{:S(2)}, u32[]{:S(2)}) collective-permute-start(bf16[512,1024]{1,0:T(8,128)(2,1)S(1)} %bitcast.146), channel_id=1, source_target_pairs={{0,48},{8,56},{16,0},{24,8},{32,16},{40,24},{48,32},{56,40},{64,11... | collective-permute-start | bytes 3145736 | tf_op jit(solution)/shard_map/ppermute | solution.py:20
  100.7 20.9 %collective-permute-done.11.refs_3_ = bf16[512,1024]{1,0:T(8,128)(2,1)S(1)} collective-permute-done((bf16[512,1024]{1,0:T(8,128)(2,1)S(1)}, bf16[512,1024]{1,0:T(8,128)(2,1)S(1)}, u32[]{:S(2)}, u32[]{:S(2)}) %collective-permute-start.11) | collective-permute-done | bytes 1048608 | tf_op jit(solution)/shard_map/ppermute | solution.py:20
  122.6 3.8 %collective-permute-start.12 = (bf16[256,1024]{1,0:T(8,128)(2,1)S(1)}, bf16[256,1024]{1,0:T(8,128)(2,1)S(1)}, u32[]{:S(2)}, u32[]{:S(2)}) collective-permute-start(bf16[256,1024]{1,0:T(8,128)(2,1)S(1)} %slice.67), channel_id=1, source_target_pairs={{0,48},{8,56},{16,0},{24,8},{32,16},{40,24},{48,32},{56,40},{64,11... | collective-permute-start | bytes 1572872 | tf_op jit(solution)/shard_map/ppermute | solution.py:20
  128.7 6.3 %partials.1 = (f32[160,1280]{1,0:T(8,128)S(1)}, bf16[160,1280]{1,0:T(8,128)(2,1)S(1)}, bf16[160,1280]{1,0:T(8,128)(2,1)S(1)}, bf16[160,1280]{1,0:T(8,128)(2,1)S(1)}) custom-call(bf16[160,2048]{1,0:T(8,128)(2,1)S(1)} %copy-done.3, bf16[160,2048]{1,0:T(8,128)(2,1)S(1)} %copy-done.5, bf16[160,2048]{1,0:T(8,128)(2,1)S(1)} %copy-done.7, ...), custom_call_target="tpu_custom_call" | custom-call | flops 3355443200 | bytes 9502720 | tf_op jit(solution)/shard_map/partials/pallas_call | solution.py:110
  135.0 3.3 %collective-permute-start.6 = (bf16[160,1280]{1,0:T(8,128)(2,1)S(1)}, bf16[160,1280]{1,0:T(8,128)(2,1)S(1)}, u32[]{:S(2)}, u32[]{:S(2)}) collective-permute-start(bf16[160,1280]{1,0:T(8,128)(2,1)S(1)} %get-tuple-element.41), channel_id=1, source_target_pairs={{0,48},{8,56},{16,0},{24,8},{32,16},{40,24},{48,32},{56,40},{64,11... | collective-permute-start | bytes 1228808 | tf_op jit(solution)/shard_map/ppermute | solution.py:20
  140.7 7.8 %collective-permute-done.13.refs_5_ = bf16[256,1024]{1,0:T(8,128)(2,1)S(1)} collective-permute-done((bf16[256,1024]{1,0:T(8,128)(2,1)S(1)}, bf16[256,1024]{1,0:T(8,128)(2,1)S(1)}, u32[]{:S(2)}, u32[]{:S(2)}) %collective-permute-start.13) | collective-permute-done | bytes 524320 | tf_op jit(solution)/shard_map/ppermute | solution.py:20
  148.6 5.0 %collective-permute-done.6 = bf16[160,1280]{1,0:T(8,128)(2,1)S(1)} collective-permute-done((bf16[160,1280]{1,0:T(8,128)(2,1)S(1)}, bf16[160,1280]{1,0:T(8,128)(2,1)S(1)}, u32[]{:S(2)}, u32[]{:S(2)}) %collective-permute-start.6) | collective-permute-done | bytes 409632 | tf_op jit(solution)/shard_map/ppermute | solution.py:20
  153.7 5.4 %collective-permute-done.8 = bf16[160,1280]{1,0:T(8,128)(2,1)S(1)} collective-permute-done((bf16[160,1280]{1,0:T(8,128)(2,1)S(1)}, bf16[160,1280]{1,0:T(8,128)(2,1)S(1)}, u32[]{:S(2)}, u32[]{:S(2)}) %collective-permute-start.8) | collective-permute-done | bytes 409632 | tf_op jit(solution)/shard_map/ppermute | solution.py:20
  165.6 2.4 collective-permute-start.15
  168.0 1.5 subtract_convert_fusion
  169.6 4.5 %collective-permute-done.17.refs_9_ = bf16[256,1024]{1,0:T(8,128)(2,1)} collective-permute-done((bf16[256,1024]{1,0:T(8,128)(2,1)S(1)}, bf16[256,1024]{1,0:T(8,128)(2,1)}, u32[]{:S(2)}, u32[]{:S(2)}) %collective-permute-start.17) | collective-permute-done | bytes 524320 | tf_op jit(solution)/shard_map/ppermute | solution.py:24
  174.1 1.8 fusion.45
  176.5 4.1 %bitcast_reduce_fusion = (f32[2,80,8]{2,0,1:T(2,128)S(1)}, f32[80,1,256,2,8]{2,4,3,0,1:T(8,128)S(1)}) fusion(bf16[2,80,256,128]{3,2,1,0:T(8,128)(2,1)} %param.10, bf16[2,80,8,64]{3,2,0,1:T(8,128)(2,1)S(1)} %get-tuple-element.46, bf16[2,80,8,64]{3,2,0,1:T(8,128)(2,1)S(1)} %get-tuple-element.45, pred[80,256]{1,0:T(8,128)(4,1)S(1)} %iota_compare_fusion), kind=kOutput, calls=%fused_computation.10 | convolution fusion | flops 85523200 | bytes 6906880 | tf_op jit(solution)/shard_map/srgjd,rpgd->srgjp/dot_general | solution.py:251
  181.6 7.2 %collective-permute-done.15.refs_7_ = bf16[512,1024]{1,0:T(8,128)(2,1)S(1)} collective-permute-done((bf16[512,1024]{1,0:T(8,128)(2,1)}, bf16[512,1024]{1,0:T(8,128)(2,1)S(1)}, u32[]{:S(2)}, u32[]{:S(2)}) %collective-permute-start.15) | collective-permute-done | bytes 1048608 | tf_op jit(solution)/shard_map/ppermute | solution.py:20
  190.4 3.1 %fusion.16 = f32[80,128,2,8]{1,3,2,0:T(8,128)S(1)} fusion(bf16[2,80,256,128]{3,2,1,0:T(8,128)(2,1)} %param.10, f32[80,1,256,2,8]{2,4,3,0,1:T(8,128)S(1)} %get-tuple-element.54, f32[2,80,8]{2,0,1:T(2,128)S(1)} %add.53, f32[2,80,8]{2,0,1:T(2,128)S(1)} %max.9), kind=kOutput, calls=%fused_computation.14 | convolution fusion | flops 84869120 | bytes 7219200 | tf_op jit(solution)/shard_map/srgjp,rpgd->srgjd/dot_general | solution.py:266
  195.7 15.7 %project_back.1 = bf16[8,160,1024]{2,1,0:T(8,128)(2,1)} custom-call(s32[2,128]{1,0:T(2,128)S(1)} %copy-done.1, bf16[160,1024]{1,0:T(8,128)(2,1)S(1)} %bitcast.155, bf16[512,1024]{1,0:T(8,128)(2,1)S(1)} %bitcast.150, bf16[512,1024]{1,0:T(8,128)(2,1)} %collective-permute-done.9.refs_1_, bf16[512,1024]{1,0:T(8,128)(2,1)} %collective-permute-done.10.refs_2_, ...), custom_call_target="tpu_custom_call" | custom-call | flops 2684354560 | bytes 19726336 | tf_op jit(solution)/shard_map/project_back/pallas_call | solution.py:171
  211.4 39.5 %all_to_all.35 = bf16[8,160,1024]{2,1,0:T(8,128)(2,1)} all-to-all(bf16[8,160,1024]{2,1,0:T(8,128)(2,1)} %project_back.1), channel_id=1, replica_groups=mesh['fsdp'=16,'tp'=8] {'tp'}, dimensions={0} | all-to-all | bytes 5242880 | tf_op jit(solution)/shard_map/all_to_all | solution.py:300
  250.9 3.0 %reduce_sum.32 = bf16[160,1024]{1,0:T(8,128)(2,1)} reduce(bf16[8,160,1024]{2,1,0:T(8,128)(2,1)} %all_to_all.35, bf16[]{:T(256)} %constant.15.clone.1), dimensions={0}, to_apply=%region_4.5 | reduce | flops 1146880 | bytes 2949122 | tf_op jit(solution)/shard_map/reduce_sum | solution.py:301
  (120 shorter events, 22.7 us)
Async XLA Ops:
  11.6 42.6 %all-to-all-start = ((bf16[64,8,1280]{2,0,1:T(8,128)(2,1)}), bf16[64,8,1280]{2,0,1:T(8,128)(2,1)S(1)}, u32[]{:S(2)}, u32[]{:S(2)}) async-start(bf16[64,8,1280]{2,0,1:T(8,128)(2,1)} %pad_maximum_fusion), calls=%async_computation | async-start | bytes 2621440 | tf_op jit(solution)/shard_map/all_to_all | solution.py:286
  18.6 19.0 %collective-permute-start = (bf16[160,2048]{1,0:T(8,128)(2,1)}, bf16[160,2048]{1,0:T(8,128)(2,1)S(1)}, u32[]{:S(2)}, u32[]{:S(2)}) collective-permute-start(bf16[160,2048]{1,0:T(8,128)(2,1)} %copy-done.11), channel_id=1, source_target_pairs={{0,16},{8,24},{16,32},{24,40},{32,48},{40,56},{48,0},{56,8},{64,80... | collective-permute-start | bytes 1966088 | tf_op jit(solution)/shard_map/ppermute | solution.py:20
  20.5 32.0 %collective-permute-start.1 = (bf16[160,2048]{1,0:T(8,128)(2,1)}, bf16[160,2048]{1,0:T(8,128)(2,1)S(1)}, u32[]{:S(2)}, u32[]{:S(2)}) collective-permute-start(bf16[160,2048]{1,0:T(8,128)(2,1)} %copy-done.10), channel_id=1, source_target_pairs={{0,32},{8,40},{16,48},{24,56},{32,0},{40,8},{48,16},{56,24},{64,96... | collective-permute-start | bytes 1966088 | tf_op jit(solution)/shard_map/ppermute | solution.py:20
  24.1 29.3 %collective-permute-start.2 = (bf16[160,2048]{1,0:T(8,128)(2,1)S(1)}, bf16[160,2048]{1,0:T(8,128)(2,1)S(1)}, u32[]{:S(2)}, u32[]{:S(2)}) collective-permute-start(bf16[160,2048]{1,0:T(8,128)(2,1)S(1)} %get-tuple-element.34), channel_id=1, source_target_pairs={{0,48},{8,56},{16,0},{24,8},{32,16},{40,24},{48,32},{56,40},{64,11... | collective-permute-start | bytes 1966088 | tf_op jit(solution)/shard_map/ppermute | solution.py:20
  54.2 39.3 %collective-permute-start.3 = (bf16[512,1280]{1,0:T(8,128)(2,1)S(1)}, bf16[512,1280]{1,0:T(8,128)(2,1)}, u32[]{:S(2)}, u32[]{:S(2)}) collective-permute-start(bf16[512,1280]{1,0:T(8,128)(2,1)S(1)} %bitcast.152), channel_id=1, source_target_pairs={{0,64},{8,72},{16,80},{24,88},{32,96},{40,104},{48,112},{56,120},{... | collective-permute-start | bytes 3932168 | tf_op jit(solution)/shard_map/ppermute | solution.py:24
  57.7 42.3 %copy-start.22 = (s32[80]{0:T(128)S(1)}, s32[80]{0:T(128)}, u32[]{:S(2)}) copy-start(s32[80]{0:T(128)} %param.11) | copy-start | bytes 964
  57.7 39.3 %all-to-all-start.1 = ((bf16[64,8,1024]{2,0,1:T(8,128)(2,1)}), bf16[64,8,1024]{2,0,1:T(8,128)(2,1)S(1)}, u32[]{:S(2)}, u32[]{:S(2)}) async-start(bf16[64,8,1024]{2,0,1:T(8,128)(2,1)} %copy.28), calls=%async_computation.1 | async-start | bytes 2097152 | tf_op jit(solution)/shard_map/all_to_all | solution.py:291
  65.4 62.2 %collective-permute-start.4 = (bf16[512,1280]{1,0:T(8,128)(2,1)S(1)}, bf16[512,1280]{1,0:T(8,128)(2,1)}, u32[]{:S(2)}, u32[]{:S(2)}) collective-permute-start(bf16[512,1280]{1,0:T(8,128)(2,1)S(1)} %bitcast.153), channel_id=1, source_target_pairs={{0,8},{8,0},{16,24},{24,16},{32,40},{40,32},{48,56},{56,48},{64,72... | collective-permute-start | bytes 3932168 | tf_op jit(solution)/shard_map/ppermute | solution.py:24
  93.5 34.1 %collective-permute-start.5 = (bf16[512,1280]{1,0:T(8,128)(2,1)}, bf16[512,1280]{1,0:T(8,128)(2,1)}, u32[]{:S(2)}, u32[]{:S(2)}) collective-permute-start(bf16[512,1280]{1,0:T(8,128)(2,1)} %collective-permute-done.3.w1), channel_id=1, source_target_pairs={{0,8},{8,0},{16,24},{24,16},{32,40},{40,32},{48,56},{56,48},{64,72... | collective-permute-start | bytes 3932168 | tf_op jit(solution)/shard_map/ppermute | solution.py:24
  97.0 24.6 %collective-permute-start.11 = (bf16[512,1024]{1,0:T(8,128)(2,1)S(1)}, bf16[512,1024]{1,0:T(8,128)(2,1)S(1)}, u32[]{:S(2)}, u32[]{:S(2)}) collective-permute-start(bf16[512,1024]{1,0:T(8,128)(2,1)S(1)} %bitcast.146), channel_id=1, source_target_pairs={{0,48},{8,56},{16,0},{24,8},{32,16},{40,24},{48,32},{56,40},{64,11... | collective-permute-start | bytes 3145736 | tf_op jit(solution)/shard_map/ppermute | solution.py:20
  99.9 26.5 %collective-permute-start.10 = (bf16[512,1024]{1,0:T(8,128)(2,1)S(1)}, bf16[512,1024]{1,0:T(8,128)(2,1)}, u32[]{:S(2)}, u32[]{:S(2)}) collective-permute-start(bf16[512,1024]{1,0:T(8,128)(2,1)S(1)} %bitcast.147), channel_id=1, source_target_pairs={{0,16},{8,24},{16,32},{24,40},{32,48},{40,56},{48,0},{56,8},{64,80... | collective-permute-start | bytes 3145736 | tf_op jit(solution)/shard_map/ppermute | solution.py:20
  99.9 38.4 %collective-permute-start.9 = (bf16[512,1024]{1,0:T(8,128)(2,1)S(1)}, bf16[512,1024]{1,0:T(8,128)(2,1)}, u32[]{:S(2)}, u32[]{:S(2)}) collective-permute-start(bf16[512,1024]{1,0:T(8,128)(2,1)S(1)} %bitcast.148), channel_id=1, source_target_pairs={{0,64},{8,72},{16,80},{24,88},{32,96},{40,104},{48,112},{56,120},{... | collective-permute-start | bytes 3145736 | tf_op jit(solution)/shard_map/ppermute | solution.py:24
  100.1 27.5 %copy-start.7 = (bf16[160,2048]{1,0:T(8,128)(2,1)S(1)}, bf16[160,2048]{1,0:T(8,128)(2,1)}, u32[]{:S(2)}) copy-start(bf16[160,2048]{1,0:T(8,128)(2,1)} %copy-done.6) | copy-start | bytes 1966084
  122.6 18.0 %collective-permute-start.12 = (bf16[256,1024]{1,0:T(8,128)(2,1)S(1)}, bf16[256,1024]{1,0:T(8,128)(2,1)S(1)}, u32[]{:S(2)}, u32[]{:S(2)}) collective-permute-start(bf16[256,1024]{1,0:T(8,128)(2,1)S(1)} %slice.67), channel_id=1, source_target_pairs={{0,48},{8,56},{16,0},{24,8},{32,16},{40,24},{48,32},{56,40},{64,11... | collective-permute-start | bytes 1572872 | tf_op jit(solution)/shard_map/ppermute | solution.py:20
  127.5 21.1 %collective-permute-start.13 = (bf16[256,1024]{1,0:T(8,128)(2,1)S(1)}, bf16[256,1024]{1,0:T(8,128)(2,1)S(1)}, u32[]{:S(2)}, u32[]{:S(2)}) collective-permute-start(bf16[256,1024]{1,0:T(8,128)(2,1)S(1)} %slice.68), channel_id=1, source_target_pairs={{0,16},{8,24},{16,32},{24,40},{32,48},{40,56},{48,0},{56,8},{64,80... | collective-permute-start | bytes 1572872 | tf_op jit(solution)/shard_map/ppermute | solution.py:20
  135.0 18.6 %collective-permute-start.6 = (bf16[160,1280]{1,0:T(8,128)(2,1)S(1)}, bf16[160,1280]{1,0:T(8,128)(2,1)S(1)}, u32[]{:S(2)}, u32[]{:S(2)}) collective-permute-start(bf16[160,1280]{1,0:T(8,128)(2,1)S(1)} %get-tuple-element.41), channel_id=1, source_target_pairs={{0,48},{8,56},{16,0},{24,8},{32,16},{40,24},{48,32},{56,40},{64,11... | collective-permute-start | bytes 1228808 | tf_op jit(solution)/shard_map/ppermute | solution.py:20
  138.2 15.5 %collective-permute-start.7 = (bf16[160,1280]{1,0:T(8,128)(2,1)S(1)}, bf16[160,1280]{1,0:T(8,128)(2,1)S(1)}, u32[]{:S(2)}, u32[]{:S(2)}) collective-permute-start(bf16[160,1280]{1,0:T(8,128)(2,1)S(1)} %get-tuple-element.42), channel_id=1, source_target_pairs={{0,32},{8,40},{16,48},{24,56},{32,0},{40,8},{48,16},{56,24},{64,96... | collective-permute-start | bytes 1228808 | tf_op jit(solution)/shard_map/ppermute | solution.py:20
  138.2 20.9 %collective-permute-start.8 = (bf16[160,1280]{1,0:T(8,128)(2,1)S(1)}, bf16[160,1280]{1,0:T(8,128)(2,1)S(1)}, u32[]{:S(2)}, u32[]{:S(2)}) collective-permute-start(bf16[160,1280]{1,0:T(8,128)(2,1)S(1)} %get-tuple-element.43), channel_id=1, source_target_pairs={{0,16},{8,24},{16,32},{24,40},{32,48},{40,56},{48,0},{56,8},{64,80... | collective-permute-start | bytes 1228808 | tf_op jit(solution)/shard_map/ppermute | solution.py:20
  140.6 24.9 %collective-permute-start.18 = (bf16[512,1024]{1,0:T(8,128)(2,1)S(1)}, bf16[512,1024]{1,0:T(8,128)(2,1)}, u32[]{:S(2)}, u32[]{:S(2)}) collective-permute-start(bf16[512,1024]{1,0:T(8,128)(2,1)S(1)} %bitcast.149), channel_id=1, source_target_pairs={{0,8},{8,0},{16,24},{24,16},{32,40},{40,32},{48,56},{56,48},{64,72... | collective-permute-start | bytes 3145736 | tf_op jit(solution)/shard_map/ppermute | solution.py:24
  148.6 32.6 %collective-permute-start.14 = (bf16[512,1024]{1,0:T(8,128)(2,1)}, bf16[512,1024]{1,0:T(8,128)(2,1)}, u32[]{:S(2)}, u32[]{:S(2)}) collective-permute-start(bf16[512,1024]{1,0:T(8,128)(2,1)} %collective-permute-done.9.refs_1_), channel_id=1, source_target_pairs={{0,16},{8,24},{16,32},{24,40},{32,48},{40,56},{48,0},{56,8},{64,80... | collective-permute-start | bytes 3145736 | tf_op jit(solution)/shard_map/ppermute | solution.py:20
  153.6 15.9 %collective-permute-start.16 = (bf16[256,1024]{1,0:T(8,128)(2,1)S(1)}, bf16[256,1024]{1,0:T(8,128)(2,1)S(1)}, u32[]{:S(2)}, u32[]{:S(2)}) collective-permute-start(bf16[256,1024]{1,0:T(8,128)(2,1)S(1)} %collective-permute-done.12.refs_4_), channel_id=1, source_target_pairs={{0,64},{8,72},{16,80},{24,88},{32,96},{40,104},{48,112},{56,120},{... | collective-permute-start | bytes 1572872 | tf_op jit(solution)/shard_map/ppermute | solution.py:24
  153.7 22.2 %collective-permute-start.22 = (bf16[256,1024]{1,0:T(8,128)(2,1)S(1)}, bf16[256,1024]{1,0:T(8,128)(2,1)S(1)}, u32[]{:S(2)}, u32[]{:S(2)}) collective-permute-start(bf16[256,1024]{1,0:T(8,128)(2,1)S(1)} %collective-permute-done.12.refs_4_), channel_id=1, source_target_pairs={{0,8},{8,0},{16,24},{24,16},{32,40},{40,32},{48,56},{56,48},{64,72... | collective-permute-start | bytes 1572872 | tf_op jit(solution)/shard_map/ppermute | solution.py:24
  159.1 15.0 %collective-permute-start.17 = (bf16[256,1024]{1,0:T(8,128)(2,1)S(1)}, bf16[256,1024]{1,0:T(8,128)(2,1)}, u32[]{:S(2)}, u32[]{:S(2)}) collective-permute-start(bf16[256,1024]{1,0:T(8,128)(2,1)S(1)} %collective-permute-done.13.refs_5_), channel_id=1, source_target_pairs={{0,64},{8,72},{16,80},{24,88},{32,96},{40,104},{48,112},{56,120},{... | collective-permute-start | bytes 1572872 | tf_op jit(solution)/shard_map/ppermute | solution.py:24
  165.6 23.3 %collective-permute-start.15 = (bf16[512,1024]{1,0:T(8,128)(2,1)}, bf16[512,1024]{1,0:T(8,128)(2,1)S(1)}, u32[]{:S(2)}, u32[]{:S(2)}) collective-permute-start(bf16[512,1024]{1,0:T(8,128)(2,1)} %collective-permute-done.9.refs_1_), channel_id=1, source_target_pairs={{0,48},{8,56},{16,0},{24,8},{32,16},{40,24},{48,32},{56,40},{64,11... | collective-permute-start | bytes 3145736 | tf_op jit(solution)/shard_map/ppermute | solution.py:20
  169.5 19.9 %collective-permute-start.19 = (bf16[512,1024]{1,0:T(8,128)(2,1)}, bf16[512,1024]{1,0:T(8,128)(2,1)S(1)}, u32[]{:S(2)}, u32[]{:S(2)}) collective-permute-start(bf16[512,1024]{1,0:T(8,128)(2,1)} %collective-permute-done.9.refs_1_), channel_id=1, source_target_pairs={{0,8},{8,0},{16,24},{24,16},{32,40},{40,32},{48,56},{56,48},{64,72... | collective-permute-start | bytes 3145736 | tf_op jit(solution)/shard_map/ppermute | solution.py:24
  174.1 15.9 %collective-permute-start.20 = (bf16[512,1024]{1,0:T(8,128)(2,1)}, bf16[512,1024]{1,0:T(8,128)(2,1)S(1)}, u32[]{:S(2)}, u32[]{:S(2)}) collective-permute-start(bf16[512,1024]{1,0:T(8,128)(2,1)} %collective-permute-done.10.refs_2_), channel_id=1, source_target_pairs={{0,8},{8,0},{16,24},{24,16},{32,40},{40,32},{48,56},{56,48},{64,72... | collective-permute-start | bytes 3145736 | tf_op jit(solution)/shard_map/ppermute | solution.py:24
  175.9 5.1 %collective-permute-start.23 = (bf16[256,1024]{1,0:T(8,128)(2,1)S(1)}, bf16[256,1024]{1,0:T(8,128)(2,1)S(1)}, u32[]{:S(2)}, u32[]{:S(2)}) collective-permute-start(bf16[256,1024]{1,0:T(8,128)(2,1)S(1)} %collective-permute-done.13.refs_5_), channel_id=1, source_target_pairs={{0,8},{8,0},{16,24},{24,16},{32,40},{40,32},{48,56},{56,48},{64,72... | collective-permute-start | bytes 1572872 | tf_op jit(solution)/shard_map/ppermute | solution.py:24
  181.0 13.0 %collective-permute-start.21 = (bf16[512,1024]{1,0:T(8,128)(2,1)S(1)}, bf16[512,1024]{1,0:T(8,128)(2,1)S(1)}, u32[]{:S(2)}, u32[]{:S(2)}) collective-permute-start(bf16[512,1024]{1,0:T(8,128)(2,1)S(1)} %copy-done.14), channel_id=1, source_target_pairs={{0,8},{8,0},{16,24},{24,16},{32,40},{40,32},{48,56},{56,48},{64,72... | collective-permute-start | bytes 3145736 | tf_op jit(solution)/shard_map/ppermute | solution.py:24
  181.2 12.8 %collective-permute-start.24 = (bf16[512,1024]{1,0:T(8,128)(2,1)}, bf16[512,1024]{1,0:T(8,128)(2,1)S(1)}, u32[]{:S(2)}, u32[]{:S(2)}) collective-permute-start(bf16[512,1024]{1,0:T(8,128)(2,1)} %collective-permute-done.14.refs_6_), channel_id=1, source_target_pairs={{0,8},{8,0},{16,24},{24,16},{32,40},{40,32},{48,56},{56,48},{64,72... | collective-permute-start | bytes 3145736 | tf_op jit(solution)/shard_map/ppermute | solution.py:24
  188.8 5.2 %collective-permute-start.25 = (bf16[512,1024]{1,0:T(8,128)(2,1)S(1)}, bf16[512,1024]{1,0:T(8,128)(2,1)S(1)}, u32[]{:S(2)}, u32[]{:S(2)}) collective-permute-start(bf16[512,1024]{1,0:T(8,128)(2,1)S(1)} %collective-permute-done.15.refs_7_), channel_id=1, source_target_pairs={{0,8},{8,0},{16,24},{24,16},{32,40},{40,32},{48,56},{56,48},{64,72... | collective-permute-start | bytes 3145736 | tf_op jit(solution)/shard_map/ppermute | solution.py:24
  189.4 4.6 %collective-permute-start.26 = (bf16[256,1024]{1,0:T(8,128)(2,1)S(1)}, bf16[256,1024]{1,0:T(8,128)(2,1)S(1)}, u32[]{:S(2)}, u32[]{:S(2)}) collective-permute-start(bf16[256,1024]{1,0:T(8,128)(2,1)S(1)} %collective-permute-done.16.refs_8_), channel_id=1, source_target_pairs={{0,8},{8,0},{16,24},{24,16},{32,40},{40,32},{48,56},{56,48},{64,72... | collective-permute-start | bytes 1572872 | tf_op jit(solution)/shard_map/ppermute | solution.py:24
  190.0 4.0 %collective-permute-start.27 = (bf16[256,1024]{1,0:T(8,128)(2,1)}, bf16[256,1024]{1,0:T(8,128)(2,1)S(1)}, u32[]{:S(2)}, u32[]{:S(2)}) collective-permute-start(bf16[256,1024]{1,0:T(8,128)(2,1)} %collective-permute-done.17.refs_9_), channel_id=1, source_target_pairs={{0,8},{8,0},{16,24},{24,16},{32,40},{40,32},{48,56},{56,48},{64,72... | collective-permute-start | bytes 1572872 | tf_op jit(solution)/shard_map/ppermute | solution.py:24
  (22 other events, 121.4 us)

commit v4 on v3

--- a/solution.py
+++ b/solution.py
@@ -12,6 +12,8 @@
 HK = 8
 HD = 128
 NZ = 4
+GROUP = 8
+AHEAD = 4
 MIB = 1024 * 1024
 
 
@@ -77,7 +79,7 @@
             pl.BlockSpec(memory_space=pltpu.VMEM),
         ],
         out_specs=[pl.BlockSpec(memory_space=pltpu.VMEM)] * NZ,
-        compiler_params=pltpu.CompilerParams(vmem_limit_bytes=24 * MIB),
+        compiler_params=pltpu.CompilerParams(vmem_limit_bytes=48 * MIB),
         cost_estimate=pl.CostEstimate(
             flops=rows * width * 8, bytes_accessed=4 * rows * width, transcendentals=0
         ),
@@ -116,7 +118,7 @@
         + [pl.BlockSpec((depth, tile), lambda j: (0, j))] * NZ,
         out_specs=[pl.BlockSpec((rows, tile), lambda j: (0, j))] * NZ,
         scratch_shapes=[pltpu.VMEM((NZ * rows, width), jnp.bfloat16)],
-        compiler_params=pltpu.CompilerParams(vmem_limit_bytes=32 * MIB),
+        compiler_params=pltpu.CompilerParams(vmem_limit_bytes=48 * MIB),
         cost_estimate=pl.CostEstimate(
             flops=2 * NZ * rows * width * cols,
             bytes_accessed=2 * (NZ * rows * width + width * cols + NZ * rows * cols),
@@ -142,8 +144,9 @@
         copies.append(
             pltpu.make_async_copy(source, held.at[pl.ds(begin, size)], sems.at[n])
         )
-        copies[-1].start()
         begin += size
+    for copy in copies[:AHEAD]:
+        copy.start()
     turned = mixed_ref[...].astype(jnp.float32).T.astype(jnp.bfloat16)
 
     begin = 0
@@ -153,6 +156,8 @@
             lax.rem(y_lo + dy, 2) * 64 + lax.rem(z + dz, NZ) * 16 + lax.rem(core + dc, 2) * 8 + t0
         )
         copies[n].wait()
+        if n + AHEAD < count:
+            copies[n + AHEAD].start()
         terms = jnp.dot(held[begin : begin + size], turned, preferred_element_type=jnp.float32)
         terms = terms.astype(jnp.bfloat16)
         for b in range(size // owned):
@@ -192,82 +197,147 @@
     )(block_owner, mixed, *sources)
 
 
-def gather_rows(own):
-    half = own.shape[0] // 2
-    across = flip(own, 8)
-    below, above = z_shift(own, 1), z_shift(own, -1)
-    far_a, far_b = z_shift(above[:half], -1), z_shift(below[half:], 1)
-    across_below, across_above = z_shift(across, 1), z_shift(across, -1)
-    across_far_a, across_far_b = flip(far_a, 8), flip(far_b, 8)
-    held = [
-        (own, (0, 0), 0),
-        (across, (1, 0), 0),
-        (below, (0, 3), 0),
-        (above, (0, 1), 0),
-        (far_a, (0, 2), 0),
-        (far_b, (0, 2), 4),
-        (across_below, (1, 3), 0),
-        (across_above, (1, 1), 0),
-        (across_far_a, (1, 2), 0),
-        (across_far_b, (1, 2), 4),
-    ]
-    sources = [value for value, _, _ in held] + [flip(value, 1) for value, _, _ in held]
-    spots = [(*at, core, t0) for core in (0, 1) for _, at, t0 in held]
-    return sources, tuple(spots)
-
-
-def rotary(values, position):
+def turns(lengths):
     half = HD // 2
+    position = (lengths[None, :] + jnp.arange(2, dtype=jnp.int32)[:, None]).reshape(-1)
     freq = 1000000.0 ** (-jnp.arange(half, dtype=jnp.float32) * 2.0 / HD)
-    angle = position.astype(jnp.float32)[..., None, None] * freq
-    cosine = jnp.cos(angle)
-    sine = jnp.sin(angle)
-    first = values[..., :half]
-    second = values[..., half:]
-    return jnp.concatenate(
-        [first * cosine - second * sine, second * cosine + first * sine], axis=-1
-    )
-
-
-def attention(proj, cache, lengths, groups):
-    rows = lengths.shape[0]
-    heads = HQ // groups
-    kv_heads = HK // groups
-    query_cols = heads * HD
-    kv_cols = kv_heads * HD
-    proj = proj.reshape(2, rows, -1)
-    position = lengths[None, :] + jnp.arange(2, dtype=jnp.int32)[:, None]
-    query = rotary(proj[..., :query_cols].reshape(2, rows, heads, HD), position).astype(
-        jnp.bfloat16
-    )
-    new_keys = rotary(
-        proj[..., query_cols : query_cols + kv_cols].reshape(2, rows, kv_heads, HD), position
-    ).astype(jnp.bfloat16)
-    new_vals = proj[..., query_cols + kv_cols :].reshape(2, rows, kv_heads, HD).astype(jnp.bfloat16)
-    query = query.reshape(2, rows, kv_heads, HQ // HK, HD)
-    keys = cache[0].reshape(rows, -1, kv_heads, HD)
-    vals = cache[1].reshape(rows, -1, kv_heads, HD)
+    angle = position.astype(jnp.float32)[:, None] * freq
+    cosine, sine = jnp.cos(angle), jnp.sin(angle)
+    return jnp.concatenate([cosine, cosine], axis=1), jnp.concatenate([-sine, sine], axis=1)
+
+
+def attention_kernel(
+    lengths_ref, p0, p1, p2, p3, cos_ref, sin_ref, cache_ref, out_ref, query, keys, values, result
+):
+    step = pl.program_id(0)
+    both = p0.shape[0]
+    rows = both // 2
+    heads = out_ref.shape[1] // HD
+    lanes = 2 * heads
+    span = GROUP * lanes
+
+    @pl.when(step == 0)
+    def _():
+        cosine, sine = cos_ref[...], sin_ref[...]
+
+        def part(begin):
+            cut = slice(begin * HD, (begin + 1) * HD)
+            total = p0[:, cut] + p1[:, cut].astype(jnp.float32)
+            return total + p2[:, cut].astype(jnp.float32) + p3[:, cut].astype(jnp.float32)
+
+        def turn(x):
+            return x * cosine + pltpu.roll(x, HD // 2, 1) * sine
+
+        for h in range(heads):
+            turned = turn(part(h))
+            for s in range(2):
+                query[pl.ds(s * heads + h, rows, stride=lanes), :] = turned[
+                    s * rows : (s + 1) * rows
+                ]
+        new_keys, new_values = turn(part(heads)), part(heads + 1)
+        for g in range(rows // GROUP):
+            for t in range(2):
+                to = slice((2 * g + t) * GROUP, (2 * g + t + 1) * GROUP)
+                begin = t * rows + g * GROUP
+                keys[to] = new_keys[begin : begin + GROUP]
+                values[to] = new_values[begin : begin + GROUP]
+
     factor = 1.0 / math.sqrt(HD)
-    old = jnp.einsum("srgjd,rpgd->srgjp", query, keys, preferred_element_type=jnp.float32) * factor
+    nt = (((1,), (1,)), ((), ()))
+    at = pl.ds(pl.multiple_of(step * span, span), span)
+    fresh_at = pl.ds(pl.multiple_of(step * 2 * GROUP, 2 * GROUP), 2 * GROUP)
+    q = query[at, :].astype(jnp.bfloat16)
     fresh = (
-        jnp.einsum("srgjd,trgd->srgjt", query, new_keys, preferred_element_type=jnp.float32)
+        lax.dot_general(
+            q, keys[fresh_at, :].astype(jnp.bfloat16), nt, preferred_element_type=jnp.float32
+        )
         * factor
     )
-    live = jnp.arange(keys.shape[1])[None, :] < lengths[:, None]
-    old = jnp.where(live[None, :, None, None, :], old, -jnp.inf)
-    seen = jnp.arange(2)[None, :] <= jnp.arange(2)[:, None]
-    fresh = jnp.where(seen[:, None, None, None, :], fresh, -jnp.inf)
-    top = jnp.maximum(jnp.max(old, -1), jnp.max(fresh, -1))[..., None]
+    of = lax.broadcasted_iota(jnp.int32, fresh.shape, 0)
+    new = lax.broadcasted_iota(jnp.int32, fresh.shape, 1)
+    seen = (of // lanes == new % GROUP) & (new // GROUP <= (of // heads) % 2)
+    fresh = jnp.where(seen, fresh, -jnp.inf)
+
+    held = cache_ref.shape[2]
+    place = lax.broadcasted_iota(jnp.int32, (lanes, held), 1)
+    pieces = []
+    for r in range(GROUP):
+        score = lax.dot_general(
+            q[r * lanes : (r + 1) * lanes], cache_ref[0, r], nt, preferred_element_type=jnp.float32
+        )
+        pieces.append(jnp.where(place < lengths_ref[step * GROUP + r], score * factor, -jnp.inf))
+    old = jnp.concatenate(pieces, axis=0)
+    top = jnp.maximum(
+        jnp.max(old, axis=1, keepdims=True), jnp.max(fresh, axis=1, keepdims=True)
+    )
     old_w = jnp.exp(old - top)
     fresh_w = jnp.exp(fresh - top)
-    total = jnp.sum(old_w, -1, keepdims=True) + jnp.sum(fresh_w, -1, keepdims=True)
-    old_p = (old_w / total).astype(jnp.bfloat16)
-    fresh_p = (fresh_w / total).astype(jnp.bfloat16)
-    mixed = jnp.einsum("srgjp,rpgd->srgjd", old_p, vals, preferred_element_type=jnp.float32)
-    mixed = mixed + jnp.einsum(
-        "srgjt,trgd->srgjd", fresh_p, new_vals, preferred_element_type=jnp.float32
-    )
-    return mixed.astype(jnp.bfloat16).reshape(2 * rows, query_cols)
+    total = jnp.sum(old_w, axis=1, keepdims=True) + jnp.sum(fresh_w, axis=1, keepdims=True)
+    scale = 1.0 / total
+    old_p = (old_w * scale).astype(jnp.bfloat16)
+    fresh_p = (fresh_w * scale).astype(jnp.bfloat16)
+    mixed = jnp.concatenate(
+        [
+            jnp.dot(
+                old_p[r * lanes : (r + 1) * lanes],
+                cache_ref[1, r],
+                preferred_element_type=jnp.float32,
+            )
+            for r in range(GROUP)
+        ],
+        axis=0,
+    )
+    mixed = mixed + jnp.dot(
+        fresh_p, values[fresh_at, :].astype(jnp.bfloat16), preferred_element_type=jnp.float32
+    )
+    result[at, :] = mixed
+
+    @pl.when(step == pl.num_programs(0) - 1)
+    def _():
+        for h in range(heads):
+            for s in range(2):
+                out_ref[s * rows : (s + 1) * rows, h * HD : (h + 1) * HD] = result[
+                    pl.ds(s * heads + h, rows, stride=lanes), :
+                ].astype(out_ref.dtype)
+
+
+def attention(sums, cos, sin, cache, lengths):
+    both, cols = sums[0].shape
+    rows = both // 2
+    width = cols - 2 * HD
+    held = cache.shape[2]
+    lanes = 2 * width // HD
+
+    def whole(*shape):
+        return pl.BlockSpec(shape, lambda g: (0,) * len(shape))
+
+    return pl.pallas_call(
+        attention_kernel,
+        grid=(rows // GROUP,),
+        out_shape=jax.ShapeDtypeStruct((both, width), jnp.bfloat16),
+        in_specs=[pl.BlockSpec(memory_space=pltpu.SMEM)]
+        + [whole(both, cols)] * NZ
+        + [whole(both, HD)] * 2
+        + [pl.BlockSpec((2, GROUP, held, HD), lambda g: (0, g, 0, 0))],
+        out_specs=whole(both, width),
+        scratch_shapes=[
+            pltpu.VMEM((rows * lanes, HD), jnp.float32),
+            pltpu.VMEM((both, HD), jnp.float32),
+            pltpu.VMEM((both, HD), jnp.float32),
+            pltpu.VMEM((rows * lanes, HD), jnp.float32),
+        ],
+        compiler_params=pltpu.CompilerParams(vmem_limit_bytes=48 * MIB),
+        cost_estimate=pl.CostEstimate(
+            flops=4 * rows * lanes * held * HD,
+            bytes_accessed=4 * rows * held * HD,
+            transcendentals=rows * lanes * held,
+        ),
+        name="attention",
+    )(lengths, *sums, cos, sin, cache)
+
+
+def after(values, *first):
+    return lax.optimization_barrier((*values, *first))[: len(values)]
 
 
 def body(hidden, qkv_rows, o_rows, block_owner, cache, lengths):
@@ -276,26 +346,48 @@
     owned = qkv_rows.shape[0]
     query_cols = HQ * HD
     kv_cols = HK * HD
-    qkv_copy = by_group(qkv_rows.astype(jnp.bfloat16), (query_cols, kv_cols, kv_cols), groups)
-    out_copy = o_rows.astype(jnp.bfloat16).reshape(owned, groups, query_cols // groups)
-
+    cols = (query_cols + 2 * kv_cols) // groups
+    copy = jnp.concatenate([qkv_rows.astype(jnp.bfloat16), o_rows.astype(jnp.bfloat16)], axis=1)
+    copy = by_group(copy, (query_cols, kv_cols, kv_cols, query_cols), groups)
+
+    cos, sin = turns(lengths)
     parts = shuffle(hidden.reshape(steps * rows, width), block_owner)
-    qkv_copy, out_copy, *parts = lax.optimization_barrier((qkv_copy, out_copy, *parts))
     parts = [parts[0]] + [z_shift(parts[k], k) for k in range(1, NZ)]
 
-    w = flatten(lax.all_to_all(qkv_copy, "tp", split_axis=1, concat_axis=0, tiled=True))
-    w, out_copy, *parts = lax.optimization_barrier((w, out_copy, *parts))
-    w_y = flip(w, 8)
-    w_c = flip(w, 1)
+    both = flatten(lax.all_to_all(copy, "tp", split_axis=1, concat_axis=0, tiled=True))
+    both, parts[0], parts[1], parts[3], cos, sin = lax.optimization_barrier(
+        (both, parts[0], parts[1], parts[3], cos, sin)
+    )
+    w, own = both[:, :cols], both[:, cols:]
+    half = own.shape[0] // 2
+
+    w_y, w_c = flip(w, 8), flip(w, 1)
+    below, above = z_shift(own, 1), z_shift(own, -1)
+    own_c = flip(own, 1)
+    w_y, below, above, own, parts[2] = lax.optimization_barrier((w_y, below, above, own, parts[2]))
     w_yc = flip(w_y, 1)
-    got_o = flatten(lax.all_to_all(out_copy, "tp", split_axis=1, concat_axis=0, tiled=True))
+    far_a, far_b = z_shift(above[:half], -1), z_shift(below[half:], 1)
+    across = flip(own, 8)
+
     sums = partials(parts, (w, w_y, w_c, w_yc))
-    sources, spots = gather_rows(got_o)
-
-    proj = sums[0]
-    for k in range(1, NZ):
-        proj = proj + z_shift(sums[k], -k).astype(jnp.float32)
-    mixed = attention(proj, cache, lengths, groups)
+    sums = [sums[0]] + [z_shift(sums[k], -k) for k in range(1, NZ)]
+    below_c, above_c = after((below, above), sums[0])
+    below_c, above_c = flip(below_c, 1), flip(above_c, 1)
+    across_n, far_an, far_bn = after((across, far_a, far_b), *sums)
+    across_below, across_above = z_shift(across_n, 1), z_shift(across_n, -1)
+    across_far_a, across_far_b = flip(far_an, 8), flip(far_bn, 8)
+    across_c, far_ac, far_bc = flip(across_n, 1), flip(far_an, 1), flip(far_bn, 1)
+    mixed = attention(sums, cos, sin, cache, lengths)
+
+    last = after((across_below, across_above, across_far_a, across_far_b), mixed)
+    last_c = [flip(value, 1) for value in last]
+    near = ((0, 0), (0, 3), (0, 1), (1, 0), (0, 2), (0, 2), (1, 3), (1, 1), (1, 2), (1, 2))
+    begins = (0, 0, 0, 0, 0, 4, 0, 0, 0, 4)
+    sources = [own, below, above, across, far_a, far_b, *last]
+    sources += [own_c, below_c, above_c, across_c, far_ac, far_bc, *last_c]
+    spots = tuple((*at, core, t0) for core in (0, 1) for at, t0 in zip(near, begins))
+    order = (0, 10, 1, 2, 11, 12, 3, 13, 4, 5, 14, 15, 6, 7, 8, 9, 16, 17, 18, 19)
+    sources, spots = [sources[n] for n in order], tuple(spots[n] for n in order)
     terms = project_back(mixed, sources, spots, block_owner, groups)
     terms = lax.all_to_all(terms, "tp", split_axis=0, concat_axis=0, tiled=True)
     summed = jnp.sum(terms.astype(jnp.float32), axis=0).astype(jnp.bfloat16)

time: 255 us -> 229 us (0.90)
  local copies, waits for them, and re-layouts: 19 us -> 6.48 us
  Pallas kernels: 26 us -> 38.4 us
  matrix products: 9.39 us -> 0 us
  starting transfers between devices: 37.9 us -> 30 us
  other arithmetic: 11.5 us -> 5.52 us
    pallas_call x0 -> x1, Pallas kernels: none -> 11.1 us  [attention(): pl.pallas_call(attention_kernel, grid=(rows // GROUP,), out_shape=jax.Sha...]
    dot_general x4 -> x0, matrix products: 9.39 us -> none  [the longest x1 4.14 us: attention(): jnp.einsum('srgjd,rpgd->srgjp', query, keys, preferred_element_type=jnp.f...]
    unnamed x53 -> x33, local copies, waits for them, and re-layouts: 11.5 us -> 3.26 us
    all_to_all x2 -> x1, starting transfers between devices: 14.7 us -> 7.28 us  [body(): lax.all_to_all(copy, 'tp', split_axis=1, concat_axis=0, tiled=True)]
    all_to_all x2 -> x1, waiting for transfers between devices: 3.52 us -> 10.3 us  [body(): lax.all_to_all(copy, 'tp', split_axis=1, concat_axis=0, tiled=True)]
    ppermute x16, waiting for transfers between devices: 32.7 us -> 27.9 us  [flip(): return lax.ppermute(value, 'fsdp', [(f, f ^ bit) for f in range(16)])]
    ppermute x12, starting transfers between devices: 19.9 us -> 16.4 us  [z_shift(): return lax.ppermute(value, 'fsdp', pairs)]
    ppermute x16, starting transfers between devices: 3.37 us -> 6.32 us  [flip(): return lax.ppermute(value, 'fsdp', [(f, f ^ bit) for f in range(16)])]
  transfers between devices with their start and end apart: 30 -> 29, of which waited for: 10 -> 14; matrix products, arithmetic and copies ran while one was open for 9% -> 1% of each run, Pallas kernels for 2% -> 10%
where the time goes in v4:
time: 229 us
  waiting for transfers between devices  110 us (48%)
  Pallas kernels  38.4 us (17%)
  blocking collectives  37.8 us (17%)
  starting transfers between devices  30 us (13%)
  local copies, waits for them, and re-layouts  6.48 us (3%)
  other arithmetic  5.52 us (2%)
    ppermute x12, waiting for transfers between devices, z_shift(): return lax.ppermute(value, 'fsdp', pairs)  72.1 us
    all_to_all x1, blocking collectives, body(): terms = lax.all_to_all(terms, 'tp', split_axis=0, concat_axis=0, tiled=True)  37.8 us
    ppermute x16, waiting for transfers between devices, flip(): return lax.ppermute(value, 'fsdp', [(f, f ^ bit) for f in range(16)])  27.9 us
    ppermute x12, starting transfers between devices, z_shift(): return lax.ppermute(value, 'fsdp', pairs)  16.4 us
    pallas_call x1, Pallas kernels, project_back(): pl.pallas_call(functools.partial(back_kernel, spots, groups), out_shape=j...  15.9 us
    pallas_call x1, Pallas kernels, attention(): pl.pallas_call(attention_kernel, grid=(rows // GROUP,), out_shape=jax.Sha...  11.1 us
    all_to_all x1, waiting for transfers between devices, body(): lax.all_to_all(copy, 'tp', split_axis=1, concat_axis=0, tiled=True)  10.3 us
    all_to_all x1, starting transfers between devices, body(): lax.all_to_all(copy, 'tp', split_axis=1, concat_axis=0, tiled=True)  7.28 us
  transfers between devices with their start and end apart: 29, of which 14 were waited for; matrix products, arithmetic and copies ran while one was open for 1% of the time, Pallas kernels for 10%

profile of v4, /device:TPU:0, one launch (start us, length us, event | category | flops | bytes accessed | tf_op | source)
XLA Modules:
  0.0 228.7 jit_solution(73703626531759994)
XLA Ops:
  0.0 2.0 convert_element_type.18
  2.7 1.6 pad_maximum_fusion
  4.4 7.3 %all-to-all-start = ((bf16[64,8,2304]{2,0,1:T(8,128)(2,1)}), bf16[64,8,2304]{2,0,1:T(8,128)(2,1)}, u32[]{:S(2)}, u32[]{:S(2)}) async-start(bf16[64,8,2304]{2,0,1:T(8,128)(2,1)} %pad_maximum_fusion), calls=%async_computation | async-start | bytes 4718592 | tf_op jit(solution)/shard_map/all_to_all | solution.py:357
  11.7 5.1 %shuffle.1 = (bf16[160,2048]{1,0:T(8,128)(2,1)S(1)}, bf16[160,2048]{1,0:T(8,128)(2,1)}, bf16[160,2048]{1,0:T(8,128)(2,1)S(1)}, bf16[160,2048]{1,0:T(8,128)(2,1)}) custom-call(s32[2,128]{1,0:T(2,128)S(1)} %copy-done.1, bf16[160,8192]{1,0:T(8,128)(2,1)S(1)} %bitcast.21), custom_call_target="tpu_custom_call" | custom-call | flops 10485760 | bytes 5242880 | tf_op jit(solution)/shard_map/shuffle/pallas_call | solution.py:74
  17.7 1.9 collective-permute-start
  19.6 2.1 collective-permute-start.1
  22.3 14.1 %collective-permute-done.h1 = bf16[160,2048]{1,0:T(8,128)(2,1)S(1)} collective-permute-done((bf16[160,2048]{1,0:T(8,128)(2,1)}, bf16[160,2048]{1,0:T(8,128)(2,1)S(1)}, u32[]{:S(2)}, u32[]{:S(2)}) %collective-permute-start) | collective-permute-done | bytes 655392 | tf_op jit(solution)/shard_map/ppermute | solution.py:22
  36.4 10.3 %all-to-all-done = bf16[64,8,2304]{2,0,1:T(8,128)(2,1)} async-done(((bf16[64,8,2304]{2,0,1:T(8,128)(2,1)}), bf16[64,8,2304]{2,0,1:T(8,128)(2,1)}, u32[]{:S(2)}, u32[]{:S(2)}) %all-to-all-start) | async-done | bytes 2359328 | tf_op jit(solution)/shard_map/all_to_all | solution.py:357
  46.7 1.5 slice.24.w0
  48.9 1.3 slice.25.refs_0_
  50.2 4.1 %collective-permute-start.4 = (bf16[512,1024]{1,0:T(8,128)(2,1)S(1)}, bf16[512,1024]{1,0:T(8,128)(2,1)S(1)}, u32[]{:S(2)}, u32[]{:S(2)}) collective-permute-start(bf16[512,1024]{1,0:T(8,128)(2,1)S(1)} %slice.25.refs_0_), channel_id=1, source_target_pairs={{0,48},{8,56},{16,0},{24,8},{32,16},{40,24},{48,32},{56,40},{64,11... | collective-permute-start | bytes 3145736 | tf_op jit(solution)/shard_map/ppermute | solution.py:22
  54.3 1.9 collective-permute-start.5
  56.2 35.5 %collective-permute-done.5.h2 = bf16[160,2048]{1,0:T(8,128)(2,1)S(1)} collective-permute-done((bf16[160,2048]{1,0:T(8,128)(2,1)S(1)}, bf16[160,2048]{1,0:T(8,128)(2,1)S(1)}, u32[]{:S(2)}, u32[]{:S(2)}) %collective-permute-start.5) | collective-permute-done | bytes 655392 | tf_op jit(solution)/shard_map/ppermute | solution.py:22
  91.7 1.3 collective-permute-done.3.refs_2_
  93.0 1.4 collective-permute-start.14
  94.9 1.8 collective-permute-start.16
  96.7 1.1 copy-done.15
  97.8 6.3 %partials.1 = (f32[160,1280]{1,0:T(8,128)S(1)}, bf16[160,1280]{1,0:T(8,128)(2,1)S(1)}, bf16[160,1280]{1,0:T(8,128)(2,1)S(1)}, bf16[160,1280]{1,0:T(8,128)(2,1)S(1)}) custom-call(bf16[160,2048]{1,0:T(8,128)(2,1)S(1)} %get-tuple-element.36.h0, bf16[160,2048]{1,0:T(8,128)(2,1)S(1)} %collective-permute-done.h1, bf16[160,2048]{1,0:T(8,128)(2,1)S(1)} %collective-permute-done.5.h2, ...), custom_call_target="tpu_custom_call" | custom-call | flops 3355443200 | bytes 9502720 | tf_op jit(solution)/shard_map/partials/pallas_call | solution.py:112
  104.1 1.6 collective-permute-start.8
  106.2 3.1 %collective-permute-done.15.refs_8_ = bf16[256,1024]{1,0:T(8,128)(2,1)S(1)} collective-permute-done((bf16[256,1024]{1,0:T(8,128)(2,1)S(1)}, bf16[256,1024]{1,0:T(8,128)(2,1)S(1)}, u32[]{:S(2)}, u32[]{:S(2)}) %collective-permute-start.15) | collective-permute-done | bytes 524320 | tf_op jit(solution)/shard_map/ppermute | solution.py:22
  109.3 9.8 %collective-permute-done.16.refs_9_ = bf16[256,1024]{1,0:T(8,128)(2,1)S(1)} collective-permute-done((bf16[256,1024]{1,0:T(8,128)(2,1)S(1)}, bf16[256,1024]{1,0:T(8,128)(2,1)S(1)}, u32[]{:S(2)}, u32[]{:S(2)}) %collective-permute-start.16) | collective-permute-done | bytes 524320 | tf_op jit(solution)/shard_map/ppermute | solution.py:22
  119.5 7.9 %collective-permute-done.10.p3 = bf16[160,1280]{1,0:T(8,128)(2,1)S(1)} collective-permute-done((bf16[160,1280]{1,0:T(8,128)(2,1)S(1)}, bf16[160,1280]{1,0:T(8,128)(2,1)S(1)}, u32[]{:S(2)}, u32[]{:S(2)}) %collective-permute-start.10) | collective-permute-done | bytes 409632 | tf_op jit(solution)/shard_map/ppermute | solution.py:22
  127.4 1.3 collective-permute-start.21
  130.1 1.3 collective-permute-start.23
  131.5 12.8 %collective-permute-done.22.refs_14_ = bf16[256,1024]{1,0:T(8,128)(2,1)S(1)} collective-permute-done((bf16[256,1024]{1,0:T(8,128)(2,1)S(1)}, bf16[256,1024]{1,0:T(8,128)(2,1)S(1)}, u32[]{:S(2)}, u32[]{:S(2)}) %collective-permute-start.22) | collective-permute-done | bytes 524320 | tf_op jit(solution)/shard_map/ppermute | solution.py:26
  144.3 9.1 %collective-permute-done.23.refs_15_ = bf16[256,1024]{1,0:T(8,128)(2,1)S(1)} collective-permute-done((bf16[256,1024]{1,0:T(8,128)(2,1)S(1)}, bf16[256,1024]{1,0:T(8,128)(2,1)S(1)}, u32[]{:S(2)}, u32[]{:S(2)}) %collective-permute-start.23) | collective-permute-done | bytes 524320 | tf_op jit(solution)/shard_map/ppermute | solution.py:26
  154.1 11.1 %attention.1.mixed_ref = bf16[160,1024]{1,0:T(8,128)(2,1)S(1)} custom-call(s32[80]{0:T(128)S(1)} %copy-done.2, f32[160,1280]{1,0:T(8,128)S(1)} %get-tuple-element.43.p0, bf16[160,1280]{1,0:T(8,128)(2,1)S(1)} %collective-permute-done.8.p1, bf16[160,1280]{1,0:T(8,128)(2,1)S(1)} %collective-permute-done.9.p2, bf16[160,1280]{1,0:T(8,128)(2,1)S(1)} %collective-permute-done.10.p3, ...), custom_call_target="tpu_custom_call" | custom-call | flops 167772160 | bytes 10485760 | tf_op jit(solution)/shard_map/attention/pallas_call | solution.py:314
  166.7 1.5 collective-permute-done.17.refs_7_
  168.1 3.7 %collective-permute-done.26.refs_18_ = bf16[256,1024]{1,0:T(8,128)(2,1)S(1)} collective-permute-done((bf16[256,1024]{1,0:T(8,128)(2,1)S(1)}, bf16[256,1024]{1,0:T(8,128)(2,1)S(1)}, u32[]{:S(2)}, u32[]{:S(2)}) %collective-permute-start.26) | collective-permute-done | bytes 524320 | tf_op jit(solution)/shard_map/ppermute | solution.py:26
  173.7 15.9 %project_back.1 = bf16[8,160,1024]{2,1,0:T(8,128)(2,1)} custom-call(s32[2,128]{1,0:T(2,128)S(1)} %copy-done.1, bf16[160,1024]{1,0:T(8,128)(2,1)S(1)} %attention.1.mixed_ref, bf16[512,1024]{1,0:T(8,128)(2,1)S(1)} %slice.25.refs_0_, bf16[512,1024]{1,0:T(8,128)(2,1)} %copy-done.11, bf16[512,1024]{1,0:T(8,128)(2,1)} %copy-done.6, bf16[512,1024]{1,0:T(8,128)(2,1)} %copy-done.5, ...), custom_call_target="tpu_custom_call" | custom-call | flops 2684354560 | bytes 19726336 | tf_op jit(solution)/shard_map/project_back/pallas_call | solution.py:176
  189.6 37.8 %all_to_all.20 = bf16[8,160,1024]{2,1,0:T(8,128)(2,1)S(1)} all-to-all(bf16[8,160,1024]{2,1,0:T(8,128)(2,1)} %project_back.1), channel_id=1, replica_groups=mesh['fsdp'=16,'tp'=8] {'tp'}, dimensions={0} | all-to-all | bytes 5242880 | tf_op jit(solution)/shard_map/all_to_all | solution.py:392
  227.5 1.3 reduce_sum.12
  (80 shorter events, 9.7 us)
Async XLA Ops:
  4.4 42.3 %all-to-all-start = ((bf16[64,8,2304]{2,0,1:T(8,128)(2,1)}), bf16[64,8,2304]{2,0,1:T(8,128)(2,1)}, u32[]{:S(2)}, u32[]{:S(2)}) async-start(bf16[64,8,2304]{2,0,1:T(8,128)(2,1)} %pad_maximum_fusion), calls=%async_computation | async-start | bytes 4718592 | tf_op jit(solution)/shard_map/all_to_all | solution.py:357
  17.7 18.7 %collective-permute-start = (bf16[160,2048]{1,0:T(8,128)(2,1)}, bf16[160,2048]{1,0:T(8,128)(2,1)S(1)}, u32[]{:S(2)}, u32[]{:S(2)}) collective-permute-start(bf16[160,2048]{1,0:T(8,128)(2,1)} %get-tuple-element.34), channel_id=1, source_target_pairs={{0,16},{8,24},{16,32},{24,40},{32,48},{40,56},{48,0},{56,8},{64,80... | collective-permute-start | bytes 1966088 | tf_op jit(solution)/shard_map/ppermute | solution.py:22
  19.6 16.8 %collective-permute-start.1 = (bf16[160,2048]{1,0:T(8,128)(2,1)}, bf16[160,2048]{1,0:T(8,128)(2,1)S(1)}, u32[]{:S(2)}, u32[]{:S(2)}) collective-permute-start(bf16[160,2048]{1,0:T(8,128)(2,1)} %get-tuple-element.35), channel_id=1, source_target_pairs={{0,48},{8,56},{16,0},{24,8},{32,16},{40,24},{48,32},{56,40},{64,11... | collective-permute-start | bytes 1966088 | tf_op jit(solution)/shard_map/ppermute | solution.py:22
  48.1 44.8 %collective-permute-start.2 = (bf16[512,1280]{1,0:T(8,128)(2,1)S(1)}, bf16[512,1280]{1,0:T(8,128)(2,1)S(1)}, u32[]{:S(2)}, u32[]{:S(2)}) collective-permute-start(bf16[512,1280]{1,0:T(8,128)(2,1)S(1)} %slice.24.w0), channel_id=1, source_target_pairs={{0,64},{8,72},{16,80},{24,88},{32,96},{40,104},{48,112},{56,120},{... | collective-permute-start | bytes 3932168 | tf_op jit(solution)/shard_map/ppermute | solution.py:26
  50.2 41.5 %collective-permute-start.4 = (bf16[512,1024]{1,0:T(8,128)(2,1)S(1)}, bf16[512,1024]{1,0:T(8,128)(2,1)S(1)}, u32[]{:S(2)}, u32[]{:S(2)}) collective-permute-start(bf16[512,1024]{1,0:T(8,128)(2,1)S(1)} %slice.25.refs_0_), channel_id=1, source_target_pairs={{0,48},{8,56},{16,0},{24,8},{32,16},{40,24},{48,32},{56,40},{64,11... | collective-permute-start | bytes 3145736 | tf_op jit(solution)/shard_map/ppermute | solution.py:22
  54.3 38.6 %collective-permute-start.3 = (bf16[512,1024]{1,0:T(8,128)(2,1)S(1)}, bf16[512,1024]{1,0:T(8,128)(2,1)S(1)}, u32[]{:S(2)}, u32[]{:S(2)}) collective-permute-start(bf16[512,1024]{1,0:T(8,128)(2,1)S(1)} %slice.25.refs_0_), channel_id=1, source_target_pairs={{0,16},{8,24},{16,32},{24,40},{32,48},{40,56},{48,0},{56,8},{64,80... | collective-permute-start | bytes 3145736 | tf_op jit(solution)/shard_map/ppermute | solution.py:22
  54.3 37.4 %collective-permute-start.5 = (bf16[160,2048]{1,0:T(8,128)(2,1)S(1)}, bf16[160,2048]{1,0:T(8,128)(2,1)S(1)}, u32[]{:S(2)}, u32[]{:S(2)}) collective-permute-start(bf16[160,2048]{1,0:T(8,128)(2,1)S(1)} %copy-done.4), channel_id=1, source_target_pairs={{0,32},{8,40},{16,48},{24,56},{32,0},{40,8},{48,16},{56,24},{64,96... | collective-permute-start | bytes 1966088 | tf_op jit(solution)/shard_map/ppermute | solution.py:22
  56.2 40.5 %collective-permute-start.6 = (bf16[512,1280]{1,0:T(8,128)(2,1)S(1)}, bf16[512,1280]{1,0:T(8,128)(2,1)S(1)}, u32[]{:S(2)}, u32[]{:S(2)}) collective-permute-start(bf16[512,1280]{1,0:T(8,128)(2,1)S(1)} %slice.24.w0), channel_id=1, source_target_pairs={{0,8},{8,0},{16,24},{24,16},{32,40},{40,32},{48,56},{56,48},{64,72... | collective-permute-start | bytes 3932168 | tf_op jit(solution)/shard_map/ppermute | solution.py:26
  91.7 61.7 %copy-start.5 = (bf16[512,1024]{1,0:T(8,128)(2,1)}, bf16[512,1024]{1,0:T(8,128)(2,1)S(1)}, u32[]{:S(2)}) copy-start(bf16[512,1024]{1,0:T(8,128)(2,1)S(1)} %collective-permute-done.4.refs_3_) | copy-start | bytes 3145732
  92.9 51.4 %copy-start.6 = (bf16[512,1024]{1,0:T(8,128)(2,1)}, bf16[512,1024]{1,0:T(8,128)(2,1)S(1)}, u32[]{:S(2)}) copy-start(bf16[512,1024]{1,0:T(8,128)(2,1)S(1)} %collective-permute-done.3.refs_2_) | copy-start | bytes 3145732
  92.9 4.8 %collective-permute-start.7 = (bf16[512,1280]{1,0:T(8,128)(2,1)S(1)}, bf16[512,1280]{1,0:T(8,128)(2,1)}, u32[]{:S(2)}, u32[]{:S(2)}) collective-permute-start(bf16[512,1280]{1,0:T(8,128)(2,1)S(1)} %collective-permute-done.2.w1), channel_id=1, source_target_pairs={{0,8},{8,0},{16,24},{24,16},{32,40},{40,32},{48,56},{56,48},{64,72... | collective-permute-start | bytes 3932168 | tf_op jit(solution)/shard_map/ppermute | solution.py:26
  93.0 26.1 %collective-permute-start.14 = (bf16[512,1024]{1,0:T(8,128)(2,1)S(1)}, bf16[512,1024]{1,0:T(8,128)(2,1)S(1)}, u32[]{:S(2)}, u32[]{:S(2)}) collective-permute-start(bf16[512,1024]{1,0:T(8,128)(2,1)S(1)} %slice.25.refs_0_), channel_id=1, source_target_pairs={{0,64},{8,72},{16,80},{24,88},{32,96},{40,104},{48,112},{56,120},{... | collective-permute-start | bytes 3145736 | tf_op jit(solution)/shard_map/ppermute | solution.py:26
  94.5 14.8 %collective-permute-start.15 = (bf16[256,1024]{1,0:T(8,128)(2,1)S(1)}, bf16[256,1024]{1,0:T(8,128)(2,1)S(1)}, u32[]{:S(2)}, u32[]{:S(2)}) collective-permute-start(bf16[256,1024]{1,0:T(8,128)(2,1)S(1)} %slice.26), channel_id=1, source_target_pairs={{0,48},{8,56},{16,0},{24,8},{32,16},{40,24},{48,32},{56,40},{64,11... | collective-permute-start | bytes 1572872 | tf_op jit(solution)/shard_map/ppermute | solution.py:22
  94.9 24.2 %collective-permute-start.16 = (bf16[256,1024]{1,0:T(8,128)(2,1)S(1)}, bf16[256,1024]{1,0:T(8,128)(2,1)S(1)}, u32[]{:S(2)}, u32[]{:S(2)}) collective-permute-start(bf16[256,1024]{1,0:T(8,128)(2,1)S(1)} %slice.27), channel_id=1, source_target_pairs={{0,16},{8,24},{16,32},{24,40},{32,48},{40,56},{48,0},{56,8},{64,80... | collective-permute-start | bytes 1572872 | tf_op jit(solution)/shard_map/ppermute | solution.py:22
  104.1 15.1 %collective-permute-start.8 = (bf16[160,1280]{1,0:T(8,128)(2,1)S(1)}, bf16[160,1280]{1,0:T(8,128)(2,1)S(1)}, u32[]{:S(2)}, u32[]{:S(2)}) collective-permute-start(bf16[160,1280]{1,0:T(8,128)(2,1)S(1)} %get-tuple-element.44), channel_id=1, source_target_pairs={{0,48},{8,56},{16,0},{24,8},{32,16},{40,24},{48,32},{56,40},{64,11... | collective-permute-start | bytes 1228808 | tf_op jit(solution)/shard_map/ppermute | solution.py:22
  105.6 13.9 %collective-permute-start.9 = (bf16[160,1280]{1,0:T(8,128)(2,1)S(1)}, bf16[160,1280]{1,0:T(8,128)(2,1)S(1)}, u32[]{:S(2)}, u32[]{:S(2)}) collective-permute-start(bf16[160,1280]{1,0:T(8,128)(2,1)S(1)} %get-tuple-element.45), channel_id=1, source_target_pairs={{0,32},{8,40},{16,48},{24,56},{32,0},{40,8},{48,16},{56,24},{64,96... | collective-permute-start | bytes 1228808 | tf_op jit(solution)/shard_map/ppermute | solution.py:22
  109.3 18.1 %collective-permute-start.10 = (bf16[160,1280]{1,0:T(8,128)(2,1)S(1)}, bf16[160,1280]{1,0:T(8,128)(2,1)S(1)}, u32[]{:S(2)}, u32[]{:S(2)}) collective-permute-start(bf16[160,1280]{1,0:T(8,128)(2,1)S(1)} %get-tuple-element.46), channel_id=1, source_target_pairs={{0,16},{8,24},{16,32},{24,40},{32,48},{40,56},{48,0},{56,8},{64,80... | collective-permute-start | bytes 1228808 | tf_op jit(solution)/shard_map/ppermute | solution.py:22
  119.1 46.1 %copy-start.8 = (bf16[512,1024]{1,0:T(8,128)(2,1)}, bf16[512,1024]{1,0:T(8,128)(2,1)S(1)}, u32[]{:S(2)}) copy-start(bf16[512,1024]{1,0:T(8,128)(2,1)S(1)} %collective-permute-done.14.refs_6_) | copy-start | bytes 3145732
  127.4 26.0 %collective-permute-start.21 = (bf16[512,1024]{1,0:T(8,128)(2,1)S(1)}, bf16[512,1024]{1,0:T(8,128)(2,1)S(1)}, u32[]{:S(2)}, u32[]{:S(2)}) collective-permute-start(bf16[512,1024]{1,0:T(8,128)(2,1)S(1)} %collective-permute-done.14.refs_6_), channel_id=1, source_target_pairs={{0,48},{8,56},{16,0},{24,8},{32,16},{40,24},{48,32},{56,40},{64,11... | collective-permute-start | bytes 3145736 | tf_op jit(solution)/shard_map/ppermute | solution.py:22
  128.8 25.3 %collective-permute-start.20 = (bf16[512,1024]{1,0:T(8,128)(2,1)S(1)}, bf16[512,1024]{1,0:T(8,128)(2,1)S(1)}, u32[]{:S(2)}, u32[]{:S(2)}) collective-permute-start(bf16[512,1024]{1,0:T(8,128)(2,1)S(1)} %collective-permute-done.14.refs_6_), channel_id=1, source_target_pairs={{0,16},{8,24},{16,32},{24,40},{32,48},{40,56},{48,0},{56,8},{64,80... | collective-permute-start | bytes 3145736 | tf_op jit(solution)/shard_map/ppermute | solution.py:22
  129.5 14.9 %collective-permute-start.22 = (bf16[256,1024]{1,0:T(8,128)(2,1)S(1)}, bf16[256,1024]{1,0:T(8,128)(2,1)S(1)}, u32[]{:S(2)}, u32[]{:S(2)}) collective-permute-start(bf16[256,1024]{1,0:T(8,128)(2,1)S(1)} %collective-permute-done.15.refs_8_), channel_id=1, source_target_pairs={{0,64},{8,72},{16,80},{24,88},{32,96},{40,104},{48,112},{56,120},{... | collective-permute-start | bytes 1572872 | tf_op jit(solution)/shard_map/ppermute | solution.py:26
  130.1 23.3 %collective-permute-start.23 = (bf16[256,1024]{1,0:T(8,128)(2,1)S(1)}, bf16[256,1024]{1,0:T(8,128)(2,1)S(1)}, u32[]{:S(2)}, u32[]{:S(2)}) collective-permute-start(bf16[256,1024]{1,0:T(8,128)(2,1)S(1)} %collective-permute-done.16.refs_9_), channel_id=1, source_target_pairs={{0,64},{8,72},{16,80},{24,88},{32,96},{40,104},{48,112},{56,120},{... | collective-permute-start | bytes 1572872 | tf_op jit(solution)/shard_map/ppermute | solution.py:26
  131.5 33.7 %collective-permute-start.11 = (bf16[512,1024]{1,0:T(8,128)(2,1)S(1)}, bf16[512,1024]{1,0:T(8,128)(2,1)S(1)}, u32[]{:S(2)}, u32[]{:S(2)}) collective-permute-start(bf16[512,1024]{1,0:T(8,128)(2,1)S(1)} %slice.25.refs_0_), channel_id=1, source_target_pairs={{0,8},{8,0},{16,24},{24,16},{32,40},{40,32},{48,56},{56,48},{64,72... | collective-permute-start | bytes 3145736 | tf_op jit(solution)/shard_map/ppermute | solution.py:26
  144.3 21.8 %collective-permute-start.12 = (bf16[512,1024]{1,0:T(8,128)(2,1)S(1)}, bf16[512,1024]{1,0:T(8,128)(2,1)}, u32[]{:S(2)}, u32[]{:S(2)}) collective-permute-start(bf16[512,1024]{1,0:T(8,128)(2,1)S(1)} %collective-permute-done.3.refs_2_), channel_id=1, source_target_pairs={{0,8},{8,0},{16,24},{24,16},{32,40},{40,32},{48,56},{56,48},{64,72... | collective-permute-start | bytes 3145736 | tf_op jit(solution)/shard_map/ppermute | solution.py:26
  153.4 12.2 %collective-permute-start.18 = (bf16[256,1024]{1,0:T(8,128)(2,1)S(1)}, bf16[256,1024]{1,0:T(8,128)(2,1)S(1)}, u32[]{:S(2)}, u32[]{:S(2)}) collective-permute-start(bf16[256,1024]{1,0:T(8,128)(2,1)S(1)} %collective-permute-done.15.refs_8_), channel_id=1, source_target_pairs={{0,8},{8,0},{16,24},{24,16},{32,40},{40,32},{48,56},{56,48},{64,72... | collective-permute-start | bytes 1572872 | tf_op jit(solution)/shard_map/ppermute | solution.py:26
  153.4 13.1 %collective-permute-start.13 = (bf16[512,1024]{1,0:T(8,128)(2,1)S(1)}, bf16[512,1024]{1,0:T(8,128)(2,1)}, u32[]{:S(2)}, u32[]{:S(2)}) collective-permute-start(bf16[512,1024]{1,0:T(8,128)(2,1)S(1)} %collective-permute-done.4.refs_3_), channel_id=1, source_target_pairs={{0,8},{8,0},{16,24},{24,16},{32,40},{40,32},{48,56},{56,48},{64,72... | collective-permute-start | bytes 3145736 | tf_op jit(solution)/shard_map/ppermute | solution.py:26
  154.1 11.9 %collective-permute-start.19 = (bf16[256,1024]{1,0:T(8,128)(2,1)S(1)}, bf16[256,1024]{1,0:T(8,128)(2,1)S(1)}, u32[]{:S(2)}, u32[]{:S(2)}) collective-permute-start(bf16[256,1024]{1,0:T(8,128)(2,1)S(1)} %collective-permute-done.16.refs_9_), channel_id=1, source_target_pairs={{0,8},{8,0},{16,24},{24,16},{32,40},{40,32},{48,56},{56,48},{64,72... | collective-permute-start | bytes 1572872 | tf_op jit(solution)/shard_map/ppermute | solution.py:26
  165.2 2.9 %collective-permute-start.17 = (bf16[512,1024]{1,0:T(8,128)(2,1)S(1)}, bf16[512,1024]{1,0:T(8,128)(2,1)S(1)}, u32[]{:S(2)}, u32[]{:S(2)}) collective-permute-start(bf16[512,1024]{1,0:T(8,128)(2,1)S(1)} %collective-permute-done.14.refs_6_), channel_id=1, source_target_pairs={{0,8},{8,0},{16,24},{24,16},{32,40},{40,32},{48,56},{56,48},{64,72... | collective-permute-start | bytes 3145736 | tf_op jit(solution)/shard_map/ppermute | solution.py:26
  165.6 7.0 %collective-permute-start.24 = (bf16[512,1024]{1,0:T(8,128)(2,1)S(1)}, bf16[512,1024]{1,0:T(8,128)(2,1)S(1)}, u32[]{:S(2)}, u32[]{:S(2)}) collective-permute-start(bf16[512,1024]{1,0:T(8,128)(2,1)S(1)} %collective-permute-done.20.refs_12_), channel_id=1, source_target_pairs={{0,8},{8,0},{16,24},{24,16},{32,40},{40,32},{48,56},{56,48},{64,72... | collective-permute-start | bytes 3145736 | tf_op jit(solution)/shard_map/ppermute | solution.py:26
  166.0 6.6 %collective-permute-start.25 = (bf16[512,1024]{1,0:T(8,128)(2,1)S(1)}, bf16[512,1024]{1,0:T(8,128)(2,1)}, u32[]{:S(2)}, u32[]{:S(2)}) collective-permute-start(bf16[512,1024]{1,0:T(8,128)(2,1)S(1)} %collective-permute-done.21.refs_13_), channel_id=1, source_target_pairs={{0,8},{8,0},{16,24},{24,16},{32,40},{40,32},{48,56},{56,48},{64,72... | collective-permute-start | bytes 3145736 | tf_op jit(solution)/shard_map/ppermute | solution.py:26
  166.1 5.7 %collective-permute-start.26 = (bf16[256,1024]{1,0:T(8,128)(2,1)S(1)}, bf16[256,1024]{1,0:T(8,128)(2,1)S(1)}, u32[]{:S(2)}, u32[]{:S(2)}) collective-permute-start(bf16[256,1024]{1,0:T(8,128)(2,1)S(1)} %collective-permute-done.22.refs_14_), channel_id=1, source_target_pairs={{0,8},{8,0},{16,24},{24,16},{32,40},{40,32},{48,56},{56,48},{64,72... | collective-permute-start | bytes 1572872 | tf_op jit(solution)/shard_map/ppermute | solution.py:26
  166.5 6.1 %collective-permute-start.27 = (bf16[256,1024]{1,0:T(8,128)(2,1)S(1)}, bf16[256,1024]{1,0:T(8,128)(2,1)S(1)}, u32[]{:S(2)}, u32[]{:S(2)}) collective-permute-start(bf16[256,1024]{1,0:T(8,128)(2,1)S(1)} %collective-permute-done.23.refs_15_), channel_id=1, source_target_pairs={{0,8},{8,0},{16,24},{24,16},{32,40},{40,32},{48,56},{56,48},{64,72... | collective-permute-start | bytes 1572872 | tf_op jit(solution)/shard_map/ppermute | solution.py:26
  (13 other events, 72.4 us)

commit v5 on v4

--- a/solution.py
+++ b/solution.py
@@ -13,7 +13,7 @@
 HD = 128
 NZ = 4
 GROUP = 8
-AHEAD = 4
+CHUNK = 4
 MIB = 1024 * 1024
 
 
@@ -130,44 +130,45 @@
 
 def back_kernel(spots, groups, owner_ref, mixed_ref, *refs):
     count = len(spots)
-    sources, out_ref, held, placed, sems = refs[:count], *refs[count:]
+    sources, out_ref, held, placed, goals, sems = refs[:count], *refs[count:]
     f = lax.axis_index("fsdp")
     y_lo, z, core = f // 8, lax.rem(f // 2, NZ), lax.rem(f, 2)
-    rows, depth = mixed_ref.shape
     width = held.shape[0]
     owned = width // owner_ref.shape[1]
-
-    copies = []
-    begin = 0
-    for n, source in enumerate(sources):
-        size = source.shape[0]
-        copies.append(
-            pltpu.make_async_copy(source, held.at[pl.ds(begin, size)], sems.at[n])
-        )
-        begin += size
-    for copy in copies[:AHEAD]:
-        copy.start()
-    turned = mixed_ref[...].astype(jnp.float32).T.astype(jnp.bfloat16)
-
-    begin = 0
-    for n, (dy, dz, dc, t0) in enumerate(spots):
-        size = sources[n].shape[0]
+    chunk = CHUNK * owned
+
+    n = 0
+    for (dy, dz, dc, t0), source in zip(spots, sources):
         first = (
             lax.rem(y_lo + dy, 2) * 64 + lax.rem(z + dz, NZ) * 16 + lax.rem(core + dc, 2) * 8 + t0
         )
-        copies[n].wait()
-        if n + AHEAD < count:
-            copies[n + AHEAD].start()
-        terms = jnp.dot(held[begin : begin + size], turned, preferred_element_type=jnp.float32)
+        for part in range(source.shape[0] // chunk):
+            pltpu.make_async_copy(
+                source.at[pl.ds(part * chunk, chunk)], held.at[pl.ds(n * chunk, chunk)], sems.at[n]
+            ).start()
+            for b in range(CHUNK):
+                goals[n * CHUNK + b] = owner_ref[1, first + part * CHUNK + b] * owned
+            n += 1
+    turned = mixed_ref[...].astype(jnp.float32).T.astype(jnp.bfloat16)
+
+    def multiply(n, carry):
+        at = pl.ds(pl.multiple_of(n * chunk, chunk), chunk)
+        pltpu.make_async_copy(held.at[at], held.at[at], sems.at[n]).wait()
+        terms = jnp.dot(held[at, :], turned, preferred_element_type=jnp.float32)
         terms = terms.astype(jnp.bfloat16)
-        for b in range(size // owned):
-            spot = pl.multiple_of(owner_ref[1, first + b] * owned, owned)
+        for b in range(CHUNK):
+            spot = pl.multiple_of(goals[n * CHUNK + b], owned)
             placed[pl.ds(spot, owned), :] = terms[b * owned : (b + 1) * owned]
-        begin += size
-
+        return carry
+
+    lax.fori_loop(0, width // chunk, multiply, 0)
     slab = width // groups
-    for t in range(groups):
-        out_ref[t] = placed[t * slab : (t + 1) * slab].T
+
+    def turn_back(t, carry):
+        out_ref[t] = placed[pl.ds(pl.multiple_of(t * slab, slab), slab), :].T
+        return carry
+
+    lax.fori_loop(0, groups, turn_back, 0)
 
 
 def project_back(mixed, sources, spots, block_owner, groups):
@@ -185,7 +186,8 @@
         scratch_shapes=[
             pltpu.VMEM((width, depth), jnp.bfloat16),
             pltpu.VMEM((width, rows), jnp.bfloat16),
-            pltpu.SemaphoreType.DMA((len(sources),)),
+            pltpu.SMEM((block_owner.shape[1],), jnp.int32),
+            pltpu.SemaphoreType.DMA((block_owner.shape[1] // CHUNK,)),
         ],
         compiler_params=pltpu.CompilerParams(vmem_limit_bytes=48 * MIB),
         cost_estimate=pl.CostEstimate(
@@ -329,7 +331,7 @@
         compiler_params=pltpu.CompilerParams(vmem_limit_bytes=48 * MIB),
         cost_estimate=pl.CostEstimate(
             flops=4 * rows * lanes * held * HD,
-            bytes_accessed=4 * rows * held * HD,
+            bytes_accessed=16 * rows * held * HD,
             transcendentals=rows * lanes * held,
         ),
         name="attention",
@@ -355,30 +357,28 @@
     parts = [parts[0]] + [z_shift(parts[k], k) for k in range(1, NZ)]
 
     both = flatten(lax.all_to_all(copy, "tp", split_axis=1, concat_axis=0, tiled=True))
-    both, parts[0], parts[1], parts[3], cos, sin = lax.optimization_barrier(
-        (both, parts[0], parts[1], parts[3], cos, sin)
-    )
+    both, cos, sin, *parts = lax.optimization_barrier((both, cos, sin, *parts))
     w, own = both[:, :cols], both[:, cols:]
     half = own.shape[0] // 2
 
     w_y, w_c = flip(w, 8), flip(w, 1)
     below, above = z_shift(own, 1), z_shift(own, -1)
     own_c = flip(own, 1)
-    w_y, below, above, own, parts[2] = lax.optimization_barrier((w_y, below, above, own, parts[2]))
+    w_y, below, above, own, own_c = lax.optimization_barrier((w_y, below, above, own, own_c))
     w_yc = flip(w_y, 1)
     far_a, far_b = z_shift(above[:half], -1), z_shift(below[half:], 1)
     across = flip(own, 8)
+    below_c, above_c = flip(below, 1), flip(above, 1)
+    w_yc, below_c, above_c = lax.optimization_barrier((w_yc, below_c, above_c))
 
     sums = partials(parts, (w, w_y, w_c, w_yc))
     sums = [sums[0]] + [z_shift(sums[k], -k) for k in range(1, NZ)]
-    below_c, above_c = after((below, above), sums[0])
-    below_c, above_c = flip(below_c, 1), flip(above_c, 1)
-    across_n, far_an, far_bn = after((across, far_a, far_b), *sums)
-    across_below, across_above = z_shift(across_n, 1), z_shift(across_n, -1)
-    across_far_a, across_far_b = flip(far_an, 8), flip(far_bn, 8)
-    across_c, far_ac, far_bc = flip(across_n, 1), flip(far_an, 1), flip(far_bn, 1)
+    across, far_a, far_b = after((across, far_a, far_b), *sums)
+    across_below, across_above = z_shift(across, 1), z_shift(across, -1)
+    across_far_a, across_far_b = flip(far_a, 8), flip(far_b, 8)
     mixed = attention(sums, cos, sin, cache, lengths)
 
+    across_c, far_ac, far_bc = (flip(v, 1) for v in after((across, far_a, far_b), mixed))
     last = after((across_below, across_above, across_far_a, across_far_b), mixed)
     last_c = [flip(value, 1) for value in last]
     near = ((0, 0), (0, 3), (0, 1), (1, 0), (0, 2), (0, 2), (1, 3), (1, 1), (1, 2), (1, 2))

time: 229 us -> 218 us (0.952)
  waiting for transfers between devices: 110 us -> 97.1 us
  blocking collectives: 37.8 us -> 40.9 us
    all_to_all x1, waiting for transfers between devices: 10.3 us -> 0.01 us  [body(): lax.all_to_all(copy, 'tp', split_axis=1, concat_axis=0, tiled=True)]
    ppermute x16, waiting for transfers between devices: 27.9 us -> 23.3 us  [flip(): return lax.ppermute(value, 'fsdp', [(f, f ^ bit) for f in range(16)])]
    all_to_all x1, blocking collectives: 37.8 us -> 40.9 us  [body(): terms = lax.all_to_all(terms, 'tp', split_axis=0, concat_axis=0, tiled=True)]
  transfers between devices with their start and end apart: 29 -> 29, of which waited for: 14 -> 15; matrix products, arithmetic and copies ran while one was open for 1% -> 1% of each run, Pallas kernels for 10% -> 10%
where the time goes in v5:
time: 218 us
  waiting for transfers between devices  97.1 us (45%)
  blocking collectives  40.9 us (19%)
  Pallas kernels  36.8 us (17%)
  starting transfers between devices  29.6 us (14%)
  local copies, waits for them, and re-layouts  7.4 us (3%)
  other arithmetic  5.5 us (3%)
    ppermute x12, waiting for transfers between devices, z_shift(): return lax.ppermute(value, 'fsdp', pairs)  73.9 us
    all_to_all x1, blocking collectives, body(): terms = lax.all_to_all(terms, 'tp', split_axis=0, concat_axis=0, tiled=True)  40.9 us
    ppermute x16, waiting for transfers between devices, flip(): return lax.ppermute(value, 'fsdp', [(f, f ^ bit) for f in range(16)])  23.3 us
    ppermute x12, starting transfers between devices, z_shift(): return lax.ppermute(value, 'fsdp', pairs)  15.8 us
    pallas_call x1, Pallas kernels, project_back(): pl.pallas_call(functools.partial(back_kernel, spots, groups), out_shape=j...  14.5 us
    pallas_call x1, Pallas kernels, attention(): pl.pallas_call(attention_kernel, grid=(rows // GROUP,), out_shape=jax.Sha...  10.7 us
    all_to_all x1, starting transfers between devices, body(): lax.all_to_all(copy, 'tp', split_axis=1, concat_axis=0, tiled=True)  7.28 us
    ppermute x16, starting transfers between devices, flip(): return lax.ppermute(value, 'fsdp', [(f, f ^ bit) for f in range(16)])  6.57 us
  transfers between devices with their start and end apart: 29, of which 15 were waited for; matrix products, arithmetic and copies ran while one was open for 1% of the time, Pallas kernels for 10%

profile of v5, /device:TPU:0, one launch (start us, length us, event | category | flops | bytes accessed | tf_op | source)
XLA Modules:
  0.0 217.7 jit_solution(2879132090399325605)
XLA Ops:
  0.0 2.0 convert_element_type.18
  2.7 1.6 pad_maximum_fusion
  4.4 7.3 %all-to-all-start = ((bf16[64,8,2304]{2,0,1:T(8,128)(2,1)}), bf16[64,8,2304]{2,0,1:T(8,128)(2,1)}, u32[]{:S(2)}, u32[]{:S(2)}) async-start(bf16[64,8,2304]{2,0,1:T(8,128)(2,1)} %pad_maximum_fusion), calls=%async_computation | async-start | bytes 4718592 | tf_op jit(solution)/shard_map/all_to_all | solution.py:359
  11.7 5.3 %shuffle.1 = (bf16[160,2048]{1,0:T(8,128)(2,1)S(1)}, bf16[160,2048]{1,0:T(8,128)(2,1)}, bf16[160,2048]{1,0:T(8,128)(2,1)}, bf16[160,2048]{1,0:T(8,128)(2,1)}) custom-call(s32[2,128]{1,0:T(2,128)S(1)} %copy-done.1, bf16[160,8192]{1,0:T(8,128)(2,1)S(1)} %bitcast.21), custom_call_target="tpu_custom_call" | custom-call | flops 10485760 | bytes 5242880 | tf_op jit(solution)/shard_map/shuffle/pallas_call | solution.py:74
  17.0 1.9 collective-permute-start
  18.9 3.6 %collective-permute-start.1 = (bf16[160,2048]{1,0:T(8,128)(2,1)}, bf16[160,2048]{1,0:T(8,128)(2,1)S(1)}, u32[]{:S(2)}, u32[]{:S(2)}) collective-permute-start(bf16[160,2048]{1,0:T(8,128)(2,1)} %get-tuple-element.40), channel_id=1, source_target_pairs={{0,32},{8,40},{16,48},{24,56},{32,0},{40,8},{48,16},{56,24},{64,96... | collective-permute-start | bytes 1966088 | tf_op jit(solution)/shard_map/ppermute | solution.py:22
  24.1 11.9 %collective-permute-done.h1 = bf16[160,2048]{1,0:T(8,128)(2,1)S(1)} collective-permute-done((bf16[160,2048]{1,0:T(8,128)(2,1)}, bf16[160,2048]{1,0:T(8,128)(2,1)S(1)}, u32[]{:S(2)}, u32[]{:S(2)}) %collective-permute-start) | collective-permute-done | bytes 655392 | tf_op jit(solution)/shard_map/ppermute | solution.py:22
  36.0 14.9 %collective-permute-done.1.h2 = bf16[160,2048]{1,0:T(8,128)(2,1)S(1)} collective-permute-done((bf16[160,2048]{1,0:T(8,128)(2,1)}, bf16[160,2048]{1,0:T(8,128)(2,1)S(1)}, u32[]{:S(2)}, u32[]{:S(2)}) %collective-permute-start.1) | collective-permute-done | bytes 655392 | tf_op jit(solution)/shard_map/ppermute | solution.py:22
  50.9 1.4 slice.24.w0
  53.1 1.3 slice.25.refs_0_
  54.5 2.1 collective-permute-start.5
  57.1 22.9 %collective-permute-done.5.refs_3_ = bf16[512,1024]{1,0:T(8,128)(2,1)S(1)} collective-permute-done((bf16[512,1024]{1,0:T(8,128)(2,1)S(1)}, bf16[512,1024]{1,0:T(8,128)(2,1)S(1)}, u32[]{:S(2)}, u32[]{:S(2)}) %collective-permute-start.5) | collective-permute-done | bytes 1048608 | tf_op jit(solution)/shard_map/ppermute | solution.py:22
  80.1 3.0 %collective-permute-done.4.refs_2_ = bf16[512,1024]{1,0:T(8,128)(2,1)S(1)} collective-permute-done((bf16[512,1024]{1,0:T(8,128)(2,1)S(1)}, bf16[512,1024]{1,0:T(8,128)(2,1)S(1)}, u32[]{:S(2)}, u32[]{:S(2)}) %collective-permute-start.4) | collective-permute-done | bytes 1048608 | tf_op jit(solution)/shard_map/ppermute | solution.py:22
  84.2 1.3 collective-permute-start.14
  85.6 5.6 %collective-permute-done.9.refs_4_ = bf16[512,1024]{1,0:T(8,128)(2,1)} collective-permute-done((bf16[512,1024]{1,0:T(8,128)(2,1)S(1)}, bf16[512,1024]{1,0:T(8,128)(2,1)}, u32[]{:S(2)}, u32[]{:S(2)}) %collective-permute-start.9) | collective-permute-done | bytes 1048608 | tf_op jit(solution)/shard_map/ppermute | solution.py:26
  91.2 2.0 collective-permute-start.15
  95.4 6.3 %partials.1 = (f32[160,1280]{1,0:T(8,128)S(1)}, bf16[160,1280]{1,0:T(8,128)(2,1)S(1)}, bf16[160,1280]{1,0:T(8,128)(2,1)S(1)}, bf16[160,1280]{1,0:T(8,128)(2,1)S(1)}) custom-call(bf16[160,2048]{1,0:T(8,128)(2,1)S(1)} %get-tuple-element.42.h0, bf16[160,2048]{1,0:T(8,128)(2,1)S(1)} %collective-permute-done.h1, bf16[160,2048]{1,0:T(8,128)(2,1)S(1)} %collective-permute-done.1.h2, ...), custom_call_target="tpu_custom_call" | custom-call | flops 3355443200 | bytes 9502720 | tf_op jit(solution)/shard_map/partials/pallas_call | solution.py:112
  101.7 2.4 %collective-permute-start.11 = (bf16[160,1280]{1,0:T(8,128)(2,1)S(1)}, bf16[160,1280]{1,0:T(8,128)(2,1)S(1)}, u32[]{:S(2)}, u32[]{:S(2)}) collective-permute-start(bf16[160,1280]{1,0:T(8,128)(2,1)S(1)} %get-tuple-element.52), channel_id=1, source_target_pairs={{0,48},{8,56},{16,0},{24,8},{32,16},{40,24},{48,32},{56,40},{64,11... | collective-permute-start | bytes 1228808 | tf_op jit(solution)/shard_map/ppermute | solution.py:22
  104.1 1.9 collective-permute-done.15.refs_8_
  106.6 10.8 %collective-permute-done.16.refs_9_ = bf16[256,1024]{1,0:T(8,128)(2,1)S(1)} collective-permute-done((bf16[256,1024]{1,0:T(8,128)(2,1)S(1)}, bf16[256,1024]{1,0:T(8,128)(2,1)S(1)}, u32[]{:S(2)}, u32[]{:S(2)}) %collective-permute-start.16) | collective-permute-done | bytes 524320 | tf_op jit(solution)/shard_map/ppermute | solution.py:22
  117.3 5.0 %collective-permute-done.11.p1 = bf16[160,1280]{1,0:T(8,128)(2,1)S(1)} collective-permute-done((bf16[160,1280]{1,0:T(8,128)(2,1)S(1)}, bf16[160,1280]{1,0:T(8,128)(2,1)S(1)}, u32[]{:S(2)}, u32[]{:S(2)}) %collective-permute-start.11) | collective-permute-done | bytes 409632 | tf_op jit(solution)/shard_map/ppermute | solution.py:22
  122.3 3.5 %collective-permute-done.13.p3 = bf16[160,1280]{1,0:T(8,128)(2,1)S(1)} collective-permute-done((bf16[160,1280]{1,0:T(8,128)(2,1)S(1)}, bf16[160,1280]{1,0:T(8,128)(2,1)S(1)}, u32[]{:S(2)}, u32[]{:S(2)}) %collective-permute-start.13) | collective-permute-done | bytes 409632 | tf_op jit(solution)/shard_map/ppermute | solution.py:22
  126.0 1.9 collective-permute-start.20
  128.5 1.3 collective-permute-start.23
  129.9 10.7 %attention.1.mixed_ref = bf16[160,1024]{1,0:T(8,128)(2,1)S(1)} custom-call(s32[80]{0:T(128)S(1)} %copy-done.2, f32[160,1280]{1,0:T(8,128)S(1)} %get-tuple-element.51.p0, bf16[160,1280]{1,0:T(8,128)(2,1)S(1)} %collective-permute-done.11.p1, bf16[160,1280]{1,0:T(8,128)(2,1)S(1)} %collective-permute-done.12.p2, ...), custom_call_target="tpu_custom_call" | custom-call | flops 167772160 | bytes 41943040 | tf_op jit(solution)/shard_map/attention/pallas_call | solution.py:316
  140.7 2.1 collective-permute-done.22.refs_14_
  142.7 9.1 %collective-permute-done.23.refs_15_ = bf16[256,1024]{1,0:T(8,128)(2,1)S(1)} collective-permute-done((bf16[256,1024]{1,0:T(8,128)(2,1)S(1)}, bf16[256,1024]{1,0:T(8,128)(2,1)S(1)}, u32[]{:S(2)}, u32[]{:S(2)}) %collective-permute-start.23) | collective-permute-done | bytes 524320 | tf_op jit(solution)/shard_map/ppermute | solution.py:26
  153.1 2.0 collective-permute-done.17.refs_7_
  155.1 3.2 %collective-permute-done.26.refs_18_ = bf16[256,1024]{1,0:T(8,128)(2,1)S(1)} collective-permute-done((bf16[256,1024]{1,0:T(8,128)(2,1)S(1)}, bf16[256,1024]{1,0:T(8,128)(2,1)S(1)}, u32[]{:S(2)}, u32[]{:S(2)}) %collective-permute-start.26) | collective-permute-done | bytes 524320 | tf_op jit(solution)/shard_map/ppermute | solution.py:26
  161.0 14.5 %project_back.1 = bf16[8,160,1024]{2,1,0:T(8,128)(2,1)} custom-call(s32[2,128]{1,0:T(2,128)S(1)} %copy-done.1, bf16[160,1024]{1,0:T(8,128)(2,1)S(1)} %attention.1.mixed_ref, bf16[512,1024]{1,0:T(8,128)(2,1)S(1)} %slice.25.refs_0_, bf16[512,1024]{1,0:T(8,128)(2,1)} %copy-done.6, bf16[512,1024]{1,0:T(8,128)(2,1)} %copy-done.4, bf16[512,1024]{1,0:T(8,128)(2,1)} %copy-done.3, ...), custom_call_target="tpu_custom_call" | custom-call | flops 2684354560 | bytes 19726336 | tf_op jit(solution)/shard_map/project_back/pallas_call | solution.py:177
  175.5 40.9 %all_to_all.20 = bf16[8,160,1024]{2,1,0:T(8,128)(2,1)S(1)} all-to-all(bf16[8,160,1024]{2,1,0:T(8,128)(2,1)} %project_back.1), channel_id=1, replica_groups=mesh['fsdp'=16,'tp'=8] {'tp'}, dimensions={0} | all-to-all | bytes 5242880 | tf_op jit(solution)/shard_map/all_to_all | solution.py:392
  216.4 1.3 reduce_sum.12
  (78 shorter events, 12.3 us)
Async XLA Ops:
  4.4 46.6 %all-to-all-start = ((bf16[64,8,2304]{2,0,1:T(8,128)(2,1)}), bf16[64,8,2304]{2,0,1:T(8,128)(2,1)}, u32[]{:S(2)}, u32[]{:S(2)}) async-start(bf16[64,8,2304]{2,0,1:T(8,128)(2,1)} %pad_maximum_fusion), calls=%async_computation | async-start | bytes 4718592 | tf_op jit(solution)/shard_map/all_to_all | solution.py:359
  17.0 19.0 %collective-permute-start = (bf16[160,2048]{1,0:T(8,128)(2,1)}, bf16[160,2048]{1,0:T(8,128)(2,1)S(1)}, u32[]{:S(2)}, u32[]{:S(2)}) collective-permute-start(bf16[160,2048]{1,0:T(8,128)(2,1)} %get-tuple-element.39), channel_id=1, source_target_pairs={{0,16},{8,24},{16,32},{24,40},{32,48},{40,56},{48,0},{56,8},{64,80... | collective-permute-start | bytes 1966088 | tf_op jit(solution)/shard_map/ppermute | solution.py:22
  18.9 32.0 %collective-permute-start.1 = (bf16[160,2048]{1,0:T(8,128)(2,1)}, bf16[160,2048]{1,0:T(8,128)(2,1)S(1)}, u32[]{:S(2)}, u32[]{:S(2)}) collective-permute-start(bf16[160,2048]{1,0:T(8,128)(2,1)} %get-tuple-element.40), channel_id=1, source_target_pairs={{0,32},{8,40},{16,48},{24,56},{32,0},{40,8},{48,16},{56,24},{64,96... | collective-permute-start | bytes 1966088 | tf_op jit(solution)/shard_map/ppermute | solution.py:22
  22.5 28.4 %collective-permute-start.2 = (bf16[160,2048]{1,0:T(8,128)(2,1)}, bf16[160,2048]{1,0:T(8,128)(2,1)S(1)}, u32[]{:S(2)}, u32[]{:S(2)}) collective-permute-start(bf16[160,2048]{1,0:T(8,128)(2,1)} %get-tuple-element.41), channel_id=1, source_target_pairs={{0,48},{8,56},{16,0},{24,8},{32,16},{40,24},{48,32},{56,40},{64,11... | collective-permute-start | bytes 1966088 | tf_op jit(solution)/shard_map/ppermute | solution.py:22
  52.3 30.7 %collective-permute-start.3 = (bf16[512,1280]{1,0:T(8,128)(2,1)S(1)}, bf16[512,1280]{1,0:T(8,128)(2,1)S(1)}, u32[]{:S(2)}, u32[]{:S(2)}) collective-permute-start(bf16[512,1280]{1,0:T(8,128)(2,1)S(1)} %slice.24.w0), channel_id=1, source_target_pairs={{0,64},{8,72},{16,80},{24,88},{32,96},{40,104},{48,112},{56,120},{... | collective-permute-start | bytes 3932168 | tf_op jit(solution)/shard_map/ppermute | solution.py:26
  54.4 2.7 %collective-permute-start.6 = (bf16[512,1024]{1,0:T(8,128)(2,1)S(1)}, bf16[512,1024]{1,0:T(8,128)(2,1)S(1)}, u32[]{:S(2)}, u32[]{:S(2)}) collective-permute-start(bf16[512,1024]{1,0:T(8,128)(2,1)S(1)} %slice.25.refs_0_), channel_id=1, source_target_pairs={{0,8},{8,0},{16,24},{24,16},{32,40},{40,32},{48,56},{56,48},{64,72... | collective-permute-start | bytes 3145736 | tf_op jit(solution)/shard_map/ppermute | solution.py:26
  54.5 25.6 %collective-permute-start.5 = (bf16[512,1024]{1,0:T(8,128)(2,1)S(1)}, bf16[512,1024]{1,0:T(8,128)(2,1)S(1)}, u32[]{:S(2)}, u32[]{:S(2)}) collective-permute-start(bf16[512,1024]{1,0:T(8,128)(2,1)S(1)} %slice.25.refs_0_), channel_id=1, source_target_pairs={{0,48},{8,56},{16,0},{24,8},{32,16},{40,24},{48,32},{56,40},{64,11... | collective-permute-start | bytes 3145736 | tf_op jit(solution)/shard_map/ppermute | solution.py:22
  56.6 26.4 %collective-permute-start.4 = (bf16[512,1024]{1,0:T(8,128)(2,1)S(1)}, bf16[512,1024]{1,0:T(8,128)(2,1)S(1)}, u32[]{:S(2)}, u32[]{:S(2)}) collective-permute-start(bf16[512,1024]{1,0:T(8,128)(2,1)S(1)} %slice.25.refs_0_), channel_id=1, source_target_pairs={{0,16},{8,24},{16,32},{24,40},{32,48},{40,56},{48,0},{56,8},{64,80... | collective-permute-start | bytes 3145736 | tf_op jit(solution)/shard_map/ppermute | solution.py:22
  57.1 44.5 %copy-start.6 = (bf16[512,1024]{1,0:T(8,128)(2,1)}, bf16[512,1024]{1,0:T(8,128)(2,1)S(1)}, u32[]{:S(2)}) copy-start(bf16[512,1024]{1,0:T(8,128)(2,1)S(1)} %collective-permute-done.6.refs_1_) | copy-start | bytes 3145732
  80.1 21.6 %copy-start.3 = (bf16[512,1024]{1,0:T(8,128)(2,1)}, bf16[512,1024]{1,0:T(8,128)(2,1)S(1)}, u32[]{:S(2)}) copy-start(bf16[512,1024]{1,0:T(8,128)(2,1)S(1)} %collective-permute-done.5.refs_3_) | copy-start | bytes 3145732
  83.1 18.6 %copy-start.4 = (bf16[512,1024]{1,0:T(8,128)(2,1)}, bf16[512,1024]{1,0:T(8,128)(2,1)S(1)}, u32[]{:S(2)}) copy-start(bf16[512,1024]{1,0:T(8,128)(2,1)S(1)} %collective-permute-done.4.refs_2_) | copy-start | bytes 3145732
  83.1 10.3 %collective-permute-start.8 = (bf16[512,1280]{1,0:T(8,128)(2,1)S(1)}, bf16[512,1280]{1,0:T(8,128)(2,1)S(1)}, u32[]{:S(2)}, u32[]{:S(2)}) collective-permute-start(bf16[512,1280]{1,0:T(8,128)(2,1)S(1)} %collective-permute-done.3.w1), channel_id=1, source_target_pairs={{0,8},{8,0},{16,24},{24,16},{32,40},{40,32},{48,56},{56,48},{64,72... | collective-permute-start | bytes 3932168 | tf_op jit(solution)/shard_map/ppermute | solution.py:26
  83.2 11.1 %collective-permute-start.7 = (bf16[512,1280]{1,0:T(8,128)(2,1)S(1)}, bf16[512,1280]{1,0:T(8,128)(2,1)}, u32[]{:S(2)}, u32[]{:S(2)}) collective-permute-start(bf16[512,1280]{1,0:T(8,128)(2,1)S(1)} %slice.24.w0), channel_id=1, source_target_pairs={{0,8},{8,0},{16,24},{24,16},{32,40},{40,32},{48,56},{56,48},{64,72... | collective-permute-start | bytes 3932168 | tf_op jit(solution)/shard_map/ppermute | solution.py:26
  83.7 7.5 %collective-permute-start.9 = (bf16[512,1024]{1,0:T(8,128)(2,1)S(1)}, bf16[512,1024]{1,0:T(8,128)(2,1)}, u32[]{:S(2)}, u32[]{:S(2)}) collective-permute-start(bf16[512,1024]{1,0:T(8,128)(2,1)S(1)} %collective-permute-done.4.refs_2_), channel_id=1, source_target_pairs={{0,8},{8,0},{16,24},{24,16},{32,40},{40,32},{48,56},{56,48},{64,72... | collective-permute-start | bytes 3145736 | tf_op jit(solution)/shard_map/ppermute | solution.py:26
  83.8 9.5 %collective-permute-start.10 = (bf16[512,1024]{1,0:T(8,128)(2,1)S(1)}, bf16[512,1024]{1,0:T(8,128)(2,1)S(1)}, u32[]{:S(2)}, u32[]{:S(2)}) collective-permute-start(bf16[512,1024]{1,0:T(8,128)(2,1)S(1)} %collective-permute-done.5.refs_3_), channel_id=1, source_target_pairs={{0,8},{8,0},{16,24},{24,16},{32,40},{40,32},{48,56},{56,48},{64,72... | collective-permute-start | bytes 3145736 | tf_op jit(solution)/shard_map/ppermute | solution.py:26
  84.2 33.2 %collective-permute-start.14 = (bf16[512,1024]{1,0:T(8,128)(2,1)S(1)}, bf16[512,1024]{1,0:T(8,128)(2,1)}, u32[]{:S(2)}, u32[]{:S(2)}) collective-permute-start(bf16[512,1024]{1,0:T(8,128)(2,1)S(1)} %slice.25.refs_0_), channel_id=1, source_target_pairs={{0,64},{8,72},{16,80},{24,88},{32,96},{40,104},{48,112},{56,120},{... | collective-permute-start | bytes 3145736 | tf_op jit(solution)/shard_map/ppermute | solution.py:26
  91.2 14.8 %collective-permute-start.15 = (bf16[256,1024]{1,0:T(8,128)(2,1)S(1)}, bf16[256,1024]{1,0:T(8,128)(2,1)S(1)}, u32[]{:S(2)}, u32[]{:S(2)}) collective-permute-start(bf16[256,1024]{1,0:T(8,128)(2,1)S(1)} %slice.26), channel_id=1, source_target_pairs={{0,48},{8,56},{16,0},{24,8},{32,16},{40,24},{48,32},{56,40},{64,11... | collective-permute-start | bytes 1572872 | tf_op jit(solution)/shard_map/ppermute | solution.py:22
  93.3 24.0 %collective-permute-start.16 = (bf16[256,1024]{1,0:T(8,128)(2,1)S(1)}, bf16[256,1024]{1,0:T(8,128)(2,1)S(1)}, u32[]{:S(2)}, u32[]{:S(2)}) collective-permute-start(bf16[256,1024]{1,0:T(8,128)(2,1)S(1)} %slice.27), channel_id=1, source_target_pairs={{0,16},{8,24},{16,32},{24,40},{32,48},{40,56},{48,0},{56,8},{64,80... | collective-permute-start | bytes 1572872 | tf_op jit(solution)/shard_map/ppermute | solution.py:22
  101.7 20.6 %collective-permute-start.11 = (bf16[160,1280]{1,0:T(8,128)(2,1)S(1)}, bf16[160,1280]{1,0:T(8,128)(2,1)S(1)}, u32[]{:S(2)}, u32[]{:S(2)}) collective-permute-start(bf16[160,1280]{1,0:T(8,128)(2,1)S(1)} %get-tuple-element.52), channel_id=1, source_target_pairs={{0,48},{8,56},{16,0},{24,8},{32,16},{40,24},{48,32},{56,40},{64,11... | collective-permute-start | bytes 1228808 | tf_op jit(solution)/shard_map/ppermute | solution.py:22
  104.1 18.2 %collective-permute-start.12 = (bf16[160,1280]{1,0:T(8,128)(2,1)S(1)}, bf16[160,1280]{1,0:T(8,128)(2,1)S(1)}, u32[]{:S(2)}, u32[]{:S(2)}) collective-permute-start(bf16[160,1280]{1,0:T(8,128)(2,1)S(1)} %get-tuple-element.53), channel_id=1, source_target_pairs={{0,32},{8,40},{16,48},{24,56},{32,0},{40,8},{48,16},{56,24},{64,96... | collective-permute-start | bytes 1228808 | tf_op jit(solution)/shard_map/ppermute | solution.py:22
  106.0 19.9 %collective-permute-start.13 = (bf16[160,1280]{1,0:T(8,128)(2,1)S(1)}, bf16[160,1280]{1,0:T(8,128)(2,1)S(1)}, u32[]{:S(2)}, u32[]{:S(2)}) collective-permute-start(bf16[160,1280]{1,0:T(8,128)(2,1)S(1)} %get-tuple-element.54), channel_id=1, source_target_pairs={{0,16},{8,24},{16,32},{24,40},{32,48},{40,56},{48,0},{56,8},{64,80... | collective-permute-start | bytes 1228808 | tf_op jit(solution)/shard_map/ppermute | solution.py:22
  125.8 26.0 %collective-permute-start.21 = (bf16[512,1024]{1,0:T(8,128)(2,1)}, bf16[512,1024]{1,0:T(8,128)(2,1)S(1)}, u32[]{:S(2)}, u32[]{:S(2)}) collective-permute-start(bf16[512,1024]{1,0:T(8,128)(2,1)} %collective-permute-done.14.refs_6_), channel_id=1, source_target_pairs={{0,48},{8,56},{16,0},{24,8},{32,16},{40,24},{48,32},{56,40},{64,11... | collective-permute-start | bytes 3145736 | tf_op jit(solution)/shard_map/ppermute | solution.py:22
  126.0 25.9 %collective-permute-start.20 = (bf16[512,1024]{1,0:T(8,128)(2,1)}, bf16[512,1024]{1,0:T(8,128)(2,1)S(1)}, u32[]{:S(2)}, u32[]{:S(2)}) collective-permute-start(bf16[512,1024]{1,0:T(8,128)(2,1)} %collective-permute-done.14.refs_6_), channel_id=1, source_target_pairs={{0,16},{8,24},{16,32},{24,40},{32,48},{40,56},{48,0},{56,8},{64,80... | collective-permute-start | bytes 3145736 | tf_op jit(solution)/shard_map/ppermute | solution.py:22
  127.8 14.9 %collective-permute-start.22 = (bf16[256,1024]{1,0:T(8,128)(2,1)S(1)}, bf16[256,1024]{1,0:T(8,128)(2,1)S(1)}, u32[]{:S(2)}, u32[]{:S(2)}) collective-permute-start(bf16[256,1024]{1,0:T(8,128)(2,1)S(1)} %collective-permute-done.15.refs_8_), channel_id=1, source_target_pairs={{0,64},{8,72},{16,80},{24,88},{32,96},{40,104},{48,112},{56,120},{... | collective-permute-start | bytes 1572872 | tf_op jit(solution)/shard_map/ppermute | solution.py:26
  128.5 23.3 %collective-permute-start.23 = (bf16[256,1024]{1,0:T(8,128)(2,1)S(1)}, bf16[256,1024]{1,0:T(8,128)(2,1)S(1)}, u32[]{:S(2)}, u32[]{:S(2)}) collective-permute-start(bf16[256,1024]{1,0:T(8,128)(2,1)S(1)} %collective-permute-done.16.refs_9_), channel_id=1, source_target_pairs={{0,64},{8,72},{16,80},{24,88},{32,96},{40,104},{48,112},{56,120},{... | collective-permute-start | bytes 1572872 | tf_op jit(solution)/shard_map/ppermute | solution.py:26
  140.6 12.0 %collective-permute-start.18 = (bf16[256,1024]{1,0:T(8,128)(2,1)S(1)}, bf16[256,1024]{1,0:T(8,128)(2,1)S(1)}, u32[]{:S(2)}, u32[]{:S(2)}) collective-permute-start(bf16[256,1024]{1,0:T(8,128)(2,1)S(1)} %collective-permute-done.15.refs_8_), channel_id=1, source_target_pairs={{0,8},{8,0},{16,24},{24,16},{32,40},{40,32},{48,56},{56,48},{64,72... | collective-permute-start | bytes 1572872 | tf_op jit(solution)/shard_map/ppermute | solution.py:26
  142.7 10.3 %collective-permute-start.19 = (bf16[256,1024]{1,0:T(8,128)(2,1)S(1)}, bf16[256,1024]{1,0:T(8,128)(2,1)S(1)}, u32[]{:S(2)}, u32[]{:S(2)}) collective-permute-start(bf16[256,1024]{1,0:T(8,128)(2,1)S(1)} %collective-permute-done.16.refs_9_), channel_id=1, source_target_pairs={{0,8},{8,0},{16,24},{24,16},{32,40},{40,32},{48,56},{56,48},{64,72... | collective-permute-start | bytes 1572872 | tf_op jit(solution)/shard_map/ppermute | solution.py:26
  151.8 3.2 %collective-permute-start.17 = (bf16[512,1024]{1,0:T(8,128)(2,1)}, bf16[512,1024]{1,0:T(8,128)(2,1)S(1)}, u32[]{:S(2)}, u32[]{:S(2)}) collective-permute-start(bf16[512,1024]{1,0:T(8,128)(2,1)} %collective-permute-done.14.refs_6_), channel_id=1, source_target_pairs={{0,8},{8,0},{16,24},{24,16},{32,40},{40,32},{48,56},{56,48},{64,72... | collective-permute-start | bytes 3145736 | tf_op jit(solution)/shard_map/ppermute | solution.py:26
  151.9 7.1 %collective-permute-start.24 = (bf16[512,1024]{1,0:T(8,128)(2,1)S(1)}, bf16[512,1024]{1,0:T(8,128)(2,1)S(1)}, u32[]{:S(2)}, u32[]{:S(2)}) collective-permute-start(bf16[512,1024]{1,0:T(8,128)(2,1)S(1)} %collective-permute-done.20.refs_12_), channel_id=1, source_target_pairs={{0,8},{8,0},{16,24},{24,16},{32,40},{40,32},{48,56},{56,48},{64,72... | collective-permute-start | bytes 3145736 | tf_op jit(solution)/shard_map/ppermute | solution.py:26
  152.4 6.6 %collective-permute-start.25 = (bf16[512,1024]{1,0:T(8,128)(2,1)S(1)}, bf16[512,1024]{1,0:T(8,128)(2,1)S(1)}, u32[]{:S(2)}, u32[]{:S(2)}) collective-permute-start(bf16[512,1024]{1,0:T(8,128)(2,1)S(1)} %collective-permute-done.21.refs_13_), channel_id=1, source_target_pairs={{0,8},{8,0},{16,24},{24,16},{32,40},{40,32},{48,56},{56,48},{64,72... | collective-permute-start | bytes 3145736 | tf_op jit(solution)/shard_map/ppermute | solution.py:26
  152.5 5.7 %collective-permute-start.26 = (bf16[256,1024]{1,0:T(8,128)(2,1)S(1)}, bf16[256,1024]{1,0:T(8,128)(2,1)S(1)}, u32[]{:S(2)}, u32[]{:S(2)}) collective-permute-start(bf16[256,1024]{1,0:T(8,128)(2,1)S(1)} %collective-permute-done.22.refs_14_), channel_id=1, source_target_pairs={{0,8},{8,0},{16,24},{24,16},{32,40},{40,32},{48,56},{56,48},{64,72... | collective-permute-start | bytes 1572872 | tf_op jit(solution)/shard_map/ppermute | solution.py:26
  153.0 6.0 %collective-permute-start.27 = (bf16[256,1024]{1,0:T(8,128)(2,1)S(1)}, bf16[256,1024]{1,0:T(8,128)(2,1)S(1)}, u32[]{:S(2)}, u32[]{:S(2)}) collective-permute-start(bf16[256,1024]{1,0:T(8,128)(2,1)S(1)} %collective-permute-done.23.refs_15_), channel_id=1, source_target_pairs={{0,8},{8,0},{16,24},{24,16},{32,40},{40,32},{48,56},{56,48},{64,72... | collective-permute-start | bytes 1572872 | tf_op jit(solution)/shard_map/ppermute | solution.py:26
  (12 other events, 62.4 us)

commit v6 on v5

--- a/solution.py
+++ b/solution.py
@@ -52,8 +52,8 @@
 
         def step(n, carry, zz=zz, out_ref=out_ref):
             q, p = n // 4, lax.rem(n, 4)
-            yy = lax.rem(y_lo + lax.rem(q, 2), 2)
-            cc = lax.rem(core + q // 2, 2)
+            yy = lax.rem(y_lo + q // 2, 2)
+            cc = lax.rem(core + lax.rem(q, 2), 2)
             i = yy * 64 + zz * 16 + cc * 8 + 2 * p
             s0, s1 = owner_ref[0, i], owner_ref[0, i + 1]
             a = hidden_ref[:, pl.ds(pl.multiple_of((s0 // 2) * 128, 128), 128)].astype(jnp.float32)
@@ -79,7 +79,7 @@
             pl.BlockSpec(memory_space=pltpu.VMEM),
         ],
         out_specs=[pl.BlockSpec(memory_space=pltpu.VMEM)] * NZ,
-        compiler_params=pltpu.CompilerParams(vmem_limit_bytes=48 * MIB),
+        compiler_params=pltpu.CompilerParams(vmem_limit_bytes=14 * MIB),
         cost_estimate=pl.CostEstimate(
             flops=rows * width * 8, bytes_accessed=4 * rows * width, transcendentals=0
         ),
@@ -87,45 +87,54 @@
     )(block_owner, hidden)
 
 
-def partial_kernel(h0, h1, h2, h3, w0, w1, w2, w3, p0, p1, p2, p3, stacked):
-    rows = h0.shape[0]
+def partial_kernel(begun, *refs):
+    held, weights = refs[:NZ], refs[NZ : NZ + 2]
+    totals = refs[NZ + 2 : 2 * NZ + 2] if begun else ()
+    *outs, stacked = refs[NZ + 2 + len(totals) :]
+    rows = held[0].shape[0]
+    depth = weights[0].shape[0]
 
     @pl.when(pl.program_id(0) == 0)
     def _():
-        for k, h in enumerate((h0, h1, h2, h3)):
+        for k, h in enumerate(held):
             stacked[pl.ds(k * rows, rows), :] = h[...]
 
-    depth = w0.shape[0]
-    total = jnp.zeros((NZ * rows, w0.shape[1]), jnp.float32)
-    for q, w in enumerate((w0, w1, w2, w3)):
-        total = total + jnp.dot(
-            stacked[:, q * depth : (q + 1) * depth], w[...], preferred_element_type=jnp.float32
-        )
-    for k, out in enumerate((p0, p1, p2, p3)):
-        out[...] = total[k * rows : (k + 1) * rows].astype(out.dtype)
-
-
-def partials(parts, weights):
+    total = jnp.dot(stacked[:, :depth], weights[0][...], preferred_element_type=jnp.float32)
+    total = total + jnp.dot(
+        stacked[:, depth:], weights[1][...], preferred_element_type=jnp.float32
+    )
+    for k, out in enumerate(outs):
+        part = total[k * rows : (k + 1) * rows]
+        if begun:
+            part = part + totals[k][...]
+        out[...] = part.astype(out.dtype)
+
+
+def partials(parts, weights, totals=()):
     rows, width = parts[0].shape
     depth, cols = weights[0].shape
     tile = 256
+    begun = len(totals) > 0
+    place = 1 if begun else 0
+    block = pl.BlockSpec((rows, tile), lambda j: (0, j))
+    types = [jnp.float32] + [jnp.bfloat16 if begun else jnp.float32] * (NZ - 1)
     return pl.pallas_call(
-        partial_kernel,
+        functools.partial(partial_kernel, begun),
         grid=(cols // tile,),
-        out_shape=[jax.ShapeDtypeStruct((rows, cols), jnp.float32)]
-        + [jax.ShapeDtypeStruct((rows, cols), jnp.bfloat16)] * 3,
-        in_specs=[pl.BlockSpec((rows, width), lambda j: (0, 0))] * NZ
-        + [pl.BlockSpec((depth, tile), lambda j: (0, j))] * NZ,
-        out_specs=[pl.BlockSpec((rows, tile), lambda j: (0, j))] * NZ,
-        scratch_shapes=[pltpu.VMEM((NZ * rows, width), jnp.bfloat16)],
-        compiler_params=pltpu.CompilerParams(vmem_limit_bytes=48 * MIB),
+        out_shape=[jax.ShapeDtypeStruct((rows, cols), kind) for kind in types],
+        in_specs=[pl.BlockSpec((rows, width // 2), lambda j: (0, place))] * NZ
+        + [pl.BlockSpec((depth, tile), lambda j: (0, j))] * 2
+        + [block] * len(totals),
+        out_specs=[block] * NZ,
+        scratch_shapes=[pltpu.VMEM((NZ * rows, width // 2), jnp.bfloat16)],
+        compiler_params=pltpu.CompilerParams(vmem_limit_bytes=14 * MIB),
         cost_estimate=pl.CostEstimate(
-            flops=2 * NZ * rows * width * cols,
-            bytes_accessed=2 * (NZ * rows * width + width * cols + NZ * rows * cols),
+            flops=NZ * rows * width * cols,
+            bytes_accessed=NZ * rows * width + width * cols + 4 * NZ * rows * cols,
             transcendentals=0,
         ),
-        name="partials",
-    )(*parts, *weights)
+        name="partials_rest" if begun else "partials",
+    )(*parts, *weights, *totals)
 
 
 def back_kernel(spots, groups, owner_ref, mixed_ref, *refs):
@@ -357,28 +366,34 @@
     parts = [parts[0]] + [z_shift(parts[k], k) for k in range(1, NZ)]
 
     both = flatten(lax.all_to_all(copy, "tp", split_axis=1, concat_axis=0, tiled=True))
-    both, cos, sin, *parts = lax.optimization_barrier((both, cos, sin, *parts))
+    both, cos, sin, parts[1], parts[3] = lax.optimization_barrier(
+        (both, cos, sin, parts[1], parts[3])
+    )
     w, own = both[:, :cols], both[:, cols:]
     half = own.shape[0] // 2
 
     w_y, w_c = flip(w, 8), flip(w, 1)
+    own, parts[2] = lax.optimization_barrier((own, parts[2]))
     below, above = z_shift(own, 1), z_shift(own, -1)
     own_c = flip(own, 1)
-    w_y, below, above, own, own_c = lax.optimization_barrier((w_y, below, above, own, own_c))
+    begun = partials(parts, (w, w_c))
+    w_y, below, above, own, own_c, *begun = lax.optimization_barrier(
+        (w_y, below, above, own, own_c, *begun)
+    )
     w_yc = flip(w_y, 1)
     far_a, far_b = z_shift(above[:half], -1), z_shift(below[half:], 1)
     across = flip(own, 8)
-    below_c, above_c = flip(below, 1), flip(above, 1)
-    w_yc, below_c, above_c = lax.optimization_barrier((w_yc, below_c, above_c))
-
-    sums = partials(parts, (w, w_y, w_c, w_yc))
+
+    sums = partials(parts, (w_y, w_yc), begun)
     sums = [sums[0]] + [z_shift(sums[k], -k) for k in range(1, NZ)]
-    across, far_a, far_b = after((across, far_a, far_b), *sums)
+    across, far_a, far_b, below, above = after((across, far_a, far_b, below, above), *sums)
     across_below, across_above = z_shift(across, 1), z_shift(across, -1)
     across_far_a, across_far_b = flip(far_a, 8), flip(far_b, 8)
     mixed = attention(sums, cos, sin, cache, lengths)
 
-    across_c, far_ac, far_bc = (flip(v, 1) for v in after((across, far_a, far_b), mixed))
+    below_c, above_c, across_c, far_ac, far_bc = (
+        flip(value, 1) for value in after((below, above, across, far_a, far_b), mixed)
+    )
     last = after((across_below, across_above, across_far_a, across_far_b), mixed)
     last_c = [flip(value, 1) for value in last]
     near = ((0, 0), (0, 3), (0, 1), (1, 0), (0, 2), (0, 2), (1, 3), (1, 1), (1, 2), (1, 2))

time: 218 us -> 212 us (0.972)
  waiting for transfers between devices: 97.1 us -> 92.5 us
  local copies, waits for them, and re-layouts: 7.4 us -> 4.5 us
    ppermute x12, waiting for transfers between devices: 73.9 us -> 66.3 us  [z_shift(): return lax.ppermute(value, 'fsdp', pairs)]
    ppermute x16, waiting for transfers between devices: 23.3 us -> 26.2 us  [flip(): return lax.ppermute(value, 'fsdp', [(f, f ^ bit) for f in range(16)])]
    unnamed x31 -> x29, local copies, waits for them, and re-layouts: 4.26 us -> 1.35 us
    pallas_call x1 -> x2, Pallas kernels: 6.26 us -> 6.67 us  [partials(): pl.pallas_call(functools.partial(partial_kernel, begun), grid=(cols // ti...]
  transfers between devices with their start and end apart: 29 -> 29, of which waited for: 15 -> 15; matrix products, arithmetic and copies ran while one was open for 1% -> 2% of each run, Pallas kernels for 10% -> 11%
where the time goes in v6:
time: 212 us
  waiting for transfers between devices  92.5 us (44%)
  blocking collectives  41.3 us (19%)
  Pallas kernels  37.3 us (18%)
  starting transfers between devices  30.3 us (14%)
  other arithmetic  5.5 us (3%)
  local copies, waits for them, and re-layouts  4.5 us (2%)
    ppermute x12, waiting for transfers between devices, z_shift(): return lax.ppermute(value, 'fsdp', pairs)  66.3 us
    all_to_all x1, blocking collectives, body(): terms = lax.all_to_all(terms, 'tp', split_axis=0, concat_axis=0, tiled=True)  41.3 us
    ppermute x16, waiting for transfers between devices, flip(): return lax.ppermute(value, 'fsdp', [(f, f ^ bit) for f in range(16)])  26.2 us
    ppermute x12, starting transfers between devices, z_shift(): return lax.ppermute(value, 'fsdp', pairs)  16.8 us
    pallas_call x1, Pallas kernels, project_back(): pl.pallas_call(functools.partial(back_kernel, spots, groups), out_shape=j...  14.5 us
    pallas_call x1, Pallas kernels, attention(): pl.pallas_call(attention_kernel, grid=(rows // GROUP,), out_shape=jax.Sha...  10.7 us
    all_to_all x1, starting transfers between devices, body(): lax.all_to_all(copy, 'tp', split_axis=1, concat_axis=0, tiled=True)  7.28 us
    pallas_call x2, Pallas kernels, partials(): pl.pallas_call(functools.partial(partial_kernel, begun), grid=(cols // ti...  6.67 us
  transfers between devices with their start and end apart: 29, of which 15 were waited for; matrix products, arithmetic and copies ran while one was open for 2% of the time, Pallas kernels for 11%

profile of v6, /device:TPU:0, one launch (start us, length us, event | category | flops | bytes accessed | tf_op | source)
XLA Modules:
  0.0 211.7 jit_solution(11086493901843979234)
XLA Ops:
  0.0 2.0 convert_element_type.18
  2.7 1.6 pad_maximum_fusion
  4.4 7.3 %all-to-all-start = ((bf16[64,8,2304]{2,0,1:T(8,128)(2,1)}), bf16[64,8,2304]{2,0,1:T(8,128)(2,1)}, u32[]{:S(2)}, u32[]{:S(2)}) async-start(bf16[64,8,2304]{2,0,1:T(8,128)(2,1)} %pad_maximum_fusion), calls=%async_computation | async-start | bytes 4718592 | tf_op jit(solution)/shard_map/all_to_all | solution.py:368
  11.7 5.5 %shuffle.1 = (bf16[160,2048]{1,0:T(8,128)(2,1)S(1)}, bf16[160,2048]{1,0:T(8,128)(2,1)}, bf16[160,2048]{1,0:T(8,128)(2,1)}, bf16[160,2048]{1,0:T(8,128)(2,1)}) custom-call(s32[2,128]{1,0:T(2,128)S(1)} %copy-done.1, bf16[160,8192]{1,0:T(8,128)(2,1)S(1)} %bitcast.21), custom_call_target="tpu_custom_call" | custom-call | flops 10485760 | bytes 5242880 | tf_op jit(solution)/shard_map/shuffle/pallas_call | solution.py:74
  17.1 1.9 collective-permute-start
  19.0 2.1 %collective-permute-start.1 = (bf16[160,2048]{1,0:T(8,128)(2,1)}, bf16[160,2048]{1,0:T(8,128)(2,1)S(1)}, u32[]{:S(2)}, u32[]{:S(2)}) collective-permute-start(bf16[160,2048]{1,0:T(8,128)(2,1)} %get-tuple-element.49), channel_id=1, source_target_pairs={{0,48},{8,56},{16,0},{24,8},{32,16},{40,24},{48,32},{56,40},{64,11... | collective-permute-start | bytes 1966088 | tf_op jit(solution)/shard_map/ppermute | solution.py:22
  21.2 1.9 collective-permute-start.2
  23.6 12.5 %collective-permute-done.refs_1_ = bf16[160,2048]{1,0:T(8,128)(2,1)S(1)} collective-permute-done((bf16[160,2048]{1,0:T(8,128)(2,1)}, bf16[160,2048]{1,0:T(8,128)(2,1)S(1)}, u32[]{:S(2)}, u32[]{:S(2)}) %collective-permute-start) | collective-permute-done | bytes 655392 | tf_op jit(solution)/shard_map/ppermute | solution.py:22
  36.1 13.2 %collective-permute-done.1.refs_3_ = bf16[160,2048]{1,0:T(8,128)(2,1)S(1)} collective-permute-done((bf16[160,2048]{1,0:T(8,128)(2,1)}, bf16[160,2048]{1,0:T(8,128)(2,1)S(1)}, u32[]{:S(2)}, u32[]{:S(2)}) %collective-permute-start.1) | collective-permute-done | bytes 655392 | tf_op jit(solution)/shard_map/ppermute | solution.py:22
  49.3 1.4 slice.25.refs_4_
  51.5 1.3 slice.24.refs_0_
  53.1 3.6 %collective-permute-start.5 = (bf16[512,1024]{1,0:T(8,128)(2,1)S(1)}, bf16[512,1024]{1,0:T(8,128)(2,1)S(1)}, u32[]{:S(2)}, u32[]{:S(2)}) collective-permute-start(bf16[512,1024]{1,0:T(8,128)(2,1)S(1)} %slice.24.refs_0_), channel_id=1, source_target_pairs={{0,48},{8,56},{16,0},{24,8},{32,16},{40,24},{48,32},{56,40},{64,11... | collective-permute-start | bytes 3145736 | tf_op jit(solution)/shard_map/ppermute | solution.py:22
  56.6 3.2 %partials.1 = (f32[160,1280]{1,0:T(8,128)S(1)}, f32[160,1280]{1,0:T(8,128)S(1)}, f32[160,1280]{1,0:T(8,128)S(1)}, f32[160,1280]{1,0:T(8,128)S(1)}) custom-call(bf16[160,2048]{1,0:T(8,128)(2,1)S(1)} %get-tuple-element.47.refs_0_, bf16[160,2048]{1,0:T(8,128)(2,1)S(1)} %collective-permute-done.refs_1_, bf16[160,2048]{1,0:T(8,128)(2,1)S(1)} %collective-permute-done.2.refs_2_, ...), custom_call_target="tpu_custom_call" | custom-call | flops 1677721600 | bytes 7208960 | tf_op jit(solution)/shard_map/partials/pallas_call | solution.py:121
  59.9 19.7 %collective-permute-done.5.refs_3_ = bf16[512,1024]{1,0:T(8,128)(2,1)S(1)} collective-permute-done((bf16[512,1024]{1,0:T(8,128)(2,1)S(1)}, bf16[512,1024]{1,0:T(8,128)(2,1)S(1)}, u32[]{:S(2)}, u32[]{:S(2)}) %collective-permute-start.5) | collective-permute-done | bytes 1048608 | tf_op jit(solution)/shard_map/ppermute | solution.py:22
  79.6 3.4 %collective-permute-done.4.refs_2_ = bf16[512,1024]{1,0:T(8,128)(2,1)S(1)} collective-permute-done((bf16[512,1024]{1,0:T(8,128)(2,1)S(1)}, bf16[512,1024]{1,0:T(8,128)(2,1)S(1)}, u32[]{:S(2)}, u32[]{:S(2)}) %collective-permute-start.4) | collective-permute-done | bytes 1048608 | tf_op jit(solution)/shard_map/ppermute | solution.py:22
  83.0 1.4 collective-permute-start.12
  84.6 3.3 %collective-permute-start.13 = (bf16[256,1024]{1,0:T(8,128)(2,1)S(1)}, bf16[256,1024]{1,0:T(8,128)(2,1)S(1)}, u32[]{:S(2)}, u32[]{:S(2)}) collective-permute-start(bf16[256,1024]{1,0:T(8,128)(2,1)S(1)} %slice.26), channel_id=1, source_target_pairs={{0,48},{8,56},{16,0},{24,8},{32,16},{40,24},{48,32},{56,40},{64,11... | collective-permute-start | bytes 1572872 | tf_op jit(solution)/shard_map/ppermute | solution.py:22
  87.9 3.4 %partials_rest.1 = (f32[160,1280]{1,0:T(8,128)S(1)}, bf16[160,1280]{1,0:T(8,128)(2,1)S(1)}, bf16[160,1280]{1,0:T(8,128)(2,1)S(1)}, bf16[160,1280]{1,0:T(8,128)(2,1)S(1)}) custom-call(bf16[160,2048]{1,0:T(8,128)(2,1)S(1)} %get-tuple-element.47.refs_0_, bf16[160,2048]{1,0:T(8,128)(2,1)S(1)} %collective-permute-done.refs_1_, ...), custom_call_target="tpu_custom_call" | custom-call | flops 1677721600 | bytes 7208960 | tf_op jit(solution)/shard_map/partials_rest/pallas_call | solution.py:121
  92.3 8.1 %collective-permute-done.14.refs_9_ = bf16[256,1024]{1,0:T(8,128)(2,1)S(1)} collective-permute-done((bf16[256,1024]{1,0:T(8,128)(2,1)S(1)}, bf16[256,1024]{1,0:T(8,128)(2,1)S(1)}, u32[]{:S(2)}, u32[]{:S(2)}) %collective-permute-start.14) | collective-permute-done | bytes 524320 | tf_op jit(solution)/shard_map/ppermute | solution.py:22
  100.3 8.2 %collective-permute-done.12.refs_6_ = bf16[512,1024]{1,0:T(8,128)(2,1)S(1)} collective-permute-done((bf16[512,1024]{1,0:T(8,128)(2,1)S(1)}, bf16[512,1024]{1,0:T(8,128)(2,1)S(1)}, u32[]{:S(2)}, u32[]{:S(2)}) %collective-permute-start.12) | collective-permute-done | bytes 1048608 | tf_op jit(solution)/shard_map/ppermute | solution.py:26
  108.6 8.1 %collective-permute-done.9.p1 = bf16[160,1280]{1,0:T(8,128)(2,1)S(1)} collective-permute-done((bf16[160,1280]{1,0:T(8,128)(2,1)S(1)}, bf16[160,1280]{1,0:T(8,128)(2,1)S(1)}, u32[]{:S(2)}, u32[]{:S(2)}) %collective-permute-start.9) | collective-permute-done | bytes 409632 | tf_op jit(solution)/shard_map/ppermute | solution.py:22
  117.4 3.0 %collective-permute-start.21 = (bf16[512,1024]{1,0:T(8,128)(2,1)S(1)}, bf16[512,1024]{1,0:T(8,128)(2,1)S(1)}, u32[]{:S(2)}, u32[]{:S(2)}) collective-permute-start(bf16[512,1024]{1,0:T(8,128)(2,1)S(1)} %collective-permute-done.12.refs_6_), channel_id=1, source_target_pairs={{0,48},{8,56},{16,0},{24,8},{32,16},{40,24},{48,32},{56,40},{64,11... | collective-permute-start | bytes 3145736 | tf_op jit(solution)/shard_map/ppermute | solution.py:22
  121.0 1.3 collective-permute-start.23
  122.4 10.7 %attention.1.mixed_ref = bf16[160,1024]{1,0:T(8,128)(2,1)S(1)} custom-call(s32[80]{0:T(128)S(1)} %copy-done.2, f32[160,1280]{1,0:T(8,128)S(1)} %get-tuple-element.65.p0, bf16[160,1280]{1,0:T(8,128)(2,1)S(1)} %collective-permute-done.9.p1, bf16[160,1280]{1,0:T(8,128)(2,1)S(1)} %collective-permute-done.10.p2, ...), custom_call_target="tpu_custom_call" | custom-call | flops 167772160 | bytes 41943040 | tf_op jit(solution)/shard_map/attention/pallas_call | solution.py:325
  133.2 2.0 collective-permute-done.22.refs_14_
  135.2 8.9 %collective-permute-done.23.refs_15_ = bf16[256,1024]{1,0:T(8,128)(2,1)S(1)} collective-permute-done((bf16[256,1024]{1,0:T(8,128)(2,1)S(1)}, bf16[256,1024]{1,0:T(8,128)(2,1)S(1)}, u32[]{:S(2)}, u32[]{:S(2)}) %collective-permute-start.23) | collective-permute-done | bytes 524320 | tf_op jit(solution)/shard_map/ppermute | solution.py:26
  145.9 1.7 collective-permute-done.19.refs_11_
  149.1 3.7 %collective-permute-done.26.refs_18_ = bf16[256,1024]{1,0:T(8,128)(2,1)S(1)} collective-permute-done((bf16[256,1024]{1,0:T(8,128)(2,1)S(1)}, bf16[256,1024]{1,0:T(8,128)(2,1)S(1)}, u32[]{:S(2)}, u32[]{:S(2)}) %collective-permute-start.26) | collective-permute-done | bytes 524320 | tf_op jit(solution)/shard_map/ppermute | solution.py:26
  153.6 1.0 copy-done.13
  154.6 14.5 %project_back.1 = bf16[8,160,1024]{2,1,0:T(8,128)(2,1)} custom-call(s32[2,128]{1,0:T(2,128)S(1)} %copy-done.1, bf16[160,1024]{1,0:T(8,128)(2,1)S(1)} %attention.1.mixed_ref, bf16[512,1024]{1,0:T(8,128)(2,1)S(1)} %slice.24.refs_0_, bf16[512,1024]{1,0:T(8,128)(2,1)} %copy-done.6, bf16[512,1024]{1,0:T(8,128)(2,1)} %copy-done.4, bf16[512,1024]{1,0:T(8,128)(2,1)} %copy-done.3, ...), custom_call_target="tpu_custom_call" | custom-call | flops 2684354560 | bytes 19726336 | tf_op jit(solution)/shard_map/project_back/pallas_call | solution.py:186
  169.1 41.3 %all_to_all.20 = bf16[8,160,1024]{2,1,0:T(8,128)(2,1)S(1)} all-to-all(bf16[8,160,1024]{2,1,0:T(8,128)(2,1)} %project_back.1), channel_id=1, replica_groups=mesh['fsdp'=16,'tp'=8] {'tp'}, dimensions={0} | all-to-all | bytes 5242880 | tf_op jit(solution)/shard_map/all_to_all | solution.py:407
  210.4 1.3 reduce_sum.12
  (77 shorter events, 8.9 us)
Async XLA Ops:
  4.4 44.9 %all-to-all-start = ((bf16[64,8,2304]{2,0,1:T(8,128)(2,1)}), bf16[64,8,2304]{2,0,1:T(8,128)(2,1)}, u32[]{:S(2)}, u32[]{:S(2)}) async-start(bf16[64,8,2304]{2,0,1:T(8,128)(2,1)} %pad_maximum_fusion), calls=%async_computation | async-start | bytes 4718592 | tf_op jit(solution)/shard_map/all_to_all | solution.py:368
  17.1 19.0 %collective-permute-start = (bf16[160,2048]{1,0:T(8,128)(2,1)}, bf16[160,2048]{1,0:T(8,128)(2,1)S(1)}, u32[]{:S(2)}, u32[]{:S(2)}) collective-permute-start(bf16[160,2048]{1,0:T(8,128)(2,1)} %get-tuple-element.48), channel_id=1, source_target_pairs={{0,16},{8,24},{16,32},{24,40},{32,48},{40,56},{48,0},{56,8},{64,80... | collective-permute-start | bytes 1966088 | tf_op jit(solution)/shard_map/ppermute | solution.py:22
  19.0 30.2 %collective-permute-start.1 = (bf16[160,2048]{1,0:T(8,128)(2,1)}, bf16[160,2048]{1,0:T(8,128)(2,1)S(1)}, u32[]{:S(2)}, u32[]{:S(2)}) collective-permute-start(bf16[160,2048]{1,0:T(8,128)(2,1)} %get-tuple-element.49), channel_id=1, source_target_pairs={{0,48},{8,56},{16,0},{24,8},{32,16},{40,24},{48,32},{56,40},{64,11... | collective-permute-start | bytes 1966088 | tf_op jit(solution)/shard_map/ppermute | solution.py:22
  21.2 31.7 %collective-permute-start.2 = (bf16[160,2048]{1,0:T(8,128)(2,1)}, bf16[160,2048]{1,0:T(8,128)(2,1)S(1)}, u32[]{:S(2)}, u32[]{:S(2)}) collective-permute-start(bf16[160,2048]{1,0:T(8,128)(2,1)} %get-tuple-element.52), channel_id=1, source_target_pairs={{0,32},{8,40},{16,48},{24,56},{32,0},{40,8},{48,16},{56,24},{64,96... | collective-permute-start | bytes 1966088 | tf_op jit(solution)/shard_map/ppermute | solution.py:22
  50.7 6.0 %collective-permute-start.7 = (bf16[512,1280]{1,0:T(8,128)(2,1)S(1)}, bf16[512,1280]{1,0:T(8,128)(2,1)S(1)}, u32[]{:S(2)}, u32[]{:S(2)}) collective-permute-start(bf16[512,1280]{1,0:T(8,128)(2,1)S(1)} %slice.25.refs_4_), channel_id=1, source_target_pairs={{0,8},{8,0},{16,24},{24,16},{32,40},{40,32},{48,56},{56,48},{64,72... | collective-permute-start | bytes 3932168 | tf_op jit(solution)/shard_map/ppermute | solution.py:26
  50.8 32.2 %collective-permute-start.3 = (bf16[512,1280]{1,0:T(8,128)(2,1)S(1)}, bf16[512,1280]{1,0:T(8,128)(2,1)S(1)}, u32[]{:S(2)}, u32[]{:S(2)}) collective-permute-start(bf16[512,1280]{1,0:T(8,128)(2,1)S(1)} %slice.25.refs_4_), channel_id=1, source_target_pairs={{0,64},{8,72},{16,80},{24,88},{32,96},{40,104},{48,112},{56,120},{... | collective-permute-start | bytes 3932168 | tf_op jit(solution)/shard_map/ppermute | solution.py:26
  52.8 7.0 %collective-permute-start.6 = (bf16[512,1024]{1,0:T(8,128)(2,1)S(1)}, bf16[512,1024]{1,0:T(8,128)(2,1)S(1)}, u32[]{:S(2)}, u32[]{:S(2)}) collective-permute-start(bf16[512,1024]{1,0:T(8,128)(2,1)S(1)} %slice.24.refs_0_), channel_id=1, source_target_pairs={{0,8},{8,0},{16,24},{24,16},{32,40},{40,32},{48,56},{56,48},{64,72... | collective-permute-start | bytes 3145736 | tf_op jit(solution)/shard_map/ppermute | solution.py:26
  53.1 26.5 %collective-permute-start.5 = (bf16[512,1024]{1,0:T(8,128)(2,1)S(1)}, bf16[512,1024]{1,0:T(8,128)(2,1)S(1)}, u32[]{:S(2)}, u32[]{:S(2)}) collective-permute-start(bf16[512,1024]{1,0:T(8,128)(2,1)S(1)} %slice.24.refs_0_), channel_id=1, source_target_pairs={{0,48},{8,56},{16,0},{24,8},{32,16},{40,24},{48,32},{56,40},{64,11... | collective-permute-start | bytes 3145736 | tf_op jit(solution)/shard_map/ppermute | solution.py:22
  56.6 26.3 %collective-permute-start.4 = (bf16[512,1024]{1,0:T(8,128)(2,1)S(1)}, bf16[512,1024]{1,0:T(8,128)(2,1)S(1)}, u32[]{:S(2)}, u32[]{:S(2)}) collective-permute-start(bf16[512,1024]{1,0:T(8,128)(2,1)S(1)} %slice.24.refs_0_), channel_id=1, source_target_pairs={{0,16},{8,24},{16,32},{24,40},{32,48},{40,56},{48,0},{56,8},{64,80... | collective-permute-start | bytes 3145736 | tf_op jit(solution)/shard_map/ppermute | solution.py:22
  79.6 64.6 %copy-start.3 = (bf16[512,1024]{1,0:T(8,128)(2,1)}, bf16[512,1024]{1,0:T(8,128)(2,1)S(1)}, u32[]{:S(2)}) copy-start(bf16[512,1024]{1,0:T(8,128)(2,1)S(1)} %collective-permute-done.5.refs_3_) | copy-start | bytes 3145732
  83.0 52.2 %copy-start.4 = (bf16[512,1024]{1,0:T(8,128)(2,1)}, bf16[512,1024]{1,0:T(8,128)(2,1)S(1)}, u32[]{:S(2)}) copy-start(bf16[512,1024]{1,0:T(8,128)(2,1)S(1)} %collective-permute-done.4.refs_2_) | copy-start | bytes 3145732
  83.0 4.9 %collective-permute-start.8 = (bf16[512,1280]{1,0:T(8,128)(2,1)S(1)}, bf16[512,1280]{1,0:T(8,128)(2,1)S(1)}, u32[]{:S(2)}, u32[]{:S(2)}) collective-permute-start(bf16[512,1280]{1,0:T(8,128)(2,1)S(1)} %collective-permute-done.3.refs_4_), channel_id=1, source_target_pairs={{0,8},{8,0},{16,24},{24,16},{32,40},{40,32},{48,56},{56,48},{64,72... | collective-permute-start | bytes 3932168 | tf_op jit(solution)/shard_map/ppermute | solution.py:26
  83.0 25.6 %collective-permute-start.12 = (bf16[512,1024]{1,0:T(8,128)(2,1)S(1)}, bf16[512,1024]{1,0:T(8,128)(2,1)S(1)}, u32[]{:S(2)}, u32[]{:S(2)}) collective-permute-start(bf16[512,1024]{1,0:T(8,128)(2,1)S(1)} %slice.24.refs_0_), channel_id=1, source_target_pairs={{0,64},{8,72},{16,80},{24,88},{32,96},{40,104},{48,112},{56,120},{... | collective-permute-start | bytes 3145736 | tf_op jit(solution)/shard_map/ppermute | solution.py:26
  84.5 15.9 %collective-permute-start.14 = (bf16[256,1024]{1,0:T(8,128)(2,1)S(1)}, bf16[256,1024]{1,0:T(8,128)(2,1)S(1)}, u32[]{:S(2)}, u32[]{:S(2)}) collective-permute-start(bf16[256,1024]{1,0:T(8,128)(2,1)S(1)} %slice.27), channel_id=1, source_target_pairs={{0,16},{8,24},{16,32},{24,40},{32,48},{40,56},{48,0},{56,8},{64,80... | collective-permute-start | bytes 1572872 | tf_op jit(solution)/shard_map/ppermute | solution.py:22
  84.6 15.8 %collective-permute-start.13 = (bf16[256,1024]{1,0:T(8,128)(2,1)S(1)}, bf16[256,1024]{1,0:T(8,128)(2,1)S(1)}, u32[]{:S(2)}, u32[]{:S(2)}) collective-permute-start(bf16[256,1024]{1,0:T(8,128)(2,1)S(1)} %slice.26), channel_id=1, source_target_pairs={{0,48},{8,56},{16,0},{24,8},{32,16},{40,24},{48,32},{56,40},{64,11... | collective-permute-start | bytes 1572872 | tf_op jit(solution)/shard_map/ppermute | solution.py:22
  91.3 25.3 %collective-permute-start.9 = (bf16[160,1280]{1,0:T(8,128)(2,1)S(1)}, bf16[160,1280]{1,0:T(8,128)(2,1)S(1)}, u32[]{:S(2)}, u32[]{:S(2)}) collective-permute-start(bf16[160,1280]{1,0:T(8,128)(2,1)S(1)} %get-tuple-element.66), channel_id=1, source_target_pairs={{0,48},{8,56},{16,0},{24,8},{32,16},{40,24},{48,32},{56,40},{64,11... | collective-permute-start | bytes 1228808 | tf_op jit(solution)/shard_map/ppermute | solution.py:22
  92.1 24.6 %collective-permute-start.10 = (bf16[160,1280]{1,0:T(8,128)(2,1)S(1)}, bf16[160,1280]{1,0:T(8,128)(2,1)S(1)}, u32[]{:S(2)}, u32[]{:S(2)}) collective-permute-start(bf16[160,1280]{1,0:T(8,128)(2,1)S(1)} %get-tuple-element.67), channel_id=1, source_target_pairs={{0,32},{8,40},{16,48},{24,56},{32,0},{40,8},{48,16},{56,24},{64,96... | collective-permute-start | bytes 1228808 | tf_op jit(solution)/shard_map/ppermute | solution.py:22
  100.3 17.0 %collective-permute-start.11 = (bf16[160,1280]{1,0:T(8,128)(2,1)S(1)}, bf16[160,1280]{1,0:T(8,128)(2,1)S(1)}, u32[]{:S(2)}, u32[]{:S(2)}) collective-permute-start(bf16[160,1280]{1,0:T(8,128)(2,1)S(1)} %get-tuple-element.68), channel_id=1, source_target_pairs={{0,16},{8,24},{16,32},{24,40},{32,48},{40,56},{48,0},{56,8},{64,80... | collective-permute-start | bytes 1228808 | tf_op jit(solution)/shard_map/ppermute | solution.py:22
  108.6 36.8 %copy-start.7 = (bf16[512,1024]{1,0:T(8,128)(2,1)}, bf16[512,1024]{1,0:T(8,128)(2,1)S(1)}, u32[]{:S(2)}) copy-start(bf16[512,1024]{1,0:T(8,128)(2,1)S(1)} %collective-permute-done.12.refs_6_) | copy-start | bytes 3145732
  117.4 26.8 %collective-permute-start.21 = (bf16[512,1024]{1,0:T(8,128)(2,1)S(1)}, bf16[512,1024]{1,0:T(8,128)(2,1)S(1)}, u32[]{:S(2)}, u32[]{:S(2)}) collective-permute-start(bf16[512,1024]{1,0:T(8,128)(2,1)S(1)} %collective-permute-done.12.refs_6_), channel_id=1, source_target_pairs={{0,48},{8,56},{16,0},{24,8},{32,16},{40,24},{48,32},{56,40},{64,11... | collective-permute-start | bytes 3145736 | tf_op jit(solution)/shard_map/ppermute | solution.py:22
  120.4 25.0 %collective-permute-start.20 = (bf16[512,1024]{1,0:T(8,128)(2,1)S(1)}, bf16[512,1024]{1,0:T(8,128)(2,1)S(1)}, u32[]{:S(2)}, u32[]{:S(2)}) collective-permute-start(bf16[512,1024]{1,0:T(8,128)(2,1)S(1)} %collective-permute-done.12.refs_6_), channel_id=1, source_target_pairs={{0,16},{8,24},{16,32},{24,40},{32,48},{40,56},{48,0},{56,8},{64,80... | collective-permute-start | bytes 3145736 | tf_op jit(solution)/shard_map/ppermute | solution.py:22
  120.4 14.9 %collective-permute-start.22 = (bf16[256,1024]{1,0:T(8,128)(2,1)S(1)}, bf16[256,1024]{1,0:T(8,128)(2,1)S(1)}, u32[]{:S(2)}, u32[]{:S(2)}) collective-permute-start(bf16[256,1024]{1,0:T(8,128)(2,1)S(1)} %collective-permute-done.13.refs_8_), channel_id=1, source_target_pairs={{0,64},{8,72},{16,80},{24,88},{32,96},{40,104},{48,112},{56,120},{... | collective-permute-start | bytes 1572872 | tf_op jit(solution)/shard_map/ppermute | solution.py:26
  121.0 23.1 %collective-permute-start.23 = (bf16[256,1024]{1,0:T(8,128)(2,1)S(1)}, bf16[256,1024]{1,0:T(8,128)(2,1)S(1)}, u32[]{:S(2)}, u32[]{:S(2)}) collective-permute-start(bf16[256,1024]{1,0:T(8,128)(2,1)S(1)} %collective-permute-done.14.refs_9_), channel_id=1, source_target_pairs={{0,64},{8,72},{16,80},{24,88},{32,96},{40,104},{48,112},{56,120},{... | collective-permute-start | bytes 1572872 | tf_op jit(solution)/shard_map/ppermute | solution.py:26
  133.1 12.3 %collective-permute-start.18 = (bf16[256,1024]{1,0:T(8,128)(2,1)S(1)}, bf16[256,1024]{1,0:T(8,128)(2,1)S(1)}, u32[]{:S(2)}, u32[]{:S(2)}) collective-permute-start(bf16[256,1024]{1,0:T(8,128)(2,1)S(1)} %collective-permute-done.13.refs_8_), channel_id=1, source_target_pairs={{0,8},{8,0},{16,24},{24,16},{32,40},{40,32},{48,56},{56,48},{64,72... | collective-permute-start | bytes 1572872 | tf_op jit(solution)/shard_map/ppermute | solution.py:26
  135.2 12.5 %collective-permute-start.15 = (bf16[512,1024]{1,0:T(8,128)(2,1)S(1)}, bf16[512,1024]{1,0:T(8,128)(2,1)S(1)}, u32[]{:S(2)}, u32[]{:S(2)}) collective-permute-start(bf16[512,1024]{1,0:T(8,128)(2,1)S(1)} %collective-permute-done.4.refs_2_), channel_id=1, source_target_pairs={{0,8},{8,0},{16,24},{24,16},{32,40},{40,32},{48,56},{56,48},{64,72... | collective-permute-start | bytes 3145736 | tf_op jit(solution)/shard_map/ppermute | solution.py:26
  144.2 3.9 %collective-permute-start.16 = (bf16[512,1024]{1,0:T(8,128)(2,1)S(1)}, bf16[512,1024]{1,0:T(8,128)(2,1)S(1)}, u32[]{:S(2)}, u32[]{:S(2)}) collective-permute-start(bf16[512,1024]{1,0:T(8,128)(2,1)S(1)} %collective-permute-done.5.refs_3_), channel_id=1, source_target_pairs={{0,8},{8,0},{16,24},{24,16},{32,40},{40,32},{48,56},{56,48},{64,72... | collective-permute-start | bytes 3145736 | tf_op jit(solution)/shard_map/ppermute | solution.py:26
  144.2 3.4 %collective-permute-start.19 = (bf16[256,1024]{1,0:T(8,128)(2,1)S(1)}, bf16[256,1024]{1,0:T(8,128)(2,1)S(1)}, u32[]{:S(2)}, u32[]{:S(2)}) collective-permute-start(bf16[256,1024]{1,0:T(8,128)(2,1)S(1)} %collective-permute-done.14.refs_9_), channel_id=1, source_target_pairs={{0,8},{8,0},{16,24},{24,16},{32,40},{40,32},{48,56},{56,48},{64,72... | collective-permute-start | bytes 1572872 | tf_op jit(solution)/shard_map/ppermute | solution.py:26
  145.4 3.7 %collective-permute-start.17 = (bf16[512,1024]{1,0:T(8,128)(2,1)S(1)}, bf16[512,1024]{1,0:T(8,128)(2,1)S(1)}, u32[]{:S(2)}, u32[]{:S(2)}) collective-permute-start(bf16[512,1024]{1,0:T(8,128)(2,1)S(1)} %collective-permute-done.12.refs_6_), channel_id=1, source_target_pairs={{0,8},{8,0},{16,24},{24,16},{32,40},{40,32},{48,56},{56,48},{64,72... | collective-permute-start | bytes 3145736 | tf_op jit(solution)/shard_map/ppermute | solution.py:26
  145.4 8.2 %collective-permute-start.24 = (bf16[512,1024]{1,0:T(8,128)(2,1)S(1)}, bf16[512,1024]{1,0:T(8,128)(2,1)S(1)}, u32[]{:S(2)}, u32[]{:S(2)}) collective-permute-start(bf16[512,1024]{1,0:T(8,128)(2,1)S(1)} %collective-permute-done.20.refs_12_), channel_id=1, source_target_pairs={{0,8},{8,0},{16,24},{24,16},{32,40},{40,32},{48,56},{56,48},{64,72... | collective-permute-start | bytes 3145736 | tf_op jit(solution)/shard_map/ppermute | solution.py:26
  147.6 7.0 %collective-permute-start.25 = (bf16[512,1024]{1,0:T(8,128)(2,1)S(1)}, bf16[512,1024]{1,0:T(8,128)(2,1)}, u32[]{:S(2)}, u32[]{:S(2)}) collective-permute-start(bf16[512,1024]{1,0:T(8,128)(2,1)S(1)} %collective-permute-done.21.refs_13_), channel_id=1, source_target_pairs={{0,8},{8,0},{16,24},{24,16},{32,40},{40,32},{48,56},{56,48},{64,72... | collective-permute-start | bytes 3145736 | tf_op jit(solution)/shard_map/ppermute | solution.py:26
  147.7 5.1 %collective-permute-start.26 = (bf16[256,1024]{1,0:T(8,128)(2,1)S(1)}, bf16[256,1024]{1,0:T(8,128)(2,1)S(1)}, u32[]{:S(2)}, u32[]{:S(2)}) collective-permute-start(bf16[256,1024]{1,0:T(8,128)(2,1)S(1)} %collective-permute-done.22.refs_14_), channel_id=1, source_target_pairs={{0,8},{8,0},{16,24},{24,16},{32,40},{40,32},{48,56},{56,48},{64,72... | collective-permute-start | bytes 1572872 | tf_op jit(solution)/shard_map/ppermute | solution.py:26
  148.1 5.5 %collective-permute-start.27 = (bf16[256,1024]{1,0:T(8,128)(2,1)S(1)}, bf16[256,1024]{1,0:T(8,128)(2,1)S(1)}, u32[]{:S(2)}, u32[]{:S(2)}) collective-permute-start(bf16[256,1024]{1,0:T(8,128)(2,1)S(1)} %collective-permute-done.23.refs_15_), channel_id=1, source_target_pairs={{0,8},{8,0},{16,24},{24,16},{32,40},{40,32},{48,56},{56,48},{64,72... | collective-permute-start | bytes 1572872 | tf_op jit(solution)/shard_map/ppermute | solution.py:26
  (11 other events, 99.6 us)

commit v7 on v6

--- a/solution.py
+++ b/solution.py
@@ -13,7 +13,7 @@
 HD = 128
 NZ = 4
 GROUP = 8
-CHUNK = 4
+CHUNK = 256
 MIB = 1024 * 1024
 
 
@@ -137,75 +137,90 @@
     )(*parts, *weights, *totals)
 
 
-def back_kernel(spots, groups, owner_ref, mixed_ref, *refs):
-    count = len(spots)
-    sources, out_ref, held, placed, goals, sems = refs[:count], *refs[count:]
-    f = lax.axis_index("fsdp")
-    y_lo, z, core = f // 8, lax.rem(f // 2, NZ), lax.rem(f, 2)
-    width = held.shape[0]
-    owned = width // owner_ref.shape[1]
-    chunk = CHUNK * owned
-
-    n = 0
-    for (dy, dz, dc, t0), source in zip(spots, sources):
-        first = (
-            lax.rem(y_lo + dy, 2) * 64 + lax.rem(z + dz, NZ) * 16 + lax.rem(core + dc, 2) * 8 + t0
-        )
-        for part in range(source.shape[0] // chunk):
-            pltpu.make_async_copy(
-                source.at[pl.ds(part * chunk, chunk)], held.at[pl.ds(n * chunk, chunk)], sems.at[n]
-            ).start()
-            for b in range(CHUNK):
-                goals[n * CHUNK + b] = owner_ref[1, first + part * CHUNK + b] * owned
-            n += 1
-    turned = mixed_ref[...].astype(jnp.float32).T.astype(jnp.bfloat16)
-
-    def multiply(n, carry):
-        at = pl.ds(pl.multiple_of(n * chunk, chunk), chunk)
-        pltpu.make_async_copy(held.at[at], held.at[at], sems.at[n]).wait()
-        terms = jnp.dot(held[at, :], turned, preferred_element_type=jnp.float32)
-        terms = terms.astype(jnp.bfloat16)
-        for b in range(CHUNK):
-            spot = pl.multiple_of(goals[n * CHUNK + b], owned)
-            placed[pl.ds(spot, owned), :] = terms[b * owned : (b + 1) * owned]
-        return carry
-
-    lax.fori_loop(0, width // chunk, multiply, 0)
-    slab = width // groups
-
-    def turn_back(t, carry):
-        out_ref[t] = placed[pl.ds(pl.multiple_of(t * slab, slab), slab), :].T
-        return carry
-
-    lax.fori_loop(0, groups, turn_back, 0)
-
-
-def project_back(mixed, sources, spots, block_owner, groups):
+def terms_kernel(mixed_ref, *refs):
+    *sources, out_ref = refs
+    spare = out_ref.shape[1] - mixed_ref.shape[0]
+    wide = jnp.pad(mixed_ref[...].astype(jnp.float32), ((0, spare), (0, 0)))
+    turned = wide.T.astype(jnp.bfloat16)
+    begin = 0
+    for source in sources:
+
+        def multiply(n, carry, source=source, begin=begin):
+            rows = source[pl.ds(pl.multiple_of(n * CHUNK, CHUNK), CHUNK), :]
+            to = pl.ds(pl.multiple_of(begin + n * CHUNK, CHUNK), CHUNK)
+            out_ref[to, :] = jnp.dot(rows, turned, preferred_element_type=jnp.float32).astype(
+                out_ref.dtype
+            )
+            return carry
+
+        lax.fori_loop(0, source.shape[0] // CHUNK, multiply, 0)
+        begin += source.shape[0]
+
+
+def terms_of(mixed, sources):
     rows, depth = mixed.shape
     width = sum(source.shape[0] for source in sources)
+    lanes = -(-rows // 128) * 128
+    vmem = pl.BlockSpec(memory_space=pltpu.VMEM)
     return pl.pallas_call(
-        functools.partial(back_kernel, spots, groups),
-        out_shape=jax.ShapeDtypeStruct((groups, rows, width // groups), jnp.bfloat16),
-        in_specs=[
-            pl.BlockSpec(memory_space=pltpu.SMEM),
-            pl.BlockSpec(memory_space=pltpu.VMEM),
-        ]
-        + [pl.BlockSpec(memory_space=pl.ANY)] * len(sources),
-        out_specs=pl.BlockSpec(memory_space=pltpu.VMEM),
-        scratch_shapes=[
-            pltpu.VMEM((width, depth), jnp.bfloat16),
-            pltpu.VMEM((width, rows), jnp.bfloat16),
-            pltpu.SMEM((block_owner.shape[1],), jnp.int32),
-            pltpu.SemaphoreType.DMA((block_owner.shape[1] // CHUNK,)),
-        ],
-        compiler_params=pltpu.CompilerParams(vmem_limit_bytes=48 * MIB),
+        terms_kernel,
+        out_shape=jax.ShapeDtypeStruct((width, lanes), jnp.bfloat16),
+        in_specs=[vmem] * (1 + len(sources)),
+        out_specs=vmem,
+        compiler_params=pltpu.CompilerParams(vmem_limit_bytes=20 * MIB),
         cost_estimate=pl.CostEstimate(
             flops=2 * rows * depth * width,
             bytes_accessed=2 * (rows * depth + depth * width + rows * width),
             transcendentals=0,
         ),
-        name="project_back",
-    )(block_owner, mixed, *sources)
+        name="terms",
+    )(mixed, *sources)
+
+
+def place_kernel(spots, groups, owner_ref, *refs):
+    *pieces, out_ref, placed = refs
+    f = lax.axis_index("fsdp")
+    y_lo, z, core = f // 8, lax.rem(f // 2, NZ), lax.rem(f, 2)
+    width = placed.shape[0]
+    owned = width // owner_ref.shape[1]
+    for n, dy, dz, dc, t0, blocks, begin in spots:
+        first = (
+            lax.rem(y_lo + dy, 2) * 64 + lax.rem(z + dz, NZ) * 16 + lax.rem(core + dc, 2) * 8 + t0
+        )
+
+        def put(b, carry, n=n, first=first, begin=begin):
+            goal = pl.multiple_of(owner_ref[1, first + b] * owned, owned)
+            start = pl.multiple_of(begin + b * owned, owned)
+            placed[pl.ds(goal, owned), :] = pieces[n][pl.ds(start, owned), :]
+            return carry
+
+        lax.fori_loop(0, blocks, put, 0)
+    slab = width // groups
+
+    def turn_back(t, carry):
+        slab_t = placed[pl.ds(pl.multiple_of(t * slab, slab), slab), :].T
+        out_ref[t] = slab_t[: out_ref.shape[1]]
+        return carry
+
+    lax.fori_loop(0, groups, turn_back, 0)
+
+
+def place(pieces, spots, block_owner, groups, rows):
+    width = sum(piece.shape[0] for piece in pieces)
+    lanes = pieces[0].shape[1]
+    vmem = pl.BlockSpec(memory_space=pltpu.VMEM)
+    return pl.pallas_call(
+        functools.partial(place_kernel, spots, groups),
+        out_shape=jax.ShapeDtypeStruct((groups, rows, width // groups), jnp.bfloat16),
+        in_specs=[pl.BlockSpec(memory_space=pltpu.SMEM)] + [vmem] * len(pieces),
+        out_specs=vmem,
+        scratch_shapes=[pltpu.VMEM((width, lanes), jnp.bfloat16)],
+        compiler_params=pltpu.CompilerParams(vmem_limit_bytes=20 * MIB),
+        cost_estimate=pl.CostEstimate(
+            flops=0, bytes_accessed=8 * rows * width, transcendentals=0
+        ),
+        name="place",
+    )(block_owner, *pieces)
 
 
 def turns(lengths):
@@ -375,35 +390,36 @@
     w_y, w_c = flip(w, 8), flip(w, 1)
     own, parts[2] = lax.optimization_barrier((own, parts[2]))
     below, above = z_shift(own, 1), z_shift(own, -1)
-    own_c = flip(own, 1)
     begun = partials(parts, (w, w_c))
-    w_y, below, above, own, own_c, *begun = lax.optimization_barrier(
-        (w_y, below, above, own, own_c, *begun)
-    )
+    w_y, below, above, own, *begun = lax.optimization_barrier((w_y, below, above, own, *begun))
     w_yc = flip(w_y, 1)
     far_a, far_b = z_shift(above[:half], -1), z_shift(below[half:], 1)
     across = flip(own, 8)
 
     sums = partials(parts, (w_y, w_yc), begun)
     sums = [sums[0]] + [z_shift(sums[k], -k) for k in range(1, NZ)]
-    across, far_a, far_b, below, above = after((across, far_a, far_b, below, above), *sums)
+    far_a, far_b, across = after((far_a, far_b, across))
+    across_far_a, across_far_b = flip(far_a, 8), flip(far_b, 8)
+    (across,) = after((across,), *sums)
     across_below, across_above = z_shift(across, 1), z_shift(across, -1)
-    across_far_a, across_far_b = flip(far_a, 8), flip(far_b, 8)
     mixed = attention(sums, cos, sin, cache, lengths)
 
-    below_c, above_c, across_c, far_ac, far_bc = (
-        flip(value, 1) for value in after((below, above, across, far_a, far_b), mixed)
-    )
-    last = after((across_below, across_above, across_far_a, across_far_b), mixed)
-    last_c = [flip(value, 1) for value in last]
-    near = ((0, 0), (0, 3), (0, 1), (1, 0), (0, 2), (0, 2), (1, 3), (1, 1), (1, 2), (1, 2))
-    begins = (0, 0, 0, 0, 0, 4, 0, 0, 0, 4)
-    sources = [own, below, above, across, far_a, far_b, *last]
-    sources += [own_c, below_c, above_c, across_c, far_ac, far_bc, *last_c]
-    spots = tuple((*at, core, t0) for core in (0, 1) for at, t0 in zip(near, begins))
-    order = (0, 10, 1, 2, 11, 12, 3, 13, 4, 5, 14, 15, 6, 7, 8, 9, 16, 17, 18, 19)
-    sources, spots = [sources[n] for n in order], tuple(spots[n] for n in order)
-    terms = project_back(mixed, sources, spots, block_owner, groups)
+    mixed_c = flip(mixed, 1)
+    sources = (own, below, above, across, far_a, far_b)
+    sources += (across_far_a, across_far_b, across_below, across_above)
+    theirs = terms_of(mixed_c, sources)
+    mine = terms_of(*after((mixed,), theirs), sources)
+    pieces = (mine, flip(theirs, 1))
+    places = ((0, 0, 0), (0, 3, 0), (0, 1, 0), (1, 0, 0), (0, 2, 0), (0, 2, 4))
+    places += ((1, 2, 0), (1, 2, 4), (1, 3, 0), (1, 1, 0))
+    spots = []
+    for core in range(2):
+        begin = 0
+        for (dy, dz, t0), source in zip(places, sources):
+            size = source.shape[0]
+            spots.append((core, dy, dz, core, t0, size // owned, begin))
+            begin += size
+    terms = place(pieces, tuple(spots), block_owner, groups, steps * rows)
     terms = lax.all_to_all(terms, "tp", split_axis=0, concat_axis=0, tiled=True)
     summed = jnp.sum(terms.astype(jnp.float32), axis=0).astype(jnp.bfloat16)
     return summed.reshape(steps, rows, width // groups)

time: 212 us -> 202 us (0.953)
  waiting for transfers between devices: 92.5 us -> 84.2 us
  Pallas kernels: 37.3 us -> 35.1 us
    ppermute x16 -> x8, waiting for transfers between devices: 26.2 us -> 12.6 us  [flip(): return lax.ppermute(value, 'fsdp', [(f, f ^ bit) for f in range(16)])]
    ppermute x12, waiting for transfers between devices: 66.3 us -> 71.6 us  [z_shift(): return lax.ppermute(value, 'fsdp', pairs)]
    ppermute x12, starting transfers between devices: 16.8 us -> 19.8 us  [z_shift(): return lax.ppermute(value, 'fsdp', pairs)]
    ppermute x16 -> x8, starting transfers between devices: 6.27 us -> 3.9 us  [flip(): return lax.ppermute(value, 'fsdp', [(f, f ^ bit) for f in range(16)])]
    pallas_call x1 -> x3, Pallas kernels: 14.5 us -> 12.3 us  [the longest x2 9.11 us: terms_of(): pl.pallas_call(terms_kernel, out_shape=jax.ShapeDtypeStruct((width, lanes...]
  transfers between devices with their start and end apart: 29 -> 21, of which waited for: 15 -> 10; matrix products, arithmetic and copies ran while one was open for 2% -> 2% of each run, Pallas kernels for 11% -> 14%
where the time goes in v7:
time: 202 us; the launch traced here: 201 us
  waiting for transfers between devices  84.2 us (42%)
  blocking collectives  41.7 us (21%)
  Pallas kernels  35.1 us (17%)
  starting transfers between devices  31 us (15%)
  other arithmetic  5.53 us (3%)
  local copies, waits for them, and re-layouts  3.43 us (2%)
    ppermute x12, waiting for transfers between devices, z_shift(): return lax.ppermute(value, 'fsdp', pairs)  71.6 us
    all_to_all x1, blocking collectives, body(): terms = lax.all_to_all(terms, 'tp', split_axis=0, concat_axis=0, tiled=True)  41.7 us
    ppermute x12, starting transfers between devices, z_shift(): return lax.ppermute(value, 'fsdp', pairs)  19.8 us
    ppermute x8, waiting for transfers between devices, flip(): return lax.ppermute(value, 'fsdp', [(f, f ^ bit) for f in range(16)])  12.6 us
    pallas_call x1, Pallas kernels, attention(): pl.pallas_call(attention_kernel, grid=(rows // GROUP,), out_shape=jax.Sha...  10.7 us
    pallas_call x2, Pallas kernels, terms_of(): pl.pallas_call(terms_kernel, out_shape=jax.ShapeDtypeStruct((width, lanes...  9.11 us
    all_to_all x1, starting transfers between devices, body(): lax.all_to_all(copy, 'tp', split_axis=1, concat_axis=0, tiled=True)  7.28 us
    pallas_call x2, Pallas kernels, partials(): pl.pallas_call(functools.partial(partial_kernel, begun), grid=(cols // ti...  6.7 us
  transfers between devices with their start and end apart: 21, of which 10 were waited for; matrix products, arithmetic and copies ran while one was open for 2% of the time, Pallas kernels for 14%

profile of v7, /device:TPU:0, one launch (start us, length us, event | category | flops | bytes accessed | tf_op | source)
XLA Modules:
  0.0 201.2 jit_solution(17391964894390262659)
XLA Ops:
  0.0 2.0 %convert_element_type.18 = bf16[64,10240]{1,0:T(8,128)(2,1)S(1)} convert(f32[64,10240]{1,0:T(8,128)} %param.7) | non-fusion elementwise | flops 655360 | bytes 3932160 | tf_op jit(solution)/shard_map/convert_element_type | solution.py:376
  2.7 1.6 pad_maximum_fusion
  4.4 7.3 %all-to-all-start = ((bf16[64,8,2304]{2,0,1:T(8,128)(2,1)}), bf16[64,8,2304]{2,0,1:T(8,128)(2,1)}, u32[]{:S(2)}, u32[]{:S(2)}) async-start(bf16[64,8,2304]{2,0,1:T(8,128)(2,1)} %pad_maximum_fusion), calls=%async_computation | async-start | bytes 4718592 | tf_op jit(solution)/shard_map/all_to_all | solution.py:383
  11.7 5.5 %shuffle.1 = (bf16[160,2048]{1,0:T(8,128)(2,1)S(1)}, bf16[160,2048]{1,0:T(8,128)(2,1)}, bf16[160,2048]{1,0:T(8,128)(2,1)}, bf16[160,2048]{1,0:T(8,128)(2,1)}) custom-call(s32[2,128]{1,0:T(2,128)S(1)} %copy-done.1, bf16[160,8192]{1,0:T(8,128)(2,1)S(1)} %bitcast.21), custom_call_target="tpu_custom_call" | custom-call | flops 10485760 | bytes 5242880 | tf_op jit(solution)/shard_map/shuffle/pallas_call | solution.py:74
  17.2 1.9 collective-permute-start
  19.1 2.1 %collective-permute-start.1 = (bf16[160,2048]{1,0:T(8,128)(2,1)}, bf16[160,2048]{1,0:T(8,128)(2,1)S(1)}, u32[]{:S(2)}, u32[]{:S(2)}) collective-permute-start(bf16[160,2048]{1,0:T(8,128)(2,1)} %get-tuple-element.39), channel_id=1, source_target_pairs={{0,48},{8,56},{16,0},{24,8},{32,16},{40,24},{48,32},{56,40},{64,11... | collective-permute-start | bytes 1966088 | tf_op jit(solution)/shard_map/ppermute | solution.py:22
  21.2 1.9 collective-permute-start.2
  23.7 12.5 %collective-permute-done.refs_1_ = bf16[160,2048]{1,0:T(8,128)(2,1)S(1)} collective-permute-done((bf16[160,2048]{1,0:T(8,128)(2,1)}, bf16[160,2048]{1,0:T(8,128)(2,1)S(1)}, u32[]{:S(2)}, u32[]{:S(2)}) %collective-permute-start) | collective-permute-done | bytes 655392 | tf_op jit(solution)/shard_map/ppermute | solution.py:22
  36.1 13.2 %collective-permute-done.1.refs_3_ = bf16[160,2048]{1,0:T(8,128)(2,1)S(1)} collective-permute-done((bf16[160,2048]{1,0:T(8,128)(2,1)}, bf16[160,2048]{1,0:T(8,128)(2,1)S(1)}, u32[]{:S(2)}, u32[]{:S(2)}) %collective-permute-start.1) | collective-permute-done | bytes 655392 | tf_op jit(solution)/shard_map/ppermute | solution.py:22
  49.3 1.4 slice.25.refs_4_
  51.6 1.3 slice.24.refs_0_
  53.0 3.6 %collective-permute-start.5 = (bf16[512,1024]{1,0:T(8,128)(2,1)S(1)}, bf16[512,1024]{1,0:T(8,128)(2,1)S(1)}, u32[]{:S(2)}, u32[]{:S(2)}) collective-permute-start(bf16[512,1024]{1,0:T(8,128)(2,1)S(1)} %slice.24.refs_0_), channel_id=1, source_target_pairs={{0,48},{8,56},{16,0},{24,8},{32,16},{40,24},{48,32},{56,40},{64,11... | collective-permute-start | bytes 3145736 | tf_op jit(solution)/shard_map/ppermute | solution.py:22
  56.6 3.2 %partials.1 = (f32[160,1280]{1,0:T(8,128)S(1)}, f32[160,1280]{1,0:T(8,128)S(1)}, f32[160,1280]{1,0:T(8,128)S(1)}, f32[160,1280]{1,0:T(8,128)S(1)}) custom-call(bf16[160,2048]{1,0:T(8,128)(2,1)S(1)} %get-tuple-element.37.refs_0_, bf16[160,2048]{1,0:T(8,128)(2,1)S(1)} %collective-permute-done.refs_1_, bf16[160,2048]{1,0:T(8,128)(2,1)S(1)} %collective-permute-done.2.refs_2_, ...), custom_call_target="tpu_custom_call" | custom-call | flops 1677721600 | bytes 7208960 | tf_op jit(solution)/shard_map/partials/pallas_call | solution.py:121
  59.8 20.2 %collective-permute-done.4.refs_1_ = bf16[512,1024]{1,0:T(8,128)(2,1)S(1)} collective-permute-done((bf16[512,1024]{1,0:T(8,128)(2,1)S(1)}, bf16[512,1024]{1,0:T(8,128)(2,1)S(1)}, u32[]{:S(2)}, u32[]{:S(2)}) %collective-permute-start.4) | collective-permute-done | bytes 1048608 | tf_op jit(solution)/shard_map/ppermute | solution.py:22
  80.0 2.0 %collective-permute-done.3.refs_4_ = bf16[512,1280]{1,0:T(8,128)(2,1)S(1)} collective-permute-done((bf16[512,1280]{1,0:T(8,128)(2,1)S(1)}, bf16[512,1280]{1,0:T(8,128)(2,1)S(1)}, u32[]{:S(2)}, u32[]{:S(2)}) %collective-permute-start.3) | collective-permute-done | bytes 1310752 | tf_op jit(solution)/shard_map/ppermute | solution.py:26
  82.7 3.6 %collective-permute-start.12 = (bf16[256,1024]{1,0:T(8,128)(2,1)S(1)}, bf16[256,1024]{1,0:T(8,128)(2,1)S(1)}, u32[]{:S(2)}, u32[]{:S(2)}) collective-permute-start(bf16[256,1024]{1,0:T(8,128)(2,1)S(1)} %slice.26), channel_id=1, source_target_pairs={{0,48},{8,56},{16,0},{24,8},{32,16},{40,24},{48,32},{56,40},{64,11... | collective-permute-start | bytes 1572872 | tf_op jit(solution)/shard_map/ppermute | solution.py:22
  86.5 3.5 %partials_rest.1 = (f32[160,1280]{1,0:T(8,128)S(1)}, bf16[160,1280]{1,0:T(8,128)(2,1)S(1)}, bf16[160,1280]{1,0:T(8,128)(2,1)S(1)}, bf16[160,1280]{1,0:T(8,128)(2,1)S(1)}) custom-call(bf16[160,2048]{1,0:T(8,128)(2,1)S(1)} %get-tuple-element.37.refs_0_, bf16[160,2048]{1,0:T(8,128)(2,1)S(1)} %collective-permute-done.refs_1_, ...), custom_call_target="tpu_custom_call" | custom-call | flops 1677721600 | bytes 7208960 | tf_op jit(solution)/shard_map/partials_rest/pallas_call | solution.py:121
  90.0 3.3 %collective-permute-start.8 = (bf16[160,1280]{1,0:T(8,128)(2,1)S(1)}, bf16[160,1280]{1,0:T(8,128)(2,1)S(1)}, u32[]{:S(2)}, u32[]{:S(2)}) collective-permute-start(bf16[160,1280]{1,0:T(8,128)(2,1)S(1)} %get-tuple-element.56), channel_id=1, source_target_pairs={{0,48},{8,56},{16,0},{24,8},{32,16},{40,24},{48,32},{56,40},{64,11... | collective-permute-start | bytes 1228808 | tf_op jit(solution)/shard_map/ppermute | solution.py:22
  93.2 5.4 %collective-permute-done.12.refs_4_ = bf16[256,1024]{1,0:T(8,128)(2,1)S(1)} collective-permute-done((bf16[256,1024]{1,0:T(8,128)(2,1)S(1)}, bf16[256,1024]{1,0:T(8,128)(2,1)S(1)}, u32[]{:S(2)}, u32[]{:S(2)}) %collective-permute-start.12) | collective-permute-done | bytes 524320 | tf_op jit(solution)/shard_map/ppermute | solution.py:22
  98.6 12.6 %collective-permute-done.13.refs_5_ = bf16[256,1024]{1,0:T(8,128)(2,1)S(1)} collective-permute-done((bf16[256,1024]{1,0:T(8,128)(2,1)S(1)}, bf16[256,1024]{1,0:T(8,128)(2,1)S(1)}, u32[]{:S(2)}, u32[]{:S(2)}) %collective-permute-start.13) | collective-permute-done | bytes 524320 | tf_op jit(solution)/shard_map/ppermute | solution.py:22
  111.2 4.2 %collective-permute-done.8.p1 = bf16[160,1280]{1,0:T(8,128)(2,1)S(1)} collective-permute-done((bf16[160,1280]{1,0:T(8,128)(2,1)S(1)}, bf16[160,1280]{1,0:T(8,128)(2,1)S(1)}, u32[]{:S(2)}, u32[]{:S(2)}) %collective-permute-start.8) | collective-permute-done | bytes 409632 | tf_op jit(solution)/shard_map/ppermute | solution.py:22
  115.5 3.5 %collective-permute-done.10.p3 = bf16[160,1280]{1,0:T(8,128)(2,1)S(1)} collective-permute-done((bf16[160,1280]{1,0:T(8,128)(2,1)S(1)}, bf16[160,1280]{1,0:T(8,128)(2,1)S(1)}, u32[]{:S(2)}, u32[]{:S(2)}) %collective-permute-start.10) | collective-permute-done | bytes 409632 | tf_op jit(solution)/shard_map/ppermute | solution.py:22
  119.0 3.2 %collective-permute-start.18 = (bf16[512,1024]{1,0:T(8,128)(2,1)S(1)}, bf16[512,1024]{1,0:T(8,128)(2,1)S(1)}, u32[]{:S(2)}, u32[]{:S(2)}) collective-permute-start(bf16[512,1024]{1,0:T(8,128)(2,1)S(1)} %collective-permute-done.14.refs_3_), channel_id=1, source_target_pairs={{0,48},{8,56},{16,0},{24,8},{32,16},{40,24},{48,32},{56,40},{64,11... | collective-permute-start | bytes 3145736 | tf_op jit(solution)/shard_map/ppermute | solution.py:22
  122.2 1.3 collective-permute-start.15
  124.3 10.7 %attention.1.mixed_ref = bf16[160,1024]{1,0:T(8,128)(2,1)S(1)} custom-call(s32[80]{0:T(128)S(1)} %copy-done.2, f32[160,1280]{1,0:T(8,128)S(1)} %get-tuple-element.55.p0, bf16[160,1280]{1,0:T(8,128)(2,1)S(1)} %collective-permute-done.8.p1, bf16[160,1280]{1,0:T(8,128)(2,1)S(1)} %collective-permute-done.9.p2, bf16[160,1280]{1,0:T(8,128)(2,1)S(1)} %collective-permute-done.10.p3, ...), custom_call_target="tpu_custom_call" | custom-call | flops 167772160 | bytes 41943040 | tf_op jit(solution)/shard_map/attention/pallas_call | solution.py:340
  135.2 1.9 collective-permute-done.15.refs_6_
  137.1 8.7 %collective-permute-done.16.refs_7_ = bf16[256,1024]{1,0:T(8,128)(2,1)S(1)} collective-permute-done((bf16[256,1024]{1,0:T(8,128)(2,1)S(1)}, bf16[256,1024]{1,0:T(8,128)(2,1)S(1)}, u32[]{:S(2)}, u32[]{:S(2)}) %collective-permute-start.16) | collective-permute-done | bytes 524320 | tf_op jit(solution)/shard_map/ppermute | solution.py:26
  145.8 4.6 %terms.2 = bf16[4096,256]{1,0:T(8,128)(2,1)S(1)} custom-call(bf16[160,1024]{1,0:T(8,128)(2,1)S(1)} %collective-permute-done.11.mixed_ref, bf16[512,1024]{1,0:T(8,128)(2,1)S(1)} %slice.24.refs_0_, bf16[512,1024]{1,0:T(8,128)(2,1)S(1)} %collective-permute-done.4.refs_1_, bf16[512,1024]{1,0:T(8,128)(2,1)S(1)} %collective-permute-done.5.refs_2_, ...), custom_call_target="tpu_custom_call" | custom-call | flops 1342177280 | bytes 10027008 | tf_op jit(solution)/shard_map/terms/pallas_call | solution.py:165
  150.5 4.6 %terms.3.refs_0_ = bf16[4096,256]{1,0:T(8,128)(2,1)S(1)} custom-call(bf16[160,1024]{1,0:T(8,128)(2,1)S(1)} %attention.1.mixed_ref, bf16[512,1024]{1,0:T(8,128)(2,1)S(1)} %slice.24.refs_0_, bf16[512,1024]{1,0:T(8,128)(2,1)S(1)} %collective-permute-done.4.refs_1_, bf16[512,1024]{1,0:T(8,128)(2,1)S(1)} %collective-permute-done.5.refs_2_, ...), custom_call_target="tpu_custom_call" | custom-call | flops 1342177280 | bytes 10027008 | tf_op jit(solution)/shard_map/terms/pallas_call | solution.py:165
  155.1 3.2 %place.1 = bf16[8,160,1024]{2,1,0:T(8,128)(2,1)S(1)} custom-call(s32[2,128]{1,0:T(2,128)S(1)} %copy-done.1, bf16[4096,256]{1,0:T(8,128)(2,1)S(1)} %terms.3.refs_0_, bf16[4096,256]{1,0:T(8,128)(2,1)S(1)} %collective-permute-done.19.refs_1_), custom_call_target="tpu_custom_call" | custom-call | bytes 10485760 | tf_op jit(solution)/shard_map/place/pallas_call | solution.py:212
  158.2 41.7 %all_to_all.20 = bf16[8,160,1024]{2,1,0:T(8,128)(2,1)S(1)} all-to-all(bf16[8,160,1024]{2,1,0:T(8,128)(2,1)S(1)} %place.1), channel_id=1, replica_groups=mesh['fsdp'=16,'tp'=8] {'tp'}, dimensions={0} | all-to-all | bytes 5242880 | tf_op jit(solution)/shard_map/all_to_all | solution.py:423
  199.9 1.3 reduce_sum.12
  (43 shorter events, 4.1 us)
Async XLA Ops:
  0.0 2.4 %copy-start.3 = (f32[64,8192]{1,0:T(8,128)S(1)}, f32[64,8192]{1,0:T(8,128)}, u32[]{:S(2)}) copy-start(f32[64,8192]{1,0:T(8,128)} %param.8) | copy-start | bytes 6291460
  4.4 7.3 %copy-start = (bf16[2,80,8192]{2,1,0:T(8,128)(2,1)S(1)}, bf16[2,80,8192]{2,1,0:T(8,128)(2,1)}, u32[]{:S(2)}) copy-start(bf16[2,80,8192]{2,1,0:T(8,128)(2,1)} %param.6) | copy-start | bytes 7864324
  4.4 7.3 %copy-start.1 = (s32[2,128]{1,0:T(2,128)S(1)}, s32[2,128]{1,0:T(2,128)}, u32[]{:S(2)}) copy-start(s32[2,128]{1,0:T(2,128)} %owner_ref.3) | copy-start | bytes 3076
  4.4 44.9 %all-to-all-start = ((bf16[64,8,2304]{2,0,1:T(8,128)(2,1)}), bf16[64,8,2304]{2,0,1:T(8,128)(2,1)}, u32[]{:S(2)}, u32[]{:S(2)}) async-start(bf16[64,8,2304]{2,0,1:T(8,128)(2,1)} %pad_maximum_fusion), calls=%async_computation | async-start | bytes 4718592 | tf_op jit(solution)/shard_map/all_to_all | solution.py:383
  11.7 11.4 %copy-start.2 = (s32[80]{0:T(128)S(1)}, s32[80]{0:T(128)}, u32[]{:S(2)}) copy-start(s32[80]{0:T(128)} %lengths_ref.1) | copy-start | bytes 964
  17.2 19.0 %collective-permute-start = (bf16[160,2048]{1,0:T(8,128)(2,1)}, bf16[160,2048]{1,0:T(8,128)(2,1)S(1)}, u32[]{:S(2)}, u32[]{:S(2)}) collective-permute-start(bf16[160,2048]{1,0:T(8,128)(2,1)} %get-tuple-element.38), channel_id=1, source_target_pairs={{0,16},{8,24},{16,32},{24,40},{32,48},{40,56},{48,0},{56,8},{64,80... | collective-permute-start | bytes 1966088 | tf_op jit(solution)/shard_map/ppermute | solution.py:22
  19.1 30.2 %collective-permute-start.1 = (bf16[160,2048]{1,0:T(8,128)(2,1)}, bf16[160,2048]{1,0:T(8,128)(2,1)S(1)}, u32[]{:S(2)}, u32[]{:S(2)}) collective-permute-start(bf16[160,2048]{1,0:T(8,128)(2,1)} %get-tuple-element.39), channel_id=1, source_target_pairs={{0,48},{8,56},{16,0},{24,8},{32,16},{40,24},{48,32},{56,40},{64,11... | collective-permute-start | bytes 1966088 | tf_op jit(solution)/shard_map/ppermute | solution.py:22
  21.2 31.7 %collective-permute-start.2 = (bf16[160,2048]{1,0:T(8,128)(2,1)}, bf16[160,2048]{1,0:T(8,128)(2,1)S(1)}, u32[]{:S(2)}, u32[]{:S(2)}) collective-permute-start(bf16[160,2048]{1,0:T(8,128)(2,1)} %get-tuple-element.42), channel_id=1, source_target_pairs={{0,32},{8,40},{16,48},{24,56},{32,0},{40,8},{48,16},{56,24},{64,96... | collective-permute-start | bytes 1966088 | tf_op jit(solution)/shard_map/ppermute | solution.py:22
  50.7 5.9 %collective-permute-start.6 = (bf16[512,1280]{1,0:T(8,128)(2,1)S(1)}, bf16[512,1280]{1,0:T(8,128)(2,1)S(1)}, u32[]{:S(2)}, u32[]{:S(2)}) collective-permute-start(bf16[512,1280]{1,0:T(8,128)(2,1)S(1)} %slice.25.refs_4_), channel_id=1, source_target_pairs={{0,8},{8,0},{16,24},{24,16},{32,40},{40,32},{48,56},{56,48},{64,72... | collective-permute-start | bytes 3932168 | tf_op jit(solution)/shard_map/ppermute | solution.py:26
  50.8 31.2 %collective-permute-start.3 = (bf16[512,1280]{1,0:T(8,128)(2,1)S(1)}, bf16[512,1280]{1,0:T(8,128)(2,1)S(1)}, u32[]{:S(2)}, u32[]{:S(2)}) collective-permute-start(bf16[512,1280]{1,0:T(8,128)(2,1)S(1)} %slice.25.refs_4_), channel_id=1, source_target_pairs={{0,64},{8,72},{16,80},{24,88},{32,96},{40,104},{48,112},{56,120},{... | collective-permute-start | bytes 3932168 | tf_op jit(solution)/shard_map/ppermute | solution.py:26
  52.9 27.1 %collective-permute-start.4 = (bf16[512,1024]{1,0:T(8,128)(2,1)S(1)}, bf16[512,1024]{1,0:T(8,128)(2,1)S(1)}, u32[]{:S(2)}, u32[]{:S(2)}) collective-permute-start(bf16[512,1024]{1,0:T(8,128)(2,1)S(1)} %slice.24.refs_0_), channel_id=1, source_target_pairs={{0,16},{8,24},{16,32},{24,40},{32,48},{40,56},{48,0},{56,8},{64,80... | collective-permute-start | bytes 3145736 | tf_op jit(solution)/shard_map/ppermute | solution.py:22
  53.0 27.0 %collective-permute-start.5 = (bf16[512,1024]{1,0:T(8,128)(2,1)S(1)}, bf16[512,1024]{1,0:T(8,128)(2,1)S(1)}, u32[]{:S(2)}, u32[]{:S(2)}) collective-permute-start(bf16[512,1024]{1,0:T(8,128)(2,1)S(1)} %slice.24.refs_0_), channel_id=1, source_target_pairs={{0,48},{8,56},{16,0},{24,8},{32,16},{40,24},{48,32},{56,40},{64,11... | collective-permute-start | bytes 3145736 | tf_op jit(solution)/shard_map/ppermute | solution.py:22
  82.0 4.5 %collective-permute-start.7 = (bf16[512,1280]{1,0:T(8,128)(2,1)S(1)}, bf16[512,1280]{1,0:T(8,128)(2,1)S(1)}, u32[]{:S(2)}, u32[]{:S(2)}) collective-permute-start(bf16[512,1280]{1,0:T(8,128)(2,1)S(1)} %collective-permute-done.3.refs_4_), channel_id=1, source_target_pairs={{0,8},{8,0},{16,24},{24,16},{32,40},{40,32},{48,56},{56,48},{64,72... | collective-permute-start | bytes 3932168 | tf_op jit(solution)/shard_map/ppermute | solution.py:26
  82.0 29.2 %collective-permute-start.14 = (bf16[512,1024]{1,0:T(8,128)(2,1)S(1)}, bf16[512,1024]{1,0:T(8,128)(2,1)S(1)}, u32[]{:S(2)}, u32[]{:S(2)}) collective-permute-start(bf16[512,1024]{1,0:T(8,128)(2,1)S(1)} %slice.24.refs_0_), channel_id=1, source_target_pairs={{0,64},{8,72},{16,80},{24,88},{32,96},{40,104},{48,112},{56,120},{... | collective-permute-start | bytes 3145736 | tf_op jit(solution)/shard_map/ppermute | solution.py:26
  82.7 15.9 %collective-permute-start.12 = (bf16[256,1024]{1,0:T(8,128)(2,1)S(1)}, bf16[256,1024]{1,0:T(8,128)(2,1)S(1)}, u32[]{:S(2)}, u32[]{:S(2)}) collective-permute-start(bf16[256,1024]{1,0:T(8,128)(2,1)S(1)} %slice.26), channel_id=1, source_target_pairs={{0,48},{8,56},{16,0},{24,8},{32,16},{40,24},{48,32},{56,40},{64,11... | collective-permute-start | bytes 1572872 | tf_op jit(solution)/shard_map/ppermute | solution.py:22
  86.4 24.9 %collective-permute-start.13 = (bf16[256,1024]{1,0:T(8,128)(2,1)S(1)}, bf16[256,1024]{1,0:T(8,128)(2,1)S(1)}, u32[]{:S(2)}, u32[]{:S(2)}) collective-permute-start(bf16[256,1024]{1,0:T(8,128)(2,1)S(1)} %slice.27), channel_id=1, source_target_pairs={{0,16},{8,24},{16,32},{24,40},{32,48},{40,56},{48,0},{56,8},{64,80... | collective-permute-start | bytes 1572872 | tf_op jit(solution)/shard_map/ppermute | solution.py:22
  90.0 25.5 %collective-permute-start.8 = (bf16[160,1280]{1,0:T(8,128)(2,1)S(1)}, bf16[160,1280]{1,0:T(8,128)(2,1)S(1)}, u32[]{:S(2)}, u32[]{:S(2)}) collective-permute-start(bf16[160,1280]{1,0:T(8,128)(2,1)S(1)} %get-tuple-element.56), channel_id=1, source_target_pairs={{0,48},{8,56},{16,0},{24,8},{32,16},{40,24},{48,32},{56,40},{64,11... | collective-permute-start | bytes 1228808 | tf_op jit(solution)/shard_map/ppermute | solution.py:22
  93.2 22.3 %collective-permute-start.9 = (bf16[160,1280]{1,0:T(8,128)(2,1)S(1)}, bf16[160,1280]{1,0:T(8,128)(2,1)S(1)}, u32[]{:S(2)}, u32[]{:S(2)}) collective-permute-start(bf16[160,1280]{1,0:T(8,128)(2,1)S(1)} %get-tuple-element.57), channel_id=1, source_target_pairs={{0,32},{8,40},{16,48},{24,56},{32,0},{40,8},{48,16},{56,24},{64,96... | collective-permute-start | bytes 1228808 | tf_op jit(solution)/shard_map/ppermute | solution.py:22
  98.6 20.4 %collective-permute-start.10 = (bf16[160,1280]{1,0:T(8,128)(2,1)S(1)}, bf16[160,1280]{1,0:T(8,128)(2,1)S(1)}, u32[]{:S(2)}, u32[]{:S(2)}) collective-permute-start(bf16[160,1280]{1,0:T(8,128)(2,1)S(1)} %get-tuple-element.58), channel_id=1, source_target_pairs={{0,16},{8,24},{16,32},{24,40},{32,48},{40,56},{48,0},{56,8},{64,80... | collective-permute-start | bytes 1228808 | tf_op jit(solution)/shard_map/ppermute | solution.py:22
  119.0 26.8 %collective-permute-start.17 = (bf16[512,1024]{1,0:T(8,128)(2,1)S(1)}, bf16[512,1024]{1,0:T(8,128)(2,1)S(1)}, u32[]{:S(2)}, u32[]{:S(2)}) collective-permute-start(bf16[512,1024]{1,0:T(8,128)(2,1)S(1)} %collective-permute-done.14.refs_3_), channel_id=1, source_target_pairs={{0,16},{8,24},{16,32},{24,40},{32,48},{40,56},{48,0},{56,8},{64,80... | collective-permute-start | bytes 3145736 | tf_op jit(solution)/shard_map/ppermute | solution.py:22
  119.0 26.8 %collective-permute-start.18 = (bf16[512,1024]{1,0:T(8,128)(2,1)S(1)}, bf16[512,1024]{1,0:T(8,128)(2,1)S(1)}, u32[]{:S(2)}, u32[]{:S(2)}) collective-permute-start(bf16[512,1024]{1,0:T(8,128)(2,1)S(1)} %collective-permute-done.14.refs_3_), channel_id=1, source_target_pairs={{0,48},{8,56},{16,0},{24,8},{32,16},{40,24},{48,32},{56,40},{64,11... | collective-permute-start | bytes 3145736 | tf_op jit(solution)/shard_map/ppermute | solution.py:22
  122.2 14.9 %collective-permute-start.15 = (bf16[256,1024]{1,0:T(8,128)(2,1)S(1)}, bf16[256,1024]{1,0:T(8,128)(2,1)S(1)}, u32[]{:S(2)}, u32[]{:S(2)}) collective-permute-start(bf16[256,1024]{1,0:T(8,128)(2,1)S(1)} %collective-permute-done.12.refs_4_), channel_id=1, source_target_pairs={{0,64},{8,72},{16,80},{24,88},{32,96},{40,104},{48,112},{56,120},{... | collective-permute-start | bytes 1572872 | tf_op jit(solution)/shard_map/ppermute | solution.py:26
  123.6 22.2 %collective-permute-start.16 = (bf16[256,1024]{1,0:T(8,128)(2,1)S(1)}, bf16[256,1024]{1,0:T(8,128)(2,1)S(1)}, u32[]{:S(2)}, u32[]{:S(2)}) collective-permute-start(bf16[256,1024]{1,0:T(8,128)(2,1)S(1)} %collective-permute-done.13.refs_5_), channel_id=1, source_target_pairs={{0,64},{8,72},{16,80},{24,88},{32,96},{40,104},{48,112},{56,120},{... | collective-permute-start | bytes 1572872 | tf_op jit(solution)/shard_map/ppermute | solution.py:26
  135.0 10.9 %collective-permute-start.11 = (bf16[160,1024]{1,0:T(8,128)(2,1)S(1)}, bf16[160,1024]{1,0:T(8,128)(2,1)S(1)}, u32[]{:S(2)}, u32[]{:S(2)}) collective-permute-start(bf16[160,1024]{1,0:T(8,128)(2,1)S(1)} %attention.1.mixed_ref), channel_id=1, source_target_pairs={{0,8},{8,0},{16,24},{24,16},{32,40},{40,32},{48,56},{56,48},{64,72... | collective-permute-start | bytes 983048 | tf_op jit(solution)/shard_map/ppermute | solution.py:26
  150.4 4.7 %collective-permute-start.19 = (bf16[4096,256]{1,0:T(8,128)(2,1)S(1)}, bf16[4096,256]{1,0:T(8,128)(2,1)S(1)}, u32[]{:S(2)}, u32[]{:S(2)}) collective-permute-start(bf16[4096,256]{1,0:T(8,128)(2,1)S(1)} %terms.2), channel_id=1, source_target_pairs={{0,8},{8,0},{16,24},{24,16},{32,40},{40,32},{48,56},{56,48},{64,72... | collective-permute-start | bytes 6291464 | tf_op jit(solution)/shard_map/ppermute | solution.py:26

commit v8 on v7

--- a/solution.py
+++ b/solution.py
@@ -12,6 +12,7 @@
 HK = 8
 HD = 128
 NZ = 4
+NX = 4
 GROUP = 8
 CHUNK = 256
 MIB = 1024 * 1024
@@ -24,6 +25,14 @@
 
 def flip(value, bit):
     return lax.ppermute(value, "fsdp", [(f, f ^ bit) for f in range(16)])
+
+
+def x_shift(value, k):
+    return lax.ppermute(value, "tp", [(t, (t // 2 + k) % NX * 2 + t % 2) for t in range(2 * NX)])
+
+
+def y_flip(value):
+    return lax.ppermute(value, "tp", [(t, t ^ 1) for t in range(2 * NX)])
 
 
 def by_group(array, sections, groups):
@@ -178,7 +187,8 @@
 
 
 def place_kernel(spots, groups, owner_ref, *refs):
-    *pieces, out_ref, placed = refs
+    pieces, firsts, seconds = refs[:-7], refs[-7:-3], refs[-3:-1]
+    placed = refs[-1]
     f = lax.axis_index("fsdp")
     y_lo, z, core = f // 8, lax.rem(f // 2, NZ), lax.rem(f, 2)
     width = placed.shape[0]
@@ -196,13 +206,14 @@
 
         lax.fori_loop(0, blocks, put, 0)
     slab = width // groups
-
-    def turn_back(t, carry):
-        slab_t = placed[pl.ds(pl.multiple_of(t * slab, slab), slab), :].T
-        out_ref[t] = slab_t[: out_ref.shape[1]]
-        return carry
-
-    lax.fori_loop(0, groups, turn_back, 0)
+    t = lax.axis_index("tp")
+    for k in range(NX):
+        for j in range(2):
+            at = lax.rem(t // 2 + k, NX) * 2 + lax.rem(lax.rem(t, 2) + j, 2)
+            turned = placed[pl.ds(pl.multiple_of(at * slab, slab), slab), :].T
+            rows = firsts[k].shape[1]
+            firsts[k][j] = turned[:rows]
+            seconds[j][k] = turned[rows : 2 * rows]
 
 
 def place(pieces, spots, block_owner, groups, rows):
@@ -211,9 +222,10 @@
     vmem = pl.BlockSpec(memory_space=pltpu.VMEM)
     return pl.pallas_call(
         functools.partial(place_kernel, spots, groups),
-        out_shape=jax.ShapeDtypeStruct((groups, rows, width // groups), jnp.bfloat16),
+        out_shape=[jax.ShapeDtypeStruct((2, rows, width // groups), jnp.bfloat16)] * NX
+        + [jax.ShapeDtypeStruct((NX, rows, width // groups), jnp.bfloat16)] * 2,
         in_specs=[pl.BlockSpec(memory_space=pltpu.SMEM)] + [vmem] * len(pieces),
-        out_specs=vmem,
+        out_specs=[vmem] * (NX + 2),
         scratch_shapes=[pltpu.VMEM((width, lanes), jnp.bfloat16)],
         compiler_params=pltpu.CompilerParams(vmem_limit_bytes=20 * MIB),
         cost_estimate=pl.CostEstimate(
@@ -419,10 +431,16 @@
             size = source.shape[0]
             spots.append((core, dy, dz, core, t0, size // owned, begin))
             begin += size
-    terms = place(pieces, tuple(spots), block_owner, groups, steps * rows)
-    terms = lax.all_to_all(terms, "tp", split_axis=0, concat_axis=0, tiled=True)
-    summed = jnp.sum(terms.astype(jnp.float32), axis=0).astype(jnp.bfloat16)
-    return summed.reshape(steps, rows, width // groups)
+    slabs = place(pieces, tuple(spots), block_owner, groups, rows)
+
+    first = [slabs[0]] + [x_shift(slabs[k], k) for k in range(1, NX)]
+    second = [slabs[NX], y_flip(slabs[NX + 1])]
+    first = sum(value.astype(jnp.float32) for value in first)
+    second = sum(value.astype(jnp.float32) for value in second)
+    first = first[0] + y_flip(first[1].astype(jnp.bfloat16)).astype(jnp.float32)
+    second = [second[0]] + [x_shift(second[k].astype(jnp.bfloat16), k) for k in range(1, NX)]
+    second = sum(value.astype(jnp.float32) for value in second)
+    return jnp.stack([first, second]).astype(jnp.bfloat16)
 
 
 def solution(mesh):

time: 202 us -> 197 us (0.975)
  blocking collectives: 41.7 us -> 0 us
  waiting for transfers between devices: 84.2 us -> 106 us
  starting transfers between devices: 31 us -> 45.2 us
    all_to_all x1 -> x0, blocking collectives: 41.7 us -> none  [body(): terms = lax.all_to_all(terms, 'tp', split_axis=0, concat_axis=0, tiled=True)]
    ppermute x0 -> x8, waiting for transfers between devices: none -> 21.7 us  [the longest x6 20 us: x_shift(): lax.ppermute(value, 'tp', [(t, (t // 2 + k) % NX * 2 + t % 2) for t in ra...]
    ppermute x0 -> x8, starting transfers between devices: none -> 14.3 us  [the longest x2 7.21 us: y_flip(): return lax.ppermute(value, 'tp', [(t, t ^ 1) for t in range(2 * NX)])]
  transfers between devices with their start and end apart: 21 -> 29, of which waited for: 10 -> 16; matrix products, arithmetic and copies ran while one was open for 2% -> 2% of each run, Pallas kernels for 14% -> 14%
where the time goes in v8:
time: 197 us; the launch traced here: 195 us
  waiting for transfers between devices  106 us (54%)
  starting transfers between devices  45.2 us (23%)
  Pallas kernels  35 us (18%)
  other arithmetic  5.6 us (3%)
  local copies, waits for them, and re-layouts  3.48 us (2%)
    ppermute x12, waiting for transfers between devices, z_shift(): return lax.ppermute(value, 'fsdp', pairs)  71.6 us
    ppermute x6, waiting for transfers between devices, x_shift(): lax.ppermute(value, 'tp', [(t, (t // 2 + k) % NX * 2 + t % 2) for t in ra...  20 us
    ppermute x12, starting transfers between devices, z_shift(): return lax.ppermute(value, 'fsdp', pairs)  19.8 us
    ppermute x8, waiting for transfers between devices, flip(): return lax.ppermute(value, 'fsdp', [(f, f ^ bit) for f in range(16)])  12.6 us
    pallas_call x1, Pallas kernels, attention(): pl.pallas_call(attention_kernel, grid=(rows // GROUP,), out_shape=jax.Sha...  10.7 us
    pallas_call x2, Pallas kernels, terms_of(): pl.pallas_call(terms_kernel, out_shape=jax.ShapeDtypeStruct((width, lanes...  9.17 us
    all_to_all x1, starting transfers between devices, body(): lax.all_to_all(copy, 'tp', split_axis=1, concat_axis=0, tiled=True)  7.28 us
    ppermute x2, starting transfers between devices, y_flip(): return lax.ppermute(value, 'tp', [(t, t ^ 1) for t in range(2 * NX)])  7.21 us
  transfers between devices with their start and end apart: 29, of which 16 were waited for; matrix products, arithmetic and copies ran while one was open for 2% of the time, Pallas kernels for 14%

profile of v8, /device:TPU:0, one launch (start us, length us, event | category | flops | bytes accessed | tf_op | source)
XLA Modules:
  0.0 195.5 jit_solution(15246663978496265516)
XLA Ops:
  0.0 2.0 %convert_element_type.63 = bf16[64,10240]{1,0:T(8,128)(2,1)S(1)} convert(f32[64,10240]{1,0:T(8,128)} %param.7) | non-fusion elementwise | flops 655360 | bytes 3932160 | tf_op jit(solution)/shard_map/convert_element_type | solution.py:388
  4.4 7.3 %all-to-all-start = ((bf16[64,8,2304]{2,0,1:T(8,128)(2,1)}), bf16[64,8,2304]{2,0,1:T(8,128)(2,1)}, u32[]{:S(2)}, u32[]{:S(2)}) async-start(bf16[64,8,2304]{2,0,1:T(8,128)(2,1)} %pad_maximum_fusion), calls=%async_computation | async-start | bytes 4718592 | tf_op jit(solution)/shard_map/all_to_all | solution.py:395
  11.7 5.5 %shuffle.1 = (bf16[160,2048]{1,0:T(8,128)(2,1)S(1)}, bf16[160,2048]{1,0:T(8,128)(2,1)}, bf16[160,2048]{1,0:T(8,128)(2,1)}, bf16[160,2048]{1,0:T(8,128)(2,1)}) custom-call(s32[2,128]{1,0:T(2,128)S(1)} %copy-done.1, bf16[160,8192]{1,0:T(8,128)(2,1)S(1)} %bitcast.52), custom_call_target="tpu_custom_call" | custom-call | flops 10485760 | bytes 5242880 | tf_op jit(solution)/shard_map/shuffle/pallas_call | solution.py:83
  17.2 1.9 collective-permute-start
  19.1 2.1 %collective-permute-start.1 = (bf16[160,2048]{1,0:T(8,128)(2,1)}, bf16[160,2048]{1,0:T(8,128)(2,1)S(1)}, u32[]{:S(2)}, u32[]{:S(2)}) collective-permute-start(bf16[160,2048]{1,0:T(8,128)(2,1)} %get-tuple-element.45), channel_id=1, source_target_pairs={{0,48},{8,56},{16,0},{24,8},{32,16},{40,24},{48,32},{56,40},{64,11... | collective-permute-start | bytes 1966088 | tf_op jit(solution)/shard_map/ppermute | solution.py:23
  23.7 12.5 %collective-permute-done.refs_1_ = bf16[160,2048]{1,0:T(8,128)(2,1)S(1)} collective-permute-done((bf16[160,2048]{1,0:T(8,128)(2,1)}, bf16[160,2048]{1,0:T(8,128)(2,1)S(1)}, u32[]{:S(2)}, u32[]{:S(2)}) %collective-permute-start) | collective-permute-done | bytes 655392 | tf_op jit(solution)/shard_map/ppermute | solution.py:23
  36.1 13.2 %collective-permute-done.1.refs_3_ = bf16[160,2048]{1,0:T(8,128)(2,1)S(1)} collective-permute-done((bf16[160,2048]{1,0:T(8,128)(2,1)}, bf16[160,2048]{1,0:T(8,128)(2,1)S(1)}, u32[]{:S(2)}, u32[]{:S(2)}) %collective-permute-start.1) | collective-permute-done | bytes 655392 | tf_op jit(solution)/shard_map/ppermute | solution.py:23
  53.0 3.6 %collective-permute-start.5 = (bf16[512,1024]{1,0:T(8,128)(2,1)S(1)}, bf16[512,1024]{1,0:T(8,128)(2,1)S(1)}, u32[]{:S(2)}, u32[]{:S(2)}) collective-permute-start(bf16[512,1024]{1,0:T(8,128)(2,1)S(1)} %slice.46.refs_0_), channel_id=1, source_target_pairs={{0,48},{8,56},{16,0},{24,8},{32,16},{40,24},{48,32},{56,40},{64,11... | collective-permute-start | bytes 3145736 | tf_op jit(solution)/shard_map/ppermute | solution.py:23
  56.6 3.2 %partials.1 = (f32[160,1280]{1,0:T(8,128)S(1)}, f32[160,1280]{1,0:T(8,128)S(1)}, f32[160,1280]{1,0:T(8,128)S(1)}, f32[160,1280]{1,0:T(8,128)S(1)}) custom-call(bf16[160,2048]{1,0:T(8,128)(2,1)S(1)} %get-tuple-element.43.refs_0_, bf16[160,2048]{1,0:T(8,128)(2,1)S(1)} %collective-permute-done.refs_1_, bf16[160,2048]{1,0:T(8,128)(2,1)S(1)} %collective-permute-done.2.refs_2_, ...), custom_call_target="tpu_custom_call" | custom-call | flops 1677721600 | bytes 7208960 | tf_op jit(solution)/shard_map/partials/pallas_call | solution.py:130
  59.8 20.2 %collective-permute-done.4.refs_1_ = bf16[512,1024]{1,0:T(8,128)(2,1)S(1)} collective-permute-done((bf16[512,1024]{1,0:T(8,128)(2,1)S(1)}, bf16[512,1024]{1,0:T(8,128)(2,1)S(1)}, u32[]{:S(2)}, u32[]{:S(2)}) %collective-permute-start.4) | collective-permute-done | bytes 1048608 | tf_op jit(solution)/shard_map/ppermute | solution.py:23
  80.0 2.0 %collective-permute-done.3.refs_4_ = bf16[512,1280]{1,0:T(8,128)(2,1)S(1)} collective-permute-done((bf16[512,1280]{1,0:T(8,128)(2,1)S(1)}, bf16[512,1280]{1,0:T(8,128)(2,1)S(1)}, u32[]{:S(2)}, u32[]{:S(2)}) %collective-permute-start.3) | collective-permute-done | bytes 1310752 | tf_op jit(solution)/shard_map/ppermute | solution.py:27
  82.7 3.6 %collective-permute-start.12 = (bf16[256,1024]{1,0:T(8,128)(2,1)S(1)}, bf16[256,1024]{1,0:T(8,128)(2,1)S(1)}, u32[]{:S(2)}, u32[]{:S(2)}) collective-permute-start(bf16[256,1024]{1,0:T(8,128)(2,1)S(1)} %slice.48), channel_id=1, source_target_pairs={{0,48},{8,56},{16,0},{24,8},{32,16},{40,24},{48,32},{56,40},{64,11... | collective-permute-start | bytes 1572872 | tf_op jit(solution)/shard_map/ppermute | solution.py:23
  86.5 3.5 %partials_rest.1 = (f32[160,1280]{1,0:T(8,128)S(1)}, bf16[160,1280]{1,0:T(8,128)(2,1)S(1)}, bf16[160,1280]{1,0:T(8,128)(2,1)S(1)}, bf16[160,1280]{1,0:T(8,128)(2,1)S(1)}) custom-call(bf16[160,2048]{1,0:T(8,128)(2,1)S(1)} %get-tuple-element.43.refs_0_, bf16[160,2048]{1,0:T(8,128)(2,1)S(1)} %collective-permute-done.refs_1_, ...), custom_call_target="tpu_custom_call" | custom-call | flops 1677721600 | bytes 7208960 | tf_op jit(solution)/shard_map/partials_rest/pallas_call | solution.py:130
  90.0 3.3 %collective-permute-start.8 = (bf16[160,1280]{1,0:T(8,128)(2,1)S(1)}, bf16[160,1280]{1,0:T(8,128)(2,1)S(1)}, u32[]{:S(2)}, u32[]{:S(2)}) collective-permute-start(bf16[160,1280]{1,0:T(8,128)(2,1)S(1)} %get-tuple-element.62), channel_id=1, source_target_pairs={{0,48},{8,56},{16,0},{24,8},{32,16},{40,24},{48,32},{56,40},{64,11... | collective-permute-start | bytes 1228808 | tf_op jit(solution)/shard_map/ppermute | solution.py:23
  93.2 5.4 %collective-permute-done.12.refs_4_ = bf16[256,1024]{1,0:T(8,128)(2,1)S(1)} collective-permute-done((bf16[256,1024]{1,0:T(8,128)(2,1)S(1)}, bf16[256,1024]{1,0:T(8,128)(2,1)S(1)}, u32[]{:S(2)}, u32[]{:S(2)}) %collective-permute-start.12) | collective-permute-done | bytes 524320 | tf_op jit(solution)/shard_map/ppermute | solution.py:23
  98.6 12.6 %collective-permute-done.13.refs_5_ = bf16[256,1024]{1,0:T(8,128)(2,1)S(1)} collective-permute-done((bf16[256,1024]{1,0:T(8,128)(2,1)S(1)}, bf16[256,1024]{1,0:T(8,128)(2,1)S(1)}, u32[]{:S(2)}, u32[]{:S(2)}) %collective-permute-start.13) | collective-permute-done | bytes 524320 | tf_op jit(solution)/shard_map/ppermute | solution.py:23
  111.2 4.2 %collective-permute-done.8.p1 = bf16[160,1280]{1,0:T(8,128)(2,1)S(1)} collective-permute-done((bf16[160,1280]{1,0:T(8,128)(2,1)S(1)}, bf16[160,1280]{1,0:T(8,128)(2,1)S(1)}, u32[]{:S(2)}, u32[]{:S(2)}) %collective-permute-start.8) | collective-permute-done | bytes 409632 | tf_op jit(solution)/shard_map/ppermute | solution.py:23
  115.5 3.5 %collective-permute-done.10.p3 = bf16[160,1280]{1,0:T(8,128)(2,1)S(1)} collective-permute-done((bf16[160,1280]{1,0:T(8,128)(2,1)S(1)}, bf16[160,1280]{1,0:T(8,128)(2,1)S(1)}, u32[]{:S(2)}, u32[]{:S(2)}) %collective-permute-start.10) | collective-permute-done | bytes 409632 | tf_op jit(solution)/shard_map/ppermute | solution.py:23
  119.0 3.2 %collective-permute-start.18 = (bf16[512,1024]{1,0:T(8,128)(2,1)S(1)}, bf16[512,1024]{1,0:T(8,128)(2,1)S(1)}, u32[]{:S(2)}, u32[]{:S(2)}) collective-permute-start(bf16[512,1024]{1,0:T(8,128)(2,1)S(1)} %collective-permute-done.14.refs_3_), channel_id=1, source_target_pairs={{0,48},{8,56},{16,0},{24,8},{32,16},{40,24},{48,32},{56,40},{64,11... | collective-permute-start | bytes 3145736 | tf_op jit(solution)/shard_map/ppermute | solution.py:23
  124.3 10.7 %attention.1.mixed_ref = bf16[160,1024]{1,0:T(8,128)(2,1)S(1)} custom-call(s32[80]{0:T(128)S(1)} %copy-done.2, f32[160,1280]{1,0:T(8,128)S(1)} %get-tuple-element.61.p0, bf16[160,1280]{1,0:T(8,128)(2,1)S(1)} %collective-permute-done.8.p1, bf16[160,1280]{1,0:T(8,128)(2,1)S(1)} %collective-permute-done.9.p2, bf16[160,1280]{1,0:T(8,128)(2,1)S(1)} %collective-permute-done.10.p3, ...), custom_call_target="tpu_custom_call" | custom-call | flops 167772160 | bytes 41943040 | tf_op jit(solution)/shard_map/attention/pallas_call | solution.py:352
  137.1 8.7 %collective-permute-done.16.refs_7_ = bf16[256,1024]{1,0:T(8,128)(2,1)S(1)} collective-permute-done((bf16[256,1024]{1,0:T(8,128)(2,1)S(1)}, bf16[256,1024]{1,0:T(8,128)(2,1)S(1)}, u32[]{:S(2)}, u32[]{:S(2)}) %collective-permute-start.16) | collective-permute-done | bytes 524320 | tf_op jit(solution)/shard_map/ppermute | solution.py:27
  145.8 4.6 %terms.2 = bf16[4096,256]{1,0:T(8,128)(2,1)S(1)} custom-call(bf16[160,1024]{1,0:T(8,128)(2,1)S(1)} %collective-permute-done.11.mixed_ref, bf16[512,1024]{1,0:T(8,128)(2,1)S(1)} %slice.46.refs_0_, bf16[512,1024]{1,0:T(8,128)(2,1)S(1)} %collective-permute-done.4.refs_1_, bf16[512,1024]{1,0:T(8,128)(2,1)S(1)} %collective-permute-done.5.refs_2_, ...), custom_call_target="tpu_custom_call" | custom-call | flops 1342177280 | bytes 10027008 | tf_op jit(solution)/shard_map/terms/pallas_call | solution.py:174
  150.5 4.6 %terms.3.refs_0_ = bf16[4096,256]{1,0:T(8,128)(2,1)S(1)} custom-call(bf16[160,1024]{1,0:T(8,128)(2,1)S(1)} %attention.1.mixed_ref, bf16[512,1024]{1,0:T(8,128)(2,1)S(1)} %slice.46.refs_0_, bf16[512,1024]{1,0:T(8,128)(2,1)S(1)} %collective-permute-done.4.refs_1_, bf16[512,1024]{1,0:T(8,128)(2,1)S(1)} %collective-permute-done.5.refs_2_, ...), custom_call_target="tpu_custom_call" | custom-call | flops 1342177280 | bytes 10027008 | tf_op jit(solution)/shard_map/terms/pallas_call | solution.py:174
  155.1 2.9 %place.1 = (bf16[2,80,1024]{2,1,0:T(8,128)(2,1)S(1)}, bf16[2,80,1024]{2,1,0:T(8,128)(2,1)S(1)}, bf16[2,80,1024]{2,1,0:T(8,128)(2,1)S(1)}, bf16[2,80,1024]{2,1,0:...) custom-call(s32[2,128]{1,0:T(2,128)S(1)} %copy-done.1, ...), custom_call_target="tpu_custom_call" | custom-call | bytes 5242880 | tf_op jit(solution)/shard_map/place/pallas_call | solution.py:223
  158.0 3.0 %collective-permute-start.22 = (bf16[2,80,1024]{2,1,0:T(8,128)(2,1)S(1)}, bf16[2,80,1024]{2,1,0:T(8,128)(2,1)S(1)}, u32[]{:S(2)}, u32[]{:S(2)}) collective-permute-start(bf16[2,80,1024]{2,1,0:T(8,128)(2,1)S(1)} %get-tuple-element.78), channel_id=1, source_target_pairs={{0,6},{1,7},{2,0},{3,1},{4,2},{5,3},{6,4},{7,5},{8,14},{9,15},{10,... | collective-permute-start | bytes 983048 | tf_op jit(solution)/shard_map/ppermute | solution.py:31
  162.8 3.6 %collective-permute-start.24 = (bf16[4,80,1024]{2,1,0:T(8,128)(2,1)S(1)}, bf16[4,80,1024]{2,1,0:T(8,128)(2,1)S(1)}, u32[]{:S(2)}, u32[]{:S(2)}) collective-permute-start(bf16[4,80,1024]{2,1,0:T(8,128)(2,1)S(1)} %get-tuple-element.80), channel_id=1, source_target_pairs={{0,1},{1,0},{2,3},{3,2},{4,5},{5,4},{6,7},{7,6},{8,9},{9,8},{10,11... | collective-permute-start | bytes 1966088 | tf_op jit(solution)/shard_map/ppermute | solution.py:35
  166.3 9.4 %collective-permute-done.22 = bf16[2,80,1024]{2,1,0:T(8,128)(2,1)S(1)} collective-permute-done((bf16[2,80,1024]{2,1,0:T(8,128)(2,1)S(1)}, bf16[2,80,1024]{2,1,0:T(8,128)(2,1)S(1)}, u32[]{:S(2)}, u32[]{:S(2)}) %collective-permute-start.22) | collective-permute-done | bytes 327712 | tf_op jit(solution)/shard_map/ppermute | solution.py:31
  175.7 3.7 %collective-permute-done.20 = bf16[2,80,1024]{2,1,0:T(8,128)(2,1)S(1)} collective-permute-done((bf16[2,80,1024]{2,1,0:T(8,128)(2,1)S(1)}, bf16[2,80,1024]{2,1,0:T(8,128)(2,1)S(1)}, u32[]{:S(2)}, u32[]{:S(2)}) %collective-permute-start.20) | collective-permute-done | bytes 327712 | tf_op jit(solution)/shard_map/ppermute | solution.py:31
  179.7 3.6 %collective-permute-start.23 = (bf16[80,1024]{1,0:T(8,128)(2,1)S(1)}, bf16[80,1024]{1,0:T(8,128)(2,1)S(1)}, u32[]{:S(2)}, u32[]{:S(2)}) collective-permute-start(bf16[80,1024]{1,0:T(8,128)(2,1)S(1)} %fusion.7), channel_id=1, source_target_pairs={{0,1},{1,0},{2,3},{3,2},{4,5},{5,4},{6,7},{7,6},{8,9},{9,8},{10,11... | collective-permute-start | bytes 491528 | tf_op jit(solution)/shard_map/ppermute | solution.py:35
  187.7 3.1 %collective-permute-done.27 = bf16[80,1024]{1,0:T(8,128)(2,1)S(1)} collective-permute-done((bf16[80,1024]{1,0:T(8,128)(2,1)S(1)}, bf16[80,1024]{1,0:T(8,128)(2,1)S(1)}, u32[]{:S(2)}, u32[]{:S(2)}) %collective-permute-start.27) | collective-permute-done | bytes 163872 | tf_op jit(solution)/shard_map/ppermute | solution.py:31
  190.8 1.9 collective-permute-done.26
  192.7 2.0 %collective-permute-done.25 = bf16[80,1024]{1,0:T(8,128)(2,1)S(1)} collective-permute-done((bf16[80,1024]{1,0:T(8,128)(2,1)S(1)}, bf16[80,1024]{1,0:T(8,128)(2,1)S(1)}, u32[]{:S(2)}, u32[]{:S(2)}) %collective-permute-start.25) | collective-permute-done | bytes 163872 | tf_op jit(solution)/shard_map/ppermute | solution.py:31
  (64 shorter events, 20.6 us)
Async XLA Ops:
  4.4 7.3 %copy-start = (bf16[2,80,8192]{2,1,0:T(8,128)(2,1)S(1)}, bf16[2,80,8192]{2,1,0:T(8,128)(2,1)}, u32[]{:S(2)}) copy-start(bf16[2,80,8192]{2,1,0:T(8,128)(2,1)} %param.6) | copy-start | bytes 7864324
  4.4 7.3 %copy-start.1 = (s32[2,128]{1,0:T(2,128)S(1)}, s32[2,128]{1,0:T(2,128)}, u32[]{:S(2)}) copy-start(s32[2,128]{1,0:T(2,128)} %owner_ref.3) | copy-start | bytes 3076
  4.4 44.9 %all-to-all-start = ((bf16[64,8,2304]{2,0,1:T(8,128)(2,1)}), bf16[64,8,2304]{2,0,1:T(8,128)(2,1)}, u32[]{:S(2)}, u32[]{:S(2)}) async-start(bf16[64,8,2304]{2,0,1:T(8,128)(2,1)} %pad_maximum_fusion), calls=%async_computation | async-start | bytes 4718592 | tf_op jit(solution)/shard_map/all_to_all | solution.py:395
  11.7 11.4 %copy-start.2 = (s32[80]{0:T(128)S(1)}, s32[80]{0:T(128)}, u32[]{:S(2)}) copy-start(s32[80]{0:T(128)} %lengths_ref.1) | copy-start | bytes 964
  17.2 19.0 %collective-permute-start = (bf16[160,2048]{1,0:T(8,128)(2,1)}, bf16[160,2048]{1,0:T(8,128)(2,1)S(1)}, u32[]{:S(2)}, u32[]{:S(2)}) collective-permute-start(bf16[160,2048]{1,0:T(8,128)(2,1)} %get-tuple-element.44), channel_id=1, source_target_pairs={{0,16},{8,24},{16,32},{24,40},{32,48},{40,56},{48,0},{56,8},{64,80... | collective-permute-start | bytes 1966088 | tf_op jit(solution)/shard_map/ppermute | solution.py:23
  19.1 30.2 %collective-permute-start.1 = (bf16[160,2048]{1,0:T(8,128)(2,1)}, bf16[160,2048]{1,0:T(8,128)(2,1)S(1)}, u32[]{:S(2)}, u32[]{:S(2)}) collective-permute-start(bf16[160,2048]{1,0:T(8,128)(2,1)} %get-tuple-element.45), channel_id=1, source_target_pairs={{0,48},{8,56},{16,0},{24,8},{32,16},{40,24},{48,32},{56,40},{64,11... | collective-permute-start | bytes 1966088 | tf_op jit(solution)/shard_map/ppermute | solution.py:23
  21.2 31.7 %collective-permute-start.2 = (bf16[160,2048]{1,0:T(8,128)(2,1)}, bf16[160,2048]{1,0:T(8,128)(2,1)S(1)}, u32[]{:S(2)}, u32[]{:S(2)}) collective-permute-start(bf16[160,2048]{1,0:T(8,128)(2,1)} %get-tuple-element.48), channel_id=1, source_target_pairs={{0,32},{8,40},{16,48},{24,56},{32,0},{40,8},{48,16},{56,24},{64,96... | collective-permute-start | bytes 1966088 | tf_op jit(solution)/shard_map/ppermute | solution.py:23
  50.7 5.9 %collective-permute-start.6 = (bf16[512,1280]{1,0:T(8,128)(2,1)S(1)}, bf16[512,1280]{1,0:T(8,128)(2,1)S(1)}, u32[]{:S(2)}, u32[]{:S(2)}) collective-permute-start(bf16[512,1280]{1,0:T(8,128)(2,1)S(1)} %slice.47.refs_4_), channel_id=1, source_target_pairs={{0,8},{8,0},{16,24},{24,16},{32,40},{40,32},{48,56},{56,48},{64,72... | collective-permute-start | bytes 3932168 | tf_op jit(solution)/shard_map/ppermute | solution.py:27
  50.8 31.2 %collective-permute-start.3 = (bf16[512,1280]{1,0:T(8,128)(2,1)S(1)}, bf16[512,1280]{1,0:T(8,128)(2,1)S(1)}, u32[]{:S(2)}, u32[]{:S(2)}) collective-permute-start(bf16[512,1280]{1,0:T(8,128)(2,1)S(1)} %slice.47.refs_4_), channel_id=1, source_target_pairs={{0,64},{8,72},{16,80},{24,88},{32,96},{40,104},{48,112},{56,120},{... | collective-permute-start | bytes 3932168 | tf_op jit(solution)/shard_map/ppermute | solution.py:27
  52.9 27.1 %collective-permute-start.4 = (bf16[512,1024]{1,0:T(8,128)(2,1)S(1)}, bf16[512,1024]{1,0:T(8,128)(2,1)S(1)}, u32[]{:S(2)}, u32[]{:S(2)}) collective-permute-start(bf16[512,1024]{1,0:T(8,128)(2,1)S(1)} %slice.46.refs_0_), channel_id=1, source_target_pairs={{0,16},{8,24},{16,32},{24,40},{32,48},{40,56},{48,0},{56,8},{64,80... | collective-permute-start | bytes 3145736 | tf_op jit(solution)/shard_map/ppermute | solution.py:23
  53.0 27.0 %collective-permute-start.5 = (bf16[512,1024]{1,0:T(8,128)(2,1)S(1)}, bf16[512,1024]{1,0:T(8,128)(2,1)S(1)}, u32[]{:S(2)}, u32[]{:S(2)}) collective-permute-start(bf16[512,1024]{1,0:T(8,128)(2,1)S(1)} %slice.46.refs_0_), channel_id=1, source_target_pairs={{0,48},{8,56},{16,0},{24,8},{32,16},{40,24},{48,32},{56,40},{64,11... | collective-permute-start | bytes 3145736 | tf_op jit(solution)/shard_map/ppermute | solution.py:23
  82.0 4.5 %collective-permute-start.7 = (bf16[512,1280]{1,0:T(8,128)(2,1)S(1)}, bf16[512,1280]{1,0:T(8,128)(2,1)S(1)}, u32[]{:S(2)}, u32[]{:S(2)}) collective-permute-start(bf16[512,1280]{1,0:T(8,128)(2,1)S(1)} %collective-permute-done.3.refs_4_), channel_id=1, source_target_pairs={{0,8},{8,0},{16,24},{24,16},{32,40},{40,32},{48,56},{56,48},{64,72... | collective-permute-start | bytes 3932168 | tf_op jit(solution)/shard_map/ppermute | solution.py:27
  82.0 29.2 %collective-permute-start.14 = (bf16[512,1024]{1,0:T(8,128)(2,1)S(1)}, bf16[512,1024]{1,0:T(8,128)(2,1)S(1)}, u32[]{:S(2)}, u32[]{:S(2)}) collective-permute-start(bf16[512,1024]{1,0:T(8,128)(2,1)S(1)} %slice.46.refs_0_), channel_id=1, source_target_pairs={{0,64},{8,72},{16,80},{24,88},{32,96},{40,104},{48,112},{56,120},{... | collective-permute-start | bytes 3145736 | tf_op jit(solution)/shard_map/ppermute | solution.py:27
  82.7 15.9 %collective-permute-start.12 = (bf16[256,1024]{1,0:T(8,128)(2,1)S(1)}, bf16[256,1024]{1,0:T(8,128)(2,1)S(1)}, u32[]{:S(2)}, u32[]{:S(2)}) collective-permute-start(bf16[256,1024]{1,0:T(8,128)(2,1)S(1)} %slice.48), channel_id=1, source_target_pairs={{0,48},{8,56},{16,0},{24,8},{32,16},{40,24},{48,32},{56,40},{64,11... | collective-permute-start | bytes 1572872 | tf_op jit(solution)/shard_map/ppermute | solution.py:23
  86.4 24.9 %collective-permute-start.13 = (bf16[256,1024]{1,0:T(8,128)(2,1)S(1)}, bf16[256,1024]{1,0:T(8,128)(2,1)S(1)}, u32[]{:S(2)}, u32[]{:S(2)}) collective-permute-start(bf16[256,1024]{1,0:T(8,128)(2,1)S(1)} %slice.49), channel_id=1, source_target_pairs={{0,16},{8,24},{16,32},{24,40},{32,48},{40,56},{48,0},{56,8},{64,80... | collective-permute-start | bytes 1572872 | tf_op jit(solution)/shard_map/ppermute | solution.py:23
  90.0 25.5 %collective-permute-start.8 = (bf16[160,1280]{1,0:T(8,128)(2,1)S(1)}, bf16[160,1280]{1,0:T(8,128)(2,1)S(1)}, u32[]{:S(2)}, u32[]{:S(2)}) collective-permute-start(bf16[160,1280]{1,0:T(8,128)(2,1)S(1)} %get-tuple-element.62), channel_id=1, source_target_pairs={{0,48},{8,56},{16,0},{24,8},{32,16},{40,24},{48,32},{56,40},{64,11... | collective-permute-start | bytes 1228808 | tf_op jit(solution)/shard_map/ppermute | solution.py:23
  93.2 22.3 %collective-permute-start.9 = (bf16[160,1280]{1,0:T(8,128)(2,1)S(1)}, bf16[160,1280]{1,0:T(8,128)(2,1)S(1)}, u32[]{:S(2)}, u32[]{:S(2)}) collective-permute-start(bf16[160,1280]{1,0:T(8,128)(2,1)S(1)} %get-tuple-element.63), channel_id=1, source_target_pairs={{0,32},{8,40},{16,48},{24,56},{32,0},{40,8},{48,16},{56,24},{64,96... | collective-permute-start | bytes 1228808 | tf_op jit(solution)/shard_map/ppermute | solution.py:23
  98.6 20.4 %collective-permute-start.10 = (bf16[160,1280]{1,0:T(8,128)(2,1)S(1)}, bf16[160,1280]{1,0:T(8,128)(2,1)S(1)}, u32[]{:S(2)}, u32[]{:S(2)}) collective-permute-start(bf16[160,1280]{1,0:T(8,128)(2,1)S(1)} %get-tuple-element.64), channel_id=1, source_target_pairs={{0,16},{8,24},{16,32},{24,40},{32,48},{40,56},{48,0},{56,8},{64,80... | collective-permute-start | bytes 1228808 | tf_op jit(solution)/shard_map/ppermute | solution.py:23
  119.0 26.8 %collective-permute-start.17 = (bf16[512,1024]{1,0:T(8,128)(2,1)S(1)}, bf16[512,1024]{1,0:T(8,128)(2,1)S(1)}, u32[]{:S(2)}, u32[]{:S(2)}) collective-permute-start(bf16[512,1024]{1,0:T(8,128)(2,1)S(1)} %collective-permute-done.14.refs_3_), channel_id=1, source_target_pairs={{0,16},{8,24},{16,32},{24,40},{32,48},{40,56},{48,0},{56,8},{64,80... | collective-permute-start | bytes 3145736 | tf_op jit(solution)/shard_map/ppermute | solution.py:23
  119.0 26.8 %collective-permute-start.18 = (bf16[512,1024]{1,0:T(8,128)(2,1)S(1)}, bf16[512,1024]{1,0:T(8,128)(2,1)S(1)}, u32[]{:S(2)}, u32[]{:S(2)}) collective-permute-start(bf16[512,1024]{1,0:T(8,128)(2,1)S(1)} %collective-permute-done.14.refs_3_), channel_id=1, source_target_pairs={{0,48},{8,56},{16,0},{24,8},{32,16},{40,24},{48,32},{56,40},{64,11... | collective-permute-start | bytes 3145736 | tf_op jit(solution)/shard_map/ppermute | solution.py:23
  122.2 14.9 %collective-permute-start.15 = (bf16[256,1024]{1,0:T(8,128)(2,1)S(1)}, bf16[256,1024]{1,0:T(8,128)(2,1)S(1)}, u32[]{:S(2)}, u32[]{:S(2)}) collective-permute-start(bf16[256,1024]{1,0:T(8,128)(2,1)S(1)} %collective-permute-done.12.refs_4_), channel_id=1, source_target_pairs={{0,64},{8,72},{16,80},{24,88},{32,96},{40,104},{48,112},{56,120},{... | collective-permute-start | bytes 1572872 | tf_op jit(solution)/shard_map/ppermute | solution.py:27
  123.6 22.2 %collective-permute-start.16 = (bf16[256,1024]{1,0:T(8,128)(2,1)S(1)}, bf16[256,1024]{1,0:T(8,128)(2,1)S(1)}, u32[]{:S(2)}, u32[]{:S(2)}) collective-permute-start(bf16[256,1024]{1,0:T(8,128)(2,1)S(1)} %collective-permute-done.13.refs_5_), channel_id=1, source_target_pairs={{0,64},{8,72},{16,80},{24,88},{32,96},{40,104},{48,112},{56,120},{... | collective-permute-start | bytes 1572872 | tf_op jit(solution)/shard_map/ppermute | solution.py:27
  135.0 10.9 %collective-permute-start.11 = (bf16[160,1024]{1,0:T(8,128)(2,1)S(1)}, bf16[160,1024]{1,0:T(8,128)(2,1)S(1)}, u32[]{:S(2)}, u32[]{:S(2)}) collective-permute-start(bf16[160,1024]{1,0:T(8,128)(2,1)S(1)} %attention.1.mixed_ref), channel_id=1, source_target_pairs={{0,8},{8,0},{16,24},{24,16},{32,40},{40,32},{48,56},{56,48},{64,72... | collective-permute-start | bytes 983048 | tf_op jit(solution)/shard_map/ppermute | solution.py:27
  150.4 4.7 %collective-permute-start.19 = (bf16[4096,256]{1,0:T(8,128)(2,1)S(1)}, bf16[4096,256]{1,0:T(8,128)(2,1)S(1)}, u32[]{:S(2)}, u32[]{:S(2)}) collective-permute-start(bf16[4096,256]{1,0:T(8,128)(2,1)S(1)} %terms.2), channel_id=1, source_target_pairs={{0,8},{8,0},{16,24},{24,16},{32,40},{40,32},{48,56},{56,48},{64,72... | collective-permute-start | bytes 6291464 | tf_op jit(solution)/shard_map/ppermute | solution.py:27
  158.0 17.7 %collective-permute-start.22 = (bf16[2,80,1024]{2,1,0:T(8,128)(2,1)S(1)}, bf16[2,80,1024]{2,1,0:T(8,128)(2,1)S(1)}, u32[]{:S(2)}, u32[]{:S(2)}) collective-permute-start(bf16[2,80,1024]{2,1,0:T(8,128)(2,1)S(1)} %get-tuple-element.78), channel_id=1, source_target_pairs={{0,6},{1,7},{2,0},{3,1},{4,2},{5,3},{6,4},{7,5},{8,14},{9,15},{10,... | collective-permute-start | bytes 983048 | tf_op jit(solution)/shard_map/ppermute | solution.py:31
  161.1 14.7 %collective-permute-start.21 = (bf16[2,80,1024]{2,1,0:T(8,128)(2,1)S(1)}, bf16[2,80,1024]{2,1,0:T(8,128)(2,1)S(1)}, u32[]{:S(2)}, u32[]{:S(2)}) collective-permute-start(bf16[2,80,1024]{2,1,0:T(8,128)(2,1)S(1)} %get-tuple-element.77), channel_id=1, source_target_pairs={{0,4},{1,5},{2,6},{3,7},{4,0},{5,1},{6,2},{7,3},{8,12},{9,13},{10,... | collective-permute-start | bytes 983048 | tf_op jit(solution)/shard_map/ppermute | solution.py:31
  161.9 17.5 %collective-permute-start.20 = (bf16[2,80,1024]{2,1,0:T(8,128)(2,1)S(1)}, bf16[2,80,1024]{2,1,0:T(8,128)(2,1)S(1)}, u32[]{:S(2)}, u32[]{:S(2)}) collective-permute-start(bf16[2,80,1024]{2,1,0:T(8,128)(2,1)S(1)} %get-tuple-element.76), channel_id=1, source_target_pairs={{0,2},{1,3},{2,4},{3,5},{4,6},{5,7},{6,0},{7,1},{8,10},{9,11},{10,... | collective-permute-start | bytes 983048 | tf_op jit(solution)/shard_map/ppermute | solution.py:31
  162.8 20.5 %collective-permute-start.24 = (bf16[4,80,1024]{2,1,0:T(8,128)(2,1)S(1)}, bf16[4,80,1024]{2,1,0:T(8,128)(2,1)S(1)}, u32[]{:S(2)}, u32[]{:S(2)}) collective-permute-start(bf16[4,80,1024]{2,1,0:T(8,128)(2,1)S(1)} %get-tuple-element.80), channel_id=1, source_target_pairs={{0,1},{1,0},{2,3},{3,2},{4,5},{5,4},{6,7},{7,6},{8,9},{9,8},{10,11... | collective-permute-start | bytes 1966088 | tf_op jit(solution)/shard_map/ppermute | solution.py:35
  179.7 8.0 %collective-permute-start.23 = (bf16[80,1024]{1,0:T(8,128)(2,1)S(1)}, bf16[80,1024]{1,0:T(8,128)(2,1)S(1)}, u32[]{:S(2)}, u32[]{:S(2)}) collective-permute-start(bf16[80,1024]{1,0:T(8,128)(2,1)S(1)} %fusion.7), channel_id=1, source_target_pairs={{0,1},{1,0},{2,3},{3,2},{4,5},{5,4},{6,7},{7,6},{8,9},{9,8},{10,11... | collective-permute-start | bytes 491528 | tf_op jit(solution)/shard_map/ppermute | solution.py:35
  183.6 7.2 %collective-permute-start.27 = (bf16[80,1024]{1,0:T(8,128)(2,1)S(1)}, bf16[80,1024]{1,0:T(8,128)(2,1)S(1)}, u32[]{:S(2)}, u32[]{:S(2)}) collective-permute-start(bf16[80,1024]{1,0:T(8,128)(2,1)S(1)} %get-tuple-element.86), channel_id=1, source_target_pairs={{0,6},{1,7},{2,0},{3,1},{4,2},{5,3},{6,4},{7,5},{8,14},{9,15},{10,... | collective-permute-start | bytes 491528 | tf_op jit(solution)/shard_map/ppermute | solution.py:31
  184.3 8.4 %collective-permute-start.26 = (bf16[80,1024]{1,0:T(8,128)(2,1)S(1)}, bf16[80,1024]{1,0:T(8,128)(2,1)S(1)}, u32[]{:S(2)}, u32[]{:S(2)}) collective-permute-start(bf16[80,1024]{1,0:T(8,128)(2,1)S(1)} %get-tuple-element.87), channel_id=1, source_target_pairs={{0,4},{1,5},{2,6},{3,7},{4,0},{5,1},{6,2},{7,3},{8,12},{9,13},{10,... | collective-permute-start | bytes 491528 | tf_op jit(solution)/shard_map/ppermute | solution.py:31
  185.1 9.5 %collective-permute-start.25 = (bf16[80,1024]{1,0:T(8,128)(2,1)S(1)}, bf16[80,1024]{1,0:T(8,128)(2,1)S(1)}, u32[]{:S(2)}, u32[]{:S(2)}) collective-permute-start(bf16[80,1024]{1,0:T(8,128)(2,1)S(1)} %get-tuple-element.85), channel_id=1, source_target_pairs={{0,2},{1,3},{2,4},{3,5},{4,6},{5,7},{6,0},{7,1},{8,10},{9,11},{10,... | collective-permute-start | bytes 491528 | tf_op jit(solution)/shard_map/ppermute | solution.py:31
  (1 other events, 2.4 us)

commit v9 on v8

--- a/solution.py
+++ b/solution.py
@@ -384,23 +384,21 @@
     owned = qkv_rows.shape[0]
     query_cols = HQ * HD
     kv_cols = HK * HD
-    cols = (query_cols + 2 * kv_cols) // groups
-    copy = jnp.concatenate([qkv_rows.astype(jnp.bfloat16), o_rows.astype(jnp.bfloat16)], axis=1)
-    copy = by_group(copy, (query_cols, kv_cols, kv_cols, query_cols), groups)
+    qkv_copy = by_group(qkv_rows.astype(jnp.bfloat16), (query_cols, kv_cols, kv_cols), groups)
+    out_copy = o_rows.astype(jnp.bfloat16).reshape(owned, groups, query_cols // groups)
 
     cos, sin = turns(lengths)
     parts = shuffle(hidden.reshape(steps * rows, width), block_owner)
     parts = [parts[0]] + [z_shift(parts[k], k) for k in range(1, NZ)]
 
-    both = flatten(lax.all_to_all(copy, "tp", split_axis=1, concat_axis=0, tiled=True))
-    both, cos, sin, parts[1], parts[3] = lax.optimization_barrier(
-        (both, cos, sin, parts[1], parts[3])
-    )
-    w, own = both[:, :cols], both[:, cols:]
+    w = flatten(lax.all_to_all(qkv_copy, "tp", split_axis=1, concat_axis=0, tiled=True))
+    w_y, w_c = flip(w, 8), flip(w, 1)
+    out_copy, parts[1], parts[3], cos, sin = after(
+        (out_copy, parts[1], parts[3], cos, sin), w
+    )
+    own = flatten(lax.all_to_all(out_copy, "tp", split_axis=1, concat_axis=0, tiled=True))
     half = own.shape[0] // 2
-
-    w_y, w_c = flip(w, 8), flip(w, 1)
-    own, parts[2] = lax.optimization_barrier((own, parts[2]))
+    own, parts[2], w_c = lax.optimization_barrier((own, parts[2], w_c))
     below, above = z_shift(own, 1), z_shift(own, -1)
     begun = partials(parts, (w, w_c))
     w_y, below, above, own, *begun = lax.optimization_barrier((w_y, below, above, own, *begun))

time: 197 us -> 200 us (1.015)
  waiting for transfers between devices: 106 us -> 94.3 us
  starting transfers between devices: 45.2 us -> 51.7 us
  local copies, waits for them, and re-layouts: 3.48 us -> 9.44 us
    ppermute x12, waiting for transfers between devices: 71.6 us -> 40.9 us  [z_shift(): return lax.ppermute(value, 'fsdp', pairs)]
    all_to_all x1 -> x2, waiting for transfers between devices: 0.01 us -> 10.5 us  [the longest x1 10.5 us: body(): lax.all_to_all(qkv_copy, 'tp', split_axis=1, concat_axis=0, tiled=True)]
    ppermute x8, waiting for transfers between devices: 12.6 us -> 21.2 us  [flip(): return lax.ppermute(value, 'fsdp', [(f, f ^ bit) for f in range(16)])]
    all_to_all x1 -> x2, starting transfers between devices: 7.28 us -> 14.2 us  [the longest x1 7.28 us: body(): lax.all_to_all(qkv_copy, 'tp', split_axis=1, concat_axis=0, tiled=True)]
    unnamed x9 -> x20, local copies, waits for them, and re-layouts: 0.28 us -> 5.77 us
    optimization_barrier x0 -> x1, local copies, waits for them, and re-layouts: none -> 3.25 us  [after(): return lax.optimization_barrier((*values, *first))[:len(values)]]
    slice x2 -> x0, local copies, waits for them, and re-layouts: 2.69 us -> none  [body(): w, own = (both[:, :cols], both[:, cols:])]
  transfers between devices with their start and end apart: 29 -> 30, of which waited for: 16 -> 17; matrix products, arithmetic and copies ran while one was open for 2% -> 4% of each run, Pallas kernels for 14% -> 15%
where the time goes in v9:
time: 200 us; the launch traced here: 199 us
  waiting for transfers between devices  94.3 us (47%)
  starting transfers between devices  51.7 us (26%)
  Pallas kernels  36.5 us (18%)
  local copies, waits for them, and re-layouts  9.44 us (5%)
  other arithmetic  6.58 us (3%)
    ppermute x12, waiting for transfers between devices, z_shift(): return lax.ppermute(value, 'fsdp', pairs)  40.9 us
    ppermute x8, waiting for transfers between devices, flip(): return lax.ppermute(value, 'fsdp', [(f, f ^ bit) for f in range(16)])  21.2 us
    ppermute x6, waiting for transfers between devices, x_shift(): lax.ppermute(value, 'tp', [(t, (t // 2 + k) % NX * 2 + t % 2) for t in ra...  20 us
    ppermute x12, starting transfers between devices, z_shift(): return lax.ppermute(value, 'fsdp', pairs)  20 us
    pallas_call x1, Pallas kernels, attention(): pl.pallas_call(attention_kernel, grid=(rows // GROUP,), out_shape=jax.Sha...  10.7 us
    all_to_all x1, waiting for transfers between devices, body(): lax.all_to_all(qkv_copy, 'tp', split_axis=1, concat_axis=0, tiled=True)  10.5 us
    pallas_call x2, Pallas kernels, terms_of(): pl.pallas_call(terms_kernel, out_shape=jax.ShapeDtypeStruct((width, lanes...  9.15 us
    pallas_call x2, Pallas kernels, partials(): pl.pallas_call(functools.partial(partial_kernel, begun), grid=(cols // ti...  8.36 us
  transfers between devices with their start and end apart: 30, of which 17 were waited for; matrix products, arithmetic and copies ran while one was open for 4% of the time, Pallas kernels for 15%

profile of v9, /device:TPU:0, one launch (start us, length us, event | category | flops | bytes accessed | tf_op | source)
XLA Modules:
  0.0 198.8 jit_solution(1645944557545433650)
XLA Ops:
  3.3 7.3 %all-to-all-start = ((bf16[64,8,1280]{2,0,1:T(8,128)(2,1)}), bf16[64,8,1280]{2,0,1:T(8,128)(2,1)}, u32[]{:S(2)}, u32[]{:S(2)}) async-start(bf16[64,8,1280]{2,0,1:T(8,128)(2,1)} %pad_maximum_fusion), calls=%async_computation | async-start | bytes 2621440 | tf_op jit(solution)/shard_map/all_to_all | solution.py:394
  10.6 5.4 %shuffle.1 = (bf16[160,2048]{1,0:T(8,128)(2,1)S(1)}, bf16[160,2048]{1,0:T(8,128)(2,1)}, bf16[160,2048]{1,0:T(8,128)(2,1)}, bf16[160,2048]{1,0:T(8,128)(2,1)}) custom-call(s32[2,128]{1,0:T(2,128)S(1)} %copy-done.7, bf16[160,8192]{1,0:T(8,128)(2,1)S(1)} %bitcast.62), custom_call_target="tpu_custom_call" | custom-call | flops 10485760 | bytes 5242880 | tf_op jit(solution)/shard_map/shuffle/pallas_call | solution.py:83
  17.9 2.1 %collective-permute-start.1 = (bf16[160,2048]{1,0:T(8,128)(2,1)}, bf16[160,2048]{1,0:T(8,128)(2,1)S(1)}, u32[]{:S(2)}, u32[]{:S(2)}) collective-permute-start(bf16[160,2048]{1,0:T(8,128)(2,1)} %get-tuple-element.46), channel_id=1, source_target_pairs={{0,48},{8,56},{16,0},{24,8},{32,16},{40,24},{48,32},{56,40},{64,11... | collective-permute-start | bytes 1966088 | tf_op jit(solution)/shard_map/ppermute | solution.py:23
  20.1 10.5 %all-to-all-done = bf16[64,8,1280]{2,0,1:T(8,128)(2,1)} async-done(((bf16[64,8,1280]{2,0,1:T(8,128)(2,1)}), bf16[64,8,1280]{2,0,1:T(8,128)(2,1)}, u32[]{:S(2)}, u32[]{:S(2)}) %all-to-all-start) | async-done | bytes 1310752 | tf_op jit(solution)/shard_map/all_to_all | solution.py:394
  34.7 3.3 %copy.10 = bf16[64,8,1024]{2,0,1:T(8,128)(2,1)} copy(bf16[64,8,1024]{2,1,0:T(8,128)(2,1)} %bitcast.64) | data formatting | bytes 2097152 | tf_op jit(solution)/shard_map/optimization_barrier | solution.py:378
  38.0 6.9 %all-to-all-start.1 = ((bf16[64,8,1024]{2,0,1:T(8,128)(2,1)}), bf16[64,8,1024]{2,0,1:T(8,128)(2,1)S(1)}, u32[]{:S(2)}, u32[]{:S(2)}) async-start(bf16[64,8,1024]{2,0,1:T(8,128)(2,1)} %copy.10), calls=%async_computation.1 | async-start | bytes 2097152 | tf_op jit(solution)/shard_map/all_to_all | solution.py:399
  44.9 2.7 %collective-permute-start.2 = (bf16[160,2048]{1,0:T(8,128)(2,1)}, bf16[160,2048]{1,0:T(8,128)(2,1)S(1)}, u32[]{:S(2)}, u32[]{:S(2)}) collective-permute-start(bf16[160,2048]{1,0:T(8,128)(2,1)} %get-tuple-element.49), channel_id=1, source_target_pairs={{0,32},{8,40},{16,48},{24,56},{32,0},{40,8},{48,16},{56,24},{64,96... | collective-permute-start | bytes 1966088 | tf_op jit(solution)/shard_map/ppermute | solution.py:23
  48.3 13.4 %collective-permute-done.2.refs_2_ = bf16[160,2048]{1,0:T(8,128)(2,1)S(1)} collective-permute-done((bf16[160,2048]{1,0:T(8,128)(2,1)}, bf16[160,2048]{1,0:T(8,128)(2,1)S(1)}, u32[]{:S(2)}, u32[]{:S(2)}) %collective-permute-start.2) | collective-permute-done | bytes 655392 | tf_op jit(solution)/shard_map/ppermute | solution.py:23
  63.1 2.7 %collective-permute-start.6 = (bf16[512,1024]{1,0:T(8,128)(2,1)S(1)}, bf16[512,1024]{1,0:T(8,128)(2,1)S(1)}, u32[]{:S(2)}, u32[]{:S(2)}) collective-permute-start(bf16[512,1024]{1,0:T(8,128)(2,1)S(1)} %bitcast.58), channel_id=1, source_target_pairs={{0,48},{8,56},{16,0},{24,8},{32,16},{40,24},{48,32},{56,40},{64,11... | collective-permute-start | bytes 3145736 | tf_op jit(solution)/shard_map/ppermute | solution.py:23
  69.0 4.9 %partials.1 = (f32[160,1280]{1,0:T(8,128)S(1)}, f32[160,1280]{1,0:T(8,128)S(1)}, f32[160,1280]{1,0:T(8,128)S(1)}, f32[160,1280]{1,0:T(8,128)S(1)}) custom-call(bf16[160,2048]{1,0:T(8,128)(2,1)S(1)} %get-tuple-element.44.refs_0_, bf16[160,2048]{1,0:T(8,128)(2,1)S(1)} %copy-done.2, bf16[160,2048]{1,0:T(8,128)(2,1)S(1)} %copy-done.6, ...), custom_call_target="tpu_custom_call" | custom-call | flops 1677721600 | bytes 7208960 | tf_op jit(solution)/shard_map/partials/pallas_call | solution.py:130
  73.9 10.4 %collective-permute-done.4.refs_4_ = bf16[512,1280]{1,0:T(8,128)(2,1)S(1)} collective-permute-done((bf16[512,1280]{1,0:T(8,128)(2,1)}, bf16[512,1280]{1,0:T(8,128)(2,1)S(1)}, u32[]{:S(2)}, u32[]{:S(2)}) %collective-permute-start.4) | collective-permute-done | bytes 1310752 | tf_op jit(solution)/shard_map/ppermute | solution.py:27
  87.0 3.0 %collective-permute-start.12 = (bf16[256,1024]{1,0:T(8,128)(2,1)S(1)}, bf16[256,1024]{1,0:T(8,128)(2,1)S(1)}, u32[]{:S(2)}, u32[]{:S(2)}) collective-permute-start(bf16[256,1024]{1,0:T(8,128)(2,1)S(1)} %slice.40), channel_id=1, source_target_pairs={{0,48},{8,56},{16,0},{24,8},{32,16},{40,24},{48,32},{56,40},{64,11... | collective-permute-start | bytes 1572872 | tf_op jit(solution)/shard_map/ppermute | solution.py:23
  90.1 3.5 %partials_rest.1 = (f32[160,1280]{1,0:T(8,128)S(1)}, bf16[160,1280]{1,0:T(8,128)(2,1)S(1)}, bf16[160,1280]{1,0:T(8,128)(2,1)S(1)}, bf16[160,1280]{1,0:T(8,128)(2,1)S(1)}) custom-call(bf16[160,2048]{1,0:T(8,128)(2,1)S(1)} %get-tuple-element.44.refs_0_, bf16[160,2048]{1,0:T(8,128)(2,1)S(1)} %copy-done.2, bf16[160,2048]{1,0:T(8,128)(2,1)S(1)} %copy-done.6, ...), custom_call_target="tpu_custom_call" | custom-call | flops 1677721600 | bytes 7208960 | tf_op jit(solution)/shard_map/partials_rest/pallas_call | solution.py:130
  93.6 3.3 %collective-permute-start.8 = (bf16[160,1280]{1,0:T(8,128)(2,1)S(1)}, bf16[160,1280]{1,0:T(8,128)(2,1)S(1)}, u32[]{:S(2)}, u32[]{:S(2)}) collective-permute-start(bf16[160,1280]{1,0:T(8,128)(2,1)S(1)} %get-tuple-element.64), channel_id=1, source_target_pairs={{0,48},{8,56},{16,0},{24,8},{32,16},{40,24},{48,32},{56,40},{64,11... | collective-permute-start | bytes 1228808 | tf_op jit(solution)/shard_map/ppermute | solution.py:23
  96.9 5.4 %collective-permute-done.12.refs_4_ = bf16[256,1024]{1,0:T(8,128)(2,1)S(1)} collective-permute-done((bf16[256,1024]{1,0:T(8,128)(2,1)S(1)}, bf16[256,1024]{1,0:T(8,128)(2,1)S(1)}, u32[]{:S(2)}, u32[]{:S(2)}) %collective-permute-start.12) | collective-permute-done | bytes 524320 | tf_op jit(solution)/shard_map/ppermute | solution.py:23
  102.7 12.2 %collective-permute-done.13.refs_5_ = bf16[256,1024]{1,0:T(8,128)(2,1)S(1)} collective-permute-done((bf16[256,1024]{1,0:T(8,128)(2,1)S(1)}, bf16[256,1024]{1,0:T(8,128)(2,1)S(1)}, u32[]{:S(2)}, u32[]{:S(2)}) %collective-permute-start.13) | collective-permute-done | bytes 524320 | tf_op jit(solution)/shard_map/ppermute | solution.py:23
  114.9 4.2 %collective-permute-done.8.p1 = bf16[160,1280]{1,0:T(8,128)(2,1)S(1)} collective-permute-done((bf16[160,1280]{1,0:T(8,128)(2,1)S(1)}, bf16[160,1280]{1,0:T(8,128)(2,1)S(1)}, u32[]{:S(2)}, u32[]{:S(2)}) %collective-permute-start.8) | collective-permute-done | bytes 409632 | tf_op jit(solution)/shard_map/ppermute | solution.py:23
  119.1 3.5 %collective-permute-done.10.p3 = bf16[160,1280]{1,0:T(8,128)(2,1)S(1)} collective-permute-done((bf16[160,1280]{1,0:T(8,128)(2,1)S(1)}, bf16[160,1280]{1,0:T(8,128)(2,1)S(1)}, u32[]{:S(2)}, u32[]{:S(2)}) %collective-permute-start.10) | collective-permute-done | bytes 409632 | tf_op jit(solution)/shard_map/ppermute | solution.py:23
  122.6 3.2 %collective-permute-start.18 = (bf16[512,1024]{1,0:T(8,128)(2,1)S(1)}, bf16[512,1024]{1,0:T(8,128)(2,1)S(1)}, u32[]{:S(2)}, u32[]{:S(2)}) collective-permute-start(bf16[512,1024]{1,0:T(8,128)(2,1)S(1)} %collective-permute-done.14.refs_3_), channel_id=1, source_target_pairs={{0,48},{8,56},{16,0},{24,8},{32,16},{40,24},{48,32},{56,40},{64,11... | collective-permute-start | bytes 3145736 | tf_op jit(solution)/shard_map/ppermute | solution.py:23
  127.9 10.7 %attention.1.mixed_ref = bf16[160,1024]{1,0:T(8,128)(2,1)S(1)} custom-call(s32[80]{0:T(128)S(1)} %copy-done.8, f32[160,1280]{1,0:T(8,128)S(1)} %get-tuple-element.63.p0, bf16[160,1280]{1,0:T(8,128)(2,1)S(1)} %collective-permute-done.8.p1, bf16[160,1280]{1,0:T(8,128)(2,1)S(1)} %collective-permute-done.9.p2, bf16[160,1280]{1,0:T(8,128)(2,1)S(1)} %collective-permute-done.10.p3, ...), custom_call_target="tpu_custom_call" | custom-call | flops 167772160 | bytes 41943040 | tf_op jit(solution)/shard_map/attention/pallas_call | solution.py:352
  138.7 2.1 %collective-permute-done.15.refs_6_ = bf16[256,1024]{1,0:T(8,128)(2,1)S(1)} collective-permute-done((bf16[256,1024]{1,0:T(8,128)(2,1)S(1)}, bf16[256,1024]{1,0:T(8,128)(2,1)S(1)}, u32[]{:S(2)}, u32[]{:S(2)}) %collective-permute-start.15) | collective-permute-done | bytes 524320 | tf_op jit(solution)/shard_map/ppermute | solution.py:27
  140.7 8.7 %collective-permute-done.16.refs_7_ = bf16[256,1024]{1,0:T(8,128)(2,1)S(1)} collective-permute-done((bf16[256,1024]{1,0:T(8,128)(2,1)S(1)}, bf16[256,1024]{1,0:T(8,128)(2,1)S(1)}, u32[]{:S(2)}, u32[]{:S(2)}) %collective-permute-start.16) | collective-permute-done | bytes 524320 | tf_op jit(solution)/shard_map/ppermute | solution.py:27
  149.5 4.6 %terms.2 = bf16[4096,256]{1,0:T(8,128)(2,1)S(1)} custom-call(bf16[160,1024]{1,0:T(8,128)(2,1)S(1)} %collective-permute-done.11.mixed_ref, bf16[512,1024]{1,0:T(8,128)(2,1)S(1)} %bitcast.60, bf16[512,1024]{1,0:T(8,128)(2,1)S(1)} %collective-permute-done.5.refs_1_, bf16[512,1024]{1,0:T(8,128)(2,1)S(1)} %collective-permute-done.6.refs_2_, ...), custom_call_target="tpu_custom_call" | custom-call | flops 1342177280 | bytes 10027008 | tf_op jit(solution)/shard_map/terms/pallas_call | solution.py:174
  154.1 4.6 %terms.3.refs_0_ = bf16[4096,256]{1,0:T(8,128)(2,1)S(1)} custom-call(bf16[160,1024]{1,0:T(8,128)(2,1)S(1)} %attention.1.mixed_ref, bf16[512,1024]{1,0:T(8,128)(2,1)S(1)} %bitcast.61, bf16[512,1024]{1,0:T(8,128)(2,1)S(1)} %collective-permute-done.5.refs_1_, bf16[512,1024]{1,0:T(8,128)(2,1)S(1)} %collective-permute-done.6.refs_2_, ...), custom_call_target="tpu_custom_call" | custom-call | flops 1342177280 | bytes 10027008 | tf_op jit(solution)/shard_map/terms/pallas_call | solution.py:174
  158.7 2.9 %place.1 = (bf16[2,80,1024]{2,1,0:T(8,128)(2,1)S(1)}, bf16[2,80,1024]{2,1,0:T(8,128)(2,1)S(1)}, bf16[2,80,1024]{2,1,0:T(8,128)(2,1)S(1)}, bf16[2,80,1024]{2,1,0:...) custom-call(s32[2,128]{1,0:T(2,128)S(1)} %copy-done.7, ...), custom_call_target="tpu_custom_call" | custom-call | bytes 5242880 | tf_op jit(solution)/shard_map/place/pallas_call | solution.py:223
  161.6 2.7 %collective-permute-start.22 = (bf16[2,80,1024]{2,1,0:T(8,128)(2,1)S(1)}, bf16[2,80,1024]{2,1,0:T(8,128)(2,1)S(1)}, u32[]{:S(2)}, u32[]{:S(2)}) collective-permute-start(bf16[2,80,1024]{2,1,0:T(8,128)(2,1)S(1)} %get-tuple-element.80), channel_id=1, source_target_pairs={{0,6},{1,7},{2,0},{3,1},{4,2},{5,3},{6,4},{7,5},{8,14},{9,15},{10,... | collective-permute-start | bytes 983048 | tf_op jit(solution)/shard_map/ppermute | solution.py:31
  166.1 3.6 %collective-permute-start.24 = (bf16[4,80,1024]{2,1,0:T(8,128)(2,1)S(1)}, bf16[4,80,1024]{2,1,0:T(8,128)(2,1)S(1)}, u32[]{:S(2)}, u32[]{:S(2)}) collective-permute-start(bf16[4,80,1024]{2,1,0:T(8,128)(2,1)S(1)} %get-tuple-element.82), channel_id=1, source_target_pairs={{0,1},{1,0},{2,3},{3,2},{4,5},{5,4},{6,7},{7,6},{8,9},{9,8},{10,11... | collective-permute-start | bytes 1966088 | tf_op jit(solution)/shard_map/ppermute | solution.py:35
  169.7 9.4 %collective-permute-done.22 = bf16[2,80,1024]{2,1,0:T(8,128)(2,1)S(1)} collective-permute-done((bf16[2,80,1024]{2,1,0:T(8,128)(2,1)S(1)}, bf16[2,80,1024]{2,1,0:T(8,128)(2,1)S(1)}, u32[]{:S(2)}, u32[]{:S(2)}) %collective-permute-start.22) | collective-permute-done | bytes 327712 | tf_op jit(solution)/shard_map/ppermute | solution.py:31
  179.1 3.7 %collective-permute-done.20 = bf16[2,80,1024]{2,1,0:T(8,128)(2,1)S(1)} collective-permute-done((bf16[2,80,1024]{2,1,0:T(8,128)(2,1)S(1)}, bf16[2,80,1024]{2,1,0:T(8,128)(2,1)S(1)}, u32[]{:S(2)}, u32[]{:S(2)}) %collective-permute-start.20) | collective-permute-done | bytes 327712 | tf_op jit(solution)/shard_map/ppermute | solution.py:31
  183.0 3.7 %collective-permute-start.23 = (bf16[80,1024]{1,0:T(8,128)(2,1)S(1)}, bf16[80,1024]{1,0:T(8,128)(2,1)S(1)}, u32[]{:S(2)}, u32[]{:S(2)}) collective-permute-start(bf16[80,1024]{1,0:T(8,128)(2,1)S(1)} %fusion.7), channel_id=1, source_target_pairs={{0,1},{1,0},{2,3},{3,2},{4,5},{5,4},{6,7},{7,6},{8,9},{9,8},{10,11... | collective-permute-start | bytes 491528 | tf_op jit(solution)/shard_map/ppermute | solution.py:35
  191.0 3.1 %collective-permute-done.27 = bf16[80,1024]{1,0:T(8,128)(2,1)S(1)} collective-permute-done((bf16[80,1024]{1,0:T(8,128)(2,1)S(1)}, bf16[80,1024]{1,0:T(8,128)(2,1)S(1)}, u32[]{:S(2)}, u32[]{:S(2)}) %collective-permute-start.27) | collective-permute-done | bytes 163872 | tf_op jit(solution)/shard_map/ppermute | solution.py:31
  196.0 2.0 collective-permute-done.25
  (76 shorter events, 29.1 us)
Async XLA Ops:
  3.3 7.3 %copy-start.7 = (s32[2,128]{1,0:T(2,128)S(1)}, s32[2,128]{1,0:T(2,128)}, u32[]{:S(2)}) copy-start(s32[2,128]{1,0:T(2,128)} %owner_ref.3) | copy-start | bytes 3076
  3.3 27.3 %all-to-all-start = ((bf16[64,8,1280]{2,0,1:T(8,128)(2,1)}), bf16[64,8,1280]{2,0,1:T(8,128)(2,1)}, u32[]{:S(2)}, u32[]{:S(2)}) async-start(bf16[64,8,1280]{2,0,1:T(8,128)(2,1)} %pad_maximum_fusion), calls=%async_computation | async-start | bytes 2621440 | tf_op jit(solution)/shard_map/all_to_all | solution.py:394
  10.6 9.5 %copy-start.8 = (s32[80]{0:T(128)S(1)}, s32[80]{0:T(128)}, u32[]{:S(2)}) copy-start(s32[80]{0:T(128)} %lengths_ref.1) | copy-start | bytes 964
  16.0 18.7 %collective-permute-start = (bf16[160,2048]{1,0:T(8,128)(2,1)}, bf16[160,2048]{1,0:T(8,128)(2,1)S(1)}, u32[]{:S(2)}, u32[]{:S(2)}) collective-permute-start(bf16[160,2048]{1,0:T(8,128)(2,1)} %get-tuple-element.45), channel_id=1, source_target_pairs={{0,16},{8,24},{16,32},{24,40},{32,48},{40,56},{48,0},{56,8},{64,80... | collective-permute-start | bytes 1966088 | tf_op jit(solution)/shard_map/ppermute | solution.py:23
  17.9 16.8 %collective-permute-start.1 = (bf16[160,2048]{1,0:T(8,128)(2,1)}, bf16[160,2048]{1,0:T(8,128)(2,1)S(1)}, u32[]{:S(2)}, u32[]{:S(2)}) collective-permute-start(bf16[160,2048]{1,0:T(8,128)(2,1)} %get-tuple-element.46), channel_id=1, source_target_pairs={{0,48},{8,56},{16,0},{24,8},{32,16},{40,24},{48,32},{56,40},{64,11... | collective-permute-start | bytes 1966088 | tf_op jit(solution)/shard_map/ppermute | solution.py:23
  30.6 31.9 %collective-permute-start.3 = (bf16[512,1280]{1,0:T(8,128)(2,1)}, bf16[512,1280]{1,0:T(8,128)(2,1)}, u32[]{:S(2)}, u32[]{:S(2)}) collective-permute-start(bf16[512,1280]{1,0:T(8,128)(2,1)} %bitcast.3.refs_4_), channel_id=1, source_target_pairs={{0,8},{8,0},{16,24},{24,16},{32,40},{40,32},{48,56},{56,48},{64,72... | collective-permute-start | bytes 3932168 | tf_op jit(solution)/shard_map/ppermute | solution.py:27
  38.0 24.5 %all-to-all-start.1 = ((bf16[64,8,1024]{2,0,1:T(8,128)(2,1)}), bf16[64,8,1024]{2,0,1:T(8,128)(2,1)S(1)}, u32[]{:S(2)}, u32[]{:S(2)}) async-start(bf16[64,8,1024]{2,0,1:T(8,128)(2,1)} %copy.10), calls=%async_computation.1 | async-start | bytes 2097152 | tf_op jit(solution)/shard_map/all_to_all | solution.py:399
  44.9 16.7 %collective-permute-start.2 = (bf16[160,2048]{1,0:T(8,128)(2,1)}, bf16[160,2048]{1,0:T(8,128)(2,1)S(1)}, u32[]{:S(2)}, u32[]{:S(2)}) collective-permute-start(bf16[160,2048]{1,0:T(8,128)(2,1)} %get-tuple-element.49), channel_id=1, source_target_pairs={{0,32},{8,40},{16,48},{24,56},{32,0},{40,8},{48,16},{56,24},{64,96... | collective-permute-start | bytes 1966088 | tf_op jit(solution)/shard_map/ppermute | solution.py:23
  47.6 36.7 %collective-permute-start.4 = (bf16[512,1280]{1,0:T(8,128)(2,1)}, bf16[512,1280]{1,0:T(8,128)(2,1)S(1)}, u32[]{:S(2)}, u32[]{:S(2)}) collective-permute-start(bf16[512,1280]{1,0:T(8,128)(2,1)} %bitcast.3.refs_4_), channel_id=1, source_target_pairs={{0,64},{8,72},{16,80},{24,88},{32,96},{40,104},{48,112},{56,120},{... | collective-permute-start | bytes 3932168 | tf_op jit(solution)/shard_map/ppermute | solution.py:27
  62.5 23.7 %collective-permute-start.5 = (bf16[512,1024]{1,0:T(8,128)(2,1)S(1)}, bf16[512,1024]{1,0:T(8,128)(2,1)S(1)}, u32[]{:S(2)}, u32[]{:S(2)}) collective-permute-start(bf16[512,1024]{1,0:T(8,128)(2,1)S(1)} %bitcast.57), channel_id=1, source_target_pairs={{0,16},{8,24},{16,32},{24,40},{32,48},{40,56},{48,0},{56,8},{64,80... | collective-permute-start | bytes 3145736 | tf_op jit(solution)/shard_map/ppermute | solution.py:23
  63.1 23.1 %collective-permute-start.6 = (bf16[512,1024]{1,0:T(8,128)(2,1)S(1)}, bf16[512,1024]{1,0:T(8,128)(2,1)S(1)}, u32[]{:S(2)}, u32[]{:S(2)}) collective-permute-start(bf16[512,1024]{1,0:T(8,128)(2,1)S(1)} %bitcast.58), channel_id=1, source_target_pairs={{0,48},{8,56},{16,0},{24,8},{32,16},{40,24},{48,32},{56,40},{64,11... | collective-permute-start | bytes 3145736 | tf_op jit(solution)/shard_map/ppermute | solution.py:23
  86.2 3.9 %collective-permute-start.7 = (bf16[512,1280]{1,0:T(8,128)(2,1)S(1)}, bf16[512,1280]{1,0:T(8,128)(2,1)S(1)}, u32[]{:S(2)}, u32[]{:S(2)}) collective-permute-start(bf16[512,1280]{1,0:T(8,128)(2,1)S(1)} %collective-permute-done.4.refs_4_), channel_id=1, source_target_pairs={{0,8},{8,0},{16,24},{24,16},{32,40},{40,32},{48,56},{56,48},{64,72... | collective-permute-start | bytes 3932168 | tf_op jit(solution)/shard_map/ppermute | solution.py:27
  86.2 28.6 %collective-permute-start.14 = (bf16[512,1024]{1,0:T(8,128)(2,1)S(1)}, bf16[512,1024]{1,0:T(8,128)(2,1)S(1)}, u32[]{:S(2)}, u32[]{:S(2)}) collective-permute-start(bf16[512,1024]{1,0:T(8,128)(2,1)S(1)} %bitcast.59), channel_id=1, source_target_pairs={{0,64},{8,72},{16,80},{24,88},{32,96},{40,104},{48,112},{56,120},{... | collective-permute-start | bytes 3145736 | tf_op jit(solution)/shard_map/ppermute | solution.py:27
  87.0 15.3 %collective-permute-start.12 = (bf16[256,1024]{1,0:T(8,128)(2,1)S(1)}, bf16[256,1024]{1,0:T(8,128)(2,1)S(1)}, u32[]{:S(2)}, u32[]{:S(2)}) collective-permute-start(bf16[256,1024]{1,0:T(8,128)(2,1)S(1)} %slice.40), channel_id=1, source_target_pairs={{0,48},{8,56},{16,0},{24,8},{32,16},{40,24},{48,32},{56,40},{64,11... | collective-permute-start | bytes 1572872 | tf_op jit(solution)/shard_map/ppermute | solution.py:23
  90.0 24.9 %collective-permute-start.13 = (bf16[256,1024]{1,0:T(8,128)(2,1)S(1)}, bf16[256,1024]{1,0:T(8,128)(2,1)S(1)}, u32[]{:S(2)}, u32[]{:S(2)}) collective-permute-start(bf16[256,1024]{1,0:T(8,128)(2,1)S(1)} %slice.41), channel_id=1, source_target_pairs={{0,16},{8,24},{16,32},{24,40},{32,48},{40,56},{48,0},{56,8},{64,80... | collective-permute-start | bytes 1572872 | tf_op jit(solution)/shard_map/ppermute | solution.py:23
  93.6 25.5 %collective-permute-start.8 = (bf16[160,1280]{1,0:T(8,128)(2,1)S(1)}, bf16[160,1280]{1,0:T(8,128)(2,1)S(1)}, u32[]{:S(2)}, u32[]{:S(2)}) collective-permute-start(bf16[160,1280]{1,0:T(8,128)(2,1)S(1)} %get-tuple-element.64), channel_id=1, source_target_pairs={{0,48},{8,56},{16,0},{24,8},{32,16},{40,24},{48,32},{56,40},{64,11... | collective-permute-start | bytes 1228808 | tf_op jit(solution)/shard_map/ppermute | solution.py:23
  96.8 22.3 %collective-permute-start.9 = (bf16[160,1280]{1,0:T(8,128)(2,1)S(1)}, bf16[160,1280]{1,0:T(8,128)(2,1)S(1)}, u32[]{:S(2)}, u32[]{:S(2)}) collective-permute-start(bf16[160,1280]{1,0:T(8,128)(2,1)S(1)} %get-tuple-element.65), channel_id=1, source_target_pairs={{0,32},{8,40},{16,48},{24,56},{32,0},{40,8},{48,16},{56,24},{64,96... | collective-permute-start | bytes 1228808 | tf_op jit(solution)/shard_map/ppermute | solution.py:23
  102.3 20.4 %collective-permute-start.10 = (bf16[160,1280]{1,0:T(8,128)(2,1)S(1)}, bf16[160,1280]{1,0:T(8,128)(2,1)S(1)}, u32[]{:S(2)}, u32[]{:S(2)}) collective-permute-start(bf16[160,1280]{1,0:T(8,128)(2,1)S(1)} %get-tuple-element.66), channel_id=1, source_target_pairs={{0,16},{8,24},{16,32},{24,40},{32,48},{40,56},{48,0},{56,8},{64,80... | collective-permute-start | bytes 1228808 | tf_op jit(solution)/shard_map/ppermute | solution.py:23
  122.6 26.8 %collective-permute-start.17 = (bf16[512,1024]{1,0:T(8,128)(2,1)S(1)}, bf16[512,1024]{1,0:T(8,128)(2,1)S(1)}, u32[]{:S(2)}, u32[]{:S(2)}) collective-permute-start(bf16[512,1024]{1,0:T(8,128)(2,1)S(1)} %collective-permute-done.14.refs_3_), channel_id=1, source_target_pairs={{0,16},{8,24},{16,32},{24,40},{32,48},{40,56},{48,0},{56,8},{64,80... | collective-permute-start | bytes 3145736 | tf_op jit(solution)/shard_map/ppermute | solution.py:23
  122.6 26.8 %collective-permute-start.18 = (bf16[512,1024]{1,0:T(8,128)(2,1)S(1)}, bf16[512,1024]{1,0:T(8,128)(2,1)S(1)}, u32[]{:S(2)}, u32[]{:S(2)}) collective-permute-start(bf16[512,1024]{1,0:T(8,128)(2,1)S(1)} %collective-permute-done.14.refs_3_), channel_id=1, source_target_pairs={{0,48},{8,56},{16,0},{24,8},{32,16},{40,24},{48,32},{56,40},{64,11... | collective-permute-start | bytes 3145736 | tf_op jit(solution)/shard_map/ppermute | solution.py:23
  125.9 14.9 %collective-permute-start.15 = (bf16[256,1024]{1,0:T(8,128)(2,1)S(1)}, bf16[256,1024]{1,0:T(8,128)(2,1)S(1)}, u32[]{:S(2)}, u32[]{:S(2)}) collective-permute-start(bf16[256,1024]{1,0:T(8,128)(2,1)S(1)} %collective-permute-done.12.refs_4_), channel_id=1, source_target_pairs={{0,64},{8,72},{16,80},{24,88},{32,96},{40,104},{48,112},{56,120},{... | collective-permute-start | bytes 1572872 | tf_op jit(solution)/shard_map/ppermute | solution.py:27
  127.2 22.2 %collective-permute-start.16 = (bf16[256,1024]{1,0:T(8,128)(2,1)S(1)}, bf16[256,1024]{1,0:T(8,128)(2,1)S(1)}, u32[]{:S(2)}, u32[]{:S(2)}) collective-permute-start(bf16[256,1024]{1,0:T(8,128)(2,1)S(1)} %collective-permute-done.13.refs_5_), channel_id=1, source_target_pairs={{0,64},{8,72},{16,80},{24,88},{32,96},{40,104},{48,112},{56,120},{... | collective-permute-start | bytes 1572872 | tf_op jit(solution)/shard_map/ppermute | solution.py:27
  138.6 10.9 %collective-permute-start.11 = (bf16[160,1024]{1,0:T(8,128)(2,1)S(1)}, bf16[160,1024]{1,0:T(8,128)(2,1)S(1)}, u32[]{:S(2)}, u32[]{:S(2)}) collective-permute-start(bf16[160,1024]{1,0:T(8,128)(2,1)S(1)} %attention.1.mixed_ref), channel_id=1, source_target_pairs={{0,8},{8,0},{16,24},{24,16},{32,40},{40,32},{48,56},{56,48},{64,72... | collective-permute-start | bytes 983048 | tf_op jit(solution)/shard_map/ppermute | solution.py:27
  154.1 4.7 %collective-permute-start.19 = (bf16[4096,256]{1,0:T(8,128)(2,1)S(1)}, bf16[4096,256]{1,0:T(8,128)(2,1)S(1)}, u32[]{:S(2)}, u32[]{:S(2)}) collective-permute-start(bf16[4096,256]{1,0:T(8,128)(2,1)S(1)} %terms.2), channel_id=1, source_target_pairs={{0,8},{8,0},{16,24},{24,16},{32,40},{40,32},{48,56},{56,48},{64,72... | collective-permute-start | bytes 6291464 | tf_op jit(solution)/shard_map/ppermute | solution.py:27
  161.6 17.4 %collective-permute-start.22 = (bf16[2,80,1024]{2,1,0:T(8,128)(2,1)S(1)}, bf16[2,80,1024]{2,1,0:T(8,128)(2,1)S(1)}, u32[]{:S(2)}, u32[]{:S(2)}) collective-permute-start(bf16[2,80,1024]{2,1,0:T(8,128)(2,1)S(1)} %get-tuple-element.80), channel_id=1, source_target_pairs={{0,6},{1,7},{2,0},{3,1},{4,2},{5,3},{6,4},{7,5},{8,14},{9,15},{10,... | collective-permute-start | bytes 983048 | tf_op jit(solution)/shard_map/ppermute | solution.py:31
  164.4 14.7 %collective-permute-start.21 = (bf16[2,80,1024]{2,1,0:T(8,128)(2,1)S(1)}, bf16[2,80,1024]{2,1,0:T(8,128)(2,1)S(1)}, u32[]{:S(2)}, u32[]{:S(2)}) collective-permute-start(bf16[2,80,1024]{2,1,0:T(8,128)(2,1)S(1)} %get-tuple-element.79), channel_id=1, source_target_pairs={{0,4},{1,5},{2,6},{3,7},{4,0},{5,1},{6,2},{7,3},{8,12},{9,13},{10,... | collective-permute-start | bytes 983048 | tf_op jit(solution)/shard_map/ppermute | solution.py:31
  165.2 17.5 %collective-permute-start.20 = (bf16[2,80,1024]{2,1,0:T(8,128)(2,1)S(1)}, bf16[2,80,1024]{2,1,0:T(8,128)(2,1)S(1)}, u32[]{:S(2)}, u32[]{:S(2)}) collective-permute-start(bf16[2,80,1024]{2,1,0:T(8,128)(2,1)S(1)} %get-tuple-element.78), channel_id=1, source_target_pairs={{0,2},{1,3},{2,4},{3,5},{4,6},{5,7},{6,0},{7,1},{8,10},{9,11},{10,... | collective-permute-start | bytes 983048 | tf_op jit(solution)/shard_map/ppermute | solution.py:31
  166.1 20.5 %collective-permute-start.24 = (bf16[4,80,1024]{2,1,0:T(8,128)(2,1)S(1)}, bf16[4,80,1024]{2,1,0:T(8,128)(2,1)S(1)}, u32[]{:S(2)}, u32[]{:S(2)}) collective-permute-start(bf16[4,80,1024]{2,1,0:T(8,128)(2,1)S(1)} %get-tuple-element.82), channel_id=1, source_target_pairs={{0,1},{1,0},{2,3},{3,2},{4,5},{5,4},{6,7},{7,6},{8,9},{9,8},{10,11... | collective-permute-start | bytes 1966088 | tf_op jit(solution)/shard_map/ppermute | solution.py:35
  183.0 8.0 %collective-permute-start.23 = (bf16[80,1024]{1,0:T(8,128)(2,1)S(1)}, bf16[80,1024]{1,0:T(8,128)(2,1)S(1)}, u32[]{:S(2)}, u32[]{:S(2)}) collective-permute-start(bf16[80,1024]{1,0:T(8,128)(2,1)S(1)} %fusion.7), channel_id=1, source_target_pairs={{0,1},{1,0},{2,3},{3,2},{4,5},{5,4},{6,7},{7,6},{8,9},{9,8},{10,11... | collective-permute-start | bytes 491528 | tf_op jit(solution)/shard_map/ppermute | solution.py:35
  186.9 7.2 %collective-permute-start.27 = (bf16[80,1024]{1,0:T(8,128)(2,1)S(1)}, bf16[80,1024]{1,0:T(8,128)(2,1)S(1)}, u32[]{:S(2)}, u32[]{:S(2)}) collective-permute-start(bf16[80,1024]{1,0:T(8,128)(2,1)S(1)} %get-tuple-element.88), channel_id=1, source_target_pairs={{0,6},{1,7},{2,0},{3,1},{4,2},{5,3},{6,4},{7,5},{8,14},{9,15},{10,... | collective-permute-start | bytes 491528 | tf_op jit(solution)/shard_map/ppermute | solution.py:31
  187.6 8.4 %collective-permute-start.26 = (bf16[80,1024]{1,0:T(8,128)(2,1)S(1)}, bf16[80,1024]{1,0:T(8,128)(2,1)S(1)}, u32[]{:S(2)}, u32[]{:S(2)}) collective-permute-start(bf16[80,1024]{1,0:T(8,128)(2,1)S(1)} %get-tuple-element.89), channel_id=1, source_target_pairs={{0,4},{1,5},{2,6},{3,7},{4,0},{5,1},{6,2},{7,3},{8,12},{9,13},{10,... | collective-permute-start | bytes 491528 | tf_op jit(solution)/shard_map/ppermute | solution.py:31
  188.5 9.5 %collective-permute-start.25 = (bf16[80,1024]{1,0:T(8,128)(2,1)S(1)}, bf16[80,1024]{1,0:T(8,128)(2,1)S(1)}, u32[]{:S(2)}, u32[]{:S(2)}) collective-permute-start(bf16[80,1024]{1,0:T(8,128)(2,1)S(1)} %get-tuple-element.87), channel_id=1, source_target_pairs={{0,2},{1,3},{2,4},{3,5},{4,6},{5,7},{6,0},{7,1},{8,10},{9,11},{10,... | collective-permute-start | bytes 491528 | tf_op jit(solution)/shard_map/ppermute | solution.py:31
  (7 other events, 17.9 us)

commit v10 on v8

--- a/solution.py
+++ b/solution.py
@@ -14,7 +14,7 @@
 NZ = 4
 NX = 4
 GROUP = 8
-CHUNK = 256
+CHUNK = 512
 MIB = 1024 * 1024
 
 
@@ -35,19 +35,41 @@
     return lax.ppermute(value, "tp", [(t, t ^ 1) for t in range(2 * NX)])
 
 
-def by_group(array, sections, groups):
-    pieces = []
+def slabs_kernel(query, key, value, back, out_ref):
     begin = 0
-    for width in sections:
-        pieces.append(
-            array[:, begin : begin + width].reshape(array.shape[0], groups, width // groups)
-        )
-        begin = begin + width
-    return jnp.concatenate(pieces, axis=2)
-
-
-def flatten(received):
-    return received.reshape(received.shape[0], received.shape[2])
+    for ref in (query, key, value, back):
+        width = ref.shape[1] // out_ref.shape[0]
+        for g in range(out_ref.shape[0]):
+            part = ref[:, g * width : (g + 1) * width]
+            out_ref[g, :, begin : begin + width] = part.astype(out_ref.dtype)
+        begin += width
+
+
+def slabs_of(qkv_rows, o_rows, groups):
+    owned = qkv_rows.shape[0]
+    query_cols = HQ * HD
+    each = 2
+    wide, narrow = each * query_cols // groups, each * HK * HD // groups
+    keys_at = query_cols // narrow
+    values_at = keys_at + HK * HD // narrow
+    cols = (2 * wide + 2 * narrow) // each
+    return pl.pallas_call(
+        slabs_kernel,
+        grid=(groups // each,),
+        out_shape=jax.ShapeDtypeStruct((groups, owned, cols), jnp.bfloat16),
+        in_specs=[
+            pl.BlockSpec((owned, wide), lambda g: (0, g)),
+            pl.BlockSpec((owned, narrow), lambda g: (0, keys_at + g)),
+            pl.BlockSpec((owned, narrow), lambda g: (0, values_at + g)),
+            pl.BlockSpec((owned, wide), lambda g: (0, g)),
+        ],
+        out_specs=pl.BlockSpec((each, owned, cols), lambda g: (g, 0, 0)),
+        compiler_params=pltpu.CompilerParams(vmem_limit_bytes=60 * MIB),
+        cost_estimate=pl.CostEstimate(
+            flops=0, bytes_accessed=6 * groups * owned * cols, transcendentals=0
+        ),
+        name="slabs",
+    )(qkv_rows, qkv_rows, qkv_rows, o_rows)
 
 
 def shuffle_kernel(owner_ref, hidden_ref, *out_refs):
@@ -74,7 +96,7 @@
             )
             return carry
 
-        lax.fori_loop(0, 16, step, 0, unroll=4)
+        lax.fori_loop(0, 16, step, 0, unroll=8)
 
 
 def shuffle(hidden, block_owner):
@@ -153,17 +175,19 @@
     turned = wide.T.astype(jnp.bfloat16)
     begin = 0
     for source in sources:
-
-        def multiply(n, carry, source=source, begin=begin):
-            rows = source[pl.ds(pl.multiple_of(n * CHUNK, CHUNK), CHUNK), :]
-            to = pl.ds(pl.multiple_of(begin + n * CHUNK, CHUNK), CHUNK)
+        size = source.shape[0]
+        chunk = min(CHUNK, size)
+
+        def multiply(n, carry, source=source, begin=begin, chunk=chunk):
+            rows = source[pl.ds(pl.multiple_of(n * chunk, chunk), chunk), :]
+            to = pl.ds(pl.multiple_of(begin + n * chunk, chunk), chunk)
             out_ref[to, :] = jnp.dot(rows, turned, preferred_element_type=jnp.float32).astype(
                 out_ref.dtype
             )
             return carry
 
-        lax.fori_loop(0, source.shape[0] // CHUNK, multiply, 0)
-        begin += source.shape[0]
+        lax.fori_loop(0, size // chunk, multiply, 0)
+        begin += size
 
 
 def terms_of(mixed, sources):
@@ -385,14 +409,14 @@
     query_cols = HQ * HD
     kv_cols = HK * HD
     cols = (query_cols + 2 * kv_cols) // groups
-    copy = jnp.concatenate([qkv_rows.astype(jnp.bfloat16), o_rows.astype(jnp.bfloat16)], axis=1)
-    copy = by_group(copy, (query_cols, kv_cols, kv_cols, query_cols), groups)
+    copy = slabs_of(qkv_rows, o_rows, groups)
 
     cos, sin = turns(lengths)
     parts = shuffle(hidden.reshape(steps * rows, width), block_owner)
     parts = [parts[0]] + [z_shift(parts[k], k) for k in range(1, NZ)]
 
-    both = flatten(lax.all_to_all(copy, "tp", split_axis=1, concat_axis=0, tiled=True))
+    both = lax.all_to_all(copy, "tp", split_axis=0, concat_axis=0, tiled=True)
+    both = both.reshape(groups * owned, -1)
     both, cos, sin, parts[1], parts[3] = lax.optimization_barrier(
         (both, cos, sin, parts[1], parts[3])
     )

time: 197 us -> 193 us (0.980)
  other arithmetic: 5.6 us -> 1.84 us
    pallas_call x0 -> x1, Pallas kernels: none -> 4.33 us  [slabs_of(): pl.pallas_call(slabs_kernel, grid=(groups // each,), out_shape=jax.ShapeD...]
    pallas_call x2, Pallas kernels: 9.17 us -> 4.88 us  [terms_of(): pl.pallas_call(terms_kernel, out_shape=jax.ShapeDtypeStruct((width, lanes...]
    convert_element_type x2 -> x0, other arithmetic: 2.12 us -> none  [the longest x1 2.02 us: body(): qkv_rows.astype(jnp.bfloat16)]
  transfers between devices with their start and end apart: 29 -> 29, of which waited for: 16 -> 17; matrix products, arithmetic and copies ran while one was open for 2% -> 2% of each run, Pallas kernels for 14% -> 13%
where the time goes in v10:
time: 193 us; the launch traced here: 192 us
  waiting for transfers between devices  107 us (55%)
  starting transfers between devices  45.3 us (23%)
  Pallas kernels  34.3 us (18%)
  local copies, waits for them, and re-layouts  2.91 us (2%)
    ppermute x12, waiting for transfers between devices, z_shift(): return lax.ppermute(value, 'fsdp', pairs)  71.6 us
    ppermute x12, starting transfers between devices, z_shift(): return lax.ppermute(value, 'fsdp', pairs)  19.8 us
    ppermute x6, waiting for transfers between devices, x_shift(): lax.ppermute(value, 'tp', [(t, (t // 2 + k) % NX * 2 + t % 2) for t in ra...  19.6 us
    ppermute x8, waiting for transfers between devices, flip(): return lax.ppermute(value, 'fsdp', [(f, f ^ bit) for f in range(16)])  14.3 us
    pallas_call x1, Pallas kernels, attention(): pl.pallas_call(attention_kernel, grid=(rows // GROUP,), out_shape=jax.Sha...  10.7 us
    all_to_all x1, starting transfers between devices, body(): both = lax.all_to_all(copy, 'tp', split_axis=0, concat_axis=0, tiled=True)  7.28 us
    ppermute x2, starting transfers between devices, y_flip(): return lax.ppermute(value, 'tp', [(t, t ^ 1) for t in range(2 * NX)])  7.22 us
    ppermute x6, starting transfers between devices, x_shift(): lax.ppermute(value, 'tp', [(t, (t // 2 + k) % NX * 2 + t % 2) for t in ra...  7.07 us
  transfers between devices with their start and end apart: 29, of which 17 were waited for; matrix products, arithmetic and copies ran while one was open for 2% of the time, Pallas kernels for 13%

profile of v10, /device:TPU:0, one launch (start us, length us, event | category | flops | bytes accessed | tf_op | source)
XLA Modules:
  0.0 191.8 jit_solution(13181206842988558291)
XLA Ops:
  0.0 4.3 %slabs.1 = bf16[8,64,2304]{2,1,0:T(8,128)(2,1)} custom-call(f32[64,10240]{1,0:T(8,128)} %value.1, f32[64,10240]{1,0:T(8,128)} %value.1, f32[64,10240]{1,0:T(8,128)} %value.1, f32[64,8192]{1,0:T(8,128)} %back.1), custom_call_target="tpu_custom_call" | custom-call | bytes 7077888 | tf_op jit(solution)/shard_map/slabs/pallas_call | solution.py:56
  4.3 7.3 %all-to-all-start = ((bf16[8,64,2304]{2,1,0:T(8,128)(2,1)}), bf16[8,64,2304]{2,1,0:T(8,128)(2,1)}, u32[]{:S(2)}, u32[]{:S(2)}) async-start(bf16[8,64,2304]{2,1,0:T(8,128)(2,1)} %slabs.1), calls=%async_computation | async-start | bytes 4718592 | tf_op jit(solution)/shard_map/all_to_all | solution.py:418
  11.6 4.8 %shuffle.1 = (bf16[160,2048]{1,0:T(8,128)(2,1)S(1)}, bf16[160,2048]{1,0:T(8,128)(2,1)}, bf16[160,2048]{1,0:T(8,128)(2,1)}, bf16[160,2048]{1,0:T(8,128)(2,1)}) custom-call(s32[2,128]{1,0:T(2,128)S(1)} %copy-done.1, bf16[160,8192]{1,0:T(8,128)(2,1)S(1)} %bitcast.34), custom_call_target="tpu_custom_call" | custom-call | flops 10485760 | bytes 5242880 | tf_op jit(solution)/shard_map/shuffle/pallas_call | solution.py:105
  16.5 1.9 collective-permute-start
  18.4 2.1 %collective-permute-start.1 = (bf16[160,2048]{1,0:T(8,128)(2,1)}, bf16[160,2048]{1,0:T(8,128)(2,1)S(1)}, u32[]{:S(2)}, u32[]{:S(2)}) collective-permute-start(bf16[160,2048]{1,0:T(8,128)(2,1)} %get-tuple-element.45), channel_id=1, source_target_pairs={{0,48},{8,56},{16,0},{24,8},{32,16},{40,24},{48,32},{56,40},{64,11... | collective-permute-start | bytes 1966088 | tf_op jit(solution)/shard_map/ppermute | solution.py:23
  23.0 12.5 %collective-permute-done.refs_1_ = bf16[160,2048]{1,0:T(8,128)(2,1)S(1)} collective-permute-done((bf16[160,2048]{1,0:T(8,128)(2,1)}, bf16[160,2048]{1,0:T(8,128)(2,1)S(1)}, u32[]{:S(2)}, u32[]{:S(2)}) %collective-permute-start) | collective-permute-done | bytes 655392 | tf_op jit(solution)/shard_map/ppermute | solution.py:23
  35.4 13.2 %collective-permute-done.1.refs_3_ = bf16[160,2048]{1,0:T(8,128)(2,1)S(1)} collective-permute-done((bf16[160,2048]{1,0:T(8,128)(2,1)}, bf16[160,2048]{1,0:T(8,128)(2,1)S(1)}, u32[]{:S(2)}, u32[]{:S(2)}) %collective-permute-start.1) | collective-permute-done | bytes 655392 | tf_op jit(solution)/shard_map/ppermute | solution.py:23
  52.3 3.6 %collective-permute-start.5 = (bf16[512,1024]{1,0:T(8,128)(2,1)S(1)}, bf16[512,1024]{1,0:T(8,128)(2,1)S(1)}, u32[]{:S(2)}, u32[]{:S(2)}) collective-permute-start(bf16[512,1024]{1,0:T(8,128)(2,1)S(1)} %slice.34.refs_0_), channel_id=1, source_target_pairs={{0,48},{8,56},{16,0},{24,8},{32,16},{40,24},{48,32},{56,40},{64,11... | collective-permute-start | bytes 3145736 | tf_op jit(solution)/shard_map/ppermute | solution.py:23
  55.9 3.2 %partials.1 = (f32[160,1280]{1,0:T(8,128)S(1)}, f32[160,1280]{1,0:T(8,128)S(1)}, f32[160,1280]{1,0:T(8,128)S(1)}, f32[160,1280]{1,0:T(8,128)S(1)}) custom-call(bf16[160,2048]{1,0:T(8,128)(2,1)S(1)} %get-tuple-element.43.refs_0_, bf16[160,2048]{1,0:T(8,128)(2,1)S(1)} %collective-permute-done.refs_1_, bf16[160,2048]{1,0:T(8,128)(2,1)S(1)} %collective-permute-done.2.refs_2_, ...), custom_call_target="tpu_custom_call" | custom-call | flops 1677721600 | bytes 7208960 | tf_op jit(solution)/shard_map/partials/pallas_call | solution.py:152
  59.1 20.2 %collective-permute-done.4.refs_1_ = bf16[512,1024]{1,0:T(8,128)(2,1)S(1)} collective-permute-done((bf16[512,1024]{1,0:T(8,128)(2,1)S(1)}, bf16[512,1024]{1,0:T(8,128)(2,1)S(1)}, u32[]{:S(2)}, u32[]{:S(2)}) %collective-permute-start.4) | collective-permute-done | bytes 1048608 | tf_op jit(solution)/shard_map/ppermute | solution.py:23
  79.3 2.0 %collective-permute-done.3.refs_4_ = bf16[512,1280]{1,0:T(8,128)(2,1)S(1)} collective-permute-done((bf16[512,1280]{1,0:T(8,128)(2,1)S(1)}, bf16[512,1280]{1,0:T(8,128)(2,1)S(1)}, u32[]{:S(2)}, u32[]{:S(2)}) %collective-permute-start.3) | collective-permute-done | bytes 1310752 | tf_op jit(solution)/shard_map/ppermute | solution.py:27
  82.0 3.6 %collective-permute-start.12 = (bf16[256,1024]{1,0:T(8,128)(2,1)S(1)}, bf16[256,1024]{1,0:T(8,128)(2,1)S(1)}, u32[]{:S(2)}, u32[]{:S(2)}) collective-permute-start(bf16[256,1024]{1,0:T(8,128)(2,1)S(1)} %slice.36), channel_id=1, source_target_pairs={{0,48},{8,56},{16,0},{24,8},{32,16},{40,24},{48,32},{56,40},{64,11... | collective-permute-start | bytes 1572872 | tf_op jit(solution)/shard_map/ppermute | solution.py:23
  85.8 3.5 %partials_rest.1 = (f32[160,1280]{1,0:T(8,128)S(1)}, bf16[160,1280]{1,0:T(8,128)(2,1)S(1)}, bf16[160,1280]{1,0:T(8,128)(2,1)S(1)}, bf16[160,1280]{1,0:T(8,128)(2,1)S(1)}) custom-call(bf16[160,2048]{1,0:T(8,128)(2,1)S(1)} %get-tuple-element.43.refs_0_, bf16[160,2048]{1,0:T(8,128)(2,1)S(1)} %collective-permute-done.refs_1_, ...), custom_call_target="tpu_custom_call" | custom-call | flops 1677721600 | bytes 7208960 | tf_op jit(solution)/shard_map/partials_rest/pallas_call | solution.py:152
  89.3 3.3 %collective-permute-start.8 = (bf16[160,1280]{1,0:T(8,128)(2,1)S(1)}, bf16[160,1280]{1,0:T(8,128)(2,1)S(1)}, u32[]{:S(2)}, u32[]{:S(2)}) collective-permute-start(bf16[160,1280]{1,0:T(8,128)(2,1)S(1)} %get-tuple-element.62), channel_id=1, source_target_pairs={{0,48},{8,56},{16,0},{24,8},{32,16},{40,24},{48,32},{56,40},{64,11... | collective-permute-start | bytes 1228808 | tf_op jit(solution)/shard_map/ppermute | solution.py:23
  92.5 5.4 %collective-permute-done.12.refs_4_ = bf16[256,1024]{1,0:T(8,128)(2,1)S(1)} collective-permute-done((bf16[256,1024]{1,0:T(8,128)(2,1)S(1)}, bf16[256,1024]{1,0:T(8,128)(2,1)S(1)}, u32[]{:S(2)}, u32[]{:S(2)}) %collective-permute-start.12) | collective-permute-done | bytes 524320 | tf_op jit(solution)/shard_map/ppermute | solution.py:23
  97.9 12.6 %collective-permute-done.13.refs_5_ = bf16[256,1024]{1,0:T(8,128)(2,1)S(1)} collective-permute-done((bf16[256,1024]{1,0:T(8,128)(2,1)S(1)}, bf16[256,1024]{1,0:T(8,128)(2,1)S(1)}, u32[]{:S(2)}, u32[]{:S(2)}) %collective-permute-start.13) | collective-permute-done | bytes 524320 | tf_op jit(solution)/shard_map/ppermute | solution.py:23
  110.5 4.2 %collective-permute-done.8.p1 = bf16[160,1280]{1,0:T(8,128)(2,1)S(1)} collective-permute-done((bf16[160,1280]{1,0:T(8,128)(2,1)S(1)}, bf16[160,1280]{1,0:T(8,128)(2,1)S(1)}, u32[]{:S(2)}, u32[]{:S(2)}) %collective-permute-start.8) | collective-permute-done | bytes 409632 | tf_op jit(solution)/shard_map/ppermute | solution.py:23
  114.8 3.5 %collective-permute-done.10.p3 = bf16[160,1280]{1,0:T(8,128)(2,1)S(1)} collective-permute-done((bf16[160,1280]{1,0:T(8,128)(2,1)S(1)}, bf16[160,1280]{1,0:T(8,128)(2,1)S(1)}, u32[]{:S(2)}, u32[]{:S(2)}) %collective-permute-start.10) | collective-permute-done | bytes 409632 | tf_op jit(solution)/shard_map/ppermute | solution.py:23
  118.3 3.2 %collective-permute-start.18 = (bf16[512,1024]{1,0:T(8,128)(2,1)S(1)}, bf16[512,1024]{1,0:T(8,128)(2,1)S(1)}, u32[]{:S(2)}, u32[]{:S(2)}) collective-permute-start(bf16[512,1024]{1,0:T(8,128)(2,1)S(1)} %collective-permute-done.14.refs_3_), channel_id=1, source_target_pairs={{0,48},{8,56},{16,0},{24,8},{32,16},{40,24},{48,32},{56,40},{64,11... | collective-permute-start | bytes 3145736 | tf_op jit(solution)/shard_map/ppermute | solution.py:23
  123.6 10.7 %attention.1.mixed_ref = bf16[160,1024]{1,0:T(8,128)(2,1)S(1)} custom-call(s32[80]{0:T(128)S(1)} %copy-done.2, f32[160,1280]{1,0:T(8,128)S(1)} %get-tuple-element.61.p0, bf16[160,1280]{1,0:T(8,128)(2,1)S(1)} %collective-permute-done.8.p1, bf16[160,1280]{1,0:T(8,128)(2,1)S(1)} %collective-permute-done.9.p2, bf16[160,1280]{1,0:T(8,128)(2,1)S(1)} %collective-permute-done.10.p3, ...), custom_call_target="tpu_custom_call" | custom-call | flops 167772160 | bytes 41943040 | tf_op jit(solution)/shard_map/attention/pallas_call | solution.py:376
  136.4 8.7 %collective-permute-done.16.refs_7_ = bf16[256,1024]{1,0:T(8,128)(2,1)S(1)} collective-permute-done((bf16[256,1024]{1,0:T(8,128)(2,1)S(1)}, bf16[256,1024]{1,0:T(8,128)(2,1)S(1)}, u32[]{:S(2)}, u32[]{:S(2)}) %collective-permute-start.16) | collective-permute-done | bytes 524320 | tf_op jit(solution)/shard_map/ppermute | solution.py:27
  145.1 2.4 %terms.2 = bf16[4096,256]{1,0:T(8,128)(2,1)S(1)} custom-call(bf16[160,1024]{1,0:T(8,128)(2,1)S(1)} %collective-permute-done.11.mixed_ref, bf16[512,1024]{1,0:T(8,128)(2,1)S(1)} %slice.34.refs_0_, bf16[512,1024]{1,0:T(8,128)(2,1)S(1)} %collective-permute-done.4.refs_1_, bf16[512,1024]{1,0:T(8,128)(2,1)S(1)} %collective-permute-done.5.refs_2_, ...), custom_call_target="tpu_custom_call" | custom-call | flops 1342177280 | bytes 10027008 | tf_op jit(solution)/shard_map/terms/pallas_call | solution.py:198
  147.7 2.4 %terms.3.refs_0_ = bf16[4096,256]{1,0:T(8,128)(2,1)S(1)} custom-call(bf16[160,1024]{1,0:T(8,128)(2,1)S(1)} %attention.1.mixed_ref, bf16[512,1024]{1,0:T(8,128)(2,1)S(1)} %slice.34.refs_0_, bf16[512,1024]{1,0:T(8,128)(2,1)S(1)} %collective-permute-done.4.refs_1_, bf16[512,1024]{1,0:T(8,128)(2,1)S(1)} %collective-permute-done.5.refs_2_, ...), custom_call_target="tpu_custom_call" | custom-call | flops 1342177280 | bytes 10027008 | tf_op jit(solution)/shard_map/terms/pallas_call | solution.py:198
  151.8 2.9 %place.1 = (bf16[2,80,1024]{2,1,0:T(8,128)(2,1)S(1)}, bf16[2,80,1024]{2,1,0:T(8,128)(2,1)S(1)}, bf16[2,80,1024]{2,1,0:T(8,128)(2,1)S(1)}, bf16[2,80,1024]{2,1,0:...) custom-call(s32[2,128]{1,0:T(2,128)S(1)} %copy-done.1, ...), custom_call_target="tpu_custom_call" | custom-call | bytes 5242880 | tf_op jit(solution)/shard_map/place/pallas_call | solution.py:247
  154.7 3.0 %collective-permute-start.22 = (bf16[2,80,1024]{2,1,0:T(8,128)(2,1)S(1)}, bf16[2,80,1024]{2,1,0:T(8,128)(2,1)S(1)}, u32[]{:S(2)}, u32[]{:S(2)}) collective-permute-start(bf16[2,80,1024]{2,1,0:T(8,128)(2,1)S(1)} %get-tuple-element.78), channel_id=1, source_target_pairs={{0,6},{1,7},{2,0},{3,1},{4,2},{5,3},{6,4},{7,5},{8,14},{9,15},{10,... | collective-permute-start | bytes 983048 | tf_op jit(solution)/shard_map/ppermute | solution.py:31
  159.5 3.6 %collective-permute-start.24 = (bf16[4,80,1024]{2,1,0:T(8,128)(2,1)S(1)}, bf16[4,80,1024]{2,1,0:T(8,128)(2,1)S(1)}, u32[]{:S(2)}, u32[]{:S(2)}) collective-permute-start(bf16[4,80,1024]{2,1,0:T(8,128)(2,1)S(1)} %get-tuple-element.80), channel_id=1, source_target_pairs={{0,1},{1,0},{2,3},{3,2},{4,5},{5,4},{6,7},{7,6},{8,9},{9,8},{10,11... | collective-permute-start | bytes 1966088 | tf_op jit(solution)/shard_map/ppermute | solution.py:35
  163.0 9.0 %collective-permute-done.22 = bf16[2,80,1024]{2,1,0:T(8,128)(2,1)S(1)} collective-permute-done((bf16[2,80,1024]{2,1,0:T(8,128)(2,1)S(1)}, bf16[2,80,1024]{2,1,0:T(8,128)(2,1)S(1)}, u32[]{:S(2)}, u32[]{:S(2)}) %collective-permute-start.22) | collective-permute-done | bytes 327712 | tf_op jit(solution)/shard_map/ppermute | solution.py:31
  172.0 3.7 %collective-permute-done.20 = bf16[2,80,1024]{2,1,0:T(8,128)(2,1)S(1)} collective-permute-done((bf16[2,80,1024]{2,1,0:T(8,128)(2,1)S(1)}, bf16[2,80,1024]{2,1,0:T(8,128)(2,1)S(1)}, u32[]{:S(2)}, u32[]{:S(2)}) %collective-permute-start.20) | collective-permute-done | bytes 327712 | tf_op jit(solution)/shard_map/ppermute | solution.py:31
  176.0 3.7 %collective-permute-start.23 = (bf16[80,1024]{1,0:T(8,128)(2,1)S(1)}, bf16[80,1024]{1,0:T(8,128)(2,1)S(1)}, u32[]{:S(2)}, u32[]{:S(2)}) collective-permute-start(bf16[80,1024]{1,0:T(8,128)(2,1)S(1)} %fusion.7), channel_id=1, source_target_pairs={{0,1},{1,0},{2,3},{3,2},{4,5},{5,4},{6,7},{7,6},{8,9},{9,8},{10,11... | collective-permute-start | bytes 491528 | tf_op jit(solution)/shard_map/ppermute | solution.py:35
  184.0 3.1 %collective-permute-done.27 = bf16[80,1024]{1,0:T(8,128)(2,1)S(1)} collective-permute-done((bf16[80,1024]{1,0:T(8,128)(2,1)S(1)}, bf16[80,1024]{1,0:T(8,128)(2,1)S(1)}, u32[]{:S(2)}, u32[]{:S(2)}) %collective-permute-start.27) | collective-permute-done | bytes 163872 | tf_op jit(solution)/shard_map/ppermute | solution.py:31
  187.1 1.9 collective-permute-done.26
  189.0 2.0 %collective-permute-done.25 = bf16[80,1024]{1,0:T(8,128)(2,1)S(1)} collective-permute-done((bf16[80,1024]{1,0:T(8,128)(2,1)S(1)}, bf16[80,1024]{1,0:T(8,128)(2,1)S(1)}, u32[]{:S(2)}, u32[]{:S(2)}) %collective-permute-start.25) | collective-permute-done | bytes 163872 | tf_op jit(solution)/shard_map/ppermute | solution.py:31
  (56 shorter events, 20.0 us)
Async XLA Ops:
  4.3 7.3 %copy-start = (bf16[2,80,8192]{2,1,0:T(8,128)(2,1)S(1)}, bf16[2,80,8192]{2,1,0:T(8,128)(2,1)}, u32[]{:S(2)}) copy-start(bf16[2,80,8192]{2,1,0:T(8,128)(2,1)} %param.6) | copy-start | bytes 7864324
  4.3 7.3 %copy-start.1 = (s32[2,128]{1,0:T(2,128)S(1)}, s32[2,128]{1,0:T(2,128)}, u32[]{:S(2)}) copy-start(s32[2,128]{1,0:T(2,128)} %owner_ref.3) | copy-start | bytes 3076
  4.3 44.3 %all-to-all-start = ((bf16[8,64,2304]{2,1,0:T(8,128)(2,1)}), bf16[8,64,2304]{2,1,0:T(8,128)(2,1)}, u32[]{:S(2)}, u32[]{:S(2)}) async-start(bf16[8,64,2304]{2,1,0:T(8,128)(2,1)} %slabs.1), calls=%async_computation | async-start | bytes 4718592 | tf_op jit(solution)/shard_map/all_to_all | solution.py:418
  11.6 10.8 %copy-start.2 = (s32[80]{0:T(128)S(1)}, s32[80]{0:T(128)}, u32[]{:S(2)}) copy-start(s32[80]{0:T(128)} %lengths_ref.1) | copy-start | bytes 964
  16.5 19.0 %collective-permute-start = (bf16[160,2048]{1,0:T(8,128)(2,1)}, bf16[160,2048]{1,0:T(8,128)(2,1)S(1)}, u32[]{:S(2)}, u32[]{:S(2)}) collective-permute-start(bf16[160,2048]{1,0:T(8,128)(2,1)} %get-tuple-element.44), channel_id=1, source_target_pairs={{0,16},{8,24},{16,32},{24,40},{32,48},{40,56},{48,0},{56,8},{64,80... | collective-permute-start | bytes 1966088 | tf_op jit(solution)/shard_map/ppermute | solution.py:23
  18.4 30.2 %collective-permute-start.1 = (bf16[160,2048]{1,0:T(8,128)(2,1)}, bf16[160,2048]{1,0:T(8,128)(2,1)S(1)}, u32[]{:S(2)}, u32[]{:S(2)}) collective-permute-start(bf16[160,2048]{1,0:T(8,128)(2,1)} %get-tuple-element.45), channel_id=1, source_target_pairs={{0,48},{8,56},{16,0},{24,8},{32,16},{40,24},{48,32},{56,40},{64,11... | collective-permute-start | bytes 1966088 | tf_op jit(solution)/shard_map/ppermute | solution.py:23
  20.5 31.7 %collective-permute-start.2 = (bf16[160,2048]{1,0:T(8,128)(2,1)}, bf16[160,2048]{1,0:T(8,128)(2,1)S(1)}, u32[]{:S(2)}, u32[]{:S(2)}) collective-permute-start(bf16[160,2048]{1,0:T(8,128)(2,1)} %get-tuple-element.48), channel_id=1, source_target_pairs={{0,32},{8,40},{16,48},{24,56},{32,0},{40,8},{48,16},{56,24},{64,96... | collective-permute-start | bytes 1966088 | tf_op jit(solution)/shard_map/ppermute | solution.py:23
  50.0 5.9 %collective-permute-start.6 = (bf16[512,1280]{1,0:T(8,128)(2,1)S(1)}, bf16[512,1280]{1,0:T(8,128)(2,1)S(1)}, u32[]{:S(2)}, u32[]{:S(2)}) collective-permute-start(bf16[512,1280]{1,0:T(8,128)(2,1)S(1)} %slice.35.refs_4_), channel_id=1, source_target_pairs={{0,8},{8,0},{16,24},{24,16},{32,40},{40,32},{48,56},{56,48},{64,72... | collective-permute-start | bytes 3932168 | tf_op jit(solution)/shard_map/ppermute | solution.py:27
  50.1 31.2 %collective-permute-start.3 = (bf16[512,1280]{1,0:T(8,128)(2,1)S(1)}, bf16[512,1280]{1,0:T(8,128)(2,1)S(1)}, u32[]{:S(2)}, u32[]{:S(2)}) collective-permute-start(bf16[512,1280]{1,0:T(8,128)(2,1)S(1)} %slice.35.refs_4_), channel_id=1, source_target_pairs={{0,64},{8,72},{16,80},{24,88},{32,96},{40,104},{48,112},{56,120},{... | collective-permute-start | bytes 3932168 | tf_op jit(solution)/shard_map/ppermute | solution.py:27
  52.2 27.1 %collective-permute-start.4 = (bf16[512,1024]{1,0:T(8,128)(2,1)S(1)}, bf16[512,1024]{1,0:T(8,128)(2,1)S(1)}, u32[]{:S(2)}, u32[]{:S(2)}) collective-permute-start(bf16[512,1024]{1,0:T(8,128)(2,1)S(1)} %slice.34.refs_0_), channel_id=1, source_target_pairs={{0,16},{8,24},{16,32},{24,40},{32,48},{40,56},{48,0},{56,8},{64,80... | collective-permute-start | bytes 3145736 | tf_op jit(solution)/shard_map/ppermute | solution.py:23
  52.3 27.0 %collective-permute-start.5 = (bf16[512,1024]{1,0:T(8,128)(2,1)S(1)}, bf16[512,1024]{1,0:T(8,128)(2,1)S(1)}, u32[]{:S(2)}, u32[]{:S(2)}) collective-permute-start(bf16[512,1024]{1,0:T(8,128)(2,1)S(1)} %slice.34.refs_0_), channel_id=1, source_target_pairs={{0,48},{8,56},{16,0},{24,8},{32,16},{40,24},{48,32},{56,40},{64,11... | collective-permute-start | bytes 3145736 | tf_op jit(solution)/shard_map/ppermute | solution.py:23
  81.3 4.5 %collective-permute-start.7 = (bf16[512,1280]{1,0:T(8,128)(2,1)S(1)}, bf16[512,1280]{1,0:T(8,128)(2,1)S(1)}, u32[]{:S(2)}, u32[]{:S(2)}) collective-permute-start(bf16[512,1280]{1,0:T(8,128)(2,1)S(1)} %collective-permute-done.3.refs_4_), channel_id=1, source_target_pairs={{0,8},{8,0},{16,24},{24,16},{32,40},{40,32},{48,56},{56,48},{64,72... | collective-permute-start | bytes 3932168 | tf_op jit(solution)/shard_map/ppermute | solution.py:27
  81.3 29.2 %collective-permute-start.14 = (bf16[512,1024]{1,0:T(8,128)(2,1)S(1)}, bf16[512,1024]{1,0:T(8,128)(2,1)S(1)}, u32[]{:S(2)}, u32[]{:S(2)}) collective-permute-start(bf16[512,1024]{1,0:T(8,128)(2,1)S(1)} %slice.34.refs_0_), channel_id=1, source_target_pairs={{0,64},{8,72},{16,80},{24,88},{32,96},{40,104},{48,112},{56,120},{... | collective-permute-start | bytes 3145736 | tf_op jit(solution)/shard_map/ppermute | solution.py:27
  82.0 15.9 %collective-permute-start.12 = (bf16[256,1024]{1,0:T(8,128)(2,1)S(1)}, bf16[256,1024]{1,0:T(8,128)(2,1)S(1)}, u32[]{:S(2)}, u32[]{:S(2)}) collective-permute-start(bf16[256,1024]{1,0:T(8,128)(2,1)S(1)} %slice.36), channel_id=1, source_target_pairs={{0,48},{8,56},{16,0},{24,8},{32,16},{40,24},{48,32},{56,40},{64,11... | collective-permute-start | bytes 1572872 | tf_op jit(solution)/shard_map/ppermute | solution.py:23
  85.7 24.9 %collective-permute-start.13 = (bf16[256,1024]{1,0:T(8,128)(2,1)S(1)}, bf16[256,1024]{1,0:T(8,128)(2,1)S(1)}, u32[]{:S(2)}, u32[]{:S(2)}) collective-permute-start(bf16[256,1024]{1,0:T(8,128)(2,1)S(1)} %slice.37), channel_id=1, source_target_pairs={{0,16},{8,24},{16,32},{24,40},{32,48},{40,56},{48,0},{56,8},{64,80... | collective-permute-start | bytes 1572872 | tf_op jit(solution)/shard_map/ppermute | solution.py:23
  89.3 25.5 %collective-permute-start.8 = (bf16[160,1280]{1,0:T(8,128)(2,1)S(1)}, bf16[160,1280]{1,0:T(8,128)(2,1)S(1)}, u32[]{:S(2)}, u32[]{:S(2)}) collective-permute-start(bf16[160,1280]{1,0:T(8,128)(2,1)S(1)} %get-tuple-element.62), channel_id=1, source_target_pairs={{0,48},{8,56},{16,0},{24,8},{32,16},{40,24},{48,32},{56,40},{64,11... | collective-permute-start | bytes 1228808 | tf_op jit(solution)/shard_map/ppermute | solution.py:23
  92.5 22.3 %collective-permute-start.9 = (bf16[160,1280]{1,0:T(8,128)(2,1)S(1)}, bf16[160,1280]{1,0:T(8,128)(2,1)S(1)}, u32[]{:S(2)}, u32[]{:S(2)}) collective-permute-start(bf16[160,1280]{1,0:T(8,128)(2,1)S(1)} %get-tuple-element.63), channel_id=1, source_target_pairs={{0,32},{8,40},{16,48},{24,56},{32,0},{40,8},{48,16},{56,24},{64,96... | collective-permute-start | bytes 1228808 | tf_op jit(solution)/shard_map/ppermute | solution.py:23
  97.9 20.4 %collective-permute-start.10 = (bf16[160,1280]{1,0:T(8,128)(2,1)S(1)}, bf16[160,1280]{1,0:T(8,128)(2,1)S(1)}, u32[]{:S(2)}, u32[]{:S(2)}) collective-permute-start(bf16[160,1280]{1,0:T(8,128)(2,1)S(1)} %get-tuple-element.64), channel_id=1, source_target_pairs={{0,16},{8,24},{16,32},{24,40},{32,48},{40,56},{48,0},{56,8},{64,80... | collective-permute-start | bytes 1228808 | tf_op jit(solution)/shard_map/ppermute | solution.py:23
  118.3 26.8 %collective-permute-start.17 = (bf16[512,1024]{1,0:T(8,128)(2,1)S(1)}, bf16[512,1024]{1,0:T(8,128)(2,1)S(1)}, u32[]{:S(2)}, u32[]{:S(2)}) collective-permute-start(bf16[512,1024]{1,0:T(8,128)(2,1)S(1)} %collective-permute-done.14.refs_3_), channel_id=1, source_target_pairs={{0,16},{8,24},{16,32},{24,40},{32,48},{40,56},{48,0},{56,8},{64,80... | collective-permute-start | bytes 3145736 | tf_op jit(solution)/shard_map/ppermute | solution.py:23
  118.3 26.8 %collective-permute-start.18 = (bf16[512,1024]{1,0:T(8,128)(2,1)S(1)}, bf16[512,1024]{1,0:T(8,128)(2,1)S(1)}, u32[]{:S(2)}, u32[]{:S(2)}) collective-permute-start(bf16[512,1024]{1,0:T(8,128)(2,1)S(1)} %collective-permute-done.14.refs_3_), channel_id=1, source_target_pairs={{0,48},{8,56},{16,0},{24,8},{32,16},{40,24},{48,32},{56,40},{64,11... | collective-permute-start | bytes 3145736 | tf_op jit(solution)/shard_map/ppermute | solution.py:23
  121.5 14.9 %collective-permute-start.15 = (bf16[256,1024]{1,0:T(8,128)(2,1)S(1)}, bf16[256,1024]{1,0:T(8,128)(2,1)S(1)}, u32[]{:S(2)}, u32[]{:S(2)}) collective-permute-start(bf16[256,1024]{1,0:T(8,128)(2,1)S(1)} %collective-permute-done.12.refs_4_), channel_id=1, source_target_pairs={{0,64},{8,72},{16,80},{24,88},{32,96},{40,104},{48,112},{56,120},{... | collective-permute-start | bytes 1572872 | tf_op jit(solution)/shard_map/ppermute | solution.py:27
  122.9 22.2 %collective-permute-start.16 = (bf16[256,1024]{1,0:T(8,128)(2,1)S(1)}, bf16[256,1024]{1,0:T(8,128)(2,1)S(1)}, u32[]{:S(2)}, u32[]{:S(2)}) collective-permute-start(bf16[256,1024]{1,0:T(8,128)(2,1)S(1)} %collective-permute-done.13.refs_5_), channel_id=1, source_target_pairs={{0,64},{8,72},{16,80},{24,88},{32,96},{40,104},{48,112},{56,120},{... | collective-permute-start | bytes 1572872 | tf_op jit(solution)/shard_map/ppermute | solution.py:27
  134.3 10.9 %collective-permute-start.11 = (bf16[160,1024]{1,0:T(8,128)(2,1)S(1)}, bf16[160,1024]{1,0:T(8,128)(2,1)S(1)}, u32[]{:S(2)}, u32[]{:S(2)}) collective-permute-start(bf16[160,1024]{1,0:T(8,128)(2,1)S(1)} %attention.1.mixed_ref), channel_id=1, source_target_pairs={{0,8},{8,0},{16,24},{24,16},{32,40},{40,32},{48,56},{56,48},{64,72... | collective-permute-start | bytes 983048 | tf_op jit(solution)/shard_map/ppermute | solution.py:27
  147.6 4.2 %collective-permute-start.19 = (bf16[4096,256]{1,0:T(8,128)(2,1)S(1)}, bf16[4096,256]{1,0:T(8,128)(2,1)S(1)}, u32[]{:S(2)}, u32[]{:S(2)}) collective-permute-start(bf16[4096,256]{1,0:T(8,128)(2,1)S(1)} %terms.2), channel_id=1, source_target_pairs={{0,8},{8,0},{16,24},{24,16},{32,40},{40,32},{48,56},{56,48},{64,72... | collective-permute-start | bytes 6291464 | tf_op jit(solution)/shard_map/ppermute | solution.py:27
  154.7 17.3 %collective-permute-start.22 = (bf16[2,80,1024]{2,1,0:T(8,128)(2,1)S(1)}, bf16[2,80,1024]{2,1,0:T(8,128)(2,1)S(1)}, u32[]{:S(2)}, u32[]{:S(2)}) collective-permute-start(bf16[2,80,1024]{2,1,0:T(8,128)(2,1)S(1)} %get-tuple-element.78), channel_id=1, source_target_pairs={{0,6},{1,7},{2,0},{3,1},{4,2},{5,3},{6,4},{7,5},{8,14},{9,15},{10,... | collective-permute-start | bytes 983048 | tf_op jit(solution)/shard_map/ppermute | solution.py:31
  157.7 14.3 %collective-permute-start.21 = (bf16[2,80,1024]{2,1,0:T(8,128)(2,1)S(1)}, bf16[2,80,1024]{2,1,0:T(8,128)(2,1)S(1)}, u32[]{:S(2)}, u32[]{:S(2)}) collective-permute-start(bf16[2,80,1024]{2,1,0:T(8,128)(2,1)S(1)} %get-tuple-element.77), channel_id=1, source_target_pairs={{0,4},{1,5},{2,6},{3,7},{4,0},{5,1},{6,2},{7,3},{8,12},{9,13},{10,... | collective-permute-start | bytes 983048 | tf_op jit(solution)/shard_map/ppermute | solution.py:31
  158.6 17.1 %collective-permute-start.20 = (bf16[2,80,1024]{2,1,0:T(8,128)(2,1)S(1)}, bf16[2,80,1024]{2,1,0:T(8,128)(2,1)S(1)}, u32[]{:S(2)}, u32[]{:S(2)}) collective-permute-start(bf16[2,80,1024]{2,1,0:T(8,128)(2,1)S(1)} %get-tuple-element.76), channel_id=1, source_target_pairs={{0,2},{1,3},{2,4},{3,5},{4,6},{5,7},{6,0},{7,1},{8,10},{9,11},{10,... | collective-permute-start | bytes 983048 | tf_op jit(solution)/shard_map/ppermute | solution.py:31
  159.5 20.2 %collective-permute-start.24 = (bf16[4,80,1024]{2,1,0:T(8,128)(2,1)S(1)}, bf16[4,80,1024]{2,1,0:T(8,128)(2,1)S(1)}, u32[]{:S(2)}, u32[]{:S(2)}) collective-permute-start(bf16[4,80,1024]{2,1,0:T(8,128)(2,1)S(1)} %get-tuple-element.80), channel_id=1, source_target_pairs={{0,1},{1,0},{2,3},{3,2},{4,5},{5,4},{6,7},{7,6},{8,9},{9,8},{10,11... | collective-permute-start | bytes 1966088 | tf_op jit(solution)/shard_map/ppermute | solution.py:35
  176.0 8.0 %collective-permute-start.23 = (bf16[80,1024]{1,0:T(8,128)(2,1)S(1)}, bf16[80,1024]{1,0:T(8,128)(2,1)S(1)}, u32[]{:S(2)}, u32[]{:S(2)}) collective-permute-start(bf16[80,1024]{1,0:T(8,128)(2,1)S(1)} %fusion.7), channel_id=1, source_target_pairs={{0,1},{1,0},{2,3},{3,2},{4,5},{5,4},{6,7},{7,6},{8,9},{9,8},{10,11... | collective-permute-start | bytes 491528 | tf_op jit(solution)/shard_map/ppermute | solution.py:35
  180.0 7.2 %collective-permute-start.27 = (bf16[80,1024]{1,0:T(8,128)(2,1)S(1)}, bf16[80,1024]{1,0:T(8,128)(2,1)S(1)}, u32[]{:S(2)}, u32[]{:S(2)}) collective-permute-start(bf16[80,1024]{1,0:T(8,128)(2,1)S(1)} %get-tuple-element.84), channel_id=1, source_target_pairs={{0,6},{1,7},{2,0},{3,1},{4,2},{5,3},{6,4},{7,5},{8,14},{9,15},{10,... | collective-permute-start | bytes 491528 | tf_op jit(solution)/shard_map/ppermute | solution.py:31
  180.6 8.4 %collective-permute-start.26 = (bf16[80,1024]{1,0:T(8,128)(2,1)S(1)}, bf16[80,1024]{1,0:T(8,128)(2,1)S(1)}, u32[]{:S(2)}, u32[]{:S(2)}) collective-permute-start(bf16[80,1024]{1,0:T(8,128)(2,1)S(1)} %get-tuple-element.85), channel_id=1, source_target_pairs={{0,4},{1,5},{2,6},{3,7},{4,0},{5,1},{6,2},{7,3},{8,12},{9,13},{10,... | collective-permute-start | bytes 491528 | tf_op jit(solution)/shard_map/ppermute | solution.py:31
  181.5 9.5 %collective-permute-start.25 = (bf16[80,1024]{1,0:T(8,128)(2,1)S(1)}, bf16[80,1024]{1,0:T(8,128)(2,1)S(1)}, u32[]{:S(2)}, u32[]{:S(2)}) collective-permute-start(bf16[80,1024]{1,0:T(8,128)(2,1)S(1)} %get-tuple-element.83), channel_id=1, source_target_pairs={{0,2},{1,3},{2,4},{3,5},{4,6},{5,7},{6,0},{7,1},{8,10},{9,11},{10,... | collective-permute-start | bytes 491528 | tf_op jit(solution)/shard_map/ppermute | solution.py:31

commit v11 on v10

--- a/solution.py
+++ b/solution.py
@@ -436,7 +436,7 @@
     sums = [sums[0]] + [z_shift(sums[k], -k) for k in range(1, NZ)]
     far_a, far_b, across = after((far_a, far_b, across))
     across_far_a, across_far_b = flip(far_a, 8), flip(far_b, 8)
-    (across,) = after((across,), *sums)
+    (across,) = after((across,), sums[1], sums[2])
     across_below, across_above = z_shift(across, 1), z_shift(across, -1)
     mixed = attention(sums, cos, sin, cache, lengths)
 

time: 193 us -> 211 us (1.093)
  waiting for transfers between devices: 107 us -> 124 us
    ppermute x12, waiting for transfers between devices: 71.6 us -> 97.5 us  [z_shift(): return lax.ppermute(value, 'fsdp', pairs)]
    ppermute x8, waiting for transfers between devices: 14.3 us -> 5.22 us  [flip(): return lax.ppermute(value, 'fsdp', [(f, f ^ bit) for f in range(16)])]
  transfers between devices with their start and end apart: 29 -> 29, of which waited for: 17 -> 16; matrix products, arithmetic and copies ran while one was open for 2% -> 2% of each run, Pallas kernels for 13% -> 12%
where the time goes in v11:
time: 211 us; the launch traced here: 209 us
  waiting for transfers between devices  124 us (59%)
  starting transfers between devices  45.9 us (22%)
  Pallas kernels  34.3 us (16%)
  local copies, waits for them, and re-layouts  2.91 us (1%)
    ppermute x12, waiting for transfers between devices, z_shift(): return lax.ppermute(value, 'fsdp', pairs)  97.5 us
    ppermute x12, starting transfers between devices, z_shift(): return lax.ppermute(value, 'fsdp', pairs)  20.3 us
    ppermute x6, waiting for transfers between devices, x_shift(): lax.ppermute(value, 'tp', [(t, (t // 2 + k) % NX * 2 + t % 2) for t in ra...  19.6 us
    pallas_call x1, Pallas kernels, attention(): pl.pallas_call(attention_kernel, grid=(rows // GROUP,), out_shape=jax.Sha...  10.7 us
    all_to_all x1, starting transfers between devices, body(): both = lax.all_to_all(copy, 'tp', split_axis=0, concat_axis=0, tiled=True)  7.28 us
    ppermute x2, starting transfers between devices, y_flip(): return lax.ppermute(value, 'tp', [(t, t ^ 1) for t in range(2 * NX)])  7.22 us
    ppermute x6, starting transfers between devices, x_shift(): lax.ppermute(value, 'tp', [(t, (t // 2 + k) % NX * 2 + t % 2) for t in ra...  7.07 us
    pallas_call x2, Pallas kernels, partials(): pl.pallas_call(functools.partial(partial_kernel, begun), grid=(cols // ti...  6.69 us
  transfers between devices with their start and end apart: 29, of which 16 were waited for; matrix products, arithmetic and copies ran while one was open for 2% of the time, Pallas kernels for 12%

profile of v11, /device:TPU:0, one launch (start us, length us, event | category | flops | bytes accessed | tf_op | source)
XLA Modules:
  0.0 209.3 jit_solution(12328602967420985888)
XLA Ops:
  0.0 4.3 %slabs.1 = bf16[8,64,2304]{2,1,0:T(8,128)(2,1)} custom-call(f32[64,10240]{1,0:T(8,128)} %value.1, f32[64,10240]{1,0:T(8,128)} %value.1, f32[64,10240]{1,0:T(8,128)} %value.1, f32[64,8192]{1,0:T(8,128)} %back.1), custom_call_target="tpu_custom_call" | custom-call | bytes 7077888 | tf_op jit(solution)/shard_map/slabs/pallas_call | solution.py:56
  4.3 7.3 %all-to-all-start = ((bf16[8,64,2304]{2,1,0:T(8,128)(2,1)}), bf16[8,64,2304]{2,1,0:T(8,128)(2,1)}, u32[]{:S(2)}, u32[]{:S(2)}) async-start(bf16[8,64,2304]{2,1,0:T(8,128)(2,1)} %slabs.1), calls=%async_computation | async-start | bytes 4718592 | tf_op jit(solution)/shard_map/all_to_all | solution.py:418
  11.6 4.8 %shuffle.1 = (bf16[160,2048]{1,0:T(8,128)(2,1)S(1)}, bf16[160,2048]{1,0:T(8,128)(2,1)}, bf16[160,2048]{1,0:T(8,128)(2,1)}, bf16[160,2048]{1,0:T(8,128)(2,1)}) custom-call(s32[2,128]{1,0:T(2,128)S(1)} %copy-done.1, bf16[160,8192]{1,0:T(8,128)(2,1)S(1)} %bitcast.34), custom_call_target="tpu_custom_call" | custom-call | flops 10485760 | bytes 5242880 | tf_op jit(solution)/shard_map/shuffle/pallas_call | solution.py:105
  16.5 1.9 collective-permute-start
  18.4 2.1 %collective-permute-start.1 = (bf16[160,2048]{1,0:T(8,128)(2,1)}, bf16[160,2048]{1,0:T(8,128)(2,1)S(1)}, u32[]{:S(2)}, u32[]{:S(2)}) collective-permute-start(bf16[160,2048]{1,0:T(8,128)(2,1)} %get-tuple-element.45), channel_id=1, source_target_pairs={{0,48},{8,56},{16,0},{24,8},{32,16},{40,24},{48,32},{56,40},{64,11... | collective-permute-start | bytes 1966088 | tf_op jit(solution)/shard_map/ppermute | solution.py:23
  20.5 1.9 collective-permute-start.2
  23.0 12.5 %collective-permute-done.refs_1_ = bf16[160,2048]{1,0:T(8,128)(2,1)S(1)} collective-permute-done((bf16[160,2048]{1,0:T(8,128)(2,1)}, bf16[160,2048]{1,0:T(8,128)(2,1)S(1)}, u32[]{:S(2)}, u32[]{:S(2)}) %collective-permute-start) | collective-permute-done | bytes 655392 | tf_op jit(solution)/shard_map/ppermute | solution.py:23
  35.4 13.2 %collective-permute-done.1.refs_3_ = bf16[160,2048]{1,0:T(8,128)(2,1)S(1)} collective-permute-done((bf16[160,2048]{1,0:T(8,128)(2,1)}, bf16[160,2048]{1,0:T(8,128)(2,1)S(1)}, u32[]{:S(2)}, u32[]{:S(2)}) %collective-permute-start.1) | collective-permute-done | bytes 655392 | tf_op jit(solution)/shard_map/ppermute | solution.py:23
  52.3 3.6 %collective-permute-start.5 = (bf16[512,1024]{1,0:T(8,128)(2,1)S(1)}, bf16[512,1024]{1,0:T(8,128)(2,1)S(1)}, u32[]{:S(2)}, u32[]{:S(2)}) collective-permute-start(bf16[512,1024]{1,0:T(8,128)(2,1)S(1)} %slice.34.refs_0_), channel_id=1, source_target_pairs={{0,48},{8,56},{16,0},{24,8},{32,16},{40,24},{48,32},{56,40},{64,11... | collective-permute-start | bytes 3145736 | tf_op jit(solution)/shard_map/ppermute | solution.py:23
  55.9 3.2 %partials.1 = (f32[160,1280]{1,0:T(8,128)S(1)}, f32[160,1280]{1,0:T(8,128)S(1)}, f32[160,1280]{1,0:T(8,128)S(1)}, f32[160,1280]{1,0:T(8,128)S(1)}) custom-call(bf16[160,2048]{1,0:T(8,128)(2,1)S(1)} %get-tuple-element.43.refs_0_, bf16[160,2048]{1,0:T(8,128)(2,1)S(1)} %collective-permute-done.refs_1_, bf16[160,2048]{1,0:T(8,128)(2,1)S(1)} %collective-permute-done.2.refs_2_, ...), custom_call_target="tpu_custom_call" | custom-call | flops 1677721600 | bytes 7208960 | tf_op jit(solution)/shard_map/partials/pallas_call | solution.py:152
  59.1 20.2 %collective-permute-done.4.refs_1_ = bf16[512,1024]{1,0:T(8,128)(2,1)S(1)} collective-permute-done((bf16[512,1024]{1,0:T(8,128)(2,1)S(1)}, bf16[512,1024]{1,0:T(8,128)(2,1)S(1)}, u32[]{:S(2)}, u32[]{:S(2)}) %collective-permute-start.4) | collective-permute-done | bytes 1048608 | tf_op jit(solution)/shard_map/ppermute | solution.py:23
  79.3 2.0 collective-permute-done.3.refs_4_
  82.0 3.6 %collective-permute-start.12 = (bf16[256,1024]{1,0:T(8,128)(2,1)S(1)}, bf16[256,1024]{1,0:T(8,128)(2,1)S(1)}, u32[]{:S(2)}, u32[]{:S(2)}) collective-permute-start(bf16[256,1024]{1,0:T(8,128)(2,1)S(1)} %slice.36), channel_id=1, source_target_pairs={{0,48},{8,56},{16,0},{24,8},{32,16},{40,24},{48,32},{56,40},{64,11... | collective-permute-start | bytes 1572872 | tf_op jit(solution)/shard_map/ppermute | solution.py:23
  85.8 3.5 %partials_rest.1 = (f32[160,1280]{1,0:T(8,128)S(1)}, bf16[160,1280]{1,0:T(8,128)(2,1)S(1)}, bf16[160,1280]{1,0:T(8,128)(2,1)S(1)}, bf16[160,1280]{1,0:T(8,128)(2,1)S(1)}) custom-call(bf16[160,2048]{1,0:T(8,128)(2,1)S(1)} %get-tuple-element.43.refs_0_, bf16[160,2048]{1,0:T(8,128)(2,1)S(1)} %collective-permute-done.refs_1_, ...), custom_call_target="tpu_custom_call" | custom-call | flops 1677721600 | bytes 7208960 | tf_op jit(solution)/shard_map/partials_rest/pallas_call | solution.py:152
  89.3 3.3 %collective-permute-start.8 = (bf16[160,1280]{1,0:T(8,128)(2,1)S(1)}, bf16[160,1280]{1,0:T(8,128)(2,1)S(1)}, u32[]{:S(2)}, u32[]{:S(2)}) collective-permute-start(bf16[160,1280]{1,0:T(8,128)(2,1)S(1)} %get-tuple-element.62), channel_id=1, source_target_pairs={{0,48},{8,56},{16,0},{24,8},{32,16},{40,24},{48,32},{56,40},{64,11... | collective-permute-start | bytes 1228808 | tf_op jit(solution)/shard_map/ppermute | solution.py:23
  92.5 5.4 %collective-permute-done.12.refs_4_ = bf16[256,1024]{1,0:T(8,128)(2,1)S(1)} collective-permute-done((bf16[256,1024]{1,0:T(8,128)(2,1)S(1)}, bf16[256,1024]{1,0:T(8,128)(2,1)S(1)}, u32[]{:S(2)}, u32[]{:S(2)}) %collective-permute-start.12) | collective-permute-done | bytes 524320 | tf_op jit(solution)/shard_map/ppermute | solution.py:23
  97.9 11.6 %collective-permute-done.13.refs_5_ = bf16[256,1024]{1,0:T(8,128)(2,1)S(1)} collective-permute-done((bf16[256,1024]{1,0:T(8,128)(2,1)S(1)}, bf16[256,1024]{1,0:T(8,128)(2,1)S(1)}, u32[]{:S(2)}, u32[]{:S(2)}) %collective-permute-start.13) | collective-permute-done | bytes 524320 | tf_op jit(solution)/shard_map/ppermute | solution.py:23
  109.5 5.3 %collective-permute-done.8.p1 = bf16[160,1280]{1,0:T(8,128)(2,1)S(1)} collective-permute-done((bf16[160,1280]{1,0:T(8,128)(2,1)S(1)}, bf16[160,1280]{1,0:T(8,128)(2,1)S(1)}, u32[]{:S(2)}, u32[]{:S(2)}) %collective-permute-start.8) | collective-permute-done | bytes 409632 | tf_op jit(solution)/shard_map/ppermute | solution.py:23
  116.4 2.1 %collective-permute-start.18 = (bf16[512,1024]{1,0:T(8,128)(2,1)S(1)}, bf16[512,1024]{1,0:T(8,128)(2,1)S(1)}, u32[]{:S(2)}, u32[]{:S(2)}) collective-permute-start(bf16[512,1024]{1,0:T(8,128)(2,1)S(1)} %collective-permute-done.14.refs_3_), channel_id=1, source_target_pairs={{0,48},{8,56},{16,0},{24,8},{32,16},{40,24},{48,32},{56,40},{64,11... | collective-permute-start | bytes 3145736 | tf_op jit(solution)/shard_map/ppermute | solution.py:23
  120.5 29.5 %collective-permute-done.10.p3 = bf16[160,1280]{1,0:T(8,128)(2,1)S(1)} collective-permute-done((bf16[160,1280]{1,0:T(8,128)(2,1)S(1)}, bf16[160,1280]{1,0:T(8,128)(2,1)S(1)}, u32[]{:S(2)}, u32[]{:S(2)}) %collective-permute-start.10) | collective-permute-done | bytes 409632 | tf_op jit(solution)/shard_map/ppermute | solution.py:23
  150.0 10.7 %attention.1.mixed_ref = bf16[160,1024]{1,0:T(8,128)(2,1)S(1)} custom-call(s32[80]{0:T(128)S(1)} %copy-done.2, f32[160,1280]{1,0:T(8,128)S(1)} %get-tuple-element.61.p0, bf16[160,1280]{1,0:T(8,128)(2,1)S(1)} %collective-permute-done.8.p1, bf16[160,1280]{1,0:T(8,128)(2,1)S(1)} %collective-permute-done.9.p2, bf16[160,1280]{1,0:T(8,128)(2,1)S(1)} %collective-permute-done.10.p3, ...), custom_call_target="tpu_custom_call" | custom-call | flops 167772160 | bytes 41943040 | tf_op jit(solution)/shard_map/attention/pallas_call | solution.py:376
  162.6 2.4 %terms.2 = bf16[4096,256]{1,0:T(8,128)(2,1)S(1)} custom-call(bf16[160,1024]{1,0:T(8,128)(2,1)S(1)} %collective-permute-done.11.mixed_ref, bf16[512,1024]{1,0:T(8,128)(2,1)S(1)} %slice.34.refs_0_, bf16[512,1024]{1,0:T(8,128)(2,1)S(1)} %collective-permute-done.4.refs_1_, bf16[512,1024]{1,0:T(8,128)(2,1)S(1)} %collective-permute-done.5.refs_2_, ...), custom_call_target="tpu_custom_call" | custom-call | flops 1342177280 | bytes 10027008 | tf_op jit(solution)/shard_map/terms/pallas_call | solution.py:198
  165.2 2.4 %terms.3.refs_0_ = bf16[4096,256]{1,0:T(8,128)(2,1)S(1)} custom-call(bf16[160,1024]{1,0:T(8,128)(2,1)S(1)} %attention.1.mixed_ref, bf16[512,1024]{1,0:T(8,128)(2,1)S(1)} %slice.34.refs_0_, bf16[512,1024]{1,0:T(8,128)(2,1)S(1)} %collective-permute-done.4.refs_1_, bf16[512,1024]{1,0:T(8,128)(2,1)S(1)} %collective-permute-done.5.refs_2_, ...), custom_call_target="tpu_custom_call" | custom-call | flops 1342177280 | bytes 10027008 | tf_op jit(solution)/shard_map/terms/pallas_call | solution.py:198
  169.3 2.9 %place.1 = (bf16[2,80,1024]{2,1,0:T(8,128)(2,1)S(1)}, bf16[2,80,1024]{2,1,0:T(8,128)(2,1)S(1)}, bf16[2,80,1024]{2,1,0:T(8,128)(2,1)S(1)}, bf16[2,80,1024]{2,1,0:...) custom-call(s32[2,128]{1,0:T(2,128)S(1)} %copy-done.1, ...), custom_call_target="tpu_custom_call" | custom-call | bytes 5242880 | tf_op jit(solution)/shard_map/place/pallas_call | solution.py:247
  172.2 3.0 %collective-permute-start.22 = (bf16[2,80,1024]{2,1,0:T(8,128)(2,1)S(1)}, bf16[2,80,1024]{2,1,0:T(8,128)(2,1)S(1)}, u32[]{:S(2)}, u32[]{:S(2)}) collective-permute-start(bf16[2,80,1024]{2,1,0:T(8,128)(2,1)S(1)} %get-tuple-element.78), channel_id=1, source_target_pairs={{0,6},{1,7},{2,0},{3,1},{4,2},{5,3},{6,4},{7,5},{8,14},{9,15},{10,... | collective-permute-start | bytes 983048 | tf_op jit(solution)/shard_map/ppermute | solution.py:31
  176.9 3.6 %collective-permute-start.24 = (bf16[4,80,1024]{2,1,0:T(8,128)(2,1)S(1)}, bf16[4,80,1024]{2,1,0:T(8,128)(2,1)S(1)}, u32[]{:S(2)}, u32[]{:S(2)}) collective-permute-start(bf16[4,80,1024]{2,1,0:T(8,128)(2,1)S(1)} %get-tuple-element.80), channel_id=1, source_target_pairs={{0,1},{1,0},{2,3},{3,2},{4,5},{5,4},{6,7},{7,6},{8,9},{9,8},{10,11... | collective-permute-start | bytes 1966088 | tf_op jit(solution)/shard_map/ppermute | solution.py:35
  180.5 9.0 %collective-permute-done.22 = bf16[2,80,1024]{2,1,0:T(8,128)(2,1)S(1)} collective-permute-done((bf16[2,80,1024]{2,1,0:T(8,128)(2,1)S(1)}, bf16[2,80,1024]{2,1,0:T(8,128)(2,1)S(1)}, u32[]{:S(2)}, u32[]{:S(2)}) %collective-permute-start.22) | collective-permute-done | bytes 327712 | tf_op jit(solution)/shard_map/ppermute | solution.py:31
  189.5 3.7 %collective-permute-done.20 = bf16[2,80,1024]{2,1,0:T(8,128)(2,1)S(1)} collective-permute-done((bf16[2,80,1024]{2,1,0:T(8,128)(2,1)S(1)}, bf16[2,80,1024]{2,1,0:T(8,128)(2,1)S(1)}, u32[]{:S(2)}, u32[]{:S(2)}) %collective-permute-start.20) | collective-permute-done | bytes 327712 | tf_op jit(solution)/shard_map/ppermute | solution.py:31
  193.4 3.7 %collective-permute-start.23 = (bf16[80,1024]{1,0:T(8,128)(2,1)S(1)}, bf16[80,1024]{1,0:T(8,128)(2,1)S(1)}, u32[]{:S(2)}, u32[]{:S(2)}) collective-permute-start(bf16[80,1024]{1,0:T(8,128)(2,1)S(1)} %fusion.7), channel_id=1, source_target_pairs={{0,1},{1,0},{2,3},{3,2},{4,5},{5,4},{6,7},{7,6},{8,9},{9,8},{10,11... | collective-permute-start | bytes 491528 | tf_op jit(solution)/shard_map/ppermute | solution.py:35
  201.5 3.1 %collective-permute-done.27 = bf16[80,1024]{1,0:T(8,128)(2,1)S(1)} collective-permute-done((bf16[80,1024]{1,0:T(8,128)(2,1)S(1)}, bf16[80,1024]{1,0:T(8,128)(2,1)S(1)}, u32[]{:S(2)}, u32[]{:S(2)}) %collective-permute-start.27) | collective-permute-done | bytes 163872 | tf_op jit(solution)/shard_map/ppermute | solution.py:31
  204.6 1.9 collective-permute-done.26
  206.4 2.0 collective-permute-done.25
  (56 shorter events, 19.5 us)
Async XLA Ops:
  4.3 7.3 %copy-start = (bf16[2,80,8192]{2,1,0:T(8,128)(2,1)S(1)}, bf16[2,80,8192]{2,1,0:T(8,128)(2,1)}, u32[]{:S(2)}) copy-start(bf16[2,80,8192]{2,1,0:T(8,128)(2,1)} %param.6) | copy-start | bytes 7864324
  4.3 7.3 %copy-start.1 = (s32[2,128]{1,0:T(2,128)S(1)}, s32[2,128]{1,0:T(2,128)}, u32[]{:S(2)}) copy-start(s32[2,128]{1,0:T(2,128)} %owner_ref.3) | copy-start | bytes 3076
  4.3 44.3 %all-to-all-start = ((bf16[8,64,2304]{2,1,0:T(8,128)(2,1)}), bf16[8,64,2304]{2,1,0:T(8,128)(2,1)}, u32[]{:S(2)}, u32[]{:S(2)}) async-start(bf16[8,64,2304]{2,1,0:T(8,128)(2,1)} %slabs.1), calls=%async_computation | async-start | bytes 4718592 | tf_op jit(solution)/shard_map/all_to_all | solution.py:418
  11.6 10.8 %copy-start.2 = (s32[80]{0:T(128)S(1)}, s32[80]{0:T(128)}, u32[]{:S(2)}) copy-start(s32[80]{0:T(128)} %lengths_ref.1) | copy-start | bytes 964
  16.5 19.0 %collective-permute-start = (bf16[160,2048]{1,0:T(8,128)(2,1)}, bf16[160,2048]{1,0:T(8,128)(2,1)S(1)}, u32[]{:S(2)}, u32[]{:S(2)}) collective-permute-start(bf16[160,2048]{1,0:T(8,128)(2,1)} %get-tuple-element.44), channel_id=1, source_target_pairs={{0,16},{8,24},{16,32},{24,40},{32,48},{40,56},{48,0},{56,8},{64,80... | collective-permute-start | bytes 1966088 | tf_op jit(solution)/shard_map/ppermute | solution.py:23
  18.4 30.2 %collective-permute-start.1 = (bf16[160,2048]{1,0:T(8,128)(2,1)}, bf16[160,2048]{1,0:T(8,128)(2,1)S(1)}, u32[]{:S(2)}, u32[]{:S(2)}) collective-permute-start(bf16[160,2048]{1,0:T(8,128)(2,1)} %get-tuple-element.45), channel_id=1, source_target_pairs={{0,48},{8,56},{16,0},{24,8},{32,16},{40,24},{48,32},{56,40},{64,11... | collective-permute-start | bytes 1966088 | tf_op jit(solution)/shard_map/ppermute | solution.py:23
  20.5 31.7 %collective-permute-start.2 = (bf16[160,2048]{1,0:T(8,128)(2,1)}, bf16[160,2048]{1,0:T(8,128)(2,1)S(1)}, u32[]{:S(2)}, u32[]{:S(2)}) collective-permute-start(bf16[160,2048]{1,0:T(8,128)(2,1)} %get-tuple-element.48), channel_id=1, source_target_pairs={{0,32},{8,40},{16,48},{24,56},{32,0},{40,8},{48,16},{56,24},{64,96... | collective-permute-start | bytes 1966088 | tf_op jit(solution)/shard_map/ppermute | solution.py:23
  50.0 5.9 %collective-permute-start.6 = (bf16[512,1280]{1,0:T(8,128)(2,1)S(1)}, bf16[512,1280]{1,0:T(8,128)(2,1)S(1)}, u32[]{:S(2)}, u32[]{:S(2)}) collective-permute-start(bf16[512,1280]{1,0:T(8,128)(2,1)S(1)} %slice.35.refs_4_), channel_id=1, source_target_pairs={{0,8},{8,0},{16,24},{24,16},{32,40},{40,32},{48,56},{56,48},{64,72... | collective-permute-start | bytes 3932168 | tf_op jit(solution)/shard_map/ppermute | solution.py:27
  50.1 31.2 %collective-permute-start.3 = (bf16[512,1280]{1,0:T(8,128)(2,1)S(1)}, bf16[512,1280]{1,0:T(8,128)(2,1)S(1)}, u32[]{:S(2)}, u32[]{:S(2)}) collective-permute-start(bf16[512,1280]{1,0:T(8,128)(2,1)S(1)} %slice.35.refs_4_), channel_id=1, source_target_pairs={{0,64},{8,72},{16,80},{24,88},{32,96},{40,104},{48,112},{56,120},{... | collective-permute-start | bytes 3932168 | tf_op jit(solution)/shard_map/ppermute | solution.py:27
  52.2 27.1 %collective-permute-start.4 = (bf16[512,1024]{1,0:T(8,128)(2,1)S(1)}, bf16[512,1024]{1,0:T(8,128)(2,1)S(1)}, u32[]{:S(2)}, u32[]{:S(2)}) collective-permute-start(bf16[512,1024]{1,0:T(8,128)(2,1)S(1)} %slice.34.refs_0_), channel_id=1, source_target_pairs={{0,16},{8,24},{16,32},{24,40},{32,48},{40,56},{48,0},{56,8},{64,80... | collective-permute-start | bytes 3145736 | tf_op jit(solution)/shard_map/ppermute | solution.py:23
  52.3 27.0 %collective-permute-start.5 = (bf16[512,1024]{1,0:T(8,128)(2,1)S(1)}, bf16[512,1024]{1,0:T(8,128)(2,1)S(1)}, u32[]{:S(2)}, u32[]{:S(2)}) collective-permute-start(bf16[512,1024]{1,0:T(8,128)(2,1)S(1)} %slice.34.refs_0_), channel_id=1, source_target_pairs={{0,48},{8,56},{16,0},{24,8},{32,16},{40,24},{48,32},{56,40},{64,11... | collective-permute-start | bytes 3145736 | tf_op jit(solution)/shard_map/ppermute | solution.py:23
  81.3 4.5 %collective-permute-start.7 = (bf16[512,1280]{1,0:T(8,128)(2,1)S(1)}, bf16[512,1280]{1,0:T(8,128)(2,1)S(1)}, u32[]{:S(2)}, u32[]{:S(2)}) collective-permute-start(bf16[512,1280]{1,0:T(8,128)(2,1)S(1)} %collective-permute-done.3.refs_4_), channel_id=1, source_target_pairs={{0,8},{8,0},{16,24},{24,16},{32,40},{40,32},{48,56},{56,48},{64,72... | collective-permute-start | bytes 3932168 | tf_op jit(solution)/shard_map/ppermute | solution.py:27
  81.3 28.2 %collective-permute-start.14 = (bf16[512,1024]{1,0:T(8,128)(2,1)S(1)}, bf16[512,1024]{1,0:T(8,128)(2,1)S(1)}, u32[]{:S(2)}, u32[]{:S(2)}) collective-permute-start(bf16[512,1024]{1,0:T(8,128)(2,1)S(1)} %slice.34.refs_0_), channel_id=1, source_target_pairs={{0,64},{8,72},{16,80},{24,88},{32,96},{40,104},{48,112},{56,120},{... | collective-permute-start | bytes 3145736 | tf_op jit(solution)/shard_map/ppermute | solution.py:27
  82.0 15.9 %collective-permute-start.12 = (bf16[256,1024]{1,0:T(8,128)(2,1)S(1)}, bf16[256,1024]{1,0:T(8,128)(2,1)S(1)}, u32[]{:S(2)}, u32[]{:S(2)}) collective-permute-start(bf16[256,1024]{1,0:T(8,128)(2,1)S(1)} %slice.36), channel_id=1, source_target_pairs={{0,48},{8,56},{16,0},{24,8},{32,16},{40,24},{48,32},{56,40},{64,11... | collective-permute-start | bytes 1572872 | tf_op jit(solution)/shard_map/ppermute | solution.py:23
  85.7 23.8 %collective-permute-start.13 = (bf16[256,1024]{1,0:T(8,128)(2,1)S(1)}, bf16[256,1024]{1,0:T(8,128)(2,1)S(1)}, u32[]{:S(2)}, u32[]{:S(2)}) collective-permute-start(bf16[256,1024]{1,0:T(8,128)(2,1)S(1)} %slice.37), channel_id=1, source_target_pairs={{0,16},{8,24},{16,32},{24,40},{32,48},{40,56},{48,0},{56,8},{64,80... | collective-permute-start | bytes 1572872 | tf_op jit(solution)/shard_map/ppermute | solution.py:23
  89.3 25.5 %collective-permute-start.8 = (bf16[160,1280]{1,0:T(8,128)(2,1)S(1)}, bf16[160,1280]{1,0:T(8,128)(2,1)S(1)}, u32[]{:S(2)}, u32[]{:S(2)}) collective-permute-start(bf16[160,1280]{1,0:T(8,128)(2,1)S(1)} %get-tuple-element.62), channel_id=1, source_target_pairs={{0,48},{8,56},{16,0},{24,8},{32,16},{40,24},{48,32},{56,40},{64,11... | collective-permute-start | bytes 1228808 | tf_op jit(solution)/shard_map/ppermute | solution.py:23
  92.5 22.3 %collective-permute-start.9 = (bf16[160,1280]{1,0:T(8,128)(2,1)S(1)}, bf16[160,1280]{1,0:T(8,128)(2,1)S(1)}, u32[]{:S(2)}, u32[]{:S(2)}) collective-permute-start(bf16[160,1280]{1,0:T(8,128)(2,1)S(1)} %get-tuple-element.63), channel_id=1, source_target_pairs={{0,32},{8,40},{16,48},{24,56},{32,0},{40,8},{48,16},{56,24},{64,96... | collective-permute-start | bytes 1228808 | tf_op jit(solution)/shard_map/ppermute | solution.py:23
  114.8 47.8 %collective-permute-start.17 = (bf16[512,1024]{1,0:T(8,128)(2,1)S(1)}, bf16[512,1024]{1,0:T(8,128)(2,1)S(1)}, u32[]{:S(2)}, u32[]{:S(2)}) collective-permute-start(bf16[512,1024]{1,0:T(8,128)(2,1)S(1)} %collective-permute-done.14.refs_3_), channel_id=1, source_target_pairs={{0,16},{8,24},{16,32},{24,40},{32,48},{40,56},{48,0},{56,8},{64,80... | collective-permute-start | bytes 3145736 | tf_op jit(solution)/shard_map/ppermute | solution.py:23
  116.4 46.2 %collective-permute-start.18 = (bf16[512,1024]{1,0:T(8,128)(2,1)S(1)}, bf16[512,1024]{1,0:T(8,128)(2,1)S(1)}, u32[]{:S(2)}, u32[]{:S(2)}) collective-permute-start(bf16[512,1024]{1,0:T(8,128)(2,1)S(1)} %collective-permute-done.14.refs_3_), channel_id=1, source_target_pairs={{0,48},{8,56},{16,0},{24,8},{32,16},{40,24},{48,32},{56,40},{64,11... | collective-permute-start | bytes 3145736 | tf_op jit(solution)/shard_map/ppermute | solution.py:23
  118.5 31.5 %collective-permute-start.10 = (bf16[160,1280]{1,0:T(8,128)(2,1)S(1)}, bf16[160,1280]{1,0:T(8,128)(2,1)S(1)}, u32[]{:S(2)}, u32[]{:S(2)}) collective-permute-start(bf16[160,1280]{1,0:T(8,128)(2,1)S(1)} %get-tuple-element.64), channel_id=1, source_target_pairs={{0,16},{8,24},{16,32},{24,40},{32,48},{40,56},{48,0},{56,8},{64,80... | collective-permute-start | bytes 1228808 | tf_op jit(solution)/shard_map/ppermute | solution.py:23
  118.5 42.5 %collective-permute-start.15 = (bf16[256,1024]{1,0:T(8,128)(2,1)S(1)}, bf16[256,1024]{1,0:T(8,128)(2,1)S(1)}, u32[]{:S(2)}, u32[]{:S(2)}) collective-permute-start(bf16[256,1024]{1,0:T(8,128)(2,1)S(1)} %collective-permute-done.12.refs_4_), channel_id=1, source_target_pairs={{0,64},{8,72},{16,80},{24,88},{32,96},{40,104},{48,112},{56,120},{... | collective-permute-start | bytes 1572872 | tf_op jit(solution)/shard_map/ppermute | solution.py:27
  119.8 41.1 %collective-permute-start.16 = (bf16[256,1024]{1,0:T(8,128)(2,1)S(1)}, bf16[256,1024]{1,0:T(8,128)(2,1)S(1)}, u32[]{:S(2)}, u32[]{:S(2)}) collective-permute-start(bf16[256,1024]{1,0:T(8,128)(2,1)S(1)} %collective-permute-done.13.refs_5_), channel_id=1, source_target_pairs={{0,64},{8,72},{16,80},{24,88},{32,96},{40,104},{48,112},{56,120},{... | collective-permute-start | bytes 1572872 | tf_op jit(solution)/shard_map/ppermute | solution.py:27
  160.7 1.9 collective-permute-start.11
  165.0 4.2 %collective-permute-start.19 = (bf16[4096,256]{1,0:T(8,128)(2,1)S(1)}, bf16[4096,256]{1,0:T(8,128)(2,1)S(1)}, u32[]{:S(2)}, u32[]{:S(2)}) collective-permute-start(bf16[4096,256]{1,0:T(8,128)(2,1)S(1)} %terms.2), channel_id=1, source_target_pairs={{0,8},{8,0},{16,24},{24,16},{32,40},{40,32},{48,56},{56,48},{64,72... | collective-permute-start | bytes 6291464 | tf_op jit(solution)/shard_map/ppermute | solution.py:27
  172.2 17.3 %collective-permute-start.22 = (bf16[2,80,1024]{2,1,0:T(8,128)(2,1)S(1)}, bf16[2,80,1024]{2,1,0:T(8,128)(2,1)S(1)}, u32[]{:S(2)}, u32[]{:S(2)}) collective-permute-start(bf16[2,80,1024]{2,1,0:T(8,128)(2,1)S(1)} %get-tuple-element.78), channel_id=1, source_target_pairs={{0,6},{1,7},{2,0},{3,1},{4,2},{5,3},{6,4},{7,5},{8,14},{9,15},{10,... | collective-permute-start | bytes 983048 | tf_op jit(solution)/shard_map/ppermute | solution.py:31
  175.2 14.3 %collective-permute-start.21 = (bf16[2,80,1024]{2,1,0:T(8,128)(2,1)S(1)}, bf16[2,80,1024]{2,1,0:T(8,128)(2,1)S(1)}, u32[]{:S(2)}, u32[]{:S(2)}) collective-permute-start(bf16[2,80,1024]{2,1,0:T(8,128)(2,1)S(1)} %get-tuple-element.77), channel_id=1, source_target_pairs={{0,4},{1,5},{2,6},{3,7},{4,0},{5,1},{6,2},{7,3},{8,12},{9,13},{10,... | collective-permute-start | bytes 983048 | tf_op jit(solution)/shard_map/ppermute | solution.py:31
  176.0 17.1 %collective-permute-start.20 = (bf16[2,80,1024]{2,1,0:T(8,128)(2,1)S(1)}, bf16[2,80,1024]{2,1,0:T(8,128)(2,1)S(1)}, u32[]{:S(2)}, u32[]{:S(2)}) collective-permute-start(bf16[2,80,1024]{2,1,0:T(8,128)(2,1)S(1)} %get-tuple-element.76), channel_id=1, source_target_pairs={{0,2},{1,3},{2,4},{3,5},{4,6},{5,7},{6,0},{7,1},{8,10},{9,11},{10,... | collective-permute-start | bytes 983048 | tf_op jit(solution)/shard_map/ppermute | solution.py:31
  176.9 20.2 %collective-permute-start.24 = (bf16[4,80,1024]{2,1,0:T(8,128)(2,1)S(1)}, bf16[4,80,1024]{2,1,0:T(8,128)(2,1)S(1)}, u32[]{:S(2)}, u32[]{:S(2)}) collective-permute-start(bf16[4,80,1024]{2,1,0:T(8,128)(2,1)S(1)} %get-tuple-element.80), channel_id=1, source_target_pairs={{0,1},{1,0},{2,3},{3,2},{4,5},{5,4},{6,7},{7,6},{8,9},{9,8},{10,11... | collective-permute-start | bytes 1966088 | tf_op jit(solution)/shard_map/ppermute | solution.py:35
  193.4 8.0 %collective-permute-start.23 = (bf16[80,1024]{1,0:T(8,128)(2,1)S(1)}, bf16[80,1024]{1,0:T(8,128)(2,1)S(1)}, u32[]{:S(2)}, u32[]{:S(2)}) collective-permute-start(bf16[80,1024]{1,0:T(8,128)(2,1)S(1)} %fusion.7), channel_id=1, source_target_pairs={{0,1},{1,0},{2,3},{3,2},{4,5},{5,4},{6,7},{7,6},{8,9},{9,8},{10,11... | collective-permute-start | bytes 491528 | tf_op jit(solution)/shard_map/ppermute | solution.py:35
  197.4 7.2 %collective-permute-start.27 = (bf16[80,1024]{1,0:T(8,128)(2,1)S(1)}, bf16[80,1024]{1,0:T(8,128)(2,1)S(1)}, u32[]{:S(2)}, u32[]{:S(2)}) collective-permute-start(bf16[80,1024]{1,0:T(8,128)(2,1)S(1)} %get-tuple-element.84), channel_id=1, source_target_pairs={{0,6},{1,7},{2,0},{3,1},{4,2},{5,3},{6,4},{7,5},{8,14},{9,15},{10,... | collective-permute-start | bytes 491528 | tf_op jit(solution)/shard_map/ppermute | solution.py:31
  198.1 8.4 %collective-permute-start.26 = (bf16[80,1024]{1,0:T(8,128)(2,1)S(1)}, bf16[80,1024]{1,0:T(8,128)(2,1)S(1)}, u32[]{:S(2)}, u32[]{:S(2)}) collective-permute-start(bf16[80,1024]{1,0:T(8,128)(2,1)S(1)} %get-tuple-element.85), channel_id=1, source_target_pairs={{0,4},{1,5},{2,6},{3,7},{4,0},{5,1},{6,2},{7,3},{8,12},{9,13},{10,... | collective-permute-start | bytes 491528 | tf_op jit(solution)/shard_map/ppermute | solution.py:31
  198.9 9.5 %collective-permute-start.25 = (bf16[80,1024]{1,0:T(8,128)(2,1)S(1)}, bf16[80,1024]{1,0:T(8,128)(2,1)S(1)}, u32[]{:S(2)}, u32[]{:S(2)}) collective-permute-start(bf16[80,1024]{1,0:T(8,128)(2,1)S(1)} %get-tuple-element.83), channel_id=1, source_target_pairs={{0,2},{1,3},{2,4},{3,5},{4,6},{5,7},{6,0},{7,1},{8,10},{9,11},{10,... | collective-permute-start | bytes 491528 | tf_op jit(solution)/shard_map/ppermute | solution.py:31

commit v12 on v10

--- a/solution.py
+++ b/solution.py
@@ -417,19 +417,18 @@
 
     both = lax.all_to_all(copy, "tp", split_axis=0, concat_axis=0, tiled=True)
     both = both.reshape(groups * owned, -1)
-    both, cos, sin, parts[1], parts[3] = lax.optimization_barrier(
-        (both, cos, sin, parts[1], parts[3])
-    )
     w, own = both[:, :cols], both[:, cols:]
     half = own.shape[0] // 2
 
     w_y, w_c = flip(w, 8), flip(w, 1)
-    own, parts[2] = lax.optimization_barrier((own, parts[2]))
+    own, cos, sin, *parts = lax.optimization_barrier((own, cos, sin, *parts))
     below, above = z_shift(own, 1), z_shift(own, -1)
     begun = partials(parts, (w, w_c))
-    w_y, below, above, own, *begun = lax.optimization_barrier((w_y, below, above, own, *begun))
+    below, above, *begun = lax.optimization_barrier((below, above, *begun))
+    above_a, below_b = above[:half], below[half:]
+    w_y, own, above_a, below_b = lax.optimization_barrier((w_y, own, above_a, below_b))
     w_yc = flip(w_y, 1)
-    far_a, far_b = z_shift(above[:half], -1), z_shift(below[half:], 1)
+    far_a, far_b = z_shift(above_a, -1), z_shift(below_b, 1)
     across = flip(own, 8)
 
     sums = partials(parts, (w_y, w_yc), begun)

time: 193 us -> 187 us (0.969)
  waiting for transfers between devices: 107 us -> 104 us
    ppermute x12, waiting for transfers between devices: 71.6 us -> 45.6 us  [z_shift(): return lax.ppermute(value, 'fsdp', pairs)]
    all_to_all x1, waiting for transfers between devices: 0.01 us -> 23.6 us  [body(): both = lax.all_to_all(copy, 'tp', split_axis=0, concat_axis=0, tiled=True)]
    ppermute x2, starting transfers between devices: 7.22 us -> 4.87 us  [y_flip(): return lax.ppermute(value, 'tp', [(t, t ^ 1) for t in range(2 * NX)])]
where the time goes in v12:
time: 187 us
  waiting for transfers between devices  104 us (56%)
  starting transfers between devices  43.5 us (23%)
  Pallas kernels  34.3 us (18%)
  local copies, waits for them, and re-layouts  2.92 us (2%)
    ppermute x12, waiting for transfers between devices, z_shift(): return lax.ppermute(value, 'fsdp', pairs)  45.6 us
    all_to_all x1, waiting for transfers between devices, body(): both = lax.all_to_all(copy, 'tp', split_axis=0, concat_axis=0, tiled=True)  23.6 us
    ppermute x12, starting transfers between devices, z_shift(): return lax.ppermute(value, 'fsdp', pairs)  21.6 us
    ppermute x6, waiting for transfers between devices, x_shift(): lax.ppermute(value, 'tp', [(t, (t // 2 + k) % NX * 2 + t % 2) for t in ra...  20.4 us
    ppermute x8, waiting for transfers between devices, flip(): return lax.ppermute(value, 'fsdp', [(f, f ^ bit) for f in range(16)])  13.2 us
    pallas_call x1, Pallas kernels, attention(): pl.pallas_call(attention_kernel, grid=(rows // GROUP,), out_shape=jax.Sha...  10.7 us
    all_to_all x1, starting transfers between devices, body(): both = lax.all_to_all(copy, 'tp', split_axis=0, concat_axis=0, tiled=True)  7.28 us
    pallas_call x2, Pallas kernels, partials(): pl.pallas_call(functools.partial(partial_kernel, begun), grid=(cols // ti...  6.68 us
  transfers between devices with their start and end apart: 29, of which 17 were waited for; matrix products, arithmetic and copies ran while one was open for 2% of the time, Pallas kernels for 13%

profile of v12, /device:TPU:0, one launch (start us, length us, event | category | flops | bytes accessed | tf_op | source)
XLA Modules:
  0.0 186.6 jit_solution(15476553011508524887)
XLA Ops:
  0.0 4.3 %slabs.1 = bf16[8,64,2304]{2,1,0:T(8,128)(2,1)} custom-call(f32[64,10240]{1,0:T(8,128)} %value.1, f32[64,10240]{1,0:T(8,128)} %value.1, f32[64,10240]{1,0:T(8,128)} %value.1, f32[64,8192]{1,0:T(8,128)} %back.1), custom_call_target="tpu_custom_call" | custom-call | bytes 7077888 | tf_op jit(solution)/shard_map/slabs/pallas_call | solution.py:56
  4.3 7.3 %all-to-all-start = ((bf16[8,64,2304]{2,1,0:T(8,128)(2,1)}), bf16[8,64,2304]{2,1,0:T(8,128)(2,1)}, u32[]{:S(2)}, u32[]{:S(2)}) async-start(bf16[8,64,2304]{2,1,0:T(8,128)(2,1)} %slabs.1), calls=%async_computation | async-start | bytes 4718592 | tf_op jit(solution)/shard_map/all_to_all | solution.py:418
  11.6 4.8 %shuffle.1 = (bf16[160,2048]{1,0:T(8,128)(2,1)S(1)}, bf16[160,2048]{1,0:T(8,128)(2,1)}, bf16[160,2048]{1,0:T(8,128)(2,1)}, bf16[160,2048]{1,0:T(8,128)(2,1)}) custom-call(s32[2,128]{1,0:T(2,128)S(1)} %copy-done.1, bf16[160,8192]{1,0:T(8,128)(2,1)S(1)} %bitcast.34), custom_call_target="tpu_custom_call" | custom-call | flops 10485760 | bytes 5242880 | tf_op jit(solution)/shard_map/shuffle/pallas_call | solution.py:105
  16.5 1.9 %collective-permute-start = (bf16[160,2048]{1,0:T(8,128)(2,1)}, bf16[160,2048]{1,0:T(8,128)(2,1)S(1)}, u32[]{:S(2)}, u32[]{:S(2)}) collective-permute-start(bf16[160,2048]{1,0:T(8,128)(2,1)} %get-tuple-element.46), channel_id=1, source_target_pairs={{0,16},{8,24},{16,32},{24,40},{32,48},{40,56},{48,0},{56,8},{64,80... | collective-permute-start | bytes 1966088 | tf_op jit(solution)/shard_map/ppermute | solution.py:23
  18.4 3.6 %collective-permute-start.1 = (bf16[160,2048]{1,0:T(8,128)(2,1)}, bf16[160,2048]{1,0:T(8,128)(2,1)S(1)}, u32[]{:S(2)}, u32[]{:S(2)}) collective-permute-start(bf16[160,2048]{1,0:T(8,128)(2,1)} %get-tuple-element.47), channel_id=1, source_target_pairs={{0,32},{8,40},{16,48},{24,56},{32,0},{40,8},{48,16},{56,24},{64,96... | collective-permute-start | bytes 1966088 | tf_op jit(solution)/shard_map/ppermute | solution.py:23
  23.1 23.6 %all-to-all-done = bf16[8,64,2304]{2,1,0:T(8,128)(2,1)} async-done(((bf16[8,64,2304]{2,1,0:T(8,128)(2,1)}), bf16[8,64,2304]{2,1,0:T(8,128)(2,1)}, u32[]{:S(2)}, u32[]{:S(2)}) %all-to-all-start) | async-done | bytes 2359328 | tf_op jit(solution)/shard_map/all_to_all | solution.py:418
  50.7 2.0 %collective-permute-start.4 = (bf16[512,1024]{1,0:T(8,128)(2,1)S(1)}, bf16[512,1024]{1,0:T(8,128)(2,1)S(1)}, u32[]{:S(2)}, u32[]{:S(2)}) collective-permute-start(bf16[512,1024]{1,0:T(8,128)(2,1)S(1)} %slice.44.refs_0_), channel_id=1, source_target_pairs={{0,16},{8,24},{16,32},{24,40},{32,48},{40,56},{48,0},{56,8},{64,80... | collective-permute-start | bytes 3145736 | tf_op jit(solution)/shard_map/ppermute | solution.py:23
  52.7 2.2 %collective-permute-start.5 = (bf16[512,1024]{1,0:T(8,128)(2,1)S(1)}, bf16[512,1024]{1,0:T(8,128)(2,1)S(1)}, u32[]{:S(2)}, u32[]{:S(2)}) collective-permute-start(bf16[512,1024]{1,0:T(8,128)(2,1)S(1)} %slice.44.refs_0_), channel_id=1, source_target_pairs={{0,48},{8,56},{16,0},{24,8},{32,16},{40,24},{48,32},{56,40},{64,11... | collective-permute-start | bytes 3145736 | tf_op jit(solution)/shard_map/ppermute | solution.py:23
  54.9 3.2 %partials.1 = (f32[160,1280]{1,0:T(8,128)S(1)}, f32[160,1280]{1,0:T(8,128)S(1)}, f32[160,1280]{1,0:T(8,128)S(1)}, f32[160,1280]{1,0:T(8,128)S(1)}) custom-call(bf16[160,2048]{1,0:T(8,128)(2,1)S(1)} %get-tuple-element.49.refs_0_, bf16[160,2048]{1,0:T(8,128)(2,1)S(1)} %collective-permute-done.refs_1_, bf16[160,2048]{1,0:T(8,128)(2,1)S(1)} %collective-permute-done.1.refs_2_, ...), custom_call_target="tpu_custom_call" | custom-call | flops 1677721600 | bytes 7208960 | tf_op jit(solution)/shard_map/partials/pallas_call | solution.py:152
  58.1 20.2 %collective-permute-done.4.refs_1_ = bf16[512,1024]{1,0:T(8,128)(2,1)S(1)} collective-permute-done((bf16[512,1024]{1,0:T(8,128)(2,1)S(1)}, bf16[512,1024]{1,0:T(8,128)(2,1)S(1)}, u32[]{:S(2)}, u32[]{:S(2)}) %collective-permute-start.4) | collective-permute-done | bytes 1048608 | tf_op jit(solution)/shard_map/ppermute | solution.py:23
  80.0 4.0 %collective-permute-start.12 = (bf16[256,1024]{1,0:T(8,128)(2,1)S(1)}, bf16[256,1024]{1,0:T(8,128)(2,1)S(1)}, u32[]{:S(2)}, u32[]{:S(2)}) collective-permute-start(bf16[256,1024]{1,0:T(8,128)(2,1)S(1)} %slice.36), channel_id=1, source_target_pairs={{0,48},{8,56},{16,0},{24,8},{32,16},{40,24},{48,32},{56,40},{64,11... | collective-permute-start | bytes 1572872 | tf_op jit(solution)/shard_map/ppermute | solution.py:23
  84.1 3.5 %partials_rest.1 = (f32[160,1280]{1,0:T(8,128)S(1)}, bf16[160,1280]{1,0:T(8,128)(2,1)S(1)}, bf16[160,1280]{1,0:T(8,128)(2,1)S(1)}, bf16[160,1280]{1,0:T(8,128)(2,1)S(1)}) custom-call(bf16[160,2048]{1,0:T(8,128)(2,1)S(1)} %get-tuple-element.49.refs_0_, bf16[160,2048]{1,0:T(8,128)(2,1)S(1)} %collective-permute-done.refs_1_, ...), custom_call_target="tpu_custom_call" | custom-call | flops 1677721600 | bytes 7208960 | tf_op jit(solution)/shard_map/partials_rest/pallas_call | solution.py:152
  87.5 3.3 %collective-permute-start.8 = (bf16[160,1280]{1,0:T(8,128)(2,1)S(1)}, bf16[160,1280]{1,0:T(8,128)(2,1)S(1)}, u32[]{:S(2)}, u32[]{:S(2)}) collective-permute-start(bf16[160,1280]{1,0:T(8,128)(2,1)S(1)} %get-tuple-element.66), channel_id=1, source_target_pairs={{0,48},{8,56},{16,0},{24,8},{32,16},{40,24},{48,32},{56,40},{64,11... | collective-permute-start | bytes 1228808 | tf_op jit(solution)/shard_map/ppermute | solution.py:23
  90.8 5.5 %collective-permute-done.12.refs_4_ = bf16[256,1024]{1,0:T(8,128)(2,1)S(1)} collective-permute-done((bf16[256,1024]{1,0:T(8,128)(2,1)S(1)}, bf16[256,1024]{1,0:T(8,128)(2,1)S(1)}, u32[]{:S(2)}, u32[]{:S(2)}) %collective-permute-start.12) | collective-permute-done | bytes 524320 | tf_op jit(solution)/shard_map/ppermute | solution.py:23
  96.7 12.2 %collective-permute-done.13.refs_5_ = bf16[256,1024]{1,0:T(8,128)(2,1)S(1)} collective-permute-done((bf16[256,1024]{1,0:T(8,128)(2,1)S(1)}, bf16[256,1024]{1,0:T(8,128)(2,1)S(1)}, u32[]{:S(2)}, u32[]{:S(2)}) %collective-permute-start.13) | collective-permute-done | bytes 524320 | tf_op jit(solution)/shard_map/ppermute | solution.py:23
  108.8 4.3 %collective-permute-done.8.p1 = bf16[160,1280]{1,0:T(8,128)(2,1)S(1)} collective-permute-done((bf16[160,1280]{1,0:T(8,128)(2,1)S(1)}, bf16[160,1280]{1,0:T(8,128)(2,1)S(1)}, u32[]{:S(2)}, u32[]{:S(2)}) %collective-permute-start.8) | collective-permute-done | bytes 409632 | tf_op jit(solution)/shard_map/ppermute | solution.py:23
  113.2 3.4 %collective-permute-done.10.p3 = bf16[160,1280]{1,0:T(8,128)(2,1)S(1)} collective-permute-done((bf16[160,1280]{1,0:T(8,128)(2,1)S(1)}, bf16[160,1280]{1,0:T(8,128)(2,1)S(1)}, u32[]{:S(2)}, u32[]{:S(2)}) %collective-permute-start.10) | collective-permute-done | bytes 409632 | tf_op jit(solution)/shard_map/ppermute | solution.py:23
  116.6 3.2 %collective-permute-start.18 = (bf16[512,1024]{1,0:T(8,128)(2,1)S(1)}, bf16[512,1024]{1,0:T(8,128)(2,1)S(1)}, u32[]{:S(2)}, u32[]{:S(2)}) collective-permute-start(bf16[512,1024]{1,0:T(8,128)(2,1)S(1)} %collective-permute-done.14.refs_3_), channel_id=1, source_target_pairs={{0,48},{8,56},{16,0},{24,8},{32,16},{40,24},{48,32},{56,40},{64,11... | collective-permute-start | bytes 3145736 | tf_op jit(solution)/shard_map/ppermute | solution.py:23
  121.9 10.7 %attention.1.mixed_ref = bf16[160,1024]{1,0:T(8,128)(2,1)S(1)} custom-call(s32[80]{0:T(128)S(1)} %copy-done.2, f32[160,1280]{1,0:T(8,128)S(1)} %get-tuple-element.65.p0, bf16[160,1280]{1,0:T(8,128)(2,1)S(1)} %collective-permute-done.8.p1, bf16[160,1280]{1,0:T(8,128)(2,1)S(1)} %collective-permute-done.9.p2, bf16[160,1280]{1,0:T(8,128)(2,1)S(1)} %collective-permute-done.10.p3, ...), custom_call_target="tpu_custom_call" | custom-call | flops 167772160 | bytes 41943040 | tf_op jit(solution)/shard_map/attention/pallas_call | solution.py:376
  132.8 1.9 collective-permute-done.15.refs_6_
  134.7 8.7 %collective-permute-done.16.refs_7_ = bf16[256,1024]{1,0:T(8,128)(2,1)S(1)} collective-permute-done((bf16[256,1024]{1,0:T(8,128)(2,1)S(1)}, bf16[256,1024]{1,0:T(8,128)(2,1)S(1)}, u32[]{:S(2)}, u32[]{:S(2)}) %collective-permute-start.16) | collective-permute-done | bytes 524320 | tf_op jit(solution)/shard_map/ppermute | solution.py:27
  143.4 2.4 %terms.2 = bf16[4096,256]{1,0:T(8,128)(2,1)S(1)} custom-call(bf16[160,1024]{1,0:T(8,128)(2,1)S(1)} %collective-permute-done.11.mixed_ref, bf16[512,1024]{1,0:T(8,128)(2,1)S(1)} %slice.44.refs_0_, bf16[512,1024]{1,0:T(8,128)(2,1)S(1)} %collective-permute-done.4.refs_1_, bf16[512,1024]{1,0:T(8,128)(2,1)S(1)} %collective-permute-done.5.refs_2_, ...), custom_call_target="tpu_custom_call" | custom-call | flops 1342177280 | bytes 10027008 | tf_op jit(solution)/shard_map/terms/pallas_call | solution.py:198
  146.0 2.4 %terms.3.refs_0_ = bf16[4096,256]{1,0:T(8,128)(2,1)S(1)} custom-call(bf16[160,1024]{1,0:T(8,128)(2,1)S(1)} %attention.1.mixed_ref, bf16[512,1024]{1,0:T(8,128)(2,1)S(1)} %slice.44.refs_0_, bf16[512,1024]{1,0:T(8,128)(2,1)S(1)} %collective-permute-done.4.refs_1_, bf16[512,1024]{1,0:T(8,128)(2,1)S(1)} %collective-permute-done.5.refs_2_, ...), custom_call_target="tpu_custom_call" | custom-call | flops 1342177280 | bytes 10027008 | tf_op jit(solution)/shard_map/terms/pallas_call | solution.py:198
  148.4 1.7 collective-permute-done.19.refs_1_
  150.1 2.9 %place.1 = (bf16[2,80,1024]{2,1,0:T(8,128)(2,1)S(1)}, bf16[2,80,1024]{2,1,0:T(8,128)(2,1)S(1)}, bf16[2,80,1024]{2,1,0:T(8,128)(2,1)S(1)}, bf16[2,80,1024]{2,1,0:...) custom-call(s32[2,128]{1,0:T(2,128)S(1)} %copy-done.1, ...), custom_call_target="tpu_custom_call" | custom-call | bytes 5242880 | tf_op jit(solution)/shard_map/place/pallas_call | solution.py:247
  155.1 2.2 %collective-permute-start.24 = (bf16[4,80,1024]{2,1,0:T(8,128)(2,1)S(1)}, bf16[4,80,1024]{2,1,0:T(8,128)(2,1)S(1)}, u32[]{:S(2)}, u32[]{:S(2)}) collective-permute-start(bf16[4,80,1024]{2,1,0:T(8,128)(2,1)S(1)} %get-tuple-element.84), channel_id=1, source_target_pairs={{0,1},{1,0},{2,3},{3,2},{4,5},{5,4},{6,7},{7,6},{8,9},{9,8},{10,11... | collective-permute-start | bytes 1966088 | tf_op jit(solution)/shard_map/ppermute | solution.py:35
  157.3 6.3 %collective-permute-done.22 = bf16[2,80,1024]{2,1,0:T(8,128)(2,1)S(1)} collective-permute-done((bf16[2,80,1024]{2,1,0:T(8,128)(2,1)S(1)}, bf16[2,80,1024]{2,1,0:T(8,128)(2,1)S(1)}, u32[]{:S(2)}, u32[]{:S(2)}) %collective-permute-start.22) | collective-permute-done | bytes 327712 | tf_op jit(solution)/shard_map/ppermute | solution.py:31
  163.6 1.6 collective-permute-done.21
  165.3 6.2 %collective-permute-done.20 = bf16[2,80,1024]{2,1,0:T(8,128)(2,1)S(1)} collective-permute-done((bf16[2,80,1024]{2,1,0:T(8,128)(2,1)S(1)}, bf16[2,80,1024]{2,1,0:T(8,128)(2,1)S(1)}, u32[]{:S(2)}, u32[]{:S(2)}) %collective-permute-start.20) | collective-permute-done | bytes 327712 | tf_op jit(solution)/shard_map/ppermute | solution.py:31
  171.7 2.7 %collective-permute-start.23 = (bf16[80,1024]{1,0:T(8,128)(2,1)S(1)}, bf16[80,1024]{1,0:T(8,128)(2,1)S(1)}, u32[]{:S(2)}, u32[]{:S(2)}) collective-permute-start(bf16[80,1024]{1,0:T(8,128)(2,1)S(1)} %fusion.7), channel_id=1, source_target_pairs={{0,1},{1,0},{2,3},{3,2},{4,5},{5,4},{6,7},{7,6},{8,9},{9,8},{10,11... | collective-permute-start | bytes 491528 | tf_op jit(solution)/shard_map/ppermute | solution.py:35
  179.4 2.4 %collective-permute-done.27 = bf16[80,1024]{1,0:T(8,128)(2,1)S(1)} collective-permute-done((bf16[80,1024]{1,0:T(8,128)(2,1)S(1)}, bf16[80,1024]{1,0:T(8,128)(2,1)S(1)}, u32[]{:S(2)}, u32[]{:S(2)}) %collective-permute-start.27) | collective-permute-done | bytes 163872 | tf_op jit(solution)/shard_map/ppermute | solution.py:31
  181.9 2.3 %collective-permute-done.26 = bf16[80,1024]{1,0:T(8,128)(2,1)S(1)} collective-permute-done((bf16[80,1024]{1,0:T(8,128)(2,1)S(1)}, bf16[80,1024]{1,0:T(8,128)(2,1)S(1)}, u32[]{:S(2)}, u32[]{:S(2)}) %collective-permute-start.26) | collective-permute-done | bytes 163872 | tf_op jit(solution)/shard_map/ppermute | solution.py:31
  (56 shorter events, 19.3 us)
Async XLA Ops:
  4.3 7.3 %copy-start = (bf16[2,80,8192]{2,1,0:T(8,128)(2,1)S(1)}, bf16[2,80,8192]{2,1,0:T(8,128)(2,1)}, u32[]{:S(2)}) copy-start(bf16[2,80,8192]{2,1,0:T(8,128)(2,1)} %param.6) | copy-start | bytes 7864324
  4.3 7.3 %copy-start.1 = (s32[2,128]{1,0:T(2,128)S(1)}, s32[2,128]{1,0:T(2,128)}, u32[]{:S(2)}) copy-start(s32[2,128]{1,0:T(2,128)} %owner_ref.3) | copy-start | bytes 3076
  4.3 42.3 %all-to-all-start = ((bf16[8,64,2304]{2,1,0:T(8,128)(2,1)}), bf16[8,64,2304]{2,1,0:T(8,128)(2,1)}, u32[]{:S(2)}, u32[]{:S(2)}) async-start(bf16[8,64,2304]{2,1,0:T(8,128)(2,1)} %slabs.1), calls=%async_computation | async-start | bytes 4718592 | tf_op jit(solution)/shard_map/all_to_all | solution.py:418
  11.6 11.4 %copy-start.2 = (s32[80]{0:T(128)S(1)}, s32[80]{0:T(128)}, u32[]{:S(2)}) copy-start(s32[80]{0:T(128)} %lengths_ref.1) | copy-start | bytes 964
  16.5 34.2 %collective-permute-start = (bf16[160,2048]{1,0:T(8,128)(2,1)}, bf16[160,2048]{1,0:T(8,128)(2,1)S(1)}, u32[]{:S(2)}, u32[]{:S(2)}) collective-permute-start(bf16[160,2048]{1,0:T(8,128)(2,1)} %get-tuple-element.46), channel_id=1, source_target_pairs={{0,16},{8,24},{16,32},{24,40},{32,48},{40,56},{48,0},{56,8},{64,80... | collective-permute-start | bytes 1966088 | tf_op jit(solution)/shard_map/ppermute | solution.py:23
  18.4 32.3 %collective-permute-start.1 = (bf16[160,2048]{1,0:T(8,128)(2,1)}, bf16[160,2048]{1,0:T(8,128)(2,1)S(1)}, u32[]{:S(2)}, u32[]{:S(2)}) collective-permute-start(bf16[160,2048]{1,0:T(8,128)(2,1)} %get-tuple-element.47), channel_id=1, source_target_pairs={{0,32},{8,40},{16,48},{24,56},{32,0},{40,8},{48,16},{56,24},{64,96... | collective-permute-start | bytes 1966088 | tf_op jit(solution)/shard_map/ppermute | solution.py:23
  22.0 28.7 %collective-permute-start.2 = (bf16[160,2048]{1,0:T(8,128)(2,1)}, bf16[160,2048]{1,0:T(8,128)(2,1)S(1)}, u32[]{:S(2)}, u32[]{:S(2)}) collective-permute-start(bf16[160,2048]{1,0:T(8,128)(2,1)} %get-tuple-element.48), channel_id=1, source_target_pairs={{0,48},{8,56},{16,0},{24,8},{32,16},{40,24},{48,32},{56,40},{64,11... | collective-permute-start | bytes 1966088 | tf_op jit(solution)/shard_map/ppermute | solution.py:23
  48.0 6.9 %collective-permute-start.6 = (bf16[512,1280]{1,0:T(8,128)(2,1)S(1)}, bf16[512,1280]{1,0:T(8,128)(2,1)S(1)}, u32[]{:S(2)}, u32[]{:S(2)}) collective-permute-start(bf16[512,1280]{1,0:T(8,128)(2,1)S(1)} %slice.45.refs_4_), channel_id=1, source_target_pairs={{0,8},{8,0},{16,24},{24,16},{32,40},{40,32},{48,56},{56,48},{64,72... | collective-permute-start | bytes 3932168 | tf_op jit(solution)/shard_map/ppermute | solution.py:27
  48.1 31.2 %collective-permute-start.3 = (bf16[512,1280]{1,0:T(8,128)(2,1)S(1)}, bf16[512,1280]{1,0:T(8,128)(2,1)S(1)}, u32[]{:S(2)}, u32[]{:S(2)}) collective-permute-start(bf16[512,1280]{1,0:T(8,128)(2,1)S(1)} %slice.45.refs_4_), channel_id=1, source_target_pairs={{0,64},{8,72},{16,80},{24,88},{32,96},{40,104},{48,112},{56,120},{... | collective-permute-start | bytes 3932168 | tf_op jit(solution)/shard_map/ppermute | solution.py:27
  50.7 27.6 %collective-permute-start.4 = (bf16[512,1024]{1,0:T(8,128)(2,1)S(1)}, bf16[512,1024]{1,0:T(8,128)(2,1)S(1)}, u32[]{:S(2)}, u32[]{:S(2)}) collective-permute-start(bf16[512,1024]{1,0:T(8,128)(2,1)S(1)} %slice.44.refs_0_), channel_id=1, source_target_pairs={{0,16},{8,24},{16,32},{24,40},{32,48},{40,56},{48,0},{56,8},{64,80... | collective-permute-start | bytes 3145736 | tf_op jit(solution)/shard_map/ppermute | solution.py:23
  52.7 25.6 %collective-permute-start.5 = (bf16[512,1024]{1,0:T(8,128)(2,1)S(1)}, bf16[512,1024]{1,0:T(8,128)(2,1)S(1)}, u32[]{:S(2)}, u32[]{:S(2)}) collective-permute-start(bf16[512,1024]{1,0:T(8,128)(2,1)S(1)} %slice.44.refs_0_), channel_id=1, source_target_pairs={{0,48},{8,56},{16,0},{24,8},{32,16},{40,24},{48,32},{56,40},{64,11... | collective-permute-start | bytes 3145736 | tf_op jit(solution)/shard_map/ppermute | solution.py:23
  79.3 4.7 %collective-permute-start.7 = (bf16[512,1280]{1,0:T(8,128)(2,1)S(1)}, bf16[512,1280]{1,0:T(8,128)(2,1)S(1)}, u32[]{:S(2)}, u32[]{:S(2)}) collective-permute-start(bf16[512,1280]{1,0:T(8,128)(2,1)S(1)} %collective-permute-done.3.refs_4_), channel_id=1, source_target_pairs={{0,8},{8,0},{16,24},{24,16},{32,40},{40,32},{48,56},{56,48},{64,72... | collective-permute-start | bytes 3932168 | tf_op jit(solution)/shard_map/ppermute | solution.py:27
  79.3 29.5 %collective-permute-start.14 = (bf16[512,1024]{1,0:T(8,128)(2,1)S(1)}, bf16[512,1024]{1,0:T(8,128)(2,1)S(1)}, u32[]{:S(2)}, u32[]{:S(2)}) collective-permute-start(bf16[512,1024]{1,0:T(8,128)(2,1)S(1)} %slice.44.refs_0_), channel_id=1, source_target_pairs={{0,64},{8,72},{16,80},{24,88},{32,96},{40,104},{48,112},{56,120},{... | collective-permute-start | bytes 3145736 | tf_op jit(solution)/shard_map/ppermute | solution.py:27
  80.0 16.3 %collective-permute-start.12 = (bf16[256,1024]{1,0:T(8,128)(2,1)S(1)}, bf16[256,1024]{1,0:T(8,128)(2,1)S(1)}, u32[]{:S(2)}, u32[]{:S(2)}) collective-permute-start(bf16[256,1024]{1,0:T(8,128)(2,1)S(1)} %slice.36), channel_id=1, source_target_pairs={{0,48},{8,56},{16,0},{24,8},{32,16},{40,24},{48,32},{56,40},{64,11... | collective-permute-start | bytes 1572872 | tf_op jit(solution)/shard_map/ppermute | solution.py:23
  84.0 24.8 %collective-permute-start.13 = (bf16[256,1024]{1,0:T(8,128)(2,1)S(1)}, bf16[256,1024]{1,0:T(8,128)(2,1)S(1)}, u32[]{:S(2)}, u32[]{:S(2)}) collective-permute-start(bf16[256,1024]{1,0:T(8,128)(2,1)S(1)} %slice.37), channel_id=1, source_target_pairs={{0,16},{8,24},{16,32},{24,40},{32,48},{40,56},{48,0},{56,8},{64,80... | collective-permute-start | bytes 1572872 | tf_op jit(solution)/shard_map/ppermute | solution.py:23
  87.5 25.7 %collective-permute-start.8 = (bf16[160,1280]{1,0:T(8,128)(2,1)S(1)}, bf16[160,1280]{1,0:T(8,128)(2,1)S(1)}, u32[]{:S(2)}, u32[]{:S(2)}) collective-permute-start(bf16[160,1280]{1,0:T(8,128)(2,1)S(1)} %get-tuple-element.66), channel_id=1, source_target_pairs={{0,48},{8,56},{16,0},{24,8},{32,16},{40,24},{48,32},{56,40},{64,11... | collective-permute-start | bytes 1228808 | tf_op jit(solution)/shard_map/ppermute | solution.py:23
  90.8 22.4 %collective-permute-start.9 = (bf16[160,1280]{1,0:T(8,128)(2,1)S(1)}, bf16[160,1280]{1,0:T(8,128)(2,1)S(1)}, u32[]{:S(2)}, u32[]{:S(2)}) collective-permute-start(bf16[160,1280]{1,0:T(8,128)(2,1)S(1)} %get-tuple-element.67), channel_id=1, source_target_pairs={{0,32},{8,40},{16,48},{24,56},{32,0},{40,8},{48,16},{56,24},{64,96... | collective-permute-start | bytes 1228808 | tf_op jit(solution)/shard_map/ppermute | solution.py:23
  96.3 20.3 %collective-permute-start.10 = (bf16[160,1280]{1,0:T(8,128)(2,1)S(1)}, bf16[160,1280]{1,0:T(8,128)(2,1)S(1)}, u32[]{:S(2)}, u32[]{:S(2)}) collective-permute-start(bf16[160,1280]{1,0:T(8,128)(2,1)S(1)} %get-tuple-element.68), channel_id=1, source_target_pairs={{0,16},{8,24},{16,32},{24,40},{32,48},{40,56},{48,0},{56,8},{64,80... | collective-permute-start | bytes 1228808 | tf_op jit(solution)/shard_map/ppermute | solution.py:23
  116.6 26.8 %collective-permute-start.17 = (bf16[512,1024]{1,0:T(8,128)(2,1)S(1)}, bf16[512,1024]{1,0:T(8,128)(2,1)S(1)}, u32[]{:S(2)}, u32[]{:S(2)}) collective-permute-start(bf16[512,1024]{1,0:T(8,128)(2,1)S(1)} %collective-permute-done.14.refs_3_), channel_id=1, source_target_pairs={{0,16},{8,24},{16,32},{24,40},{32,48},{40,56},{48,0},{56,8},{64,80... | collective-permute-start | bytes 3145736 | tf_op jit(solution)/shard_map/ppermute | solution.py:23
  116.6 26.8 %collective-permute-start.18 = (bf16[512,1024]{1,0:T(8,128)(2,1)S(1)}, bf16[512,1024]{1,0:T(8,128)(2,1)S(1)}, u32[]{:S(2)}, u32[]{:S(2)}) collective-permute-start(bf16[512,1024]{1,0:T(8,128)(2,1)S(1)} %collective-permute-done.14.refs_3_), channel_id=1, source_target_pairs={{0,48},{8,56},{16,0},{24,8},{32,16},{40,24},{48,32},{56,40},{64,11... | collective-permute-start | bytes 3145736 | tf_op jit(solution)/shard_map/ppermute | solution.py:23
  119.8 14.9 %collective-permute-start.15 = (bf16[256,1024]{1,0:T(8,128)(2,1)S(1)}, bf16[256,1024]{1,0:T(8,128)(2,1)S(1)}, u32[]{:S(2)}, u32[]{:S(2)}) collective-permute-start(bf16[256,1024]{1,0:T(8,128)(2,1)S(1)} %collective-permute-done.12.refs_4_), channel_id=1, source_target_pairs={{0,64},{8,72},{16,80},{24,88},{32,96},{40,104},{48,112},{56,120},{... | collective-permute-start | bytes 1572872 | tf_op jit(solution)/shard_map/ppermute | solution.py:27
  121.2 22.2 %collective-permute-start.16 = (bf16[256,1024]{1,0:T(8,128)(2,1)S(1)}, bf16[256,1024]{1,0:T(8,128)(2,1)S(1)}, u32[]{:S(2)}, u32[]{:S(2)}) collective-permute-start(bf16[256,1024]{1,0:T(8,128)(2,1)S(1)} %collective-permute-done.13.refs_5_), channel_id=1, source_target_pairs={{0,64},{8,72},{16,80},{24,88},{32,96},{40,104},{48,112},{56,120},{... | collective-permute-start | bytes 1572872 | tf_op jit(solution)/shard_map/ppermute | solution.py:27
  132.6 10.9 %collective-permute-start.11 = (bf16[160,1024]{1,0:T(8,128)(2,1)S(1)}, bf16[160,1024]{1,0:T(8,128)(2,1)S(1)}, u32[]{:S(2)}, u32[]{:S(2)}) collective-permute-start(bf16[160,1024]{1,0:T(8,128)(2,1)S(1)} %attention.1.mixed_ref), channel_id=1, source_target_pairs={{0,8},{8,0},{16,24},{24,16},{32,40},{40,32},{48,56},{56,48},{64,72... | collective-permute-start | bytes 983048 | tf_op jit(solution)/shard_map/ppermute | solution.py:27
  145.9 4.2 %collective-permute-start.19 = (bf16[4096,256]{1,0:T(8,128)(2,1)S(1)}, bf16[4096,256]{1,0:T(8,128)(2,1)S(1)}, u32[]{:S(2)}, u32[]{:S(2)}) collective-permute-start(bf16[4096,256]{1,0:T(8,128)(2,1)S(1)} %terms.2), channel_id=1, source_target_pairs={{0,8},{8,0},{16,24},{24,16},{32,40},{40,32},{48,56},{56,48},{64,72... | collective-permute-start | bytes 6291464 | tf_op jit(solution)/shard_map/ppermute | solution.py:27
  153.0 10.6 %collective-permute-start.22 = (bf16[2,80,1024]{2,1,0:T(8,128)(2,1)S(1)}, bf16[2,80,1024]{2,1,0:T(8,128)(2,1)S(1)}, u32[]{:S(2)}, u32[]{:S(2)}) collective-permute-start(bf16[2,80,1024]{2,1,0:T(8,128)(2,1)S(1)} %get-tuple-element.82), channel_id=1, source_target_pairs={{0,6},{1,7},{2,0},{3,1},{4,2},{5,3},{6,4},{7,5},{8,14},{9,15},{10,... | collective-permute-start | bytes 983048 | tf_op jit(solution)/shard_map/ppermute | solution.py:31
  153.1 12.2 %collective-permute-start.21 = (bf16[2,80,1024]{2,1,0:T(8,128)(2,1)S(1)}, bf16[2,80,1024]{2,1,0:T(8,128)(2,1)S(1)}, u32[]{:S(2)}, u32[]{:S(2)}) collective-permute-start(bf16[2,80,1024]{2,1,0:T(8,128)(2,1)S(1)} %get-tuple-element.81), channel_id=1, source_target_pairs={{0,4},{1,5},{2,6},{3,7},{4,0},{5,1},{6,2},{7,3},{8,12},{9,13},{10,... | collective-permute-start | bytes 983048 | tf_op jit(solution)/shard_map/ppermute | solution.py:31
  154.2 17.3 %collective-permute-start.20 = (bf16[2,80,1024]{2,1,0:T(8,128)(2,1)S(1)}, bf16[2,80,1024]{2,1,0:T(8,128)(2,1)S(1)}, u32[]{:S(2)}, u32[]{:S(2)}) collective-permute-start(bf16[2,80,1024]{2,1,0:T(8,128)(2,1)S(1)} %get-tuple-element.80), channel_id=1, source_target_pairs={{0,2},{1,3},{2,4},{3,5},{4,6},{5,7},{6,0},{7,1},{8,10},{9,11},{10,... | collective-permute-start | bytes 983048 | tf_op jit(solution)/shard_map/ppermute | solution.py:31
  155.1 19.3 %collective-permute-start.24 = (bf16[4,80,1024]{2,1,0:T(8,128)(2,1)S(1)}, bf16[4,80,1024]{2,1,0:T(8,128)(2,1)S(1)}, u32[]{:S(2)}, u32[]{:S(2)}) collective-permute-start(bf16[4,80,1024]{2,1,0:T(8,128)(2,1)S(1)} %get-tuple-element.84), channel_id=1, source_target_pairs={{0,1},{1,0},{2,3},{3,2},{4,5},{5,4},{6,7},{7,6},{8,9},{9,8},{10,11... | collective-permute-start | bytes 1966088 | tf_op jit(solution)/shard_map/ppermute | solution.py:35
  171.7 7.7 %collective-permute-start.23 = (bf16[80,1024]{1,0:T(8,128)(2,1)S(1)}, bf16[80,1024]{1,0:T(8,128)(2,1)S(1)}, u32[]{:S(2)}, u32[]{:S(2)}) collective-permute-start(bf16[80,1024]{1,0:T(8,128)(2,1)S(1)} %fusion.7), channel_id=1, source_target_pairs={{0,1},{1,0},{2,3},{3,2},{4,5},{5,4},{6,7},{7,6},{8,9},{9,8},{10,11... | collective-permute-start | bytes 491528 | tf_op jit(solution)/shard_map/ppermute | solution.py:35
  174.7 7.2 %collective-permute-start.27 = (bf16[80,1024]{1,0:T(8,128)(2,1)S(1)}, bf16[80,1024]{1,0:T(8,128)(2,1)S(1)}, u32[]{:S(2)}, u32[]{:S(2)}) collective-permute-start(bf16[80,1024]{1,0:T(8,128)(2,1)S(1)} %get-tuple-element.88), channel_id=1, source_target_pairs={{0,6},{1,7},{2,0},{3,1},{4,2},{5,3},{6,4},{7,5},{8,14},{9,15},{10,... | collective-permute-start | bytes 491528 | tf_op jit(solution)/shard_map/ppermute | solution.py:31
  175.9 8.3 %collective-permute-start.26 = (bf16[80,1024]{1,0:T(8,128)(2,1)S(1)}, bf16[80,1024]{1,0:T(8,128)(2,1)S(1)}, u32[]{:S(2)}, u32[]{:S(2)}) collective-permute-start(bf16[80,1024]{1,0:T(8,128)(2,1)S(1)} %get-tuple-element.89), channel_id=1, source_target_pairs={{0,4},{1,5},{2,6},{3,7},{4,0},{5,1},{6,2},{7,3},{8,12},{9,13},{10,... | collective-permute-start | bytes 491528 | tf_op jit(solution)/shard_map/ppermute | solution.py:31
  177.2 8.6 %collective-permute-start.25 = (bf16[80,1024]{1,0:T(8,128)(2,1)S(1)}, bf16[80,1024]{1,0:T(8,128)(2,1)S(1)}, u32[]{:S(2)}, u32[]{:S(2)}) collective-permute-start(bf16[80,1024]{1,0:T(8,128)(2,1)S(1)} %get-tuple-element.87), channel_id=1, source_target_pairs={{0,2},{1,3},{2,4},{3,5},{4,6},{5,7},{6,0},{7,1},{8,10},{9,11},{10,... | collective-permute-start | bytes 491528 | tf_op jit(solution)/shard_map/ppermute | solution.py:31

commit v13 on v12

--- a/solution.py
+++ b/solution.py
@@ -201,11 +201,7 @@
         in_specs=[vmem] * (1 + len(sources)),
         out_specs=vmem,
         compiler_params=pltpu.CompilerParams(vmem_limit_bytes=20 * MIB),
-        cost_estimate=pl.CostEstimate(
-            flops=2 * rows * depth * width,
-            bytes_accessed=2 * (rows * depth + depth * width + rows * width),
-            transcendentals=0,
-        ),
+        cost_estimate=pl.CostEstimate(flops=0, bytes_accessed=rows, transcendentals=0),
         name="terms",
     )(mixed, *sources)
 
@@ -217,10 +213,8 @@
     y_lo, z, core = f // 8, lax.rem(f // 2, NZ), lax.rem(f, 2)
     width = placed.shape[0]
     owned = width // owner_ref.shape[1]
-    for n, dy, dz, dc, t0, blocks, begin in spots:
-        first = (
-            lax.rem(y_lo + dy, 2) * 64 + lax.rem(z + dz, NZ) * 16 + lax.rem(core + dc, 2) * 8 + t0
-        )
+    for n, dy, dz, dc, blocks, begin in spots:
+        first = lax.rem(y_lo + dy, 2) * 64 + lax.rem(z + dz, NZ) * 16 + lax.rem(core + dc, 2) * 8
 
         def put(b, carry, n=n, first=first, begin=begin):
             goal = pl.multiple_of(owner_ref[1, first + b] * owned, owned)
@@ -434,25 +428,27 @@
     sums = partials(parts, (w_y, w_yc), begun)
     sums = [sums[0]] + [z_shift(sums[k], -k) for k in range(1, NZ)]
     far_a, far_b, across = after((far_a, far_b, across))
-    across_far_a, across_far_b = flip(far_a, 8), flip(far_b, 8)
+    far = jnp.concatenate([far_a, far_b])
+    across_far = flip(far, 8)
     (across,) = after((across,), *sums)
     across_below, across_above = z_shift(across, 1), z_shift(across, -1)
     mixed = attention(sums, cos, sin, cache, lengths)
 
     mixed_c = flip(mixed, 1)
-    sources = (own, below, above, across, far_a, far_b)
-    sources += (across_far_a, across_far_b, across_below, across_above)
-    theirs = terms_of(mixed_c, sources)
-    mine = terms_of(*after((mixed,), theirs), sources)
-    pieces = (mine, flip(theirs, 1))
-    places = ((0, 0, 0), (0, 3, 0), (0, 1, 0), (1, 0, 0), (0, 2, 0), (0, 2, 4))
-    places += ((1, 2, 0), (1, 2, 4), (1, 3, 0), (1, 1, 0))
+    sources = (own, below, above, across, far, across_far, across_below, across_above)
+    parts_of = (sources[:5], sources[5:])
+    theirs = [terms_of(mixed_c, part) for part in parts_of]
+    mine = terms_of(*after((mixed,), *theirs), sources)
+    pieces = (mine, *(flip(value, 1) for value in theirs))
+    places = ((0, 0), (0, 3), (0, 1), (1, 0), (0, 2), (1, 2), (1, 3), (1, 1))
     spots = []
     for core in range(2):
-        begin = 0
-        for (dy, dz, t0), source in zip(places, sources):
+        begin, piece = 0, core
+        for n, ((dy, dz), source) in enumerate(zip(places, sources)):
+            if core == 1 and n == len(parts_of[0]):
+                begin, piece = 0, 2
             size = source.shape[0]
-            spots.append((core, dy, dz, core, t0, size // owned, begin))
+            spots.append((piece, dy, dz, core, size // owned, begin))
             begin += size
     slabs = place(pieces, tuple(spots), block_owner, groups, rows)
 

time: 187 us -> 183 us (0.979)
  waiting for transfers between devices: 104 us -> 99.7 us
    ppermute x8, waiting for transfers between devices: 13.2 us -> 2.58 us  [flip(): return lax.ppermute(value, 'fsdp', [(f, f ^ bit) for f in range(16)])]
    ppermute x12, waiting for transfers between devices: 45.6 us -> 51.8 us  [z_shift(): return lax.ppermute(value, 'fsdp', pairs)]
    pallas_call x2 -> x3, Pallas kernels: 4.88 us -> 5.17 us  [terms_of(): pl.pallas_call(terms_kernel, out_shape=jax.ShapeDtypeStruct((width, lanes...]
  transfers between devices with their start and end apart: 29 -> 29, of which waited for: 17 -> 16; matrix products, arithmetic and copies ran while one was open for 2% -> 2% of each run, Pallas kernels for 13% -> 15%
where the time goes in v13:
time: 183 us
  waiting for transfers between devices  99.7 us (54%)
  starting transfers between devices  43.2 us (24%)
  Pallas kernels  34.6 us (19%)
  local copies, waits for them, and re-layouts  2.99 us (2%)
  other arithmetic  1.83 us (1%)
    ppermute x12, waiting for transfers between devices, z_shift(): return lax.ppermute(value, 'fsdp', pairs)  51.8 us
    all_to_all x1, waiting for transfers between devices, body(): both = lax.all_to_all(copy, 'tp', split_axis=0, concat_axis=0, tiled=True)  23.6 us
    ppermute x12, starting transfers between devices, z_shift(): return lax.ppermute(value, 'fsdp', pairs)  21.6 us
    ppermute x6, waiting for transfers between devices, x_shift(): lax.ppermute(value, 'tp', [(t, (t // 2 + k) % NX * 2 + t % 2) for t in ra...  20.8 us
    pallas_call x1, Pallas kernels, attention(): pl.pallas_call(attention_kernel, grid=(rows // GROUP,), out_shape=jax.Sha...  10.7 us
    all_to_all x1, starting transfers between devices, body(): both = lax.all_to_all(copy, 'tp', split_axis=0, concat_axis=0, tiled=True)  7.28 us
    pallas_call x2, Pallas kernels, partials(): pl.pallas_call(functools.partial(partial_kernel, begun), grid=(cols // ti...  6.68 us
    ppermute x6, starting transfers between devices, x_shift(): lax.ppermute(value, 'tp', [(t, (t // 2 + k) % NX * 2 + t % 2) for t in ra...  5.87 us
  transfers between devices with their start and end apart: 29, of which 16 were waited for; matrix products, arithmetic and copies ran while one was open for 2% of the time, Pallas kernels for 15%

profile of v13, /device:TPU:0, one launch (start us, length us, event | category | flops | bytes accessed | tf_op | source)
XLA Modules:
  0.0 182.5 jit_solution(7618115292358357541)
XLA Ops:
  0.0 4.3 %slabs.1 = bf16[8,64,2304]{2,1,0:T(8,128)(2,1)} custom-call(f32[64,10240]{1,0:T(8,128)} %value.1, f32[64,10240]{1,0:T(8,128)} %value.1, f32[64,10240]{1,0:T(8,128)} %value.1, f32[64,8192]{1,0:T(8,128)} %back.1), custom_call_target="tpu_custom_call" | custom-call | bytes 7077888 | tf_op jit(solution)/shard_map/slabs/pallas_call | solution.py:56
  4.3 7.3 %all-to-all-start = ((bf16[8,64,2304]{2,1,0:T(8,128)(2,1)}), bf16[8,64,2304]{2,1,0:T(8,128)(2,1)}, u32[]{:S(2)}, u32[]{:S(2)}) async-start(bf16[8,64,2304]{2,1,0:T(8,128)(2,1)} %slabs.1), calls=%async_computation | async-start | bytes 4718592 | tf_op jit(solution)/shard_map/all_to_all | solution.py:412
  11.7 4.8 %shuffle.1 = (bf16[160,2048]{1,0:T(8,128)(2,1)S(1)}, bf16[160,2048]{1,0:T(8,128)(2,1)}, bf16[160,2048]{1,0:T(8,128)(2,1)}, bf16[160,2048]{1,0:T(8,128)(2,1)}) custom-call(s32[2,128]{1,0:T(2,128)S(1)} %copy-done.1, bf16[160,8192]{1,0:T(8,128)(2,1)S(1)} %bitcast.34), custom_call_target="tpu_custom_call" | custom-call | flops 10485760 | bytes 5242880 | tf_op jit(solution)/shard_map/shuffle/pallas_call | solution.py:105
  16.5 1.9 %collective-permute-start = (bf16[160,2048]{1,0:T(8,128)(2,1)}, bf16[160,2048]{1,0:T(8,128)(2,1)S(1)}, u32[]{:S(2)}, u32[]{:S(2)}) collective-permute-start(bf16[160,2048]{1,0:T(8,128)(2,1)} %get-tuple-element.46), channel_id=1, source_target_pairs={{0,16},{8,24},{16,32},{24,40},{32,48},{40,56},{48,0},{56,8},{64,80... | collective-permute-start | bytes 1966088 | tf_op jit(solution)/shard_map/ppermute | solution.py:23
  18.4 3.6 %collective-permute-start.1 = (bf16[160,2048]{1,0:T(8,128)(2,1)}, bf16[160,2048]{1,0:T(8,128)(2,1)S(1)}, u32[]{:S(2)}, u32[]{:S(2)}) collective-permute-start(bf16[160,2048]{1,0:T(8,128)(2,1)} %get-tuple-element.47), channel_id=1, source_target_pairs={{0,32},{8,40},{16,48},{24,56},{32,0},{40,8},{48,16},{56,24},{64,96... | collective-permute-start | bytes 1966088 | tf_op jit(solution)/shard_map/ppermute | solution.py:23
  23.1 23.6 %all-to-all-done = bf16[8,64,2304]{2,1,0:T(8,128)(2,1)} async-done(((bf16[8,64,2304]{2,1,0:T(8,128)(2,1)}), bf16[8,64,2304]{2,1,0:T(8,128)(2,1)}, u32[]{:S(2)}, u32[]{:S(2)}) %all-to-all-start) | async-done | bytes 2359328 | tf_op jit(solution)/shard_map/all_to_all | solution.py:412
  50.7 2.0 %collective-permute-start.4 = (bf16[512,1024]{1,0:T(8,128)(2,1)S(1)}, bf16[512,1024]{1,0:T(8,128)(2,1)S(1)}, u32[]{:S(2)}, u32[]{:S(2)}) collective-permute-start(bf16[512,1024]{1,0:T(8,128)(2,1)S(1)} %slice.44.refs_0_), channel_id=1, source_target_pairs={{0,16},{8,24},{16,32},{24,40},{32,48},{40,56},{48,0},{56,8},{64,80... | collective-permute-start | bytes 3145736 | tf_op jit(solution)/shard_map/ppermute | solution.py:23
  52.7 2.2 %collective-permute-start.5 = (bf16[512,1024]{1,0:T(8,128)(2,1)S(1)}, bf16[512,1024]{1,0:T(8,128)(2,1)S(1)}, u32[]{:S(2)}, u32[]{:S(2)}) collective-permute-start(bf16[512,1024]{1,0:T(8,128)(2,1)S(1)} %slice.44.refs_0_), channel_id=1, source_target_pairs={{0,48},{8,56},{16,0},{24,8},{32,16},{40,24},{48,32},{56,40},{64,11... | collective-permute-start | bytes 3145736 | tf_op jit(solution)/shard_map/ppermute | solution.py:23
  54.9 3.2 %partials.1 = (f32[160,1280]{1,0:T(8,128)S(1)}, f32[160,1280]{1,0:T(8,128)S(1)}, f32[160,1280]{1,0:T(8,128)S(1)}, f32[160,1280]{1,0:T(8,128)S(1)}) custom-call(bf16[160,2048]{1,0:T(8,128)(2,1)S(1)} %get-tuple-element.49.refs_0_, bf16[160,2048]{1,0:T(8,128)(2,1)S(1)} %collective-permute-done.refs_1_, bf16[160,2048]{1,0:T(8,128)(2,1)S(1)} %collective-permute-done.1.refs_2_, ...), custom_call_target="tpu_custom_call" | custom-call | flops 1677721600 | bytes 7208960 | tf_op jit(solution)/shard_map/partials/pallas_call | solution.py:152
  58.1 20.2 %collective-permute-done.4.refs_1_ = bf16[512,1024]{1,0:T(8,128)(2,1)S(1)} collective-permute-done((bf16[512,1024]{1,0:T(8,128)(2,1)S(1)}, bf16[512,1024]{1,0:T(8,128)(2,1)S(1)}, u32[]{:S(2)}, u32[]{:S(2)}) %collective-permute-start.4) | collective-permute-done | bytes 1048608 | tf_op jit(solution)/shard_map/ppermute | solution.py:23
  80.0 4.0 %collective-permute-start.12 = (bf16[256,1024]{1,0:T(8,128)(2,1)S(1)}, bf16[256,1024]{1,0:T(8,128)(2,1)S(1)}, u32[]{:S(2)}, u32[]{:S(2)}) collective-permute-start(bf16[256,1024]{1,0:T(8,128)(2,1)S(1)} %slice.36), channel_id=1, source_target_pairs={{0,48},{8,56},{16,0},{24,8},{32,16},{40,24},{48,32},{56,40},{64,11... | collective-permute-start | bytes 1572872 | tf_op jit(solution)/shard_map/ppermute | solution.py:23
  84.1 3.5 %partials_rest.1 = (f32[160,1280]{1,0:T(8,128)S(1)}, bf16[160,1280]{1,0:T(8,128)(2,1)S(1)}, bf16[160,1280]{1,0:T(8,128)(2,1)S(1)}, bf16[160,1280]{1,0:T(8,128)(2,1)S(1)}) custom-call(bf16[160,2048]{1,0:T(8,128)(2,1)S(1)} %get-tuple-element.49.refs_0_, bf16[160,2048]{1,0:T(8,128)(2,1)S(1)} %collective-permute-done.refs_1_, ...), custom_call_target="tpu_custom_call" | custom-call | flops 1677721600 | bytes 7208960 | tf_op jit(solution)/shard_map/partials_rest/pallas_call | solution.py:152
  87.5 3.3 %collective-permute-start.8 = (bf16[160,1280]{1,0:T(8,128)(2,1)S(1)}, bf16[160,1280]{1,0:T(8,128)(2,1)S(1)}, u32[]{:S(2)}, u32[]{:S(2)}) collective-permute-start(bf16[160,1280]{1,0:T(8,128)(2,1)S(1)} %get-tuple-element.66), channel_id=1, source_target_pairs={{0,48},{8,56},{16,0},{24,8},{32,16},{40,24},{48,32},{56,40},{64,11... | collective-permute-start | bytes 1228808 | tf_op jit(solution)/shard_map/ppermute | solution.py:23
  90.8 5.5 %collective-permute-done.12 = bf16[256,1024]{1,0:T(8,128)(2,1)S(1)} collective-permute-done((bf16[256,1024]{1,0:T(8,128)(2,1)S(1)}, bf16[256,1024]{1,0:T(8,128)(2,1)S(1)}, u32[]{:S(2)}, u32[]{:S(2)}) %collective-permute-start.12) | collective-permute-done | bytes 524320 | tf_op jit(solution)/shard_map/ppermute | solution.py:23
  96.7 12.2 %collective-permute-done.13 = bf16[256,1024]{1,0:T(8,128)(2,1)S(1)} collective-permute-done((bf16[256,1024]{1,0:T(8,128)(2,1)S(1)}, bf16[256,1024]{1,0:T(8,128)(2,1)S(1)}, u32[]{:S(2)}, u32[]{:S(2)}) %collective-permute-start.13) | collective-permute-done | bytes 524320 | tf_op jit(solution)/shard_map/ppermute | solution.py:23
  110.3 2.8 %collective-permute-done.8.p1 = bf16[160,1280]{1,0:T(8,128)(2,1)S(1)} collective-permute-done((bf16[160,1280]{1,0:T(8,128)(2,1)S(1)}, bf16[160,1280]{1,0:T(8,128)(2,1)S(1)}, u32[]{:S(2)}, u32[]{:S(2)}) %collective-permute-start.8) | collective-permute-done | bytes 409632 | tf_op jit(solution)/shard_map/ppermute | solution.py:23
  113.2 3.4 %collective-permute-done.10.p3 = bf16[160,1280]{1,0:T(8,128)(2,1)S(1)} collective-permute-done((bf16[160,1280]{1,0:T(8,128)(2,1)S(1)}, bf16[160,1280]{1,0:T(8,128)(2,1)S(1)}, u32[]{:S(2)}, u32[]{:S(2)}) %collective-permute-start.10) | collective-permute-done | bytes 409632 | tf_op jit(solution)/shard_map/ppermute | solution.py:23
  116.6 3.2 %collective-permute-start.17 = (bf16[512,1024]{1,0:T(8,128)(2,1)S(1)}, bf16[512,1024]{1,0:T(8,128)(2,1)S(1)}, u32[]{:S(2)}, u32[]{:S(2)}) collective-permute-start(bf16[512,1024]{1,0:T(8,128)(2,1)S(1)} %collective-permute-done.14.refs_3_), channel_id=1, source_target_pairs={{0,48},{8,56},{16,0},{24,8},{32,16},{40,24},{48,32},{56,40},{64,11... | collective-permute-start | bytes 3145736 | tf_op jit(solution)/shard_map/ppermute | solution.py:23
  119.8 10.7 %attention.1.mixed_ref = bf16[160,1024]{1,0:T(8,128)(2,1)S(1)} custom-call(s32[80]{0:T(128)S(1)} %copy-done.2, f32[160,1280]{1,0:T(8,128)S(1)} %get-tuple-element.65.p0, bf16[160,1280]{1,0:T(8,128)(2,1)S(1)} %collective-permute-done.8.p1, bf16[160,1280]{1,0:T(8,128)(2,1)S(1)} %collective-permute-done.9.p2, bf16[160,1280]{1,0:T(8,128)(2,1)S(1)} %collective-permute-done.10.p3, ...), custom_call_target="tpu_custom_call" | custom-call | flops 167772160 | bytes 41943040 | tf_op jit(solution)/shard_map/attention/pallas_call | solution.py:370
  130.8 1.6 collective-permute-done.11.mixed_ref
  132.4 1.6 terms.3
  134.3 7.7 %collective-permute-done.16.refs_1_.refs_6_ = bf16[512,1024]{1,0:T(8,128)(2,1)S(1)} collective-permute-done((bf16[512,1024]{1,0:T(8,128)(2,1)S(1)}, bf16[512,1024]{1,0:T(8,128)(2,1)S(1)}, u32[]{:S(2)}, u32[]{:S(2)}) %collective-permute-start.16) | collective-permute-done | bytes 1048608 | tf_op jit(solution)/shard_map/ppermute | solution.py:23
  143.1 2.4 %terms.5.refs_0_ = bf16[4096,256]{1,0:T(8,128)(2,1)S(1)} custom-call(bf16[160,1024]{1,0:T(8,128)(2,1)S(1)} %attention.1.mixed_ref, bf16[512,1024]{1,0:T(8,128)(2,1)S(1)} %slice.44.refs_0_, bf16[512,1024]{1,0:T(8,128)(2,1)S(1)} %collective-permute-done.4.refs_1_, bf16[512,1024]{1,0:T(8,128)(2,1)S(1)} %collective-permute-done.5.refs_2_, ...), custom_call_target="tpu_custom_call" | custom-call | bytes 160 | tf_op jit(solution)/shard_map/terms/pallas_call | solution.py:198
  145.6 2.9 %place.1 = (bf16[2,80,1024]{2,1,0:T(8,128)(2,1)S(1)}, bf16[2,80,1024]{2,1,0:T(8,128)(2,1)S(1)}, bf16[2,80,1024]{2,1,0:T(8,128)(2,1)S(1)}, bf16[2,80,1024]{2,1,0:...) custom-call(s32[2,128]{1,0:T(2,128)S(1)} %copy-done.1, ...), custom_call_target="tpu_custom_call" | custom-call | bytes 5242880 | tf_op jit(solution)/shard_map/place/pallas_call | solution.py:241
  150.6 2.2 %collective-permute-start.24 = (bf16[4,80,1024]{2,1,0:T(8,128)(2,1)S(1)}, bf16[4,80,1024]{2,1,0:T(8,128)(2,1)S(1)}, u32[]{:S(2)}, u32[]{:S(2)}) collective-permute-start(bf16[4,80,1024]{2,1,0:T(8,128)(2,1)S(1)} %get-tuple-element.84), channel_id=1, source_target_pairs={{0,1},{1,0},{2,3},{3,2},{4,5},{5,4},{6,7},{7,6},{8,9},{9,8},{10,11... | collective-permute-start | bytes 1966088 | tf_op jit(solution)/shard_map/ppermute | solution.py:35
  152.8 6.3 %collective-permute-done.22 = bf16[2,80,1024]{2,1,0:T(8,128)(2,1)S(1)} collective-permute-done((bf16[2,80,1024]{2,1,0:T(8,128)(2,1)S(1)}, bf16[2,80,1024]{2,1,0:T(8,128)(2,1)S(1)}, u32[]{:S(2)}, u32[]{:S(2)}) %collective-permute-start.22) | collective-permute-done | bytes 327712 | tf_op jit(solution)/shard_map/ppermute | solution.py:31
  159.1 1.6 collective-permute-done.21
  160.7 6.6 %collective-permute-done.20 = bf16[2,80,1024]{2,1,0:T(8,128)(2,1)S(1)} collective-permute-done((bf16[2,80,1024]{2,1,0:T(8,128)(2,1)S(1)}, bf16[2,80,1024]{2,1,0:T(8,128)(2,1)S(1)}, u32[]{:S(2)}, u32[]{:S(2)}) %collective-permute-start.20) | collective-permute-done | bytes 327712 | tf_op jit(solution)/shard_map/ppermute | solution.py:31
  167.6 2.7 %collective-permute-start.23 = (bf16[80,1024]{1,0:T(8,128)(2,1)S(1)}, bf16[80,1024]{1,0:T(8,128)(2,1)S(1)}, u32[]{:S(2)}, u32[]{:S(2)}) collective-permute-start(bf16[80,1024]{1,0:T(8,128)(2,1)S(1)} %fusion.7), channel_id=1, source_target_pairs={{0,1},{1,0},{2,3},{3,2},{4,5},{5,4},{6,7},{7,6},{8,9},{9,8},{10,11... | collective-permute-start | bytes 491528 | tf_op jit(solution)/shard_map/ppermute | solution.py:35
  175.3 2.4 %collective-permute-done.27 = bf16[80,1024]{1,0:T(8,128)(2,1)S(1)} collective-permute-done((bf16[80,1024]{1,0:T(8,128)(2,1)S(1)}, bf16[80,1024]{1,0:T(8,128)(2,1)S(1)}, u32[]{:S(2)}, u32[]{:S(2)}) %collective-permute-start.27) | collective-permute-done | bytes 163872 | tf_op jit(solution)/shard_map/ppermute | solution.py:31
  177.8 2.4 %collective-permute-done.26 = bf16[80,1024]{1,0:T(8,128)(2,1)S(1)} collective-permute-done((bf16[80,1024]{1,0:T(8,128)(2,1)S(1)}, bf16[80,1024]{1,0:T(8,128)(2,1)S(1)}, u32[]{:S(2)}, u32[]{:S(2)}) %collective-permute-start.26) | collective-permute-done | bytes 163872 | tf_op jit(solution)/shard_map/ppermute | solution.py:31
  180.1 1.6 collective-permute-done.25
  (59 shorter events, 18.6 us)
Async XLA Ops:
  4.3 7.3 %copy-start = (bf16[2,80,8192]{2,1,0:T(8,128)(2,1)S(1)}, bf16[2,80,8192]{2,1,0:T(8,128)(2,1)}, u32[]{:S(2)}) copy-start(bf16[2,80,8192]{2,1,0:T(8,128)(2,1)} %param.6) | copy-start | bytes 7864324
  4.3 7.3 %copy-start.1 = (s32[2,128]{1,0:T(2,128)S(1)}, s32[2,128]{1,0:T(2,128)}, u32[]{:S(2)}) copy-start(s32[2,128]{1,0:T(2,128)} %owner_ref.3) | copy-start | bytes 3076
  4.3 42.3 %all-to-all-start = ((bf16[8,64,2304]{2,1,0:T(8,128)(2,1)}), bf16[8,64,2304]{2,1,0:T(8,128)(2,1)}, u32[]{:S(2)}, u32[]{:S(2)}) async-start(bf16[8,64,2304]{2,1,0:T(8,128)(2,1)} %slabs.1), calls=%async_computation | async-start | bytes 4718592 | tf_op jit(solution)/shard_map/all_to_all | solution.py:412
  11.6 11.3 %copy-start.2 = (s32[80]{0:T(128)S(1)}, s32[80]{0:T(128)}, u32[]{:S(2)}) copy-start(s32[80]{0:T(128)} %lengths_ref.1) | copy-start | bytes 964
  16.5 34.2 %collective-permute-start = (bf16[160,2048]{1,0:T(8,128)(2,1)}, bf16[160,2048]{1,0:T(8,128)(2,1)S(1)}, u32[]{:S(2)}, u32[]{:S(2)}) collective-permute-start(bf16[160,2048]{1,0:T(8,128)(2,1)} %get-tuple-element.46), channel_id=1, source_target_pairs={{0,16},{8,24},{16,32},{24,40},{32,48},{40,56},{48,0},{56,8},{64,80... | collective-permute-start | bytes 1966088 | tf_op jit(solution)/shard_map/ppermute | solution.py:23
  18.4 32.3 %collective-permute-start.1 = (bf16[160,2048]{1,0:T(8,128)(2,1)}, bf16[160,2048]{1,0:T(8,128)(2,1)S(1)}, u32[]{:S(2)}, u32[]{:S(2)}) collective-permute-start(bf16[160,2048]{1,0:T(8,128)(2,1)} %get-tuple-element.47), channel_id=1, source_target_pairs={{0,32},{8,40},{16,48},{24,56},{32,0},{40,8},{48,16},{56,24},{64,96... | collective-permute-start | bytes 1966088 | tf_op jit(solution)/shard_map/ppermute | solution.py:23
  22.0 28.7 %collective-permute-start.2 = (bf16[160,2048]{1,0:T(8,128)(2,1)}, bf16[160,2048]{1,0:T(8,128)(2,1)S(1)}, u32[]{:S(2)}, u32[]{:S(2)}) collective-permute-start(bf16[160,2048]{1,0:T(8,128)(2,1)} %get-tuple-element.48), channel_id=1, source_target_pairs={{0,48},{8,56},{16,0},{24,8},{32,16},{40,24},{48,32},{56,40},{64,11... | collective-permute-start | bytes 1966088 | tf_op jit(solution)/shard_map/ppermute | solution.py:23
  48.0 6.9 %collective-permute-start.6 = (bf16[512,1280]{1,0:T(8,128)(2,1)S(1)}, bf16[512,1280]{1,0:T(8,128)(2,1)S(1)}, u32[]{:S(2)}, u32[]{:S(2)}) collective-permute-start(bf16[512,1280]{1,0:T(8,128)(2,1)S(1)} %slice.45.refs_4_), channel_id=1, source_target_pairs={{0,8},{8,0},{16,24},{24,16},{32,40},{40,32},{48,56},{56,48},{64,72... | collective-permute-start | bytes 3932168 | tf_op jit(solution)/shard_map/ppermute | solution.py:27
  48.1 31.2 %collective-permute-start.3 = (bf16[512,1280]{1,0:T(8,128)(2,1)S(1)}, bf16[512,1280]{1,0:T(8,128)(2,1)S(1)}, u32[]{:S(2)}, u32[]{:S(2)}) collective-permute-start(bf16[512,1280]{1,0:T(8,128)(2,1)S(1)} %slice.45.refs_4_), channel_id=1, source_target_pairs={{0,64},{8,72},{16,80},{24,88},{32,96},{40,104},{48,112},{56,120},{... | collective-permute-start | bytes 3932168 | tf_op jit(solution)/shard_map/ppermute | solution.py:27
  50.7 27.6 %collective-permute-start.4 = (bf16[512,1024]{1,0:T(8,128)(2,1)S(1)}, bf16[512,1024]{1,0:T(8,128)(2,1)S(1)}, u32[]{:S(2)}, u32[]{:S(2)}) collective-permute-start(bf16[512,1024]{1,0:T(8,128)(2,1)S(1)} %slice.44.refs_0_), channel_id=1, source_target_pairs={{0,16},{8,24},{16,32},{24,40},{32,48},{40,56},{48,0},{56,8},{64,80... | collective-permute-start | bytes 3145736 | tf_op jit(solution)/shard_map/ppermute | solution.py:23
  52.7 25.6 %collective-permute-start.5 = (bf16[512,1024]{1,0:T(8,128)(2,1)S(1)}, bf16[512,1024]{1,0:T(8,128)(2,1)S(1)}, u32[]{:S(2)}, u32[]{:S(2)}) collective-permute-start(bf16[512,1024]{1,0:T(8,128)(2,1)S(1)} %slice.44.refs_0_), channel_id=1, source_target_pairs={{0,48},{8,56},{16,0},{24,8},{32,16},{40,24},{48,32},{56,40},{64,11... | collective-permute-start | bytes 3145736 | tf_op jit(solution)/shard_map/ppermute | solution.py:23
  79.3 4.7 %collective-permute-start.7 = (bf16[512,1280]{1,0:T(8,128)(2,1)S(1)}, bf16[512,1280]{1,0:T(8,128)(2,1)S(1)}, u32[]{:S(2)}, u32[]{:S(2)}) collective-permute-start(bf16[512,1280]{1,0:T(8,128)(2,1)S(1)} %collective-permute-done.3.refs_4_), channel_id=1, source_target_pairs={{0,8},{8,0},{16,24},{24,16},{32,40},{40,32},{48,56},{56,48},{64,72... | collective-permute-start | bytes 3932168 | tf_op jit(solution)/shard_map/ppermute | solution.py:27
  79.3 29.5 %collective-permute-start.14 = (bf16[512,1024]{1,0:T(8,128)(2,1)S(1)}, bf16[512,1024]{1,0:T(8,128)(2,1)S(1)}, u32[]{:S(2)}, u32[]{:S(2)}) collective-permute-start(bf16[512,1024]{1,0:T(8,128)(2,1)S(1)} %slice.44.refs_0_), channel_id=1, source_target_pairs={{0,64},{8,72},{16,80},{24,88},{32,96},{40,104},{48,112},{56,120},{... | collective-permute-start | bytes 3145736 | tf_op jit(solution)/shard_map/ppermute | solution.py:27
  80.0 16.3 %collective-permute-start.12 = (bf16[256,1024]{1,0:T(8,128)(2,1)S(1)}, bf16[256,1024]{1,0:T(8,128)(2,1)S(1)}, u32[]{:S(2)}, u32[]{:S(2)}) collective-permute-start(bf16[256,1024]{1,0:T(8,128)(2,1)S(1)} %slice.36), channel_id=1, source_target_pairs={{0,48},{8,56},{16,0},{24,8},{32,16},{40,24},{48,32},{56,40},{64,11... | collective-permute-start | bytes 1572872 | tf_op jit(solution)/shard_map/ppermute | solution.py:23
  84.0 24.8 %collective-permute-start.13 = (bf16[256,1024]{1,0:T(8,128)(2,1)S(1)}, bf16[256,1024]{1,0:T(8,128)(2,1)S(1)}, u32[]{:S(2)}, u32[]{:S(2)}) collective-permute-start(bf16[256,1024]{1,0:T(8,128)(2,1)S(1)} %slice.37), channel_id=1, source_target_pairs={{0,16},{8,24},{16,32},{24,40},{32,48},{40,56},{48,0},{56,8},{64,80... | collective-permute-start | bytes 1572872 | tf_op jit(solution)/shard_map/ppermute | solution.py:23
  87.5 25.7 %collective-permute-start.8 = (bf16[160,1280]{1,0:T(8,128)(2,1)S(1)}, bf16[160,1280]{1,0:T(8,128)(2,1)S(1)}, u32[]{:S(2)}, u32[]{:S(2)}) collective-permute-start(bf16[160,1280]{1,0:T(8,128)(2,1)S(1)} %get-tuple-element.66), channel_id=1, source_target_pairs={{0,48},{8,56},{16,0},{24,8},{32,16},{40,24},{48,32},{56,40},{64,11... | collective-permute-start | bytes 1228808 | tf_op jit(solution)/shard_map/ppermute | solution.py:23
  90.8 22.4 %collective-permute-start.9 = (bf16[160,1280]{1,0:T(8,128)(2,1)S(1)}, bf16[160,1280]{1,0:T(8,128)(2,1)S(1)}, u32[]{:S(2)}, u32[]{:S(2)}) collective-permute-start(bf16[160,1280]{1,0:T(8,128)(2,1)S(1)} %get-tuple-element.67), channel_id=1, source_target_pairs={{0,32},{8,40},{16,48},{24,56},{32,0},{40,8},{48,16},{56,24},{64,96... | collective-permute-start | bytes 1228808 | tf_op jit(solution)/shard_map/ppermute | solution.py:23
  96.3 20.3 %collective-permute-start.10 = (bf16[160,1280]{1,0:T(8,128)(2,1)S(1)}, bf16[160,1280]{1,0:T(8,128)(2,1)S(1)}, u32[]{:S(2)}, u32[]{:S(2)}) collective-permute-start(bf16[160,1280]{1,0:T(8,128)(2,1)S(1)} %get-tuple-element.68), channel_id=1, source_target_pairs={{0,16},{8,24},{16,32},{24,40},{32,48},{40,56},{48,0},{56,8},{64,80... | collective-permute-start | bytes 1228808 | tf_op jit(solution)/shard_map/ppermute | solution.py:23
  108.9 25.4 %collective-permute-start.15 = (bf16[512,1024]{1,0:T(8,128)(2,1)S(1)}, bf16[512,1024]{1,0:T(8,128)(2,1)S(1)}, u32[]{:S(2)}, u32[]{:S(2)}) collective-permute-start(bf16[512,1024]{1,0:T(8,128)(2,1)S(1)} %constant_dynamic-update-slice_fusion.refs_4_), channel_id=1, source_target_pairs={{0,64},{8,72},{16,80},{24,88},{32,96},{40,104},{48,112},{56,120},{... | collective-permute-start | bytes 3145736 | tf_op jit(solution)/shard_map/ppermute | solution.py:27
  116.6 25.4 %collective-permute-start.16 = (bf16[512,1024]{1,0:T(8,128)(2,1)S(1)}, bf16[512,1024]{1,0:T(8,128)(2,1)S(1)}, u32[]{:S(2)}, u32[]{:S(2)}) collective-permute-start(bf16[512,1024]{1,0:T(8,128)(2,1)S(1)} %collective-permute-done.14.refs_3_), channel_id=1, source_target_pairs={{0,16},{8,24},{16,32},{24,40},{32,48},{40,56},{48,0},{56,8},{64,80... | collective-permute-start | bytes 3145736 | tf_op jit(solution)/shard_map/ppermute | solution.py:23
  116.6 25.4 %collective-permute-start.17 = (bf16[512,1024]{1,0:T(8,128)(2,1)S(1)}, bf16[512,1024]{1,0:T(8,128)(2,1)S(1)}, u32[]{:S(2)}, u32[]{:S(2)}) collective-permute-start(bf16[512,1024]{1,0:T(8,128)(2,1)S(1)} %collective-permute-done.14.refs_3_), channel_id=1, source_target_pairs={{0,48},{8,56},{16,0},{24,8},{32,16},{40,24},{48,32},{56,40},{64,11... | collective-permute-start | bytes 3145736 | tf_op jit(solution)/shard_map/ppermute | solution.py:23
  130.5 1.9 %collective-permute-start.11 = (bf16[160,1024]{1,0:T(8,128)(2,1)S(1)}, bf16[160,1024]{1,0:T(8,128)(2,1)S(1)}, u32[]{:S(2)}, u32[]{:S(2)}) collective-permute-start(bf16[160,1024]{1,0:T(8,128)(2,1)S(1)} %attention.1.mixed_ref), channel_id=1, source_target_pairs={{0,8},{8,0},{16,24},{24,16},{32,40},{40,32},{48,56},{56,48},{64,72... | collective-permute-start | bytes 983048 | tf_op jit(solution)/shard_map/ppermute | solution.py:27
  134.1 11.5 %collective-permute-start.18 = (bf16[2560,256]{1,0:T(8,128)(2,1)S(1)}, bf16[2560,256]{1,0:T(8,128)(2,1)S(1)}, u32[]{:S(2)}, u32[]{:S(2)}) collective-permute-start(bf16[2560,256]{1,0:T(8,128)(2,1)S(1)} %terms.3), channel_id=1, source_target_pairs={{0,8},{8,0},{16,24},{24,16},{32,40},{40,32},{48,56},{56,48},{64,72... | collective-permute-start | bytes 3932168 | tf_op jit(solution)/shard_map/ppermute | solution.py:27
  143.1 2.6 %collective-permute-start.19 = (bf16[1536,256]{1,0:T(8,128)(2,1)S(1)}, bf16[1536,256]{1,0:T(8,128)(2,1)S(1)}, u32[]{:S(2)}, u32[]{:S(2)}) collective-permute-start(bf16[1536,256]{1,0:T(8,128)(2,1)S(1)} %terms.4), channel_id=1, source_target_pairs={{0,8},{8,0},{16,24},{24,16},{32,40},{40,32},{48,56},{56,48},{64,72... | collective-permute-start | bytes 2359304 | tf_op jit(solution)/shard_map/ppermute | solution.py:27
  148.5 10.6 %collective-permute-start.22 = (bf16[2,80,1024]{2,1,0:T(8,128)(2,1)S(1)}, bf16[2,80,1024]{2,1,0:T(8,128)(2,1)S(1)}, u32[]{:S(2)}, u32[]{:S(2)}) collective-permute-start(bf16[2,80,1024]{2,1,0:T(8,128)(2,1)S(1)} %get-tuple-element.82), channel_id=1, source_target_pairs={{0,6},{1,7},{2,0},{3,1},{4,2},{5,3},{6,4},{7,5},{8,14},{9,15},{10,... | collective-permute-start | bytes 983048 | tf_op jit(solution)/shard_map/ppermute | solution.py:31
  148.6 12.1 %collective-permute-start.21 = (bf16[2,80,1024]{2,1,0:T(8,128)(2,1)S(1)}, bf16[2,80,1024]{2,1,0:T(8,128)(2,1)S(1)}, u32[]{:S(2)}, u32[]{:S(2)}) collective-permute-start(bf16[2,80,1024]{2,1,0:T(8,128)(2,1)S(1)} %get-tuple-element.81), channel_id=1, source_target_pairs={{0,4},{1,5},{2,6},{3,7},{4,0},{5,1},{6,2},{7,3},{8,12},{9,13},{10,... | collective-permute-start | bytes 983048 | tf_op jit(solution)/shard_map/ppermute | solution.py:31
  149.7 17.6 %collective-permute-start.20 = (bf16[2,80,1024]{2,1,0:T(8,128)(2,1)S(1)}, bf16[2,80,1024]{2,1,0:T(8,128)(2,1)S(1)}, u32[]{:S(2)}, u32[]{:S(2)}) collective-permute-start(bf16[2,80,1024]{2,1,0:T(8,128)(2,1)S(1)} %get-tuple-element.80), channel_id=1, source_target_pairs={{0,2},{1,3},{2,4},{3,5},{4,6},{5,7},{6,0},{7,1},{8,10},{9,11},{10,... | collective-permute-start | bytes 983048 | tf_op jit(solution)/shard_map/ppermute | solution.py:31
  150.6 19.6 %collective-permute-start.24 = (bf16[4,80,1024]{2,1,0:T(8,128)(2,1)S(1)}, bf16[4,80,1024]{2,1,0:T(8,128)(2,1)S(1)}, u32[]{:S(2)}, u32[]{:S(2)}) collective-permute-start(bf16[4,80,1024]{2,1,0:T(8,128)(2,1)S(1)} %get-tuple-element.84), channel_id=1, source_target_pairs={{0,1},{1,0},{2,3},{3,2},{4,5},{5,4},{6,7},{7,6},{8,9},{9,8},{10,11... | collective-permute-start | bytes 1966088 | tf_op jit(solution)/shard_map/ppermute | solution.py:35
  167.6 7.7 %collective-permute-start.23 = (bf16[80,1024]{1,0:T(8,128)(2,1)S(1)}, bf16[80,1024]{1,0:T(8,128)(2,1)S(1)}, u32[]{:S(2)}, u32[]{:S(2)}) collective-permute-start(bf16[80,1024]{1,0:T(8,128)(2,1)S(1)} %fusion.7), channel_id=1, source_target_pairs={{0,1},{1,0},{2,3},{3,2},{4,5},{5,4},{6,7},{7,6},{8,9},{9,8},{10,11... | collective-permute-start | bytes 491528 | tf_op jit(solution)/shard_map/ppermute | solution.py:35
  170.6 7.2 %collective-permute-start.27 = (bf16[80,1024]{1,0:T(8,128)(2,1)S(1)}, bf16[80,1024]{1,0:T(8,128)(2,1)S(1)}, u32[]{:S(2)}, u32[]{:S(2)}) collective-permute-start(bf16[80,1024]{1,0:T(8,128)(2,1)S(1)} %get-tuple-element.88), channel_id=1, source_target_pairs={{0,6},{1,7},{2,0},{3,1},{4,2},{5,3},{6,4},{7,5},{8,14},{9,15},{10,... | collective-permute-start | bytes 491528 | tf_op jit(solution)/shard_map/ppermute | solution.py:31
  171.8 8.4 %collective-permute-start.26 = (bf16[80,1024]{1,0:T(8,128)(2,1)S(1)}, bf16[80,1024]{1,0:T(8,128)(2,1)S(1)}, u32[]{:S(2)}, u32[]{:S(2)}) collective-permute-start(bf16[80,1024]{1,0:T(8,128)(2,1)S(1)} %get-tuple-element.89), channel_id=1, source_target_pairs={{0,4},{1,5},{2,6},{3,7},{4,0},{5,1},{6,2},{7,3},{8,12},{9,13},{10,... | collective-permute-start | bytes 491528 | tf_op jit(solution)/shard_map/ppermute | solution.py:31
  173.0 8.6 %collective-permute-start.25 = (bf16[80,1024]{1,0:T(8,128)(2,1)S(1)}, bf16[80,1024]{1,0:T(8,128)(2,1)S(1)}, u32[]{:S(2)}, u32[]{:S(2)}) collective-permute-start(bf16[80,1024]{1,0:T(8,128)(2,1)S(1)} %get-tuple-element.87), channel_id=1, source_target_pairs={{0,2},{1,3},{2,4},{3,5},{4,6},{5,7},{6,0},{7,1},{8,10},{9,11},{10,... | collective-permute-start | bytes 491528 | tf_op jit(solution)/shard_map/ppermute | solution.py:31

commit v14 on v13

--- a/solution.py
+++ b/solution.py
@@ -48,7 +48,7 @@
 def slabs_of(qkv_rows, o_rows, groups):
     owned = qkv_rows.shape[0]
     query_cols = HQ * HD
-    each = 2
+    each = 1
     wide, narrow = each * query_cols // groups, each * HK * HD // groups
     keys_at = query_cols // narrow
     values_at = keys_at + HK * HD // narrow
@@ -437,16 +437,19 @@
     mixed_c = flip(mixed, 1)
     sources = (own, below, above, across, far, across_far, across_below, across_above)
     parts_of = (sources[:5], sources[5:])
-    theirs = [terms_of(mixed_c, part) for part in parts_of]
-    mine = terms_of(*after((mixed,), *theirs), sources)
-    pieces = (mine, *(flip(value, 1) for value in theirs))
+    early, late = parts_of
+    theirs = [terms_of(mixed_c, early)]
+    mine = [terms_of(*after((mixed,), theirs[0]), early)]
+    theirs.append(terms_of(*after((mixed_c,), mine[0]), late))
+    mine.append(terms_of(*after((mixed,), theirs[1]), late))
+    pieces = (*mine, *(flip(value, 1) for value in theirs))
     places = ((0, 0), (0, 3), (0, 1), (1, 0), (0, 2), (1, 2), (1, 3), (1, 1))
     spots = []
     for core in range(2):
-        begin, piece = 0, core
+        begin, piece = 0, 2 * core
         for n, ((dy, dz), source) in enumerate(zip(places, sources)):
-            if core == 1 and n == len(parts_of[0]):
-                begin, piece = 0, 2
+            if n == len(parts_of[0]):
+                begin, piece = 0, 2 * core + 1
             size = source.shape[0]
             spots.append((piece, dy, dz, core, size // owned, begin))
             begin += size

time: 183 us -> 184 us (level)
  Pallas kernels: 34.6 us -> 36.8 us
    pallas_call x1, Pallas kernels: 4.33 us -> 6.28 us  [slabs_of(): pl.pallas_call(slabs_kernel, grid=(groups // each,), out_shape=jax.ShapeD...]
    pallas_call x3 -> x4, Pallas kernels: 5.17 us -> 5.45 us  [terms_of(): pl.pallas_call(terms_kernel, out_shape=jax.ShapeDtypeStruct((width, lanes...]
  transfers between devices with their start and end apart: 29 -> 29, of which waited for: 16 -> 17; matrix products, arithmetic and copies ran while one was open for 2% -> 2% of each run, Pallas kernels for 15% -> 15%
where the time goes in v14:
time: 184 us
  waiting for transfers between devices  98.8 us (54%)
  starting transfers between devices  43.2 us (23%)
  Pallas kernels  36.8 us (20%)
  local copies, waits for them, and re-layouts  2.99 us (2%)
    ppermute x12, waiting for transfers between devices, z_shift(): return lax.ppermute(value, 'fsdp', pairs)  50.1 us
    all_to_all x1, waiting for transfers between devices, body(): both = lax.all_to_all(copy, 'tp', split_axis=0, concat_axis=0, tiled=True)  23.6 us
    ppermute x12, starting transfers between devices, z_shift(): return lax.ppermute(value, 'fsdp', pairs)  21.6 us
    ppermute x6, waiting for transfers between devices, x_shift(): lax.ppermute(value, 'tp', [(t, (t // 2 + k) % NX * 2 + t % 2) for t in ra...  20.4 us
    pallas_call x1, Pallas kernels, attention(): pl.pallas_call(attention_kernel, grid=(rows // GROUP,), out_shape=jax.Sha...  10.7 us
    all_to_all x1, starting transfers between devices, body(): both = lax.all_to_all(copy, 'tp', split_axis=0, concat_axis=0, tiled=True)  7.29 us
    pallas_call x2, Pallas kernels, partials(): pl.pallas_call(functools.partial(partial_kernel, begun), grid=(cols // ti...  6.68 us
    pallas_call x1, Pallas kernels, slabs_of(): pl.pallas_call(slabs_kernel, grid=(groups // each,), out_shape=jax.ShapeD...  6.28 us
  transfers between devices with their start and end apart: 29, of which 17 were waited for; matrix products, arithmetic and copies ran while one was open for 2% of the time, Pallas kernels for 15%

profile of v14, /device:TPU:0, one launch (start us, length us, event | category | flops | bytes accessed | tf_op | source)
XLA Modules:
  0.0 183.8 jit_solution(12978028215381230916)
XLA Ops:
  0.0 6.3 %slabs.1 = bf16[8,64,2304]{2,1,0:T(8,128)(2,1)} custom-call(f32[64,10240]{1,0:T(8,128)} %value.1, f32[64,10240]{1,0:T(8,128)} %value.1, f32[64,10240]{1,0:T(8,128)} %value.1, f32[64,8192]{1,0:T(8,128)} %back.1), custom_call_target="tpu_custom_call" | custom-call | bytes 7077888 | tf_op jit(solution)/shard_map/slabs/pallas_call | solution.py:56
  6.3 7.3 %all-to-all-start = ((bf16[8,64,2304]{2,1,0:T(8,128)(2,1)}), bf16[8,64,2304]{2,1,0:T(8,128)(2,1)}, u32[]{:S(2)}, u32[]{:S(2)}) async-start(bf16[8,64,2304]{2,1,0:T(8,128)(2,1)} %slabs.1), calls=%async_computation | async-start | bytes 4718592 | tf_op jit(solution)/shard_map/all_to_all | solution.py:412
  13.6 4.8 %shuffle.1 = (bf16[160,2048]{1,0:T(8,128)(2,1)S(1)}, bf16[160,2048]{1,0:T(8,128)(2,1)}, bf16[160,2048]{1,0:T(8,128)(2,1)}, bf16[160,2048]{1,0:T(8,128)(2,1)}) custom-call(s32[2,128]{1,0:T(2,128)S(1)} %copy-done.1, bf16[160,8192]{1,0:T(8,128)(2,1)S(1)} %bitcast.34), custom_call_target="tpu_custom_call" | custom-call | flops 10485760 | bytes 5242880 | tf_op jit(solution)/shard_map/shuffle/pallas_call | solution.py:105
  18.4 1.9 %collective-permute-start = (bf16[160,2048]{1,0:T(8,128)(2,1)}, bf16[160,2048]{1,0:T(8,128)(2,1)S(1)}, u32[]{:S(2)}, u32[]{:S(2)}) collective-permute-start(bf16[160,2048]{1,0:T(8,128)(2,1)} %get-tuple-element.48), channel_id=1, source_target_pairs={{0,16},{8,24},{16,32},{24,40},{32,48},{40,56},{48,0},{56,8},{64,80... | collective-permute-start | bytes 1966088 | tf_op jit(solution)/shard_map/ppermute | solution.py:23
  20.3 3.6 %collective-permute-start.1 = (bf16[160,2048]{1,0:T(8,128)(2,1)}, bf16[160,2048]{1,0:T(8,128)(2,1)S(1)}, u32[]{:S(2)}, u32[]{:S(2)}) collective-permute-start(bf16[160,2048]{1,0:T(8,128)(2,1)} %get-tuple-element.49), channel_id=1, source_target_pairs={{0,32},{8,40},{16,48},{24,56},{32,0},{40,8},{48,16},{56,24},{64,96... | collective-permute-start | bytes 1966088 | tf_op jit(solution)/shard_map/ppermute | solution.py:23
  25.0 23.6 %all-to-all-done = bf16[8,64,2304]{2,1,0:T(8,128)(2,1)} async-done(((bf16[8,64,2304]{2,1,0:T(8,128)(2,1)}), bf16[8,64,2304]{2,1,0:T(8,128)(2,1)}, u32[]{:S(2)}, u32[]{:S(2)}) %all-to-all-start) | async-done | bytes 2359328 | tf_op jit(solution)/shard_map/all_to_all | solution.py:412
  52.7 2.0 %collective-permute-start.4 = (bf16[512,1024]{1,0:T(8,128)(2,1)S(1)}, bf16[512,1024]{1,0:T(8,128)(2,1)S(1)}, u32[]{:S(2)}, u32[]{:S(2)}) collective-permute-start(bf16[512,1024]{1,0:T(8,128)(2,1)S(1)} %slice.44.refs_0_), channel_id=1, source_target_pairs={{0,16},{8,24},{16,32},{24,40},{32,48},{40,56},{48,0},{56,8},{64,80... | collective-permute-start | bytes 3145736 | tf_op jit(solution)/shard_map/ppermute | solution.py:23
  54.6 2.2 %collective-permute-start.5 = (bf16[512,1024]{1,0:T(8,128)(2,1)S(1)}, bf16[512,1024]{1,0:T(8,128)(2,1)S(1)}, u32[]{:S(2)}, u32[]{:S(2)}) collective-permute-start(bf16[512,1024]{1,0:T(8,128)(2,1)S(1)} %slice.44.refs_0_), channel_id=1, source_target_pairs={{0,48},{8,56},{16,0},{24,8},{32,16},{40,24},{48,32},{56,40},{64,11... | collective-permute-start | bytes 3145736 | tf_op jit(solution)/shard_map/ppermute | solution.py:23
  56.8 3.2 %partials.1 = (f32[160,1280]{1,0:T(8,128)S(1)}, f32[160,1280]{1,0:T(8,128)S(1)}, f32[160,1280]{1,0:T(8,128)S(1)}, f32[160,1280]{1,0:T(8,128)S(1)}) custom-call(bf16[160,2048]{1,0:T(8,128)(2,1)S(1)} %get-tuple-element.51.refs_0_, bf16[160,2048]{1,0:T(8,128)(2,1)S(1)} %collective-permute-done.refs_1_, bf16[160,2048]{1,0:T(8,128)(2,1)S(1)} %collective-permute-done.1.refs_2_, ...), custom_call_target="tpu_custom_call" | custom-call | flops 1677721600 | bytes 7208960 | tf_op jit(solution)/shard_map/partials/pallas_call | solution.py:152
  60.1 20.2 %collective-permute-done.4.refs_1_ = bf16[512,1024]{1,0:T(8,128)(2,1)S(1)} collective-permute-done((bf16[512,1024]{1,0:T(8,128)(2,1)S(1)}, bf16[512,1024]{1,0:T(8,128)(2,1)S(1)}, u32[]{:S(2)}, u32[]{:S(2)}) %collective-permute-start.4) | collective-permute-done | bytes 1048608 | tf_op jit(solution)/shard_map/ppermute | solution.py:23
  82.0 4.0 %collective-permute-start.12 = (bf16[256,1024]{1,0:T(8,128)(2,1)S(1)}, bf16[256,1024]{1,0:T(8,128)(2,1)S(1)}, u32[]{:S(2)}, u32[]{:S(2)}) collective-permute-start(bf16[256,1024]{1,0:T(8,128)(2,1)S(1)} %slice.36), channel_id=1, source_target_pairs={{0,48},{8,56},{16,0},{24,8},{32,16},{40,24},{48,32},{56,40},{64,11... | collective-permute-start | bytes 1572872 | tf_op jit(solution)/shard_map/ppermute | solution.py:23
  86.0 3.5 %partials_rest.1 = (f32[160,1280]{1,0:T(8,128)S(1)}, bf16[160,1280]{1,0:T(8,128)(2,1)S(1)}, bf16[160,1280]{1,0:T(8,128)(2,1)S(1)}, bf16[160,1280]{1,0:T(8,128)(2,1)S(1)}) custom-call(bf16[160,2048]{1,0:T(8,128)(2,1)S(1)} %get-tuple-element.51.refs_0_, bf16[160,2048]{1,0:T(8,128)(2,1)S(1)} %collective-permute-done.refs_1_, ...), custom_call_target="tpu_custom_call" | custom-call | flops 1677721600 | bytes 7208960 | tf_op jit(solution)/shard_map/partials_rest/pallas_call | solution.py:152
  89.5 3.3 %collective-permute-start.8 = (bf16[160,1280]{1,0:T(8,128)(2,1)S(1)}, bf16[160,1280]{1,0:T(8,128)(2,1)S(1)}, u32[]{:S(2)}, u32[]{:S(2)}) collective-permute-start(bf16[160,1280]{1,0:T(8,128)(2,1)S(1)} %get-tuple-element.68), channel_id=1, source_target_pairs={{0,48},{8,56},{16,0},{24,8},{32,16},{40,24},{48,32},{56,40},{64,11... | collective-permute-start | bytes 1228808 | tf_op jit(solution)/shard_map/ppermute | solution.py:23
  92.8 5.5 %collective-permute-done.12 = bf16[256,1024]{1,0:T(8,128)(2,1)S(1)} collective-permute-done((bf16[256,1024]{1,0:T(8,128)(2,1)S(1)}, bf16[256,1024]{1,0:T(8,128)(2,1)S(1)}, u32[]{:S(2)}, u32[]{:S(2)}) %collective-permute-start.12) | collective-permute-done | bytes 524320 | tf_op jit(solution)/shard_map/ppermute | solution.py:23
  98.6 12.2 %collective-permute-done.13 = bf16[256,1024]{1,0:T(8,128)(2,1)S(1)} collective-permute-done((bf16[256,1024]{1,0:T(8,128)(2,1)S(1)}, bf16[256,1024]{1,0:T(8,128)(2,1)S(1)}, u32[]{:S(2)}, u32[]{:S(2)}) %collective-permute-start.13) | collective-permute-done | bytes 524320 | tf_op jit(solution)/shard_map/ppermute | solution.py:23
  112.3 2.8 %collective-permute-done.8.p1 = bf16[160,1280]{1,0:T(8,128)(2,1)S(1)} collective-permute-done((bf16[160,1280]{1,0:T(8,128)(2,1)S(1)}, bf16[160,1280]{1,0:T(8,128)(2,1)S(1)}, u32[]{:S(2)}, u32[]{:S(2)}) %collective-permute-start.8) | collective-permute-done | bytes 409632 | tf_op jit(solution)/shard_map/ppermute | solution.py:23
  115.1 3.4 %collective-permute-done.10.p3 = bf16[160,1280]{1,0:T(8,128)(2,1)S(1)} collective-permute-done((bf16[160,1280]{1,0:T(8,128)(2,1)S(1)}, bf16[160,1280]{1,0:T(8,128)(2,1)S(1)}, u32[]{:S(2)}, u32[]{:S(2)}) %collective-permute-start.10) | collective-permute-done | bytes 409632 | tf_op jit(solution)/shard_map/ppermute | solution.py:23
  118.5 3.2 %collective-permute-start.17 = (bf16[512,1024]{1,0:T(8,128)(2,1)S(1)}, bf16[512,1024]{1,0:T(8,128)(2,1)S(1)}, u32[]{:S(2)}, u32[]{:S(2)}) collective-permute-start(bf16[512,1024]{1,0:T(8,128)(2,1)S(1)} %collective-permute-done.14.refs_3_), channel_id=1, source_target_pairs={{0,48},{8,56},{16,0},{24,8},{32,16},{40,24},{48,32},{56,40},{64,11... | collective-permute-start | bytes 3145736 | tf_op jit(solution)/shard_map/ppermute | solution.py:23
  121.8 10.7 %attention.1.mixed_ref = bf16[160,1024]{1,0:T(8,128)(2,1)S(1)} custom-call(s32[80]{0:T(128)S(1)} %copy-done.2, f32[160,1280]{1,0:T(8,128)S(1)} %get-tuple-element.67.p0, bf16[160,1280]{1,0:T(8,128)(2,1)S(1)} %collective-permute-done.8.p1, bf16[160,1280]{1,0:T(8,128)(2,1)S(1)} %collective-permute-done.9.p2, bf16[160,1280]{1,0:T(8,128)(2,1)S(1)} %collective-permute-done.10.p3, ...), custom_call_target="tpu_custom_call" | custom-call | flops 167772160 | bytes 41943040 | tf_op jit(solution)/shard_map/attention/pallas_call | solution.py:370
  132.7 1.6 collective-permute-done.11.mixed_ref
  134.3 1.6 terms.4
  136.2 1.6 terms.5.refs_0_
  137.8 6.1 %collective-permute-done.16.refs_1_ = bf16[512,1024]{1,0:T(8,128)(2,1)S(1)} collective-permute-done((bf16[512,1024]{1,0:T(8,128)(2,1)S(1)}, bf16[512,1024]{1,0:T(8,128)(2,1)S(1)}, u32[]{:S(2)}, u32[]{:S(2)}) %collective-permute-start.16) | collective-permute-done | bytes 1048608 | tf_op jit(solution)/shard_map/ppermute | solution.py:23
  147.4 2.9 %place.1 = (bf16[2,80,1024]{2,1,0:T(8,128)(2,1)S(1)}, bf16[2,80,1024]{2,1,0:T(8,128)(2,1)S(1)}, bf16[2,80,1024]{2,1,0:T(8,128)(2,1)S(1)}, bf16[2,80,1024]{2,1,0:...) custom-call(s32[2,128]{1,0:T(2,128)S(1)} %copy-done.1, ...), custom_call_target="tpu_custom_call" | custom-call | bytes 5242880 | tf_op jit(solution)/shard_map/place/pallas_call | solution.py:241
  152.4 2.2 %collective-permute-start.24 = (bf16[4,80,1024]{2,1,0:T(8,128)(2,1)S(1)}, bf16[4,80,1024]{2,1,0:T(8,128)(2,1)S(1)}, u32[]{:S(2)}, u32[]{:S(2)}) collective-permute-start(bf16[4,80,1024]{2,1,0:T(8,128)(2,1)S(1)} %get-tuple-element.88), channel_id=1, source_target_pairs={{0,1},{1,0},{2,3},{3,2},{4,5},{5,4},{6,7},{7,6},{8,9},{9,8},{10,11... | collective-permute-start | bytes 1966088 | tf_op jit(solution)/shard_map/ppermute | solution.py:35
  154.6 6.3 %collective-permute-done.22 = bf16[2,80,1024]{2,1,0:T(8,128)(2,1)S(1)} collective-permute-done((bf16[2,80,1024]{2,1,0:T(8,128)(2,1)S(1)}, bf16[2,80,1024]{2,1,0:T(8,128)(2,1)S(1)}, u32[]{:S(2)}, u32[]{:S(2)}) %collective-permute-start.22) | collective-permute-done | bytes 327712 | tf_op jit(solution)/shard_map/ppermute | solution.py:31
  160.9 1.6 collective-permute-done.21
  162.5 6.2 %collective-permute-done.20 = bf16[2,80,1024]{2,1,0:T(8,128)(2,1)S(1)} collective-permute-done((bf16[2,80,1024]{2,1,0:T(8,128)(2,1)S(1)}, bf16[2,80,1024]{2,1,0:T(8,128)(2,1)S(1)}, u32[]{:S(2)}, u32[]{:S(2)}) %collective-permute-start.20) | collective-permute-done | bytes 327712 | tf_op jit(solution)/shard_map/ppermute | solution.py:31
  168.9 2.7 %collective-permute-start.23 = (bf16[80,1024]{1,0:T(8,128)(2,1)S(1)}, bf16[80,1024]{1,0:T(8,128)(2,1)S(1)}, u32[]{:S(2)}, u32[]{:S(2)}) collective-permute-start(bf16[80,1024]{1,0:T(8,128)(2,1)S(1)} %fusion.7), channel_id=1, source_target_pairs={{0,1},{1,0},{2,3},{3,2},{4,5},{5,4},{6,7},{7,6},{8,9},{9,8},{10,11... | collective-permute-start | bytes 491528 | tf_op jit(solution)/shard_map/ppermute | solution.py:35
  176.7 2.4 %collective-permute-done.27 = bf16[80,1024]{1,0:T(8,128)(2,1)S(1)} collective-permute-done((bf16[80,1024]{1,0:T(8,128)(2,1)S(1)}, bf16[80,1024]{1,0:T(8,128)(2,1)S(1)}, u32[]{:S(2)}, u32[]{:S(2)}) %collective-permute-start.27) | collective-permute-done | bytes 163872 | tf_op jit(solution)/shard_map/ppermute | solution.py:31
  179.1 2.3 %collective-permute-done.26 = bf16[80,1024]{1,0:T(8,128)(2,1)S(1)} collective-permute-done((bf16[80,1024]{1,0:T(8,128)(2,1)S(1)}, bf16[80,1024]{1,0:T(8,128)(2,1)S(1)}, u32[]{:S(2)}, u32[]{:S(2)}) %collective-permute-start.26) | collective-permute-done | bytes 163872 | tf_op jit(solution)/shard_map/ppermute | solution.py:31
  181.5 1.5 collective-permute-done.25
  (60 shorter events, 20.8 us)
Async XLA Ops:
  6.3 7.3 %copy-start = (bf16[2,80,8192]{2,1,0:T(8,128)(2,1)S(1)}, bf16[2,80,8192]{2,1,0:T(8,128)(2,1)}, u32[]{:S(2)}) copy-start(bf16[2,80,8192]{2,1,0:T(8,128)(2,1)} %param.6) | copy-start | bytes 7864324
  6.3 7.3 %copy-start.1 = (s32[2,128]{1,0:T(2,128)S(1)}, s32[2,128]{1,0:T(2,128)}, u32[]{:S(2)}) copy-start(s32[2,128]{1,0:T(2,128)} %owner_ref.3) | copy-start | bytes 3076
  6.3 42.3 %all-to-all-start = ((bf16[8,64,2304]{2,1,0:T(8,128)(2,1)}), bf16[8,64,2304]{2,1,0:T(8,128)(2,1)}, u32[]{:S(2)}, u32[]{:S(2)}) async-start(bf16[8,64,2304]{2,1,0:T(8,128)(2,1)} %slabs.1), calls=%async_computation | async-start | bytes 4718592 | tf_op jit(solution)/shard_map/all_to_all | solution.py:412
  13.6 11.3 %copy-start.2 = (s32[80]{0:T(128)S(1)}, s32[80]{0:T(128)}, u32[]{:S(2)}) copy-start(s32[80]{0:T(128)} %lengths_ref.1) | copy-start | bytes 964
  18.4 34.2 %collective-permute-start = (bf16[160,2048]{1,0:T(8,128)(2,1)}, bf16[160,2048]{1,0:T(8,128)(2,1)S(1)}, u32[]{:S(2)}, u32[]{:S(2)}) collective-permute-start(bf16[160,2048]{1,0:T(8,128)(2,1)} %get-tuple-element.48), channel_id=1, source_target_pairs={{0,16},{8,24},{16,32},{24,40},{32,48},{40,56},{48,0},{56,8},{64,80... | collective-permute-start | bytes 1966088 | tf_op jit(solution)/shard_map/ppermute | solution.py:23
  20.3 32.3 %collective-permute-start.1 = (bf16[160,2048]{1,0:T(8,128)(2,1)}, bf16[160,2048]{1,0:T(8,128)(2,1)S(1)}, u32[]{:S(2)}, u32[]{:S(2)}) collective-permute-start(bf16[160,2048]{1,0:T(8,128)(2,1)} %get-tuple-element.49), channel_id=1, source_target_pairs={{0,32},{8,40},{16,48},{24,56},{32,0},{40,8},{48,16},{56,24},{64,96... | collective-permute-start | bytes 1966088 | tf_op jit(solution)/shard_map/ppermute | solution.py:23
  23.9 28.7 %collective-permute-start.2 = (bf16[160,2048]{1,0:T(8,128)(2,1)}, bf16[160,2048]{1,0:T(8,128)(2,1)S(1)}, u32[]{:S(2)}, u32[]{:S(2)}) collective-permute-start(bf16[160,2048]{1,0:T(8,128)(2,1)} %get-tuple-element.50), channel_id=1, source_target_pairs={{0,48},{8,56},{16,0},{24,8},{32,16},{40,24},{48,32},{56,40},{64,11... | collective-permute-start | bytes 1966088 | tf_op jit(solution)/shard_map/ppermute | solution.py:23
  50.0 6.9 %collective-permute-start.6 = (bf16[512,1280]{1,0:T(8,128)(2,1)S(1)}, bf16[512,1280]{1,0:T(8,128)(2,1)S(1)}, u32[]{:S(2)}, u32[]{:S(2)}) collective-permute-start(bf16[512,1280]{1,0:T(8,128)(2,1)S(1)} %slice.45.refs_4_), channel_id=1, source_target_pairs={{0,8},{8,0},{16,24},{24,16},{32,40},{40,32},{48,56},{56,48},{64,72... | collective-permute-start | bytes 3932168 | tf_op jit(solution)/shard_map/ppermute | solution.py:27
  50.1 31.2 %collective-permute-start.3 = (bf16[512,1280]{1,0:T(8,128)(2,1)S(1)}, bf16[512,1280]{1,0:T(8,128)(2,1)S(1)}, u32[]{:S(2)}, u32[]{:S(2)}) collective-permute-start(bf16[512,1280]{1,0:T(8,128)(2,1)S(1)} %slice.45.refs_4_), channel_id=1, source_target_pairs={{0,64},{8,72},{16,80},{24,88},{32,96},{40,104},{48,112},{56,120},{... | collective-permute-start | bytes 3932168 | tf_op jit(solution)/shard_map/ppermute | solution.py:27
  52.7 27.6 %collective-permute-start.4 = (bf16[512,1024]{1,0:T(8,128)(2,1)S(1)}, bf16[512,1024]{1,0:T(8,128)(2,1)S(1)}, u32[]{:S(2)}, u32[]{:S(2)}) collective-permute-start(bf16[512,1024]{1,0:T(8,128)(2,1)S(1)} %slice.44.refs_0_), channel_id=1, source_target_pairs={{0,16},{8,24},{16,32},{24,40},{32,48},{40,56},{48,0},{56,8},{64,80... | collective-permute-start | bytes 3145736 | tf_op jit(solution)/shard_map/ppermute | solution.py:23
  54.6 25.6 %collective-permute-start.5 = (bf16[512,1024]{1,0:T(8,128)(2,1)S(1)}, bf16[512,1024]{1,0:T(8,128)(2,1)S(1)}, u32[]{:S(2)}, u32[]{:S(2)}) collective-permute-start(bf16[512,1024]{1,0:T(8,128)(2,1)S(1)} %slice.44.refs_0_), channel_id=1, source_target_pairs={{0,48},{8,56},{16,0},{24,8},{32,16},{40,24},{48,32},{56,40},{64,11... | collective-permute-start | bytes 3145736 | tf_op jit(solution)/shard_map/ppermute | solution.py:23
  81.3 4.7 %collective-permute-start.7 = (bf16[512,1280]{1,0:T(8,128)(2,1)S(1)}, bf16[512,1280]{1,0:T(8,128)(2,1)S(1)}, u32[]{:S(2)}, u32[]{:S(2)}) collective-permute-start(bf16[512,1280]{1,0:T(8,128)(2,1)S(1)} %collective-permute-done.3.refs_4_), channel_id=1, source_target_pairs={{0,8},{8,0},{16,24},{24,16},{32,40},{40,32},{48,56},{56,48},{64,72... | collective-permute-start | bytes 3932168 | tf_op jit(solution)/shard_map/ppermute | solution.py:27
  81.3 29.5 %collective-permute-start.14 = (bf16[512,1024]{1,0:T(8,128)(2,1)S(1)}, bf16[512,1024]{1,0:T(8,128)(2,1)S(1)}, u32[]{:S(2)}, u32[]{:S(2)}) collective-permute-start(bf16[512,1024]{1,0:T(8,128)(2,1)S(1)} %slice.44.refs_0_), channel_id=1, source_target_pairs={{0,64},{8,72},{16,80},{24,88},{32,96},{40,104},{48,112},{56,120},{... | collective-permute-start | bytes 3145736 | tf_op jit(solution)/shard_map/ppermute | solution.py:27
  82.0 16.3 %collective-permute-start.12 = (bf16[256,1024]{1,0:T(8,128)(2,1)S(1)}, bf16[256,1024]{1,0:T(8,128)(2,1)S(1)}, u32[]{:S(2)}, u32[]{:S(2)}) collective-permute-start(bf16[256,1024]{1,0:T(8,128)(2,1)S(1)} %slice.36), channel_id=1, source_target_pairs={{0,48},{8,56},{16,0},{24,8},{32,16},{40,24},{48,32},{56,40},{64,11... | collective-permute-start | bytes 1572872 | tf_op jit(solution)/shard_map/ppermute | solution.py:23
  86.0 24.8 %collective-permute-start.13 = (bf16[256,1024]{1,0:T(8,128)(2,1)S(1)}, bf16[256,1024]{1,0:T(8,128)(2,1)S(1)}, u32[]{:S(2)}, u32[]{:S(2)}) collective-permute-start(bf16[256,1024]{1,0:T(8,128)(2,1)S(1)} %slice.37), channel_id=1, source_target_pairs={{0,16},{8,24},{16,32},{24,40},{32,48},{40,56},{48,0},{56,8},{64,80... | collective-permute-start | bytes 1572872 | tf_op jit(solution)/shard_map/ppermute | solution.py:23
  89.5 25.7 %collective-permute-start.8 = (bf16[160,1280]{1,0:T(8,128)(2,1)S(1)}, bf16[160,1280]{1,0:T(8,128)(2,1)S(1)}, u32[]{:S(2)}, u32[]{:S(2)}) collective-permute-start(bf16[160,1280]{1,0:T(8,128)(2,1)S(1)} %get-tuple-element.68), channel_id=1, source_target_pairs={{0,48},{8,56},{16,0},{24,8},{32,16},{40,24},{48,32},{56,40},{64,11... | collective-permute-start | bytes 1228808 | tf_op jit(solution)/shard_map/ppermute | solution.py:23
  92.8 22.4 %collective-permute-start.9 = (bf16[160,1280]{1,0:T(8,128)(2,1)S(1)}, bf16[160,1280]{1,0:T(8,128)(2,1)S(1)}, u32[]{:S(2)}, u32[]{:S(2)}) collective-permute-start(bf16[160,1280]{1,0:T(8,128)(2,1)S(1)} %get-tuple-element.69), channel_id=1, source_target_pairs={{0,32},{8,40},{16,48},{24,56},{32,0},{40,8},{48,16},{56,24},{64,96... | collective-permute-start | bytes 1228808 | tf_op jit(solution)/shard_map/ppermute | solution.py:23
  98.3 20.3 %collective-permute-start.10 = (bf16[160,1280]{1,0:T(8,128)(2,1)S(1)}, bf16[160,1280]{1,0:T(8,128)(2,1)S(1)}, u32[]{:S(2)}, u32[]{:S(2)}) collective-permute-start(bf16[160,1280]{1,0:T(8,128)(2,1)S(1)} %get-tuple-element.70), channel_id=1, source_target_pairs={{0,16},{8,24},{16,32},{24,40},{32,48},{40,56},{48,0},{56,8},{64,80... | collective-permute-start | bytes 1228808 | tf_op jit(solution)/shard_map/ppermute | solution.py:23
  110.9 27.0 %collective-permute-start.15 = (bf16[512,1024]{1,0:T(8,128)(2,1)S(1)}, bf16[512,1024]{1,0:T(8,128)(2,1)S(1)}, u32[]{:S(2)}, u32[]{:S(2)}) collective-permute-start(bf16[512,1024]{1,0:T(8,128)(2,1)S(1)} %constant_dynamic-update-slice_fusion.refs_4_), channel_id=1, source_target_pairs={{0,64},{8,72},{16,80},{24,88},{32,96},{40,104},{48,112},{56,120},{... | collective-permute-start | bytes 3145736 | tf_op jit(solution)/shard_map/ppermute | solution.py:27
  118.5 25.4 %collective-permute-start.16 = (bf16[512,1024]{1,0:T(8,128)(2,1)S(1)}, bf16[512,1024]{1,0:T(8,128)(2,1)S(1)}, u32[]{:S(2)}, u32[]{:S(2)}) collective-permute-start(bf16[512,1024]{1,0:T(8,128)(2,1)S(1)} %collective-permute-done.14.refs_3_), channel_id=1, source_target_pairs={{0,16},{8,24},{16,32},{24,40},{32,48},{40,56},{48,0},{56,8},{64,80... | collective-permute-start | bytes 3145736 | tf_op jit(solution)/shard_map/ppermute | solution.py:23
  118.5 25.4 %collective-permute-start.17 = (bf16[512,1024]{1,0:T(8,128)(2,1)S(1)}, bf16[512,1024]{1,0:T(8,128)(2,1)S(1)}, u32[]{:S(2)}, u32[]{:S(2)}) collective-permute-start(bf16[512,1024]{1,0:T(8,128)(2,1)S(1)} %collective-permute-done.14.refs_3_), channel_id=1, source_target_pairs={{0,48},{8,56},{16,0},{24,8},{32,16},{40,24},{48,32},{56,40},{64,11... | collective-permute-start | bytes 3145736 | tf_op jit(solution)/shard_map/ppermute | solution.py:23
  132.4 1.9 %collective-permute-start.11 = (bf16[160,1024]{1,0:T(8,128)(2,1)S(1)}, bf16[160,1024]{1,0:T(8,128)(2,1)S(1)}, u32[]{:S(2)}, u32[]{:S(2)}) collective-permute-start(bf16[160,1024]{1,0:T(8,128)(2,1)S(1)} %attention.1.mixed_ref), channel_id=1, source_target_pairs={{0,8},{8,0},{16,24},{24,16},{32,40},{40,32},{48,56},{56,48},{64,72... | collective-permute-start | bytes 983048 | tf_op jit(solution)/shard_map/ppermute | solution.py:27
  136.0 10.2 %collective-permute-start.18 = (bf16[2560,256]{1,0:T(8,128)(2,1)S(1)}, bf16[2560,256]{1,0:T(8,128)(2,1)S(1)}, u32[]{:S(2)}, u32[]{:S(2)}) collective-permute-start(bf16[2560,256]{1,0:T(8,128)(2,1)S(1)} %terms.4), channel_id=1, source_target_pairs={{0,8},{8,0},{16,24},{24,16},{32,40},{40,32},{48,56},{56,48},{64,72... | collective-permute-start | bytes 3932168 | tf_op jit(solution)/shard_map/ppermute | solution.py:27
  145.0 2.4 %collective-permute-start.19 = (bf16[1536,256]{1,0:T(8,128)(2,1)S(1)}, bf16[1536,256]{1,0:T(8,128)(2,1)S(1)}, u32[]{:S(2)}, u32[]{:S(2)}) collective-permute-start(bf16[1536,256]{1,0:T(8,128)(2,1)S(1)} %terms.6), channel_id=1, source_target_pairs={{0,8},{8,0},{16,24},{24,16},{32,40},{40,32},{48,56},{56,48},{64,72... | collective-permute-start | bytes 2359304 | tf_op jit(solution)/shard_map/ppermute | solution.py:27
  150.3 10.6 %collective-permute-start.22 = (bf16[2,80,1024]{2,1,0:T(8,128)(2,1)S(1)}, bf16[2,80,1024]{2,1,0:T(8,128)(2,1)S(1)}, u32[]{:S(2)}, u32[]{:S(2)}) collective-permute-start(bf16[2,80,1024]{2,1,0:T(8,128)(2,1)S(1)} %get-tuple-element.86), channel_id=1, source_target_pairs={{0,6},{1,7},{2,0},{3,1},{4,2},{5,3},{6,4},{7,5},{8,14},{9,15},{10,... | collective-permute-start | bytes 983048 | tf_op jit(solution)/shard_map/ppermute | solution.py:31
  150.4 12.2 %collective-permute-start.21 = (bf16[2,80,1024]{2,1,0:T(8,128)(2,1)S(1)}, bf16[2,80,1024]{2,1,0:T(8,128)(2,1)S(1)}, u32[]{:S(2)}, u32[]{:S(2)}) collective-permute-start(bf16[2,80,1024]{2,1,0:T(8,128)(2,1)S(1)} %get-tuple-element.85), channel_id=1, source_target_pairs={{0,4},{1,5},{2,6},{3,7},{4,0},{5,1},{6,2},{7,3},{8,12},{9,13},{10,... | collective-permute-start | bytes 983048 | tf_op jit(solution)/shard_map/ppermute | solution.py:31
  151.5 17.3 %collective-permute-start.20 = (bf16[2,80,1024]{2,1,0:T(8,128)(2,1)S(1)}, bf16[2,80,1024]{2,1,0:T(8,128)(2,1)S(1)}, u32[]{:S(2)}, u32[]{:S(2)}) collective-permute-start(bf16[2,80,1024]{2,1,0:T(8,128)(2,1)S(1)} %get-tuple-element.84), channel_id=1, source_target_pairs={{0,2},{1,3},{2,4},{3,5},{4,6},{5,7},{6,0},{7,1},{8,10},{9,11},{10,... | collective-permute-start | bytes 983048 | tf_op jit(solution)/shard_map/ppermute | solution.py:31
  152.4 19.3 %collective-permute-start.24 = (bf16[4,80,1024]{2,1,0:T(8,128)(2,1)S(1)}, bf16[4,80,1024]{2,1,0:T(8,128)(2,1)S(1)}, u32[]{:S(2)}, u32[]{:S(2)}) collective-permute-start(bf16[4,80,1024]{2,1,0:T(8,128)(2,1)S(1)} %get-tuple-element.88), channel_id=1, source_target_pairs={{0,1},{1,0},{2,3},{3,2},{4,5},{5,4},{6,7},{7,6},{8,9},{9,8},{10,11... | collective-permute-start | bytes 1966088 | tf_op jit(solution)/shard_map/ppermute | solution.py:35
  168.9 7.7 %collective-permute-start.23 = (bf16[80,1024]{1,0:T(8,128)(2,1)S(1)}, bf16[80,1024]{1,0:T(8,128)(2,1)S(1)}, u32[]{:S(2)}, u32[]{:S(2)}) collective-permute-start(bf16[80,1024]{1,0:T(8,128)(2,1)S(1)} %fusion.7), channel_id=1, source_target_pairs={{0,1},{1,0},{2,3},{3,2},{4,5},{5,4},{6,7},{7,6},{8,9},{9,8},{10,11... | collective-permute-start | bytes 491528 | tf_op jit(solution)/shard_map/ppermute | solution.py:35
  172.0 7.2 %collective-permute-start.27 = (bf16[80,1024]{1,0:T(8,128)(2,1)S(1)}, bf16[80,1024]{1,0:T(8,128)(2,1)S(1)}, u32[]{:S(2)}, u32[]{:S(2)}) collective-permute-start(bf16[80,1024]{1,0:T(8,128)(2,1)S(1)} %get-tuple-element.92), channel_id=1, source_target_pairs={{0,6},{1,7},{2,0},{3,1},{4,2},{5,3},{6,4},{7,5},{8,14},{9,15},{10,... | collective-permute-start | bytes 491528 | tf_op jit(solution)/shard_map/ppermute | solution.py:31
  173.1 8.3 %collective-permute-start.26 = (bf16[80,1024]{1,0:T(8,128)(2,1)S(1)}, bf16[80,1024]{1,0:T(8,128)(2,1)S(1)}, u32[]{:S(2)}, u32[]{:S(2)}) collective-permute-start(bf16[80,1024]{1,0:T(8,128)(2,1)S(1)} %get-tuple-element.93), channel_id=1, source_target_pairs={{0,4},{1,5},{2,6},{3,7},{4,0},{5,1},{6,2},{7,3},{8,12},{9,13},{10,... | collective-permute-start | bytes 491528 | tf_op jit(solution)/shard_map/ppermute | solution.py:31
  174.4 8.6 %collective-permute-start.25 = (bf16[80,1024]{1,0:T(8,128)(2,1)S(1)}, bf16[80,1024]{1,0:T(8,128)(2,1)S(1)}, u32[]{:S(2)}, u32[]{:S(2)}) collective-permute-start(bf16[80,1024]{1,0:T(8,128)(2,1)S(1)} %get-tuple-element.91), channel_id=1, source_target_pairs={{0,2},{1,3},{2,4},{3,5},{4,6},{5,7},{6,0},{7,1},{8,10},{9,11},{10,... | collective-permute-start | bytes 491528 | tf_op jit(solution)/shard_map/ppermute | solution.py:31

commit v15 on v13

--- a/solution.py
+++ b/solution.py
@@ -48,7 +48,7 @@
 def slabs_of(qkv_rows, o_rows, groups):
     owned = qkv_rows.shape[0]
     query_cols = HQ * HD
-    each = 2
+    each = 4
     wide, narrow = each * query_cols // groups, each * HK * HD // groups
     keys_at = query_cols // narrow
     values_at = keys_at + HK * HD // narrow

time: 183 us -> 182 us (level)
  no operation moved by 1% of the time
where the time goes in v15:
time: 182 us
  waiting for transfers between devices  99.7 us (55%)
  starting transfers between devices  43.2 us (24%)
  Pallas kernels  33.7 us (19%)
  local copies, waits for them, and re-layouts  2.99 us (2%)
  other arithmetic  1.83 us (1%)
    ppermute x12, waiting for transfers between devices, z_shift(): return lax.ppermute(value, 'fsdp', pairs)  51.8 us
    all_to_all x1, waiting for transfers between devices, body(): both = lax.all_to_all(copy, 'tp', split_axis=0, concat_axis=0, tiled=True)  23.6 us
    ppermute x12, starting transfers between devices, z_shift(): return lax.ppermute(value, 'fsdp', pairs)  21.6 us
    ppermute x6, waiting for transfers between devices, x_shift(): lax.ppermute(value, 'tp', [(t, (t // 2 + k) % NX * 2 + t % 2) for t in ra...  20.9 us
    pallas_call x1, Pallas kernels, attention(): pl.pallas_call(attention_kernel, grid=(rows // GROUP,), out_shape=jax.Sha...  10.7 us
    all_to_all x1, starting transfers between devices, body(): both = lax.all_to_all(copy, 'tp', split_axis=0, concat_axis=0, tiled=True)  7.3 us
    pallas_call x2, Pallas kernels, partials(): pl.pallas_call(functools.partial(partial_kernel, begun), grid=(cols // ti...  6.67 us
    ppermute x6, starting transfers between devices, x_shift(): lax.ppermute(value, 'tp', [(t, (t // 2 + k) % NX * 2 + t % 2) for t in ra...  5.88 us
  transfers between devices with their start and end apart: 29, of which 16 were waited for; matrix products, arithmetic and copies ran while one was open for 2% of the time, Pallas kernels for 15%

profile of v15, /device:TPU:0, one launch (start us, length us, event | category | flops | bytes accessed | tf_op | source)
XLA Modules:
  0.0 181.7 jit_solution(3322557356976670257)
XLA Ops:
  0.0 3.5 %slabs.1 = bf16[8,64,2304]{2,1,0:T(8,128)(2,1)} custom-call(f32[64,10240]{1,0:T(8,128)} %value.1, f32[64,10240]{1,0:T(8,128)} %value.1, f32[64,10240]{1,0:T(8,128)} %value.1, f32[64,8192]{1,0:T(8,128)} %back.1), custom_call_target="tpu_custom_call" | custom-call | bytes 7077888 | tf_op jit(solution)/shard_map/slabs/pallas_call | solution.py:56
  3.5 7.3 %all-to-all-start = ((bf16[8,64,2304]{2,1,0:T(8,128)(2,1)}), bf16[8,64,2304]{2,1,0:T(8,128)(2,1)}, u32[]{:S(2)}, u32[]{:S(2)}) async-start(bf16[8,64,2304]{2,1,0:T(8,128)(2,1)} %slabs.1), calls=%async_computation | async-start | bytes 4718592 | tf_op jit(solution)/shard_map/all_to_all | solution.py:412
  10.8 4.8 %shuffle.1 = (bf16[160,2048]{1,0:T(8,128)(2,1)S(1)}, bf16[160,2048]{1,0:T(8,128)(2,1)}, bf16[160,2048]{1,0:T(8,128)(2,1)}, bf16[160,2048]{1,0:T(8,128)(2,1)}) custom-call(s32[2,128]{1,0:T(2,128)S(1)} %copy-done.1, bf16[160,8192]{1,0:T(8,128)(2,1)S(1)} %bitcast.34), custom_call_target="tpu_custom_call" | custom-call | flops 10485760 | bytes 5242880 | tf_op jit(solution)/shard_map/shuffle/pallas_call | solution.py:105
  15.6 1.9 %collective-permute-start = (bf16[160,2048]{1,0:T(8,128)(2,1)}, bf16[160,2048]{1,0:T(8,128)(2,1)S(1)}, u32[]{:S(2)}, u32[]{:S(2)}) collective-permute-start(bf16[160,2048]{1,0:T(8,128)(2,1)} %get-tuple-element.46), channel_id=1, source_target_pairs={{0,16},{8,24},{16,32},{24,40},{32,48},{40,56},{48,0},{56,8},{64,80... | collective-permute-start | bytes 1966088 | tf_op jit(solution)/shard_map/ppermute | solution.py:23
  17.5 3.6 %collective-permute-start.1 = (bf16[160,2048]{1,0:T(8,128)(2,1)}, bf16[160,2048]{1,0:T(8,128)(2,1)S(1)}, u32[]{:S(2)}, u32[]{:S(2)}) collective-permute-start(bf16[160,2048]{1,0:T(8,128)(2,1)} %get-tuple-element.47), channel_id=1, source_target_pairs={{0,32},{8,40},{16,48},{24,56},{32,0},{40,8},{48,16},{56,24},{64,96... | collective-permute-start | bytes 1966088 | tf_op jit(solution)/shard_map/ppermute | solution.py:23
  22.2 23.6 %all-to-all-done = bf16[8,64,2304]{2,1,0:T(8,128)(2,1)} async-done(((bf16[8,64,2304]{2,1,0:T(8,128)(2,1)}), bf16[8,64,2304]{2,1,0:T(8,128)(2,1)}, u32[]{:S(2)}, u32[]{:S(2)}) %all-to-all-start) | async-done | bytes 2359328 | tf_op jit(solution)/shard_map/all_to_all | solution.py:412
  49.8 2.0 %collective-permute-start.4 = (bf16[512,1024]{1,0:T(8,128)(2,1)S(1)}, bf16[512,1024]{1,0:T(8,128)(2,1)S(1)}, u32[]{:S(2)}, u32[]{:S(2)}) collective-permute-start(bf16[512,1024]{1,0:T(8,128)(2,1)S(1)} %slice.44.refs_0_), channel_id=1, source_target_pairs={{0,16},{8,24},{16,32},{24,40},{32,48},{40,56},{48,0},{56,8},{64,80... | collective-permute-start | bytes 3145736 | tf_op jit(solution)/shard_map/ppermute | solution.py:23
  51.8 2.2 %collective-permute-start.5 = (bf16[512,1024]{1,0:T(8,128)(2,1)S(1)}, bf16[512,1024]{1,0:T(8,128)(2,1)S(1)}, u32[]{:S(2)}, u32[]{:S(2)}) collective-permute-start(bf16[512,1024]{1,0:T(8,128)(2,1)S(1)} %slice.44.refs_0_), channel_id=1, source_target_pairs={{0,48},{8,56},{16,0},{24,8},{32,16},{40,24},{48,32},{56,40},{64,11... | collective-permute-start | bytes 3145736 | tf_op jit(solution)/shard_map/ppermute | solution.py:23
  54.0 3.2 %partials.1 = (f32[160,1280]{1,0:T(8,128)S(1)}, f32[160,1280]{1,0:T(8,128)S(1)}, f32[160,1280]{1,0:T(8,128)S(1)}, f32[160,1280]{1,0:T(8,128)S(1)}) custom-call(bf16[160,2048]{1,0:T(8,128)(2,1)S(1)} %get-tuple-element.49.refs_0_, bf16[160,2048]{1,0:T(8,128)(2,1)S(1)} %collective-permute-done.refs_1_, bf16[160,2048]{1,0:T(8,128)(2,1)S(1)} %collective-permute-done.1.refs_2_, ...), custom_call_target="tpu_custom_call" | custom-call | flops 1677721600 | bytes 7208960 | tf_op jit(solution)/shard_map/partials/pallas_call | solution.py:152
  57.3 20.2 %collective-permute-done.4.refs_1_ = bf16[512,1024]{1,0:T(8,128)(2,1)S(1)} collective-permute-done((bf16[512,1024]{1,0:T(8,128)(2,1)S(1)}, bf16[512,1024]{1,0:T(8,128)(2,1)S(1)}, u32[]{:S(2)}, u32[]{:S(2)}) %collective-permute-start.4) | collective-permute-done | bytes 1048608 | tf_op jit(solution)/shard_map/ppermute | solution.py:23
  79.1 4.0 %collective-permute-start.12 = (bf16[256,1024]{1,0:T(8,128)(2,1)S(1)}, bf16[256,1024]{1,0:T(8,128)(2,1)S(1)}, u32[]{:S(2)}, u32[]{:S(2)}) collective-permute-start(bf16[256,1024]{1,0:T(8,128)(2,1)S(1)} %slice.36), channel_id=1, source_target_pairs={{0,48},{8,56},{16,0},{24,8},{32,16},{40,24},{48,32},{56,40},{64,11... | collective-permute-start | bytes 1572872 | tf_op jit(solution)/shard_map/ppermute | solution.py:23
  83.2 3.5 %partials_rest.1 = (f32[160,1280]{1,0:T(8,128)S(1)}, bf16[160,1280]{1,0:T(8,128)(2,1)S(1)}, bf16[160,1280]{1,0:T(8,128)(2,1)S(1)}, bf16[160,1280]{1,0:T(8,128)(2,1)S(1)}) custom-call(bf16[160,2048]{1,0:T(8,128)(2,1)S(1)} %get-tuple-element.49.refs_0_, bf16[160,2048]{1,0:T(8,128)(2,1)S(1)} %collective-permute-done.refs_1_, ...), custom_call_target="tpu_custom_call" | custom-call | flops 1677721600 | bytes 7208960 | tf_op jit(solution)/shard_map/partials_rest/pallas_call | solution.py:152
  86.6 3.3 %collective-permute-start.8 = (bf16[160,1280]{1,0:T(8,128)(2,1)S(1)}, bf16[160,1280]{1,0:T(8,128)(2,1)S(1)}, u32[]{:S(2)}, u32[]{:S(2)}) collective-permute-start(bf16[160,1280]{1,0:T(8,128)(2,1)S(1)} %get-tuple-element.66), channel_id=1, source_target_pairs={{0,48},{8,56},{16,0},{24,8},{32,16},{40,24},{48,32},{56,40},{64,11... | collective-permute-start | bytes 1228808 | tf_op jit(solution)/shard_map/ppermute | solution.py:23
  90.0 5.5 %collective-permute-done.12 = bf16[256,1024]{1,0:T(8,128)(2,1)S(1)} collective-permute-done((bf16[256,1024]{1,0:T(8,128)(2,1)S(1)}, bf16[256,1024]{1,0:T(8,128)(2,1)S(1)}, u32[]{:S(2)}, u32[]{:S(2)}) %collective-permute-start.12) | collective-permute-done | bytes 524320 | tf_op jit(solution)/shard_map/ppermute | solution.py:23
  95.8 12.2 %collective-permute-done.13 = bf16[256,1024]{1,0:T(8,128)(2,1)S(1)} collective-permute-done((bf16[256,1024]{1,0:T(8,128)(2,1)S(1)}, bf16[256,1024]{1,0:T(8,128)(2,1)S(1)}, u32[]{:S(2)}, u32[]{:S(2)}) %collective-permute-start.13) | collective-permute-done | bytes 524320 | tf_op jit(solution)/shard_map/ppermute | solution.py:23
  109.5 2.8 %collective-permute-done.8.p1 = bf16[160,1280]{1,0:T(8,128)(2,1)S(1)} collective-permute-done((bf16[160,1280]{1,0:T(8,128)(2,1)S(1)}, bf16[160,1280]{1,0:T(8,128)(2,1)S(1)}, u32[]{:S(2)}, u32[]{:S(2)}) %collective-permute-start.8) | collective-permute-done | bytes 409632 | tf_op jit(solution)/shard_map/ppermute | solution.py:23
  112.3 3.4 %collective-permute-done.10.p3 = bf16[160,1280]{1,0:T(8,128)(2,1)S(1)} collective-permute-done((bf16[160,1280]{1,0:T(8,128)(2,1)S(1)}, bf16[160,1280]{1,0:T(8,128)(2,1)S(1)}, u32[]{:S(2)}, u32[]{:S(2)}) %collective-permute-start.10) | collective-permute-done | bytes 409632 | tf_op jit(solution)/shard_map/ppermute | solution.py:23
  115.7 3.2 %collective-permute-start.17 = (bf16[512,1024]{1,0:T(8,128)(2,1)S(1)}, bf16[512,1024]{1,0:T(8,128)(2,1)S(1)}, u32[]{:S(2)}, u32[]{:S(2)}) collective-permute-start(bf16[512,1024]{1,0:T(8,128)(2,1)S(1)} %collective-permute-done.14.refs_3_), channel_id=1, source_target_pairs={{0,48},{8,56},{16,0},{24,8},{32,16},{40,24},{48,32},{56,40},{64,11... | collective-permute-start | bytes 3145736 | tf_op jit(solution)/shard_map/ppermute | solution.py:23
  119.0 10.7 %attention.1.mixed_ref = bf16[160,1024]{1,0:T(8,128)(2,1)S(1)} custom-call(s32[80]{0:T(128)S(1)} %copy-done.2, f32[160,1280]{1,0:T(8,128)S(1)} %get-tuple-element.65.p0, bf16[160,1280]{1,0:T(8,128)(2,1)S(1)} %collective-permute-done.8.p1, bf16[160,1280]{1,0:T(8,128)(2,1)S(1)} %collective-permute-done.9.p2, bf16[160,1280]{1,0:T(8,128)(2,1)S(1)} %collective-permute-done.10.p3, ...), custom_call_target="tpu_custom_call" | custom-call | flops 167772160 | bytes 41943040 | tf_op jit(solution)/shard_map/attention/pallas_call | solution.py:370
  129.9 1.6 collective-permute-done.11.mixed_ref
  131.6 1.6 terms.3
  133.4 7.7 %collective-permute-done.16.refs_1_.refs_6_ = bf16[512,1024]{1,0:T(8,128)(2,1)S(1)} collective-permute-done((bf16[512,1024]{1,0:T(8,128)(2,1)S(1)}, bf16[512,1024]{1,0:T(8,128)(2,1)S(1)}, u32[]{:S(2)}, u32[]{:S(2)}) %collective-permute-start.16) | collective-permute-done | bytes 1048608 | tf_op jit(solution)/shard_map/ppermute | solution.py:23
  142.3 2.4 %terms.5.refs_0_ = bf16[4096,256]{1,0:T(8,128)(2,1)S(1)} custom-call(bf16[160,1024]{1,0:T(8,128)(2,1)S(1)} %attention.1.mixed_ref, bf16[512,1024]{1,0:T(8,128)(2,1)S(1)} %slice.44.refs_0_, bf16[512,1024]{1,0:T(8,128)(2,1)S(1)} %collective-permute-done.4.refs_1_, bf16[512,1024]{1,0:T(8,128)(2,1)S(1)} %collective-permute-done.5.refs_2_, ...), custom_call_target="tpu_custom_call" | custom-call | bytes 160 | tf_op jit(solution)/shard_map/terms/pallas_call | solution.py:198
  144.8 2.9 %place.1 = (bf16[2,80,1024]{2,1,0:T(8,128)(2,1)S(1)}, bf16[2,80,1024]{2,1,0:T(8,128)(2,1)S(1)}, bf16[2,80,1024]{2,1,0:T(8,128)(2,1)S(1)}, bf16[2,80,1024]{2,1,0:...) custom-call(s32[2,128]{1,0:T(2,128)S(1)} %copy-done.1, ...), custom_call_target="tpu_custom_call" | custom-call | bytes 5242880 | tf_op jit(solution)/shard_map/place/pallas_call | solution.py:241
  149.8 2.2 %collective-permute-start.24 = (bf16[4,80,1024]{2,1,0:T(8,128)(2,1)S(1)}, bf16[4,80,1024]{2,1,0:T(8,128)(2,1)S(1)}, u32[]{:S(2)}, u32[]{:S(2)}) collective-permute-start(bf16[4,80,1024]{2,1,0:T(8,128)(2,1)S(1)} %get-tuple-element.84), channel_id=1, source_target_pairs={{0,1},{1,0},{2,3},{3,2},{4,5},{5,4},{6,7},{7,6},{8,9},{9,8},{10,11... | collective-permute-start | bytes 1966088 | tf_op jit(solution)/shard_map/ppermute | solution.py:35
  152.0 6.3 %collective-permute-done.22 = bf16[2,80,1024]{2,1,0:T(8,128)(2,1)S(1)} collective-permute-done((bf16[2,80,1024]{2,1,0:T(8,128)(2,1)S(1)}, bf16[2,80,1024]{2,1,0:T(8,128)(2,1)S(1)}, u32[]{:S(2)}, u32[]{:S(2)}) %collective-permute-start.22) | collective-permute-done | bytes 327712 | tf_op jit(solution)/shard_map/ppermute | solution.py:31
  158.2 1.6 collective-permute-done.21
  159.9 6.6 %collective-permute-done.20 = bf16[2,80,1024]{2,1,0:T(8,128)(2,1)S(1)} collective-permute-done((bf16[2,80,1024]{2,1,0:T(8,128)(2,1)S(1)}, bf16[2,80,1024]{2,1,0:T(8,128)(2,1)S(1)}, u32[]{:S(2)}, u32[]{:S(2)}) %collective-permute-start.20) | collective-permute-done | bytes 327712 | tf_op jit(solution)/shard_map/ppermute | solution.py:31
  166.7 2.7 %collective-permute-start.23 = (bf16[80,1024]{1,0:T(8,128)(2,1)S(1)}, bf16[80,1024]{1,0:T(8,128)(2,1)S(1)}, u32[]{:S(2)}, u32[]{:S(2)}) collective-permute-start(bf16[80,1024]{1,0:T(8,128)(2,1)S(1)} %fusion.7), channel_id=1, source_target_pairs={{0,1},{1,0},{2,3},{3,2},{4,5},{5,4},{6,7},{7,6},{8,9},{9,8},{10,11... | collective-permute-start | bytes 491528 | tf_op jit(solution)/shard_map/ppermute | solution.py:35
  174.5 2.4 %collective-permute-done.27 = bf16[80,1024]{1,0:T(8,128)(2,1)S(1)} collective-permute-done((bf16[80,1024]{1,0:T(8,128)(2,1)S(1)}, bf16[80,1024]{1,0:T(8,128)(2,1)S(1)}, u32[]{:S(2)}, u32[]{:S(2)}) %collective-permute-start.27) | collective-permute-done | bytes 163872 | tf_op jit(solution)/shard_map/ppermute | solution.py:31
  176.9 2.4 %collective-permute-done.26 = bf16[80,1024]{1,0:T(8,128)(2,1)S(1)} collective-permute-done((bf16[80,1024]{1,0:T(8,128)(2,1)S(1)}, bf16[80,1024]{1,0:T(8,128)(2,1)S(1)}, u32[]{:S(2)}, u32[]{:S(2)}) %collective-permute-start.26) | collective-permute-done | bytes 163872 | tf_op jit(solution)/shard_map/ppermute | solution.py:31
  179.3 1.6 collective-permute-done.25
  (59 shorter events, 18.6 us)
Async XLA Ops:
  3.5 7.3 %copy-start = (bf16[2,80,8192]{2,1,0:T(8,128)(2,1)S(1)}, bf16[2,80,8192]{2,1,0:T(8,128)(2,1)}, u32[]{:S(2)}) copy-start(bf16[2,80,8192]{2,1,0:T(8,128)(2,1)} %param.6) | copy-start | bytes 7864324
  3.5 7.3 %copy-start.1 = (s32[2,128]{1,0:T(2,128)S(1)}, s32[2,128]{1,0:T(2,128)}, u32[]{:S(2)}) copy-start(s32[2,128]{1,0:T(2,128)} %owner_ref.3) | copy-start | bytes 3076
  3.5 42.3 %all-to-all-start = ((bf16[8,64,2304]{2,1,0:T(8,128)(2,1)}), bf16[8,64,2304]{2,1,0:T(8,128)(2,1)}, u32[]{:S(2)}, u32[]{:S(2)}) async-start(bf16[8,64,2304]{2,1,0:T(8,128)(2,1)} %slabs.1), calls=%async_computation | async-start | bytes 4718592 | tf_op jit(solution)/shard_map/all_to_all | solution.py:412
  10.8 11.3 %copy-start.2 = (s32[80]{0:T(128)S(1)}, s32[80]{0:T(128)}, u32[]{:S(2)}) copy-start(s32[80]{0:T(128)} %lengths_ref.1) | copy-start | bytes 964
  15.6 34.2 %collective-permute-start = (bf16[160,2048]{1,0:T(8,128)(2,1)}, bf16[160,2048]{1,0:T(8,128)(2,1)S(1)}, u32[]{:S(2)}, u32[]{:S(2)}) collective-permute-start(bf16[160,2048]{1,0:T(8,128)(2,1)} %get-tuple-element.46), channel_id=1, source_target_pairs={{0,16},{8,24},{16,32},{24,40},{32,48},{40,56},{48,0},{56,8},{64,80... | collective-permute-start | bytes 1966088 | tf_op jit(solution)/shard_map/ppermute | solution.py:23
  17.5 32.3 %collective-permute-start.1 = (bf16[160,2048]{1,0:T(8,128)(2,1)}, bf16[160,2048]{1,0:T(8,128)(2,1)S(1)}, u32[]{:S(2)}, u32[]{:S(2)}) collective-permute-start(bf16[160,2048]{1,0:T(8,128)(2,1)} %get-tuple-element.47), channel_id=1, source_target_pairs={{0,32},{8,40},{16,48},{24,56},{32,0},{40,8},{48,16},{56,24},{64,96... | collective-permute-start | bytes 1966088 | tf_op jit(solution)/shard_map/ppermute | solution.py:23
  21.1 28.7 %collective-permute-start.2 = (bf16[160,2048]{1,0:T(8,128)(2,1)}, bf16[160,2048]{1,0:T(8,128)(2,1)S(1)}, u32[]{:S(2)}, u32[]{:S(2)}) collective-permute-start(bf16[160,2048]{1,0:T(8,128)(2,1)} %get-tuple-element.48), channel_id=1, source_target_pairs={{0,48},{8,56},{16,0},{24,8},{32,16},{40,24},{48,32},{56,40},{64,11... | collective-permute-start | bytes 1966088 | tf_op jit(solution)/shard_map/ppermute | solution.py:23
  47.2 6.9 %collective-permute-start.6 = (bf16[512,1280]{1,0:T(8,128)(2,1)S(1)}, bf16[512,1280]{1,0:T(8,128)(2,1)S(1)}, u32[]{:S(2)}, u32[]{:S(2)}) collective-permute-start(bf16[512,1280]{1,0:T(8,128)(2,1)S(1)} %slice.45.refs_4_), channel_id=1, source_target_pairs={{0,8},{8,0},{16,24},{24,16},{32,40},{40,32},{48,56},{56,48},{64,72... | collective-permute-start | bytes 3932168 | tf_op jit(solution)/shard_map/ppermute | solution.py:27
  47.3 31.2 %collective-permute-start.3 = (bf16[512,1280]{1,0:T(8,128)(2,1)S(1)}, bf16[512,1280]{1,0:T(8,128)(2,1)S(1)}, u32[]{:S(2)}, u32[]{:S(2)}) collective-permute-start(bf16[512,1280]{1,0:T(8,128)(2,1)S(1)} %slice.45.refs_4_), channel_id=1, source_target_pairs={{0,64},{8,72},{16,80},{24,88},{32,96},{40,104},{48,112},{56,120},{... | collective-permute-start | bytes 3932168 | tf_op jit(solution)/shard_map/ppermute | solution.py:27
  49.8 27.6 %collective-permute-start.4 = (bf16[512,1024]{1,0:T(8,128)(2,1)S(1)}, bf16[512,1024]{1,0:T(8,128)(2,1)S(1)}, u32[]{:S(2)}, u32[]{:S(2)}) collective-permute-start(bf16[512,1024]{1,0:T(8,128)(2,1)S(1)} %slice.44.refs_0_), channel_id=1, source_target_pairs={{0,16},{8,24},{16,32},{24,40},{32,48},{40,56},{48,0},{56,8},{64,80... | collective-permute-start | bytes 3145736 | tf_op jit(solution)/shard_map/ppermute | solution.py:23
  51.8 25.6 %collective-permute-start.5 = (bf16[512,1024]{1,0:T(8,128)(2,1)S(1)}, bf16[512,1024]{1,0:T(8,128)(2,1)S(1)}, u32[]{:S(2)}, u32[]{:S(2)}) collective-permute-start(bf16[512,1024]{1,0:T(8,128)(2,1)S(1)} %slice.44.refs_0_), channel_id=1, source_target_pairs={{0,48},{8,56},{16,0},{24,8},{32,16},{40,24},{48,32},{56,40},{64,11... | collective-permute-start | bytes 3145736 | tf_op jit(solution)/shard_map/ppermute | solution.py:23
  78.5 4.7 %collective-permute-start.7 = (bf16[512,1280]{1,0:T(8,128)(2,1)S(1)}, bf16[512,1280]{1,0:T(8,128)(2,1)S(1)}, u32[]{:S(2)}, u32[]{:S(2)}) collective-permute-start(bf16[512,1280]{1,0:T(8,128)(2,1)S(1)} %collective-permute-done.3.refs_4_), channel_id=1, source_target_pairs={{0,8},{8,0},{16,24},{24,16},{32,40},{40,32},{48,56},{56,48},{64,72... | collective-permute-start | bytes 3932168 | tf_op jit(solution)/shard_map/ppermute | solution.py:27
  78.5 29.5 %collective-permute-start.14 = (bf16[512,1024]{1,0:T(8,128)(2,1)S(1)}, bf16[512,1024]{1,0:T(8,128)(2,1)S(1)}, u32[]{:S(2)}, u32[]{:S(2)}) collective-permute-start(bf16[512,1024]{1,0:T(8,128)(2,1)S(1)} %slice.44.refs_0_), channel_id=1, source_target_pairs={{0,64},{8,72},{16,80},{24,88},{32,96},{40,104},{48,112},{56,120},{... | collective-permute-start | bytes 3145736 | tf_op jit(solution)/shard_map/ppermute | solution.py:27
  79.1 16.3 %collective-permute-start.12 = (bf16[256,1024]{1,0:T(8,128)(2,1)S(1)}, bf16[256,1024]{1,0:T(8,128)(2,1)S(1)}, u32[]{:S(2)}, u32[]{:S(2)}) collective-permute-start(bf16[256,1024]{1,0:T(8,128)(2,1)S(1)} %slice.36), channel_id=1, source_target_pairs={{0,48},{8,56},{16,0},{24,8},{32,16},{40,24},{48,32},{56,40},{64,11... | collective-permute-start | bytes 1572872 | tf_op jit(solution)/shard_map/ppermute | solution.py:23
  83.2 24.8 %collective-permute-start.13 = (bf16[256,1024]{1,0:T(8,128)(2,1)S(1)}, bf16[256,1024]{1,0:T(8,128)(2,1)S(1)}, u32[]{:S(2)}, u32[]{:S(2)}) collective-permute-start(bf16[256,1024]{1,0:T(8,128)(2,1)S(1)} %slice.37), channel_id=1, source_target_pairs={{0,16},{8,24},{16,32},{24,40},{32,48},{40,56},{48,0},{56,8},{64,80... | collective-permute-start | bytes 1572872 | tf_op jit(solution)/shard_map/ppermute | solution.py:23
  86.6 25.7 %collective-permute-start.8 = (bf16[160,1280]{1,0:T(8,128)(2,1)S(1)}, bf16[160,1280]{1,0:T(8,128)(2,1)S(1)}, u32[]{:S(2)}, u32[]{:S(2)}) collective-permute-start(bf16[160,1280]{1,0:T(8,128)(2,1)S(1)} %get-tuple-element.66), channel_id=1, source_target_pairs={{0,48},{8,56},{16,0},{24,8},{32,16},{40,24},{48,32},{56,40},{64,11... | collective-permute-start | bytes 1228808 | tf_op jit(solution)/shard_map/ppermute | solution.py:23
  89.9 22.4 %collective-permute-start.9 = (bf16[160,1280]{1,0:T(8,128)(2,1)S(1)}, bf16[160,1280]{1,0:T(8,128)(2,1)S(1)}, u32[]{:S(2)}, u32[]{:S(2)}) collective-permute-start(bf16[160,1280]{1,0:T(8,128)(2,1)S(1)} %get-tuple-element.67), channel_id=1, source_target_pairs={{0,32},{8,40},{16,48},{24,56},{32,0},{40,8},{48,16},{56,24},{64,96... | collective-permute-start | bytes 1228808 | tf_op jit(solution)/shard_map/ppermute | solution.py:23
  95.5 20.3 %collective-permute-start.10 = (bf16[160,1280]{1,0:T(8,128)(2,1)S(1)}, bf16[160,1280]{1,0:T(8,128)(2,1)S(1)}, u32[]{:S(2)}, u32[]{:S(2)}) collective-permute-start(bf16[160,1280]{1,0:T(8,128)(2,1)S(1)} %get-tuple-element.68), channel_id=1, source_target_pairs={{0,16},{8,24},{16,32},{24,40},{32,48},{40,56},{48,0},{56,8},{64,80... | collective-permute-start | bytes 1228808 | tf_op jit(solution)/shard_map/ppermute | solution.py:23
  108.1 25.4 %collective-permute-start.15 = (bf16[512,1024]{1,0:T(8,128)(2,1)S(1)}, bf16[512,1024]{1,0:T(8,128)(2,1)S(1)}, u32[]{:S(2)}, u32[]{:S(2)}) collective-permute-start(bf16[512,1024]{1,0:T(8,128)(2,1)S(1)} %constant_dynamic-update-slice_fusion.refs_4_), channel_id=1, source_target_pairs={{0,64},{8,72},{16,80},{24,88},{32,96},{40,104},{48,112},{56,120},{... | collective-permute-start | bytes 3145736 | tf_op jit(solution)/shard_map/ppermute | solution.py:27
  115.7 25.4 %collective-permute-start.16 = (bf16[512,1024]{1,0:T(8,128)(2,1)S(1)}, bf16[512,1024]{1,0:T(8,128)(2,1)S(1)}, u32[]{:S(2)}, u32[]{:S(2)}) collective-permute-start(bf16[512,1024]{1,0:T(8,128)(2,1)S(1)} %collective-permute-done.14.refs_3_), channel_id=1, source_target_pairs={{0,16},{8,24},{16,32},{24,40},{32,48},{40,56},{48,0},{56,8},{64,80... | collective-permute-start | bytes 3145736 | tf_op jit(solution)/shard_map/ppermute | solution.py:23
  115.7 25.4 %collective-permute-start.17 = (bf16[512,1024]{1,0:T(8,128)(2,1)S(1)}, bf16[512,1024]{1,0:T(8,128)(2,1)S(1)}, u32[]{:S(2)}, u32[]{:S(2)}) collective-permute-start(bf16[512,1024]{1,0:T(8,128)(2,1)S(1)} %collective-permute-done.14.refs_3_), channel_id=1, source_target_pairs={{0,48},{8,56},{16,0},{24,8},{32,16},{40,24},{48,32},{56,40},{64,11... | collective-permute-start | bytes 3145736 | tf_op jit(solution)/shard_map/ppermute | solution.py:23
  129.7 1.9 %collective-permute-start.11 = (bf16[160,1024]{1,0:T(8,128)(2,1)S(1)}, bf16[160,1024]{1,0:T(8,128)(2,1)S(1)}, u32[]{:S(2)}, u32[]{:S(2)}) collective-permute-start(bf16[160,1024]{1,0:T(8,128)(2,1)S(1)} %attention.1.mixed_ref), channel_id=1, source_target_pairs={{0,8},{8,0},{16,24},{24,16},{32,40},{40,32},{48,56},{56,48},{64,72... | collective-permute-start | bytes 983048 | tf_op jit(solution)/shard_map/ppermute | solution.py:27
  133.2 11.5 %collective-permute-start.18 = (bf16[2560,256]{1,0:T(8,128)(2,1)S(1)}, bf16[2560,256]{1,0:T(8,128)(2,1)S(1)}, u32[]{:S(2)}, u32[]{:S(2)}) collective-permute-start(bf16[2560,256]{1,0:T(8,128)(2,1)S(1)} %terms.3), channel_id=1, source_target_pairs={{0,8},{8,0},{16,24},{24,16},{32,40},{40,32},{48,56},{56,48},{64,72... | collective-permute-start | bytes 3932168 | tf_op jit(solution)/shard_map/ppermute | solution.py:27
  142.2 2.6 %collective-permute-start.19 = (bf16[1536,256]{1,0:T(8,128)(2,1)S(1)}, bf16[1536,256]{1,0:T(8,128)(2,1)S(1)}, u32[]{:S(2)}, u32[]{:S(2)}) collective-permute-start(bf16[1536,256]{1,0:T(8,128)(2,1)S(1)} %terms.4), channel_id=1, source_target_pairs={{0,8},{8,0},{16,24},{24,16},{32,40},{40,32},{48,56},{56,48},{64,72... | collective-permute-start | bytes 2359304 | tf_op jit(solution)/shard_map/ppermute | solution.py:27
  147.7 10.6 %collective-permute-start.22 = (bf16[2,80,1024]{2,1,0:T(8,128)(2,1)S(1)}, bf16[2,80,1024]{2,1,0:T(8,128)(2,1)S(1)}, u32[]{:S(2)}, u32[]{:S(2)}) collective-permute-start(bf16[2,80,1024]{2,1,0:T(8,128)(2,1)S(1)} %get-tuple-element.82), channel_id=1, source_target_pairs={{0,6},{1,7},{2,0},{3,1},{4,2},{5,3},{6,4},{7,5},{8,14},{9,15},{10,... | collective-permute-start | bytes 983048 | tf_op jit(solution)/shard_map/ppermute | solution.py:31
  147.8 12.1 %collective-permute-start.21 = (bf16[2,80,1024]{2,1,0:T(8,128)(2,1)S(1)}, bf16[2,80,1024]{2,1,0:T(8,128)(2,1)S(1)}, u32[]{:S(2)}, u32[]{:S(2)}) collective-permute-start(bf16[2,80,1024]{2,1,0:T(8,128)(2,1)S(1)} %get-tuple-element.81), channel_id=1, source_target_pairs={{0,4},{1,5},{2,6},{3,7},{4,0},{5,1},{6,2},{7,3},{8,12},{9,13},{10,... | collective-permute-start | bytes 983048 | tf_op jit(solution)/shard_map/ppermute | solution.py:31
  148.9 17.6 %collective-permute-start.20 = (bf16[2,80,1024]{2,1,0:T(8,128)(2,1)S(1)}, bf16[2,80,1024]{2,1,0:T(8,128)(2,1)S(1)}, u32[]{:S(2)}, u32[]{:S(2)}) collective-permute-start(bf16[2,80,1024]{2,1,0:T(8,128)(2,1)S(1)} %get-tuple-element.80), channel_id=1, source_target_pairs={{0,2},{1,3},{2,4},{3,5},{4,6},{5,7},{6,0},{7,1},{8,10},{9,11},{10,... | collective-permute-start | bytes 983048 | tf_op jit(solution)/shard_map/ppermute | solution.py:31
  149.8 19.6 %collective-permute-start.24 = (bf16[4,80,1024]{2,1,0:T(8,128)(2,1)S(1)}, bf16[4,80,1024]{2,1,0:T(8,128)(2,1)S(1)}, u32[]{:S(2)}, u32[]{:S(2)}) collective-permute-start(bf16[4,80,1024]{2,1,0:T(8,128)(2,1)S(1)} %get-tuple-element.84), channel_id=1, source_target_pairs={{0,1},{1,0},{2,3},{3,2},{4,5},{5,4},{6,7},{7,6},{8,9},{9,8},{10,11... | collective-permute-start | bytes 1966088 | tf_op jit(solution)/shard_map/ppermute | solution.py:35
  166.7 7.7 %collective-permute-start.23 = (bf16[80,1024]{1,0:T(8,128)(2,1)S(1)}, bf16[80,1024]{1,0:T(8,128)(2,1)S(1)}, u32[]{:S(2)}, u32[]{:S(2)}) collective-permute-start(bf16[80,1024]{1,0:T(8,128)(2,1)S(1)} %fusion.7), channel_id=1, source_target_pairs={{0,1},{1,0},{2,3},{3,2},{4,5},{5,4},{6,7},{7,6},{8,9},{9,8},{10,11... | collective-permute-start | bytes 491528 | tf_op jit(solution)/shard_map/ppermute | solution.py:35
  169.7 7.2 %collective-permute-start.27 = (bf16[80,1024]{1,0:T(8,128)(2,1)S(1)}, bf16[80,1024]{1,0:T(8,128)(2,1)S(1)}, u32[]{:S(2)}, u32[]{:S(2)}) collective-permute-start(bf16[80,1024]{1,0:T(8,128)(2,1)S(1)} %get-tuple-element.88), channel_id=1, source_target_pairs={{0,6},{1,7},{2,0},{3,1},{4,2},{5,3},{6,4},{7,5},{8,14},{9,15},{10,... | collective-permute-start | bytes 491528 | tf_op jit(solution)/shard_map/ppermute | solution.py:31
  170.9 8.4 %collective-permute-start.26 = (bf16[80,1024]{1,0:T(8,128)(2,1)S(1)}, bf16[80,1024]{1,0:T(8,128)(2,1)S(1)}, u32[]{:S(2)}, u32[]{:S(2)}) collective-permute-start(bf16[80,1024]{1,0:T(8,128)(2,1)S(1)} %get-tuple-element.89), channel_id=1, source_target_pairs={{0,4},{1,5},{2,6},{3,7},{4,0},{5,1},{6,2},{7,3},{8,12},{9,13},{10,... | collective-permute-start | bytes 491528 | tf_op jit(solution)/shard_map/ppermute | solution.py:31
  172.2 8.6 %collective-permute-start.25 = (bf16[80,1024]{1,0:T(8,128)(2,1)S(1)}, bf16[80,1024]{1,0:T(8,128)(2,1)S(1)}, u32[]{:S(2)}, u32[]{:S(2)}) collective-permute-start(bf16[80,1024]{1,0:T(8,128)(2,1)S(1)} %get-tuple-element.87), channel_id=1, source_target_pairs={{0,2},{1,3},{2,4},{3,5},{4,6},{5,7},{6,0},{7,1},{8,10},{9,11},{10,... | collective-permute-start | bytes 491528 | tf_op jit(solution)/shard_map/ppermute | solution.py:31
